TPU v7x, 512 devices: a whole 4x4x16 slice. The times are simulated.
512 devices in a mesh: row: 32 (over z, core), col: 16 (over y, x).
Axes of the slice: x: 4, y: 4, z: 16, core: 2. Of those that a mesh axis runs over, the one named last changes fastest.
Arguments:
- flow_tiles: bfloat16 [32, 32, 256, 256], P('row', 'col'), may hold values from 0.1 to 25
- tile_cols: int32 [32, 32], P('row', 'col'), may hold values from -1 to 31, as said below
- pairs: int32 [32768, 2], P(('row', 'col')), may hold values from -1 to 31, as said below
Outputs:
- new_flow: float32 [32, 32, 256, 256], P('row', 'col')
Inputs may be any that keep to these rules, and one draw needn't show every extreme that they name: `tile_cols`: the stored slots of device (r, c) have distinct tile columns, each congruent to c modulo the col axis's size; tile row r stores tile column r. `pairs`: device (r, c) lists, in some order and without repeats, exactly the (k, s) for which slot s of the device is stored and M[r, k] and M[k, tile_cols[r, c * 2 + s]] are both stored tiles; its other rows are (-1, -1). Some device uses all 64 rows.
All inputs are finite; a program needn't handle non-finite values.
Results may differ from a plain program's by a relative error of at most 0.0003.
Values may be sent and summed in bfloat16 or wider, within the bound.
No kernel may reach another device: no remote copies, remote signals or barrier semaphores. Data moves between devices by JAX's collectives and lax.ppermute only.
A program may use at most 64 MiB of HBM per device.

v0:
```python
import jax
import jax.numpy as jnp
from jax import lax
from jax.sharding import PartitionSpec as P


def copy_for_each(shard, axis):
    length = lax.axis_size(axis)
    return lax.all_to_all(
        jnp.broadcast_to(shard[None], (length, *shard.shape)), axis, 0, 0, tiled=True
    )


def over_copies(shard, axis):
    return copy_for_each(shard, axis).sum(axis=0)


def block_products(
    initial, left_source, right_source, left_index, right_row, right_slot, weight, groups
):
    tile_count = weight.shape[1]
    left_index = left_index.reshape(groups, -1)
    right_row = right_row.reshape(groups, -1)
    right_slot = right_slot.reshape(groups, -1)
    weight = weight.reshape(groups, -1, tile_count)

    def block_step(carried, inputs):
        left_pick, row_pick, slot_pick, weight_block = inputs
        left_tiles = left_source[left_pick]
        right_tiles = right_source[row_pick, slot_pick]
        products = jnp.einsum(
            "pab,pbc->pac", left_tiles, right_tiles, preferred_element_type=jnp.float32
        )
        added = jnp.einsum("ps,pac->sac", weight_block, products, precision=lax.Precision.HIGHEST)
        return (carried + added, None)

    result, unused = lax.scan(block_step, initial, (left_index, right_row, right_slot, weight))
    return result


def on_device(flow_tiles, tile_cols, pairs):
    tile_count = flow_tiles.shape[1]
    tile_width = flow_tiles.shape[3]
    col_count = lax.axis_size("col")
    rows_total = lax.axis_size("row") * tile_width
    col_index = lax.axis_index("col")
    row_tiles, row_cols = (
        lax.all_gather(flow_tiles, "col", axis=1, tiled=True),
        lax.all_gather(tile_cols, "col", axis=1, tiled=True),
    )
    own_cols = tile_cols[0]
    inner_tile = pairs[:, 0]
    slot_list = pairs[:, 1]
    is_live = inner_tile >= 0
    inner_safe = jnp.maximum(inner_tile, 0)
    slot_safe = jnp.maximum(slot_list, 0)
    wanted = own_cols[slot_safe]
    left_index = jnp.argmax(row_cols[0][None, :] == inner_safe[:, None], axis=1)
    slot_ids = jnp.arange(tile_count, dtype=jnp.int32)
    weight = (is_live[:, None] & (slot_list[:, None] == slot_ids[None, :])).astype(jnp.float32)
    initial = jnp.zeros((tile_count, tile_width, tile_width), jnp.float32)
    column_tiles, column_cols = (
        lax.all_gather(flow_tiles, "row", axis=0, tiled=True),
        lax.all_gather(tile_cols, "row", axis=0, tiled=True),
    )
    right_slot = jnp.argmax(column_cols[inner_safe] == wanted[:, None], axis=1)
    expanded = block_products(
        initial, row_tiles[0], column_tiles, left_index, inner_safe, right_slot, weight, 4
    )
    inflated = expanded * expanded
    partial_sums = jnp.sum(inflated, axis=1)
    targets = col_index + col_count * slot_ids
    matches = own_cols[None, :] == targets[:, None]
    canonical = jnp.sum(jnp.where(matches[:, :, None], partial_sums[None, :, :], 0.0), axis=1)
    totals = over_copies(canonical, "row")
    per_slot = jnp.sum(jnp.where(matches[:, :, None], totals[:, None, :], 0.0), axis=0)
    stored = own_cols >= 0
    per_slot = jnp.where(stored[:, None], per_slot, 1.0)
    normed = inflated * jnp.float32(rows_total) / per_slot[:, None, :]
    blended = 0.5 * flow_tiles[0].astype(jnp.float32) + 0.5 * normed
    blended = jnp.where(stored[:, None, None], blended, 0.0)
    return blended[None]


def solution(mesh):
    placed = (P("row", "col", None, None), P("row", "col"), P(("row", "col"), None))
    return jax.shard_map(
        on_device,
        mesh=mesh,
        in_specs=placed,
        out_specs=P("row", "col", None, None),
        check_vma=False,
    )
```

profile of v0, /device:TPU:1, one launch (start us, length us, event | category | flops | bytes accessed | tf_op | source)
XLA Modules:
  0.0 273.2 jit_solution(3193878392183024058)
XLA Ops:
  6.5 0.0 all-gather.4.cloned.1.call-start
  6.5 0.7 all-gather.4.cloned.1.call-update
  7.3 0.0 all-gather.6.cloned.1.call-start
  7.3 0.7 all-gather.6.cloned.1.call-update
  8.0 37.5 %all-gather = s32[32,1,2]{2,1,0:T(1,128)S(1)} all-gather(s32[1,1,2]{2,1,0:T(1,128)} %bitcast.62), channel_id=1, replica_groups=mesh['row'=32,'col'=16] {'row'}, dimensions={0}, use_global_device_ids=true | all-gather | bytes 264 | tf_op jit(solution)/shard_map/all_gather | solution.py:64
  45.5 1.3 fusion.17
  46.9 2.0 maximum_reduce_fusion
  48.9 0.6 gather_fusion.2
  49.5 0.7 iota_reduce_fusion
  50.2 0.1 reshape.172
  50.3 1.3 dynamic-slice
  52.2 0.8 bitcast_dynamic-update-slice_fusion
  52.9 12.9 %all-reduce = s32[32]{0:T(128)S(1)} all-reduce(s32[32]{0:T(128)S(1)} %bitcast_dynamic-update-slice_fusion), channel_id=1, replica_groups=mesh['row'=32,'col'=16] {'col'}, use_global_device_ids=true, to_apply=%add | all-reduce | flops 32 | bytes 256
  65.8 0.6 iota_reduce_fusion.1
  66.5 0.1 reshape.171
  66.5 0.1 eq.62
  66.6 0.7 compare_reduce_fusion
  67.3 0.1 and.16
  67.4 0.1 max.14
  67.5 0.7 broadcast_compare_fusion
  68.2 14.4 %all-gather.4.cloned.1.call-done = bf16[1,32,256,256]{3,2,0,1:T(8,128)(2,1)} async-done(((bf16[1,2,256,256]{3,2,0,1:T(8,128)(2,1)}), bf16[1,32,256,256]{3,2,0,1:T(8,128)(2,1)}) %all-gather.4.cloned.1.call-update) | async-done | bytes 4194320 | tf_op jit(solution)/shard_map/all_gather | solution.py:48
  82.6 81.8 %all-gather.6.cloned.1.call-done = bf16[32,2,256,256]{3,2,1,0:T(8,128)(2,1)} async-done(((bf16[1,2,256,256]{3,2,1,0:T(8,128)(2,1)}), bf16[32,2,256,256]{3,2,1,0:T(8,128)(2,1)}) %all-gather.6.cloned.1.call-update) | async-done | bytes 8388624 | tf_op jit(solution)/shard_map/all_gather | solution.py:63
  164.5 0.0 copy-start.1
  164.5 0.0 copy-start
  164.5 79.1 %while.11 = (s32[]{:T(128)}, f32[2,256,256]{2,0,1:T(2,128)S(1)}, f32[4,16,2]{1,2,0:T(2,128)S(1)}, s32[4,16]{1,0:T(4,128)S(1)}, bf16[32,256,256]{2,1,0:T(8,128)(2...) while((s32[]{:T(128)}, f32[2,256,256]{2,0,1:T(2,128)S(1)}, ...), condition=%wide.region_3.4_spmd.clone, body=%wide.region_2.3_spmd.clone.sunk | while | flops 562300160 | bytes 22025908 | solution.py:37
  164.5 2.9 %gather_fusion = bf16[16,256,256]{2,1,0:T(8,128)(2,1)S(1)} fusion(bf16[32,256,256]{2,1,0:T(8,128)(2,1)} %get-tuple-element.180, s32[1024]{0:T(1024)S(1)} %pad_clamp_fusion.3), kind=kCustom, calls=%fused_computation.clone.clone.1 | custom fusion | bytes 4194368 | tf_op jit(solution)/shard_map/while/body/eval_jaxpr/gather | solution.py:29
  167.4 5.4 %gather_fusion.1 = bf16[16,256,256]{2,1,0:T(8,128)(2,1)} fusion(bf16[32,2,256,256]{3,2,1,0:T(8,128)(2,1)} %get-tuple-element.183, s32[16]{0:T(128)S(1)} %get-tuple-element.155), kind=kCustom, calls=%fused_computation.1.clone.clone.1 | custom fusion | bytes 4194432 | tf_op jit(solution)/shard_map/while/body/eval_jaxpr/gather | solution.py:30
  172.8 4.3 %fusion.31 = f32[16,256,256]{2,1,0:T(8,128)} fusion(bf16[16,256,256]{2,1,0:T(8,128)(2,1)S(1)} %gather_fusion, bf16[16,256,256]{2,1,0:T(8,128)(2,1)} %gather_fusion.1), kind=kOutput, calls=%fused_computation.45.clone.1 | convolution fusion | flops 536870912 | bytes 8388608 | tf_op jit(solution)/shard_map/while/body/eval_jaxpr/pab,pbc->pac/dot_general | solution.py:31
  177.1 7.2 %fusion.32 = f32[2,256,256]{2,0,1:T(2,128)S(1)} fusion(f32[16,256,256]{2,1,0:T(8,128)} %fusion.31, f32[2,256,256]{2,0,1:T(2,128)S(1)} %get-tuple-element.167, pred[]{:T(512)S(6)} %compare.10, f32[4,16,2]{1,2,0:T(2,128)S(1)} %get-tuple-element.178, s32[]{:T(128)} %get-tuple-element.166), kind=kOutput, calls=%fused_computation.5.clone.1 | convolution fusion | flops 25427968 | bytes 5243909 | tf_op jit(solution)/shard_map/while/body/eval_jaxpr/ps,pac->sac/dot_general | solution.py:34
  184.3 2.9 %gather_fusion = bf16[16,256,256]{2,1,0:T(8,128)(2,1)S(1)} fusion(bf16[32,256,256]{2,1,0:T(8,128)(2,1)} %get-tuple-element.180, s32[1024]{0:T(1024)S(1)} %pad_clamp_fusion.3), kind=kCustom, calls=%fused_computation.clone.clone.1 | custom fusion | bytes 4194368 | tf_op jit(solution)/shard_map/while/body/eval_jaxpr/gather | solution.py:29
  187.2 5.4 %gather_fusion.1 = bf16[16,256,256]{2,1,0:T(8,128)(2,1)} fusion(bf16[32,2,256,256]{3,2,1,0:T(8,128)(2,1)} %get-tuple-element.183, s32[16]{0:T(128)S(1)} %get-tuple-element.155), kind=kCustom, calls=%fused_computation.1.clone.clone.1 | custom fusion | bytes 4194432 | tf_op jit(solution)/shard_map/while/body/eval_jaxpr/gather | solution.py:30
  192.6 4.3 %fusion.31 = f32[16,256,256]{2,1,0:T(8,128)} fusion(bf16[16,256,256]{2,1,0:T(8,128)(2,1)S(1)} %gather_fusion, bf16[16,256,256]{2,1,0:T(8,128)(2,1)} %gather_fusion.1), kind=kOutput, calls=%fused_computation.45.clone.1 | convolution fusion | flops 536870912 | bytes 8388608 | tf_op jit(solution)/shard_map/while/body/eval_jaxpr/pab,pbc->pac/dot_general | solution.py:31
  196.9 7.2 %fusion.32 = f32[2,256,256]{2,0,1:T(2,128)S(1)} fusion(f32[16,256,256]{2,1,0:T(8,128)} %fusion.31, f32[2,256,256]{2,0,1:T(2,128)S(1)} %get-tuple-element.167, pred[]{:T(512)S(6)} %compare.10, f32[4,16,2]{1,2,0:T(2,128)S(1)} %get-tuple-element.178, s32[]{:T(128)} %get-tuple-element.166), kind=kOutput, calls=%fused_computation.5.clone.1 | convolution fusion | flops 25427968 | bytes 5243909 | tf_op jit(solution)/shard_map/while/body/eval_jaxpr/ps,pac->sac/dot_general | solution.py:34
  204.1 2.9 %gather_fusion = bf16[16,256,256]{2,1,0:T(8,128)(2,1)S(1)} fusion(bf16[32,256,256]{2,1,0:T(8,128)(2,1)} %get-tuple-element.180, s32[1024]{0:T(1024)S(1)} %pad_clamp_fusion.3), kind=kCustom, calls=%fused_computation.clone.clone.1 | custom fusion | bytes 4194368 | tf_op jit(solution)/shard_map/while/body/eval_jaxpr/gather | solution.py:29
  207.0 5.4 %gather_fusion.1 = bf16[16,256,256]{2,1,0:T(8,128)(2,1)} fusion(bf16[32,2,256,256]{3,2,1,0:T(8,128)(2,1)} %get-tuple-element.183, s32[16]{0:T(128)S(1)} %get-tuple-element.155), kind=kCustom, calls=%fused_computation.1.clone.clone.1 | custom fusion | bytes 4194432 | tf_op jit(solution)/shard_map/while/body/eval_jaxpr/gather | solution.py:30
  212.4 4.3 %fusion.31 = f32[16,256,256]{2,1,0:T(8,128)} fusion(bf16[16,256,256]{2,1,0:T(8,128)(2,1)S(1)} %gather_fusion, bf16[16,256,256]{2,1,0:T(8,128)(2,1)} %gather_fusion.1), kind=kOutput, calls=%fused_computation.45.clone.1 | convolution fusion | flops 536870912 | bytes 8388608 | tf_op jit(solution)/shard_map/while/body/eval_jaxpr/pab,pbc->pac/dot_general | solution.py:31
  216.6 7.2 %fusion.32 = f32[2,256,256]{2,0,1:T(2,128)S(1)} fusion(f32[16,256,256]{2,1,0:T(8,128)} %fusion.31, f32[2,256,256]{2,0,1:T(2,128)S(1)} %get-tuple-element.167, pred[]{:T(512)S(6)} %compare.10, f32[4,16,2]{1,2,0:T(2,128)S(1)} %get-tuple-element.178, s32[]{:T(128)} %get-tuple-element.166), kind=kOutput, calls=%fused_computation.5.clone.1 | convolution fusion | flops 25427968 | bytes 5243909 | tf_op jit(solution)/shard_map/while/body/eval_jaxpr/ps,pac->sac/dot_general | solution.py:34
  223.9 2.9 %gather_fusion = bf16[16,256,256]{2,1,0:T(8,128)(2,1)S(1)} fusion(bf16[32,256,256]{2,1,0:T(8,128)(2,1)} %get-tuple-element.180, s32[1024]{0:T(1024)S(1)} %pad_clamp_fusion.3), kind=kCustom, calls=%fused_computation.clone.clone.1 | custom fusion | bytes 4194368 | tf_op jit(solution)/shard_map/while/body/eval_jaxpr/gather | solution.py:29
  226.7 5.4 %gather_fusion.1 = bf16[16,256,256]{2,1,0:T(8,128)(2,1)} fusion(bf16[32,2,256,256]{3,2,1,0:T(8,128)(2,1)} %get-tuple-element.183, s32[16]{0:T(128)S(1)} %get-tuple-element.155), kind=kCustom, calls=%fused_computation.1.clone.clone.1 | custom fusion | bytes 4194432 | tf_op jit(solution)/shard_map/while/body/eval_jaxpr/gather | solution.py:30
  232.2 4.3 %fusion.31 = f32[16,256,256]{2,1,0:T(8,128)} fusion(bf16[16,256,256]{2,1,0:T(8,128)(2,1)S(1)} %gather_fusion, bf16[16,256,256]{2,1,0:T(8,128)(2,1)} %gather_fusion.1), kind=kOutput, calls=%fused_computation.45.clone.1 | convolution fusion | flops 536870912 | bytes 8388608 | tf_op jit(solution)/shard_map/while/body/eval_jaxpr/pab,pbc->pac/dot_general | solution.py:31
  236.4 7.2 %fusion.32 = f32[2,256,256]{2,0,1:T(2,128)S(1)} fusion(f32[16,256,256]{2,1,0:T(8,128)} %fusion.31, f32[2,256,256]{2,0,1:T(2,128)S(1)} %get-tuple-element.167, pred[]{:T(512)S(6)} %compare.10, f32[4,16,2]{1,2,0:T(2,128)S(1)} %get-tuple-element.178, s32[]{:T(128)} %get-tuple-element.166), kind=kOutput, calls=%fused_computation.5.clone.1 | convolution fusion | flops 25427968 | bytes 5243909 | tf_op jit(solution)/shard_map/while/body/eval_jaxpr/ps,pac->sac/dot_general | solution.py:34
  243.6 0.1 fusion.15
  243.7 0.1 select_reduce_fusion.1
  243.8 0.7 broadcast_in_dim.93
  244.4 7.8 %all-to-all-start = ((f32[32,2,256]{2,1,0:T(2,128)}), f32[32,2,256]{2,1,0:T(2,128)S(1)}, u32[]{:S(2)}, u32[]{:S(2)}) async-start(f32[32,2,256]{2,1,0:T(2,128)} %broadcast_in_dim.93), calls=%async_computation | async-start | bytes 131072 | tf_op jit(solution)/shard_map/all_to_all | solution.py:9
  252.2 0.0 copy-done.1
  252.2 13.0 %all-to-all-done = f32[32,2,256]{2,1,0:T(2,128)S(1)} async-done(((f32[32,2,256]{2,1,0:T(2,128)}), f32[32,2,256]{2,1,0:T(2,128)S(1)}, u32[]{:S(2)}, u32[]{:S(2)}) %all-to-all-start) | async-done | bytes 65568 | tf_op jit(solution)/shard_map/all_to_all | solution.py:9
  265.3 0.1 select_reduce_fusion
  265.4 0.1 broadcast_select_fusion
  265.5 0.0 copy-done
  265.5 0.9 fusion.14
  (15 shorter events, 0.1 us)
Async XLA Ops:
  6.5 76.1 %all-gather.4.cloned.1.call-start = ((), (), s32[]{:S(2)}) async-start(), calls=%async_computation.1 | async-start | bytes 4456448 | tf_op jit(solution)/shard_map/all_gather | solution.py:48
  7.3 157.2 %all-gather.6.cloned.1.call-start = ((), (), s32[]{:S(2)}) async-start(), calls=%async_computation.2 | async-start | bytes 8650752 | tf_op jit(solution)/shard_map/all_gather | solution.py:63
  164.5 87.7 %copy-start.1 = (s32[1,2]{1,0:T(1,128)S(1)}, s32[1,2]{1,0:T(1,128)}, u32[]{:S(2)}) copy-start(s32[1,2]{1,0:T(1,128)} %param.6) | copy-start | bytes 28
  164.5 101.0 %copy-start = (bf16[1,2,256,256]{3,2,1,0:T(8,128)(2,1)S(1)}, bf16[1,2,256,256]{3,2,1,0:T(8,128)(2,1)}, u32[]{:S(2)}) copy-start(bf16[1,2,256,256]{3,2,1,0:T(8,128)(2,1)} %param.5) | copy-start | bytes 786436
  244.4 20.9 %all-to-all-start = ((f32[32,2,256]{2,1,0:T(2,128)}), f32[32,2,256]{2,1,0:T(2,128)S(1)}, u32[]{:S(2)}, u32[]{:S(2)}) async-start(f32[32,2,256]{2,1,0:T(2,128)} %broadcast_in_dim.93), calls=%async_computation | async-start | bytes 131072 | tf_op jit(solution)/shard_map/all_to_all | solution.py:9
Sparse Core Ops, SparseCore 0:
  10.4 72.2 all-gather.3
  84.8 79.6 all-gather.5
where the time goes:
time: 274 us; the launch traced here: 273 us
  waiting for transfers between devices  111 us (41%)
  blocking collectives  50.4 us (18%)
  matrix products  45.8 us (17%)
  local copies, waits for them, and re-layouts  38.2 us (14%)
  between operations  14.1 us (5%)
  starting transfers between devices  7.82 us (3%)
  other arithmetic  6.17 us (2%)
    all_gather x1, waiting for transfers between devices, on_device(): lax.all_gather(flow_tiles, 'row', axis=0, tiled=True)  81.8 us
    all_gather x1, blocking collectives, on_device(): lax.all_gather(tile_cols, 'row', axis=0, tiled=True)  37.5 us
    dot_general x4, matrix products, block_step(): jnp.einsum('ps,pac->sac', weight_block, products, precision=lax.Precision...  28.7 us
    gather x4, local copies, waits for them, and re-layouts, block_step(): right_tiles = right_source[row_pick, slot_pick]  21.7 us
    dot_general x4, matrix products, block_step(): jnp.einsum('pab,pbc->pac', left_tiles, right_tiles, preferred_element_typ...  17 us
    all_gather x1, waiting for transfers between devices, on_device(): lax.all_gather(flow_tiles, 'col', axis=1, tiled=True)  14.4 us
    all_to_all x1, waiting for transfers between devices, copy_for_each(): lax.all_to_all(jnp.broadcast_to(shard[None], (length, *shard.shape)), axi...  13 us
    unnamed x1, blocking collectives  12.9 us
  transfers between devices with their start and end apart: 3, of which 3 were waited for; matrix products, arithmetic and copies ran while one was open for 3% of the time, Pallas kernels for 0%

commit v1 on v0

v1 whole, which is shorter than its diff:
```python
import jax
import jax.numpy as jnp
from jax import lax
from jax.experimental import pallas as pl
from jax.experimental.pallas import tpu as pltpu
from jax.sharding import Mesh, PartitionSpec as P

ROWS = ("z", "core")
COLS = ("y", "x")


def product_kernel(keep_ref, left_ref, right_ref, inflated_ref, sums_ref, total):
    step = pl.program_id(0)

    @pl.when(step == 0)
    def _():
        total[...] = jnp.zeros_like(total)

    for column in range(2):
        total[column] += jnp.dot(
            left_ref[0, 0], right_ref[0, 0, column], preferred_element_type=jnp.float32
        ) + jnp.dot(
            left_ref[0, 1], right_ref[1, 0, column], preferred_element_type=jnp.float32
        )

    @pl.when(step == pl.num_programs(0) - 1)
    def _():
        for column in range(2):
            kept = keep_ref[column] > 0
            value = total[column]
            value = jnp.where(kept, value * value, 0.0)
            inflated_ref[column] = value
            sums_ref[column : column + 1, :] = jnp.sum(value, axis=0, keepdims=True)


def block_products(keep, left, right):
    steps, _, width, _ = left.shape
    return pl.pallas_call(
        product_kernel,
        grid=(steps,),
        in_specs=[
            pl.BlockSpec(memory_space=pltpu.SMEM),
            pl.BlockSpec((1, 2, width, width), lambda i: (i, 0, 0, 0)),
            pl.BlockSpec((2, 1, 2, width, width), lambda i: (0, i, 0, 0, 0)),
        ],
        out_specs=[
            pl.BlockSpec((2, width, width), lambda i: (0, 0, 0)),
            pl.BlockSpec((2, width), lambda i: (0, 0)),
        ],
        out_shape=[
            jax.ShapeDtypeStruct((2, width, width), jnp.float32),
            jax.ShapeDtypeStruct((2, width), jnp.float32),
        ],
        scratch_shapes=[pltpu.VMEM((2, width, width), jnp.float32)],
        cost_estimate=pl.CostEstimate(
            flops=8 * steps * width**3, bytes_accessed=12 * steps * width**2, transcendentals=0
        ),
    )(keep, left, right)


def copy_for_each(shard, axis):
    length = lax.axis_size(axis)
    return lax.all_to_all(
        jnp.broadcast_to(shard[None], (length, *shard.shape)), axis, 0, 0, tiled=True
    )


def on_device(flow_tiles, tile_cols, pairs):
    width = flow_tiles.shape[3]
    col_count = lax.axis_size(COLS)
    row_count = lax.axis_size(ROWS)
    targets = lax.axis_index(COLS) + col_count * jnp.arange(2, dtype=jnp.int32)
    own = tile_cols[0]
    tiles = flow_tiles[0]
    matches = own[None, :] == targets[:, None]
    kept = jnp.any(matches, axis=1)
    zero = jnp.zeros((), tiles.dtype)
    ordered = jnp.where(
        matches[:, 0, None, None],
        tiles[0][None],
        jnp.where(matches[:, 1, None, None], tiles[1][None], zero),
    )
    right = lax.all_gather(ordered, ROWS, axis=0)
    left = copy_for_each(ordered, COLS)
    right = right.reshape(2, col_count, 2, width, width)
    inflated, sums = block_products(kept.astype(jnp.int32), left, right)
    sums = lax.all_gather(sums, "core", axis=0).sum(axis=0)
    totals = copy_for_each(sums, "z").sum(axis=0)
    totals = jnp.where(kept[:, None], totals, 1.0)
    normed = inflated * jnp.float32(row_count * width) / totals[:, None, :]
    normed = jnp.where(
        matches[0][:, None, None],
        normed[0][None],
        jnp.where(matches[1][:, None, None], normed[1][None], 0.0),
    )
    blended = 0.5 * tiles.astype(jnp.float32) + 0.5 * normed
    return jnp.where((own >= 0)[:, None, None], blended, 0.0)[None]


def solution(mesh):
    physical = Mesh(mesh.devices.reshape(16, 2, 4, 4), (*ROWS, *COLS))
    tiled = P(ROWS, COLS, None, None)
    return jax.shard_map(
        on_device,
        mesh=physical,
        in_specs=(tiled, P(ROWS, COLS), P((*ROWS, *COLS), None)),
        out_specs=tiled,
        check_vma=False,
    )
```

time: 274 us -> 139 us (0.51)
  blocking collectives: 50.4 us -> 1.98 us
  matrix products: 45.8 us -> 0 us
  local copies, waits for them, and re-layouts: 38.2 us -> 4.28 us
  waiting for transfers between devices: 111 us -> 85.8 us
  Pallas kernels: 0 us -> 13.3 us
  starting transfers between devices: 7.82 us -> 14.8 us
    all_gather x2 -> x1, waiting for transfers between devices: 96.2 us -> 21.5 us  [on_device(): right = lax.all_gather(ordered, ROWS, axis=0)]
    all_to_all x1 -> x2, waiting for transfers between devices: 13 us -> 64.2 us  [copy_for_each(): lax.all_to_all(jnp.broadcast_to(shard[None], (length, *shard.shape)), axi...]
    dot_general x8 -> x0, matrix products: 45.8 us -> none  [the longest x4 28.7 us: block_step(): jnp.einsum('ps,pac->sac', weight_block, products, precision=lax.Precision...]
    all_gather x1, blocking collectives: 37.5 us -> 1.98 us  [on_device(): sums = lax.all_gather(sums, 'core', axis=0).sum(axis=0)]
    gather x10 -> x0, local copies, waits for them, and re-layouts: 35.1 us -> none  [the longest x4 21.7 us: block_step(): right_tiles = right_source[row_pick, slot_pick]]
    pallas_call x0 -> x1, Pallas kernels: none -> 13.3 us  [block_products(): pl.pallas_call(product_kernel, grid=(steps,), in_specs=[pl.BlockSpec(memo...]
    unnamed x1 -> x0, blocking collectives: 12.9 us -> none
    all_to_all x1 -> x2, starting transfers between devices: 7.78 us -> 14.8 us  [copy_for_each(): lax.all_to_all(jnp.broadcast_to(shard[None], (length, *shard.shape)), axi...]
  transfers between devices with their start and end apart: 3 -> 3, of which waited for: 3 -> 3; matrix products, arithmetic and copies ran while one was open for 3% -> 2% of each run, Pallas kernels for 0% -> 0%
where the time goes in v1:
time: 139 us; the launch traced here: 138 us
  waiting for transfers between devices  85.8 us (62%)
  starting transfers between devices  14.8 us (11%)
  between operations  13.5 us (10%)
  Pallas kernels  13.3 us (10%)
  other arithmetic  4.51 us (3%)
  local copies, waits for them, and re-layouts  4.28 us (3%)
  blocking collectives  1.98 us (1%)
    all_to_all x2, waiting for transfers between devices, copy_for_each(): lax.all_to_all(jnp.broadcast_to(shard[None], (length, *shard.shape)), axi...  64.2 us
    all_gather x1, waiting for transfers between devices, on_device(): right = lax.all_gather(ordered, ROWS, axis=0)  21.5 us
    all_to_all x2, starting transfers between devices, copy_for_each(): lax.all_to_all(jnp.broadcast_to(shard[None], (length, *shard.shape)), axi...  14.8 us
    pallas_call x1, Pallas kernels, block_products(): pl.pallas_call(product_kernel, grid=(steps,), in_specs=[pl.BlockSpec(memo...  13.3 us
    broadcast_in_dim x2, local copies, waits for them, and re-layouts, copy_for_each(): jnp.broadcast_to(shard[None], (length, *shard.shape))  3.06 us
  transfers between devices with their start and end apart: 3, of which 3 were waited for; matrix products, arithmetic and copies ran while one was open for 2% of the time, Pallas kernels for 0%

profile of v1, /device:TPU:1, one launch (start us, length us, event | category | flops | bytes accessed | tf_op | source)
XLA Modules:
  0.0 138.1 jit_solution(16379137483958764391)
XLA Ops:
  6.5 0.0 all-gather.4.cloned.1.call-start
  6.5 0.8 fusion
  7.4 0.2 slice_reduce_fusion.1
  7.6 1.0 slice_bitcast_fusion.3
  8.6 0.8 select_select_fusion
  9.4 0.0 all-gather.4.cloned.1.call-update
  9.4 0.1 select_select_fusion.1
  9.5 2.4 %broadcast_in_dim.149 = bf16[16,2,256,256]{3,2,1,0:T(8,128)(2,1)} broadcast(bf16[2,256,256]{2,1,0:T(8,128)(2,1)S(1)} %select_select_fusion.1), dimensions={1,2,3} | broadcast | bytes 4456448 | tf_op jit(solution)/shard_map/broadcast_in_dim | solution.py:64
  11.9 7.6 %all-to-all-start = ((bf16[16,2,256,256]{3,2,1,0:T(8,128)(2,1)}), bf16[16,2,256,256]{3,2,1,0:T(8,128)(2,1)}, u32[]{:S(2)}, u32[]{:S(2)}) async-start(bf16[16,2,256,256]{3,2,1,0:T(8,128)(2,1)} %broadcast_in_dim.149), calls=%async_computation | async-start | bytes 8388608 | tf_op jit(solution)/shard_map/all_to_all | solution.py:63
  19.6 0.6 convert_element_type.8.keep_ref
  20.2 52.8 %all-to-all-done.left_ref = bf16[16,2,256,256]{3,2,1,0:T(8,128)(2,1)} async-done(((bf16[16,2,256,256]{3,2,1,0:T(8,128)(2,1)}), bf16[16,2,256,256]{3,2,1,0:T(8,128)(2,1)}, u32[]{:S(2)}, u32[]{:S(2)}) %all-to-all-start) | async-done | bytes 4194336 | tf_op jit(solution)/shard_map/all_to_all | solution.py:63
  72.9 21.5 %all-gather.4.cloned.1.call-done = bf16[32,2,256,256]{3,2,1,0:T(8,128)(2,1)} async-done(((bf16[1,2,256,256]{3,2,1,0:T(8,128)(2,1)}), bf16[32,2,256,256]{3,2,1,0:T(8,128)(2,1)}) %all-gather.4.cloned.1.call-update) | async-done | bytes 8388624 | tf_op jit(solution)/shard_map/all_gather | solution.py:83
  94.5 0.0 copy-start.1
  94.5 0.0 copy-start
  94.5 13.3 %shard_map.28 = (f32[2,256,256]{2,1,0:T(8,128)}, f32[2,256]{1,0:T(2,128)}) custom-call(s32[2]{0:T(128)} %convert_element_type.8.keep_ref, bf16[16,2,256,256]{3,2,1,0:T(8,128)(2,1)} %all-to-all-done.left_ref, bf16[2,16,2,256,256]{4,3,2,1,0:T(8,128)(2,1)} %bitcast.16), custom_call_target="tpu_custom_call" | custom-call | flops 2147483648 | bytes 12582912 | tf_op jit(solution)/shard_map/pallas_call | solution.py:38
  107.8 2.0 %all-gather.1 = f32[2,2,256]{2,1,0:T(2,128)S(1)} all-gather(f32[1,2,256]{2,1,0:T(2,128)} %bitcast.17), channel_id=2, replica_groups=mesh['z'=16,'core'=2,'y'=4,'x'=4] {'core'}, dimensions={0}, use_global_device_ids=true | all-gather | bytes 6144 | tf_op jit(solution)/shard_map/all_gather | solution.py:87
  109.7 0.6 broadcast_in_dim.156
  110.4 7.2 %all-to-all-start.1 = ((f32[16,2,256]{2,1,0:T(2,128)}), f32[16,2,256]{2,1,0:T(2,128)S(1)}, u32[]{:S(2)}, u32[]{:S(2)}) async-start(f32[16,2,256]{2,1,0:T(2,128)} %broadcast_in_dim.156), calls=%async_computation.1 | async-start | bytes 65536 | tf_op jit(solution)/shard_map/all_to_all | solution.py:63
  117.6 0.0 copy-done.1
  117.6 11.5 %all-to-all-done.1 = f32[16,2,256]{2,1,0:T(2,128)S(1)} async-done(((f32[16,2,256]{2,1,0:T(2,128)}), f32[16,2,256]{2,1,0:T(2,128)S(1)}, u32[]{:S(2)}, u32[]{:S(2)}) %all-to-all-start.1) | async-done | bytes 32800 | tf_op jit(solution)/shard_map/all_to_all | solution.py:63
  129.1 0.1 broadcast_select_fusion
  129.2 1.1 multiply_divide_fusion
  130.3 0.0 copy-done
  130.3 1.0 multiply_select_fusion
  (6 shorter events, 0.1 us)
Async XLA Ops:
  6.5 87.9 %all-gather.4.cloned.1.call-start = ((), (), s32[]{:S(2)}) async-start(), calls=%async_computation.2 | async-start | bytes 8650752 | tf_op jit(solution)/shard_map/all_gather | solution.py:83
  11.9 61.0 %all-to-all-start = ((bf16[16,2,256,256]{3,2,1,0:T(8,128)(2,1)}), bf16[16,2,256,256]{3,2,1,0:T(8,128)(2,1)}, u32[]{:S(2)}, u32[]{:S(2)}) async-start(bf16[16,2,256,256]{3,2,1,0:T(8,128)(2,1)} %broadcast_in_dim.149), calls=%async_computation | async-start | bytes 8388608 | tf_op jit(solution)/shard_map/all_to_all | solution.py:63
  94.5 23.1 %copy-start.1 = (s32[1,2]{1,0:T(1,128)S(1)}, s32[1,2]{1,0:T(1,128)}, u32[]{:S(2)}) copy-start(s32[1,2]{1,0:T(1,128)} %param.4) | copy-start | bytes 28
  94.5 35.8 %copy-start = (bf16[1,2,256,256]{3,2,1,0:T(8,128)(2,1)S(1)}, bf16[1,2,256,256]{3,2,1,0:T(8,128)(2,1)}, u32[]{:S(2)}) copy-start(bf16[1,2,256,256]{3,2,1,0:T(8,128)(2,1)} %param.3) | copy-start | bytes 786436
  110.4 18.7 %all-to-all-start.1 = ((f32[16,2,256]{2,1,0:T(2,128)}), f32[16,2,256]{2,1,0:T(2,128)S(1)}, u32[]{:S(2)}, u32[]{:S(2)}) async-start(f32[16,2,256]{2,1,0:T(2,128)} %broadcast_in_dim.156), calls=%async_computation.1 | async-start | bytes 65536 | tf_op jit(solution)/shard_map/all_to_all | solution.py:63
Sparse Core Ops, SparseCore 0:
  9.5 84.9 all-gather.3

commit v2 on v1

v2 whole, which is shorter than its diff:
```python
import jax
import jax.numpy as jnp
from jax import lax
from jax.experimental import pallas as pl
from jax.experimental.pallas import tpu as pltpu
from jax.sharding import Mesh, PartitionSpec as P

ROWS = ("z", "core")
COLS = ("y", "x")
SMEM = pl.BlockSpec(memory_space=pltpu.SMEM)
VMEM = pl.BlockSpec(memory_space=pltpu.VMEM)
LIMIT = 48 * 1024 * 1024


def order_kernel(own_ref, target_ref, tiles_ref, ordered_ref):
    for place in range(2):
        target = target_ref[place]
        first = (own_ref[0] == target).astype(jnp.float32)
        second = (own_ref[1] == target).astype(jnp.float32)
        value = tiles_ref[0].astype(jnp.float32) * first + tiles_ref[1].astype(jnp.float32) * second
        ordered_ref[place] = value.astype(ordered_ref.dtype)


def product_kernel(count, guards, carried, index_ref, *refs):
    del index_ref
    lefts = refs[: 2 * count]
    rights = refs[2 * count : 4 * count]
    rest = refs[4 * count :]
    core_ref, rest = rest[0], rest[1:]
    if carried:
        for into, given in zip(rest[2:], rest[:2]):
            into[...] = given[...]
        rest = rest[2:]
    else:
        for into in rest:
            into[...] = jnp.zeros_like(into)
    for i in range(count):
        def add(i=i):
            left = [lefts[2 * i + j][0].reshape(-1, lefts[0].shape[-1]) for j in range(2)]
            left = jnp.concatenate(left, axis=1)
            half = left.shape[0] // 2
            for column in range(2):
                right = jnp.concatenate([rights[2 * i + j][column] for j in range(2)], axis=0)
                product = jnp.dot(left, right, preferred_element_type=jnp.float32)
                rest[0][column] += product[:half]
                rest[1][column] += product[half:]

        if guards[i] is None:
            add()
        else:
            pl.when(core_ref[0] == guards[i])(add)


def products(totals, left, pairs, index, core, guards):
    count = len(pairs)
    width = left.shape[-1]
    flat = [tile for pair in pairs for tile in pair]
    carried = [] if totals is None else list(totals)
    whole = pl.BlockSpec((2, width, width), lambda g, s: (0, 0, 0))

    def pick(j):
        return pl.BlockSpec((1, 2, width, width), lambda g, s: (s[j], 0, 0, 0))

    total = jax.ShapeDtypeStruct((2, width, width), jnp.float32)

    def kernel(*refs):
        product_kernel(count, guards, bool(carried), *refs)

    return pl.pallas_call(
        kernel,
        grid_spec=pltpu.PrefetchScalarGridSpec(
            num_scalar_prefetch=1,
            grid=(1,),
            in_specs=[pick(j) for j in range(2 * count)]
            + [whole] * (2 * count)
            + [SMEM]
            + [whole] * len(carried),
            out_specs=[whole, whole],
        ),
        out_shape=[total, total],
        compiler_params=pltpu.CompilerParams(vmem_limit_bytes=LIMIT),
        cost_estimate=pl.CostEstimate(
            flops=16 * count * width**3, bytes_accessed=16 * count * width**2, transcendentals=0
        ),
    )(index, *[left] * (2 * count), *flat, core, *carried)


def square_kernel(kept_ref, mine_ref, other_ref, inflated_ref, sums_ref):
    for place in range(2):
        value = mine_ref[place] + other_ref[place]
        value = jnp.where(kept_ref[place] > 0, value * value, 0.0)
        inflated_ref[place] = value
        sums_ref[place : place + 1, :] = jnp.sum(value, axis=0, keepdims=True)


def blend_kernel(scale, own_ref, target_ref, tiles_ref, inflated_ref, parts_ref, out_ref):
    totals = jnp.sum(parts_ref[...], axis=0)
    for slot in range(2):
        tile = tiles_ref[slot].astype(jnp.float32)
        for place in range(2):
            @pl.when(own_ref[slot] == target_ref[place])
            def _():
                normed = inflated_ref[place] * scale / totals[place : place + 1, :]
                out_ref[slot] = 0.5 * tile + 0.5 * normed

        @pl.when(own_ref[slot] < 0)
        def _():
            out_ref[slot] = jnp.zeros_like(tile)


def copy_for_each(shard, axis):
    length = lax.axis_size(axis)
    return lax.all_to_all(
        jnp.broadcast_to(shard[None], (length, *shard.shape)), axis, 0, 0, tiled=True
    )


def on_device(flow_tiles, tile_cols, pairs):
    width = flow_tiles.shape[3]
    planes, cores = lax.axis_size("z"), lax.axis_size("core")
    columns = lax.axis_size(COLS)
    plane, core, column = lax.axis_index("z"), lax.axis_index("core"), lax.axis_index(COLS)
    core_scalar = core.reshape(1).astype(jnp.int32)
    targets = (column + columns * jnp.arange(2, dtype=jnp.int32)).astype(jnp.int32)
    own = tile_cols[0]
    tiles = flow_tiles[0]
    tile_shape = jax.ShapeDtypeStruct((2, width, width), tiles.dtype)
    mine = pl.pallas_call(
        order_kernel, in_specs=[SMEM, SMEM, VMEM], out_specs=VMEM, out_shape=tile_shape
    )(own, targets, tiles)
    other = lax.ppermute(mine, "core", [(0, 1), (1, 0)])

    low = lax.rem(column - (2 * plane - 14) + 64, 32)
    place = jnp.where((low < 16) == (core == 0), 0, 1)
    sent = jnp.stack([jnp.where(place == 0, t[0], t[1]) for t in (mine, other)])
    left = copy_for_each(sent, COLS)

    ring = [(2 * z, 2 * ((z + 1) % planes)) for z in range(planes)]
    back = [(2 * z + 1, 2 * ((z - 1) % planes) + 1) for z in range(planes)]
    held = [(mine, other)]
    half = planes // 2
    for step in range(1, half + 1):
        perm = ring + back if step < half else back
        held.append(tuple(lax.ppermute(t, ROWS, perm) for t in held[-1]))

    def index_of(steps):
        shift = jnp.where(core == 0, -1, 1)
        out = []
        for step in steps:
            base = 2 * (plane + shift * step) + 64
            out += [lax.rem(base + core, columns), lax.rem(base + 1 - core, columns)]
        return jnp.stack(out).astype(jnp.int32)

    cut = half - 1
    first = list(range(cut))
    last = list(range(cut, half + 1))
    totals = products(
        None, left, held[:cut], index_of(first), core_scalar, [0] + [None] * (cut - 1)
    )
    totals = products(
        totals, left, held[cut:], index_of(last), core_scalar, [None] * (half - cut) + [1]
    )
    received = lax.ppermute(totals[1], "core", [(0, 1), (1, 0)])
    kept = jnp.any(own[None, :] == targets[:, None], axis=1).astype(jnp.int32)
    inflated, sums = pl.pallas_call(
        square_kernel,
        in_specs=[SMEM, VMEM, VMEM],
        out_specs=[VMEM, VMEM],
        out_shape=[
            jax.ShapeDtypeStruct((2, width, width), jnp.float32),
            jax.ShapeDtypeStruct((2, width), jnp.float32),
        ],
    )(kept, totals[0], received)
    sums = lax.all_gather(sums, "core", axis=0).sum(axis=0)
    parts = copy_for_each(sums, "z")
    scale = float(planes * cores * width)

    def blend(*refs):
        blend_kernel(scale, *refs)

    out = pl.pallas_call(
        blend,
        in_specs=[SMEM, SMEM, VMEM, VMEM, VMEM],
        out_specs=VMEM,
        out_shape=jax.ShapeDtypeStruct((2, width, width), jnp.float32),
    )(own, targets, tiles, inflated, parts)
    return out[None]


def solution(mesh):
    physical = Mesh(mesh.devices.reshape(16, 2, 4, 4), (*ROWS, *COLS))
    tiled = P(ROWS, COLS, None, None)
    return jax.shard_map(
        on_device,
        mesh=physical,
        in_specs=(tiled, P(ROWS, COLS), P((*ROWS, *COLS), None)),
        out_specs=tiled,
        check_vma=False,
    )
```

time: 139 us -> 135 us (0.971)
  waiting for transfers between devices: 85.8 us -> 4.81 us
  starting transfers between devices: 14.8 us -> 85.8 us
  blocking collectives: 1.98 us -> 22.2 us
  between operations: 13.5 us -> 0.53 us
  other arithmetic: 4.51 us -> 2.38 us
    ppermute x0 -> x18, starting transfers between devices: none -> 81.1 us  [the longest x16 67.7 us: on_device(): held.append(tuple((lax.ppermute(t, ROWS, perm) for t in held[-1])))]
    all_to_all x2 -> x1, waiting for transfers between devices: 64.2 us -> 0.01 us  [copy_for_each(): lax.all_to_all(jnp.broadcast_to(shard[None], (length, *shard.shape)), axi...]
    all_gather x1 -> x0, waiting for transfers between devices: 21.5 us -> none  [on_device(): right = lax.all_gather(ordered, ROWS, axis=0)]
    all_to_all x0 -> x1, blocking collectives: none -> 20.2 us  [copy_for_each(): lax.all_to_all(jnp.broadcast_to(shard[None], (length, *shard.shape)), axi...]
    all_to_all x2 -> x1, starting transfers between devices: 14.8 us -> 4.67 us  [copy_for_each(): lax.all_to_all(jnp.broadcast_to(shard[None], (length, *shard.shape)), axi...]
    ppermute x0 -> x18, waiting for transfers between devices: none -> 4.81 us  [the longest x16 3.7 us: on_device(): held.append(tuple((lax.ppermute(t, ROWS, perm) for t in held[-1])))]
    unnamed x4 -> x10, local copies, waits for them, and re-layouts: 0.01 us -> 1.6 us
    pallas_call x1 -> x5, Pallas kernels: 13.3 us -> 13.2 us  [the longest x2 7.38 us: products(): pl.pallas_call(kernel, grid_spec=pltpu.PrefetchScalarGridSpec(num_scalar_...]
  transfers between devices with their start and end apart: 3 -> 19, of which waited for: 3 -> 9; matrix products, arithmetic and copies ran while one was open for 2% -> 1% of each run, Pallas kernels for 0% -> 3%
where the time goes in v2:
time: 135 us; the launch traced here: 133 us
  starting transfers between devices  85.8 us (64%)
  blocking collectives  22.2 us (16%)
  Pallas kernels  13.2 us (10%)
  waiting for transfers between devices  4.81 us (4%)
  local copies, waits for them, and re-layouts  4.18 us (3%)
  other arithmetic  2.38 us (2%)
    ppermute x16, starting transfers between devices, on_device(): held.append(tuple((lax.ppermute(t, ROWS, perm) for t in held[-1])))  67.7 us
    all_to_all x1, blocking collectives, copy_for_each(): lax.all_to_all(jnp.broadcast_to(shard[None], (length, *shard.shape)), axi...  20.2 us
    ppermute x1, starting transfers between devices, on_device(): other = lax.ppermute(mine, 'core', [(0, 1), (1, 0)])  8.77 us
    pallas_call x2, Pallas kernels, products(): pl.pallas_call(kernel, grid_spec=pltpu.PrefetchScalarGridSpec(num_scalar_...  7.38 us
    ppermute x1, starting transfers between devices, on_device(): received = lax.ppermute(totals[1], 'core', [(0, 1), (1, 0)])  4.7 us
    all_to_all x1, starting transfers between devices, copy_for_each(): lax.all_to_all(jnp.broadcast_to(shard[None], (length, *shard.shape)), axi...  4.67 us
    ppermute x16, waiting for transfers between devices, on_device(): held.append(tuple((lax.ppermute(t, ROWS, perm) for t in held[-1])))  3.7 us
  transfers between devices with their start and end apart: 19, of which 9 were waited for; matrix products, arithmetic and copies ran while one was open for 1% of the time, Pallas kernels for 3%

profile of v2, /device:TPU:1, one launch (start us, length us, event | category | flops | bytes accessed | tf_op | source)
XLA Modules:
  0.0 133.2 jit_solution(3106374439136444474)
XLA Ops:
  0.0 0.5 multiply_add_fusion.target_ref.refs_1_
  0.5 1.8 %shard_map.28.refs_15_ = bf16[2,256,256]{2,1,0:T(8,128)(2,1)} custom-call(s32[2]{0:T(128)} %bitcast.26, s32[2]{0:T(128)} %multiply_add_fusion.target_ref.refs_1_, bf16[2,256,256]{2,1,0:T(8,128)(2,1)} %bitcast.23), custom_call_target="tpu_custom_call" | custom-call | tf_op jit(solution)/shard_map/pallas_call | solution.py:128
  2.3 8.8 %collective-permute-start = (bf16[2,256,256]{2,1,0:T(8,128)(2,1)}, bf16[2,256,256]{2,1,0:T(8,128)(2,1)S(1)}, u32[]{:S(2)}, u32[]{:S(2)}) collective-permute-start(bf16[2,256,256]{2,1,0:T(8,128)(2,1)} %shard_map.28.refs_15_), channel_id=1, source_target_pairs={{0,16},{16,0},{1,17},{17,1},{2,18},{18,2},{3,19},{19,3},{4,20},{20... | collective-permute-start | bytes 786440 | tf_op jit(solution)/shard_map/ppermute | solution.py:131
  11.1 1.0 slice_select_fusion.1
  12.1 0.3 collective-permute-done.refs_16_
  12.5 2.5 %broadcast_in_dim.6 = bf16[16,2,256,256]{3,2,1,0:T(8,128)(2,1)} broadcast(bf16[2,256,256]{2,1,0:T(8,128)(2,1)S(1)} %pad_maximum_fusion), dimensions={1,2,3} | broadcast | bytes 4456448 | tf_op jit(solution)/shard_map/broadcast_in_dim | solution.py:114
  15.0 0.0 copy-start
  15.0 4.7 %all-to-all-start = ((bf16[16,2,256,256]{3,2,1,0:T(8,128)(2,1)}), bf16[16,2,256,256]{3,2,1,0:T(8,128)(2,1)}, u32[]{:S(2)}, u32[]{:S(2)}) async-start(bf16[16,2,256,256]{3,2,1,0:T(8,128)(2,1)} %broadcast_in_dim.6), calls=%async_computation | async-start | bytes 8388608 | tf_op jit(solution)/shard_map/all_to_all | solution.py:113
  19.6 0.0 copy-done
  19.7 8.0 %collective-permute-start.1 = (bf16[2,256,256]{2,1,0:T(8,128)(2,1)S(1)}, bf16[2,256,256]{2,1,0:T(8,128)(2,1)S(1)}, u32[]{:S(2)}, u32[]{:S(2)}) collective-permute-start(bf16[2,256,256]{2,1,0:T(8,128)(2,1)S(1)} %copy-done), channel_id=1, source_target_pairs={{0,32},{32,64},{64,96},{96,128},{128,160},{160,192},{192,224},{224... | collective-permute-start | bytes 786440 | tf_op jit(solution)/shard_map/ppermute | solution.py:144
  27.7 2.6 %collective-permute-start.8 = (bf16[2,256,256]{2,1,0:T(8,128)(2,1)S(1)}, bf16[2,256,256]{2,1,0:T(8,128)(2,1)S(1)}, u32[]{:S(2)}, u32[]{:S(2)}) collective-permute-start(bf16[2,256,256]{2,1,0:T(8,128)(2,1)S(1)} %collective-permute-done.refs_16_), channel_id=1, source_target_pairs={{0,32},{32,64},{64,96},{96,128},{128,160},{160,192},{192,224},{224... | collective-permute-start | bytes 786440 | tf_op jit(solution)/shard_map/ppermute | solution.py:144
  30.3 0.7 collective-permute-done.1.refs_17_
  31.0 5.4 %collective-permute-start.2 = (bf16[2,256,256]{2,1,0:T(8,128)(2,1)S(1)}, bf16[2,256,256]{2,1,0:T(8,128)(2,1)S(1)}, u32[]{:S(2)}, u32[]{:S(2)}) collective-permute-start(bf16[2,256,256]{2,1,0:T(8,128)(2,1)S(1)} %collective-permute-done.1.refs_17_), channel_id=1, source_target_pairs={{0,32},{32,64},{64,96},{96,128},{128,160},{160,192},{192,224},{224... | collective-permute-start | bytes 786440 | tf_op jit(solution)/shard_map/ppermute | solution.py:144
  36.4 0.0 collective-permute-done.8.refs_18_
  36.4 2.8 %collective-permute-start.9 = (bf16[2,256,256]{2,1,0:T(8,128)(2,1)S(1)}, bf16[2,256,256]{2,1,0:T(8,128)(2,1)S(1)}, u32[]{:S(2)}, u32[]{:S(2)}) collective-permute-start(bf16[2,256,256]{2,1,0:T(8,128)(2,1)S(1)} %collective-permute-done.8.refs_18_), channel_id=1, source_target_pairs={{0,32},{32,64},{64,96},{96,128},{128,160},{160,192},{192,224},{224... | collective-permute-start | bytes 786440 | tf_op jit(solution)/shard_map/ppermute | solution.py:144
  39.2 0.5 collective-permute-done.2.refs_19_
  39.7 5.4 %collective-permute-start.3 = (bf16[2,256,256]{2,1,0:T(8,128)(2,1)S(1)}, bf16[2,256,256]{2,1,0:T(8,128)(2,1)S(1)}, u32[]{:S(2)}, u32[]{:S(2)}) collective-permute-start(bf16[2,256,256]{2,1,0:T(8,128)(2,1)S(1)} %collective-permute-done.2.refs_19_), channel_id=1, source_target_pairs={{0,32},{32,64},{64,96},{96,128},{128,160},{160,192},{192,224},{224... | collective-permute-start | bytes 786440 | tf_op jit(solution)/shard_map/ppermute | solution.py:144
  45.1 0.0 collective-permute-done.9.refs_20_
  45.1 2.8 %collective-permute-start.10 = (bf16[2,256,256]{2,1,0:T(8,128)(2,1)S(1)}, bf16[2,256,256]{2,1,0:T(8,128)(2,1)S(1)}, u32[]{:S(2)}, u32[]{:S(2)}) collective-permute-start(bf16[2,256,256]{2,1,0:T(8,128)(2,1)S(1)} %collective-permute-done.9.refs_20_), channel_id=1, source_target_pairs={{0,32},{32,64},{64,96},{96,128},{128,160},{160,192},{192,224},{224... | collective-permute-start | bytes 786440 | tf_op jit(solution)/shard_map/ppermute | solution.py:144
  47.9 0.5 collective-permute-done.3.refs_21_
  48.4 5.4 %collective-permute-start.4 = (bf16[2,256,256]{2,1,0:T(8,128)(2,1)S(1)}, bf16[2,256,256]{2,1,0:T(8,128)(2,1)S(1)}, u32[]{:S(2)}, u32[]{:S(2)}) collective-permute-start(bf16[2,256,256]{2,1,0:T(8,128)(2,1)S(1)} %collective-permute-done.3.refs_21_), channel_id=1, source_target_pairs={{0,32},{32,64},{64,96},{96,128},{128,160},{160,192},{192,224},{224... | collective-permute-start | bytes 786440 | tf_op jit(solution)/shard_map/ppermute | solution.py:144
  53.8 0.0 collective-permute-done.10.refs_22_
  53.8 2.8 %collective-permute-start.11 = (bf16[2,256,256]{2,1,0:T(8,128)(2,1)S(1)}, bf16[2,256,256]{2,1,0:T(8,128)(2,1)S(1)}, u32[]{:S(2)}, u32[]{:S(2)}) collective-permute-start(bf16[2,256,256]{2,1,0:T(8,128)(2,1)S(1)} %collective-permute-done.10.refs_22_), channel_id=1, source_target_pairs={{0,32},{32,64},{64,96},{96,128},{128,160},{160,192},{192,224},{224... | collective-permute-start | bytes 786440 | tf_op jit(solution)/shard_map/ppermute | solution.py:144
  56.6 0.5 collective-permute-done.4.refs_23_
  57.1 5.4 %collective-permute-start.5 = (bf16[2,256,256]{2,1,0:T(8,128)(2,1)S(1)}, bf16[2,256,256]{2,1,0:T(8,128)(2,1)S(1)}, u32[]{:S(2)}, u32[]{:S(2)}) collective-permute-start(bf16[2,256,256]{2,1,0:T(8,128)(2,1)S(1)} %collective-permute-done.4.refs_23_), channel_id=1, source_target_pairs={{0,32},{32,64},{64,96},{96,128},{128,160},{160,192},{192,224},{224... | collective-permute-start | bytes 786440 | tf_op jit(solution)/shard_map/ppermute | solution.py:144
  62.5 0.0 collective-permute-done.11.refs_24_
  62.6 2.8 %collective-permute-start.12 = (bf16[2,256,256]{2,1,0:T(8,128)(2,1)S(1)}, bf16[2,256,256]{2,1,0:T(8,128)(2,1)S(1)}, u32[]{:S(2)}, u32[]{:S(2)}) collective-permute-start(bf16[2,256,256]{2,1,0:T(8,128)(2,1)S(1)} %collective-permute-done.11.refs_24_), channel_id=1, source_target_pairs={{0,32},{32,64},{64,96},{96,128},{128,160},{160,192},{192,224},{224... | collective-permute-start | bytes 786440 | tf_op jit(solution)/shard_map/ppermute | solution.py:144
  65.4 0.5 collective-permute-done.5.refs_25_
  65.8 5.4 %collective-permute-start.6 = (bf16[2,256,256]{2,1,0:T(8,128)(2,1)S(1)}, bf16[2,256,256]{2,1,0:T(8,128)(2,1)}, u32[]{:S(2)}, u32[]{:S(2)}) collective-permute-start(bf16[2,256,256]{2,1,0:T(8,128)(2,1)S(1)} %collective-permute-done.5.refs_25_), channel_id=1, source_target_pairs={{0,32},{32,64},{64,96},{96,128},{128,160},{160,192},{192,224},{224... | collective-permute-start | bytes 786440 | tf_op jit(solution)/shard_map/ppermute | solution.py:144
  71.3 0.0 collective-permute-done.12.refs_26_
  71.3 2.8 %collective-permute-start.13 = (bf16[2,256,256]{2,1,0:T(8,128)(2,1)S(1)}, bf16[2,256,256]{2,1,0:T(8,128)(2,1)}, u32[]{:S(2)}, u32[]{:S(2)}) collective-permute-start(bf16[2,256,256]{2,1,0:T(8,128)(2,1)S(1)} %collective-permute-done.12.refs_26_), channel_id=1, source_target_pairs={{0,32},{32,64},{64,96},{96,128},{128,160},{160,192},{192,224},{224... | collective-permute-start | bytes 786440 | tf_op jit(solution)/shard_map/ppermute | solution.py:144
  74.1 0.5 collective-permute-done.6.refs_27_
  74.6 5.2 %collective-permute-start.7 = (bf16[2,256,256]{2,1,0:T(8,128)(2,1)}, bf16[2,256,256]{2,1,0:T(8,128)(2,1)S(1)}, u32[]{:S(2)}, u32[]{:S(2)}) collective-permute-start(bf16[2,256,256]{2,1,0:T(8,128)(2,1)} %collective-permute-done.6.refs_27_), channel_id=1, source_target_pairs={{0,32},{32,64},{64,96},{96,128},{128,160},{160,192},{192,224},{224... | collective-permute-start | bytes 786440 | tf_op jit(solution)/shard_map/ppermute | solution.py:144
  79.8 0.0 collective-permute-done.13.refs_28_
  79.8 2.7 %collective-permute-start.14 = (bf16[2,256,256]{2,1,0:T(8,128)(2,1)}, bf16[2,256,256]{2,1,0:T(8,128)(2,1)}, u32[]{:S(2)}, u32[]{:S(2)}) collective-permute-start(bf16[2,256,256]{2,1,0:T(8,128)(2,1)} %collective-permute-done.13.refs_28_), channel_id=1, source_target_pairs={{0,32},{32,64},{64,96},{96,128},{128,160},{160,192},{192,224},{224... | collective-permute-start | bytes 786440 | tf_op jit(solution)/shard_map/ppermute | solution.py:144
  82.7 0.1 stack.85.refs_0_
  82.8 0.6 collective-permute-done.7.refs_5_
  83.4 5.3 %collective-permute-start.15 = (bf16[2,256,256]{2,1,0:T(8,128)(2,1)S(1)}, bf16[2,256,256]{2,1,0:T(8,128)(2,1)}, u32[]{:S(2)}, u32[]{:S(2)}) collective-permute-start(bf16[2,256,256]{2,1,0:T(8,128)(2,1)S(1)} %collective-permute-done.7.refs_5_), channel_id=1, source_target_pairs={{16,496},{48,16},{80,48},{112,80},{144,112},{176,144},{208,176},{2... | collective-permute-start | bytes 786440 | tf_op jit(solution)/shard_map/ppermute | solution.py:144
  88.7 0.0 collective-permute-done.14.refs_6_
  88.7 2.8 %collective-permute-start.16 = (bf16[2,256,256]{2,1,0:T(8,128)(2,1)}, bf16[2,256,256]{2,1,0:T(8,128)(2,1)}, u32[]{:S(2)}, u32[]{:S(2)}) collective-permute-start(bf16[2,256,256]{2,1,0:T(8,128)(2,1)} %collective-permute-done.14.refs_6_), channel_id=1, source_target_pairs={{16,496},{48,16},{80,48},{112,80},{144,112},{176,144},{208,176},{2... | collective-permute-start | bytes 786440 | tf_op jit(solution)/shard_map/ppermute | solution.py:144
  91.5 0.1 pad_add_fusion.refs_0_
  91.6 0.0 all-to-all-done.refs_1_.refs_2_.refs_3_.refs_4_.refs_5_.refs_6_.refs_7_.refs_8_.refs_9_.refs_10_.refs_11_.refs_12_.refs_13_.refs_14_
  91.6 4.5 %shard_map.29 = (f32[2,256,256]{2,1,0:T(8,128)S(1)}, f32[2,256,256]{2,1,0:T(8,128)S(1)}) custom-call(s32[14]{0:T(128)S(1)} %stack.85.refs_0_, bf16[16,2,256,256]{3,2,1,0:T(8,128)(2,1)} %all-to-all-done.refs_1_.refs_2_.refs_3_.refs_4_.refs_5_.refs_6_.refs_7_.refs_8_.refs_9_.refs_10_.refs_11_.refs_12_.refs_13_.refs_14_, ...), custom_call_target="tpu_custom_call" | custom-call | flops 1879048192 | bytes 7340032 | tf_op jit(solution)/shard_map/pallas_call | solution.py:69
  96.1 0.0 collective-permute-done.15.refs_7_
  96.1 0.0 collective-permute-done.16.refs_8_
  96.1 0.0 copy-start.3
  96.2 0.0 copy-start.4
  96.2 2.8 %shard_map.30 = (f32[2,256,256]{2,1,0:T(8,128)S(1)}, f32[2,256,256]{2,1,0:T(8,128)S(1)}) custom-call(s32[4]{0:T(128)S(1)} %pad_add_fusion.refs_0_, bf16[16,2,256,256]{3,2,1,0:T(8,128)(2,1)} %all-to-all-done.refs_1_.refs_2_.refs_3_.refs_4_.refs_5_.refs_6_.refs_7_.refs_8_.refs_9_.refs_10_.refs_11_.refs_12_.refs_13_.refs_14_, ...), custom_call_target="tpu_custom_call" | custom-call | flops 536870912 | bytes 2097152 | tf_op jit(solution)/shard_map/pallas_call | solution.py:69
  99.0 0.0 copy-start.1
  99.0 0.8 copy-done.1
  99.8 4.7 %collective-permute-start.17 = (f32[2,256,256]{2,1,0:T(8,128)S(1)}, f32[2,256,256]{2,1,0:T(8,128)S(1)}, u32[]{:S(2)}, u32[]{:S(2)}) collective-permute-start(f32[2,256,256]{2,1,0:T(8,128)S(1)} %get-tuple-element.14), channel_id=1, source_target_pairs={{0,16},{16,0},{1,17},{17,1},{2,18},{18,2},{3,19},{19,3},{4,20},{20... | collective-permute-start | bytes 1572872 | tf_op jit(solution)/shard_map/ppermute | solution.py:163
  104.5 0.0 copy-done.3
  104.5 0.0 copy-done.4
  104.5 0.2 compare_reduce_fusion
  104.7 0.5 convert_element_type.3.kept_ref
  105.3 0.8 collective-permute-done.17.other_ref
  106.0 0.0 copy-start.2
  106.0 0.8 copy-done.2
  106.8 2.1 %shard_map.31 = (f32[2,256,256]{2,1,0:T(8,128)}, f32[2,256]{1,0:T(2,128)}) custom-call(s32[2]{0:T(128)} %convert_element_type.3.kept_ref, f32[2,256,256]{2,1,0:T(8,128)} %copy-done.1, f32[2,256,256]{2,1,0:T(8,128)} %copy-done.2), custom_call_target="tpu_custom_call" | custom-call | tf_op jit(solution)/shard_map/pallas_call | solution.py:165
  108.9 2.0 %all-gather.1 = f32[2,2,256]{2,1,0:T(2,128)S(1)} all-gather(f32[1,2,256]{2,1,0:T(2,128)} %bitcast.25), channel_id=2, replica_groups=mesh['z'=16,'core'=2,'y'=4,'x'=4] {'core'}, dimensions={0}, use_global_device_ids=true | all-gather | bytes 6144 | tf_op jit(solution)/shard_map/all_gather | solution.py:174
  111.0 20.2 %all_to_all.10.refs_4_ = f32[16,2,256]{2,1,0:T(2,128)} all-to-all(f32[16,2,256]{2,1,0:T(2,128)S(1)} %broadcast_in_dim.7), channel_id=1, replica_groups=mesh['z'=16,'core'=2,'y'=4,'x'=4] {'z'}, dimensions={0} | all-to-all | bytes 65536 | tf_op jit(solution)/shard_map/all_to_all | solution.py:113
  131.2 2.0 %shard_map.32 = f32[2,256,256]{2,1,0:T(8,128)} custom-call(s32[2]{0:T(128)} %bitcast.27, s32[2]{0:T(128)} %multiply_add_fusion.target_ref.refs_1_, bf16[2,256,256]{2,1,0:T(8,128)(2,1)} %bitcast.24, f32[2,256,256]{2,1,0:T(8,128)} %get-tuple-element.15.refs_3_, f32[16,2,256]{2,1,0:T(2,128)} %all_to_all.10.refs_4_), custom_call_target="tpu_custom_call" | custom-call | tf_op jit(solution)/shard_map/pallas_call | solution.py:181
  (4 shorter events, 0.1 us)
Async XLA Ops:
  2.3 10.1 %collective-permute-start = (bf16[2,256,256]{2,1,0:T(8,128)(2,1)}, bf16[2,256,256]{2,1,0:T(8,128)(2,1)S(1)}, u32[]{:S(2)}, u32[]{:S(2)}) collective-permute-start(bf16[2,256,256]{2,1,0:T(8,128)(2,1)} %shard_map.28.refs_15_), channel_id=1, source_target_pairs={{0,16},{16,0},{1,17},{17,1},{2,18},{18,2},{3,19},{19,3},{4,20},{20... | collective-permute-start | bytes 786440 | tf_op jit(solution)/shard_map/ppermute | solution.py:131
  15.0 4.7 %copy-start = (bf16[2,256,256]{2,1,0:T(8,128)(2,1)S(1)}, bf16[2,256,256]{2,1,0:T(8,128)(2,1)}, u32[]{:S(2)}) copy-start(bf16[2,256,256]{2,1,0:T(8,128)(2,1)} %shard_map.28.refs_15_) | copy-start | bytes 786436
  15.0 76.6 %all-to-all-start = ((bf16[16,2,256,256]{3,2,1,0:T(8,128)(2,1)}), bf16[16,2,256,256]{3,2,1,0:T(8,128)(2,1)}, u32[]{:S(2)}, u32[]{:S(2)}) async-start(bf16[16,2,256,256]{3,2,1,0:T(8,128)(2,1)} %broadcast_in_dim.6), calls=%async_computation | async-start | bytes 8388608 | tf_op jit(solution)/shard_map/all_to_all | solution.py:113
  19.7 11.3 %collective-permute-start.1 = (bf16[2,256,256]{2,1,0:T(8,128)(2,1)S(1)}, bf16[2,256,256]{2,1,0:T(8,128)(2,1)S(1)}, u32[]{:S(2)}, u32[]{:S(2)}) collective-permute-start(bf16[2,256,256]{2,1,0:T(8,128)(2,1)S(1)} %copy-done), channel_id=1, source_target_pairs={{0,32},{32,64},{64,96},{96,128},{128,160},{160,192},{192,224},{224... | collective-permute-start | bytes 786440 | tf_op jit(solution)/shard_map/ppermute | solution.py:144
  27.7 8.7 %collective-permute-start.8 = (bf16[2,256,256]{2,1,0:T(8,128)(2,1)S(1)}, bf16[2,256,256]{2,1,0:T(8,128)(2,1)S(1)}, u32[]{:S(2)}, u32[]{:S(2)}) collective-permute-start(bf16[2,256,256]{2,1,0:T(8,128)(2,1)S(1)} %collective-permute-done.refs_16_), channel_id=1, source_target_pairs={{0,32},{32,64},{64,96},{96,128},{128,160},{160,192},{192,224},{224... | collective-permute-start | bytes 786440 | tf_op jit(solution)/shard_map/ppermute | solution.py:144
  31.0 8.7 %collective-permute-start.2 = (bf16[2,256,256]{2,1,0:T(8,128)(2,1)S(1)}, bf16[2,256,256]{2,1,0:T(8,128)(2,1)S(1)}, u32[]{:S(2)}, u32[]{:S(2)}) collective-permute-start(bf16[2,256,256]{2,1,0:T(8,128)(2,1)S(1)} %collective-permute-done.1.refs_17_), channel_id=1, source_target_pairs={{0,32},{32,64},{64,96},{96,128},{128,160},{160,192},{192,224},{224... | collective-permute-start | bytes 786440 | tf_op jit(solution)/shard_map/ppermute | solution.py:144
  36.4 8.7 %collective-permute-start.9 = (bf16[2,256,256]{2,1,0:T(8,128)(2,1)S(1)}, bf16[2,256,256]{2,1,0:T(8,128)(2,1)S(1)}, u32[]{:S(2)}, u32[]{:S(2)}) collective-permute-start(bf16[2,256,256]{2,1,0:T(8,128)(2,1)S(1)} %collective-permute-done.8.refs_18_), channel_id=1, source_target_pairs={{0,32},{32,64},{64,96},{96,128},{128,160},{160,192},{192,224},{224... | collective-permute-start | bytes 786440 | tf_op jit(solution)/shard_map/ppermute | solution.py:144
  39.7 8.7 %collective-permute-start.3 = (bf16[2,256,256]{2,1,0:T(8,128)(2,1)S(1)}, bf16[2,256,256]{2,1,0:T(8,128)(2,1)S(1)}, u32[]{:S(2)}, u32[]{:S(2)}) collective-permute-start(bf16[2,256,256]{2,1,0:T(8,128)(2,1)S(1)} %collective-permute-done.2.refs_19_), channel_id=1, source_target_pairs={{0,32},{32,64},{64,96},{96,128},{128,160},{160,192},{192,224},{224... | collective-permute-start | bytes 786440 | tf_op jit(solution)/shard_map/ppermute | solution.py:144
  45.1 8.7 %collective-permute-start.10 = (bf16[2,256,256]{2,1,0:T(8,128)(2,1)S(1)}, bf16[2,256,256]{2,1,0:T(8,128)(2,1)S(1)}, u32[]{:S(2)}, u32[]{:S(2)}) collective-permute-start(bf16[2,256,256]{2,1,0:T(8,128)(2,1)S(1)} %collective-permute-done.9.refs_20_), channel_id=1, source_target_pairs={{0,32},{32,64},{64,96},{96,128},{128,160},{160,192},{192,224},{224... | collective-permute-start | bytes 786440 | tf_op jit(solution)/shard_map/ppermute | solution.py:144
  48.4 8.7 %collective-permute-start.4 = (bf16[2,256,256]{2,1,0:T(8,128)(2,1)S(1)}, bf16[2,256,256]{2,1,0:T(8,128)(2,1)S(1)}, u32[]{:S(2)}, u32[]{:S(2)}) collective-permute-start(bf16[2,256,256]{2,1,0:T(8,128)(2,1)S(1)} %collective-permute-done.3.refs_21_), channel_id=1, source_target_pairs={{0,32},{32,64},{64,96},{96,128},{128,160},{160,192},{192,224},{224... | collective-permute-start | bytes 786440 | tf_op jit(solution)/shard_map/ppermute | solution.py:144
  53.8 8.7 %collective-permute-start.11 = (bf16[2,256,256]{2,1,0:T(8,128)(2,1)S(1)}, bf16[2,256,256]{2,1,0:T(8,128)(2,1)S(1)}, u32[]{:S(2)}, u32[]{:S(2)}) collective-permute-start(bf16[2,256,256]{2,1,0:T(8,128)(2,1)S(1)} %collective-permute-done.10.refs_22_), channel_id=1, source_target_pairs={{0,32},{32,64},{64,96},{96,128},{128,160},{160,192},{192,224},{224... | collective-permute-start | bytes 786440 | tf_op jit(solution)/shard_map/ppermute | solution.py:144
  57.1 8.7 %collective-permute-start.5 = (bf16[2,256,256]{2,1,0:T(8,128)(2,1)S(1)}, bf16[2,256,256]{2,1,0:T(8,128)(2,1)S(1)}, u32[]{:S(2)}, u32[]{:S(2)}) collective-permute-start(bf16[2,256,256]{2,1,0:T(8,128)(2,1)S(1)} %collective-permute-done.4.refs_23_), channel_id=1, source_target_pairs={{0,32},{32,64},{64,96},{96,128},{128,160},{160,192},{192,224},{224... | collective-permute-start | bytes 786440 | tf_op jit(solution)/shard_map/ppermute | solution.py:144
  62.6 8.7 %collective-permute-start.12 = (bf16[2,256,256]{2,1,0:T(8,128)(2,1)S(1)}, bf16[2,256,256]{2,1,0:T(8,128)(2,1)S(1)}, u32[]{:S(2)}, u32[]{:S(2)}) collective-permute-start(bf16[2,256,256]{2,1,0:T(8,128)(2,1)S(1)} %collective-permute-done.11.refs_24_), channel_id=1, source_target_pairs={{0,32},{32,64},{64,96},{96,128},{128,160},{160,192},{192,224},{224... | collective-permute-start | bytes 786440 | tf_op jit(solution)/shard_map/ppermute | solution.py:144
  65.8 8.7 %collective-permute-start.6 = (bf16[2,256,256]{2,1,0:T(8,128)(2,1)S(1)}, bf16[2,256,256]{2,1,0:T(8,128)(2,1)}, u32[]{:S(2)}, u32[]{:S(2)}) collective-permute-start(bf16[2,256,256]{2,1,0:T(8,128)(2,1)S(1)} %collective-permute-done.5.refs_25_), channel_id=1, source_target_pairs={{0,32},{32,64},{64,96},{96,128},{128,160},{160,192},{192,224},{224... | collective-permute-start | bytes 786440 | tf_op jit(solution)/shard_map/ppermute | solution.py:144
  71.3 8.5 %collective-permute-start.13 = (bf16[2,256,256]{2,1,0:T(8,128)(2,1)S(1)}, bf16[2,256,256]{2,1,0:T(8,128)(2,1)}, u32[]{:S(2)}, u32[]{:S(2)}) collective-permute-start(bf16[2,256,256]{2,1,0:T(8,128)(2,1)S(1)} %collective-permute-done.12.refs_26_), channel_id=1, source_target_pairs={{0,32},{32,64},{64,96},{96,128},{128,160},{160,192},{192,224},{224... | collective-permute-start | bytes 786440 | tf_op jit(solution)/shard_map/ppermute | solution.py:144
  74.6 8.8 %collective-permute-start.7 = (bf16[2,256,256]{2,1,0:T(8,128)(2,1)}, bf16[2,256,256]{2,1,0:T(8,128)(2,1)S(1)}, u32[]{:S(2)}, u32[]{:S(2)}) collective-permute-start(bf16[2,256,256]{2,1,0:T(8,128)(2,1)} %collective-permute-done.6.refs_27_), channel_id=1, source_target_pairs={{0,32},{32,64},{64,96},{96,128},{128,160},{160,192},{192,224},{224... | collective-permute-start | bytes 786440 | tf_op jit(solution)/shard_map/ppermute | solution.py:144
  79.8 8.9 %collective-permute-start.14 = (bf16[2,256,256]{2,1,0:T(8,128)(2,1)}, bf16[2,256,256]{2,1,0:T(8,128)(2,1)}, u32[]{:S(2)}, u32[]{:S(2)}) collective-permute-start(bf16[2,256,256]{2,1,0:T(8,128)(2,1)} %collective-permute-done.13.refs_28_), channel_id=1, source_target_pairs={{0,32},{32,64},{64,96},{96,128},{128,160},{160,192},{192,224},{224... | collective-permute-start | bytes 786440 | tf_op jit(solution)/shard_map/ppermute | solution.py:144
  83.4 12.8 %collective-permute-start.15 = (bf16[2,256,256]{2,1,0:T(8,128)(2,1)S(1)}, bf16[2,256,256]{2,1,0:T(8,128)(2,1)}, u32[]{:S(2)}, u32[]{:S(2)}) collective-permute-start(bf16[2,256,256]{2,1,0:T(8,128)(2,1)S(1)} %collective-permute-done.7.refs_5_), channel_id=1, source_target_pairs={{16,496},{48,16},{80,48},{112,80},{144,112},{176,144},{208,176},{2... | collective-permute-start | bytes 786440 | tf_op jit(solution)/shard_map/ppermute | solution.py:144
  88.7 7.4 %collective-permute-start.16 = (bf16[2,256,256]{2,1,0:T(8,128)(2,1)}, bf16[2,256,256]{2,1,0:T(8,128)(2,1)}, u32[]{:S(2)}, u32[]{:S(2)}) collective-permute-start(bf16[2,256,256]{2,1,0:T(8,128)(2,1)} %collective-permute-done.14.refs_6_), channel_id=1, source_target_pairs={{16,496},{48,16},{80,48},{112,80},{144,112},{176,144},{208,176},{2... | collective-permute-start | bytes 786440 | tf_op jit(solution)/shard_map/ppermute | solution.py:144
  96.1 8.4 %copy-start.3 = (s32[1,2]{1,0:T(1,128)S(1)}, s32[1,2]{1,0:T(1,128)}, u32[]{:S(2)}) copy-start(s32[1,2]{1,0:T(1,128)} %param.4) | copy-start | bytes 28
  96.2 8.4 %copy-start.4 = (s32[2]{0:T(128)S(1)}, s32[2]{0:T(128)}, u32[]{:S(2)}) copy-start(s32[2]{0:T(128)} %multiply_add_fusion.target_ref.refs_1_) | copy-start | bytes 28
  99.0 0.8 copy-start.1
  99.8 6.2 %collective-permute-start.17 = (f32[2,256,256]{2,1,0:T(8,128)S(1)}, f32[2,256,256]{2,1,0:T(8,128)S(1)}, u32[]{:S(2)}, u32[]{:S(2)}) collective-permute-start(f32[2,256,256]{2,1,0:T(8,128)S(1)} %get-tuple-element.14), channel_id=1, source_target_pairs={{0,16},{16,0},{1,17},{17,1},{2,18},{18,2},{3,19},{19,3},{4,20},{20... | collective-permute-start | bytes 1572872 | tf_op jit(solution)/shard_map/ppermute | solution.py:163
  106.0 0.8 copy-start.2

commit v3 on v2

v3 whole, which is shorter than its diff:
```python
import jax
import jax.numpy as jnp
from jax import lax
from jax.experimental import pallas as pl
from jax.experimental.pallas import tpu as pltpu
from jax.sharding import Mesh, PartitionSpec as P

ROWS = ("z", "core")
COLS = ("y", "x")
SMEM = pl.BlockSpec(memory_space=pltpu.SMEM)
VMEM = pl.BlockSpec(memory_space=pltpu.VMEM)
ANY = pl.BlockSpec(memory_space=pl.ANY)
HBM = pl.BlockSpec(memory_space=pltpu.HBM)
MIB = 1024 * 1024
SWAP = [(0, 1), (1, 0)]
FLOPS = 25 * 10**9


def params(mib):
    return pltpu.CompilerParams(vmem_limit_bytes=mib * MIB)


def order_kernel(own_ref, target_ref, tiles_ref, ordered_ref):
    for place in range(2):
        target = target_ref[place]
        first = (own_ref[0] == target).astype(jnp.float32)
        second = (own_ref[1] == target).astype(jnp.float32)
        value = tiles_ref[0].astype(jnp.float32) * first + tiles_ref[1].astype(jnp.float32) * second
        ordered_ref[place] = value.astype(ordered_ref.dtype)


def spread_kernel(place_ref, mine_ref, other_ref, out_ref, sems):
    place = place_ref[0]
    copies = []
    for i in range(out_ref.shape[0]):
        for j, source in enumerate((mine_ref, other_ref)):
            copies.append(
                pltpu.make_async_copy(source.at[place], out_ref.at[i, j], sems.at[i, j])
            )
    for copy in copies:
        copy.start()
    for copy in copies:
        copy.wait()


def product_kernel(groups, rows, carried, first, index_ref, guard_ref, left_ref, *refs):
    count = 2 * sum(len(g) for g, _ in groups)
    rights, refs = refs[:count], refs[count:]
    given, refs = (refs[: len(rows)], refs[len(rows) :]) if carried else ((), refs)
    totals, (held, kept, sems) = refs[: len(rows)], refs[len(rows) :]
    copies = []
    for i in range(count):
        for n, row in enumerate(rows):
            source = left_ref.at[index_ref[first + i], row]
            copies.append(pltpu.make_async_copy(source, held.at[i, n], sems.at[i, n]))
        copies.append(pltpu.make_async_copy(rights[i], kept.at[i], sems.at[i, len(rows)]))
    each = len(rows) + 1
    for copy in copies:
        copy.start()
    for n, total in enumerate(totals):
        total[...] = given[n][...] if carried else jnp.zeros_like(total)
    width = held.shape[-1]
    for copy in copies if len(groups) == 1 else []:
        copy.wait()
    for group, guard in groups:
        pairs = [2 * i + j for i in group for j in range(2)]
        for i in pairs if len(groups) > 1 else []:
            for copy in copies[each * i : each * (i + 1)]:
                copy.wait()

        def add(pairs=pairs):
            left = jnp.concatenate(
                [held[i].reshape(len(rows) * width, width) for i in pairs], axis=1
            )
            for column in range(2):
                right = jnp.concatenate([kept[i, column] for i in pairs], axis=0)
                product = jnp.dot(left, right, preferred_element_type=jnp.float32)
                for n, total in enumerate(totals):
                    total[column] += product[n * width : (n + 1) * width]

        if guard is None:
            add()
        else:
            pl.when(guard_ref[0] == guard)(add)


def index_kernel(columns, place_ref, after_ref, index_ref):
    del after_ref
    plane, core = place_ref[0], place_ref[1]
    for step in range(index_ref.shape[0] // 2):
        base = 2 * (plane + jnp.where(core == 0, -step, step)) + 2 * columns
        index_ref[2 * step] = lax.rem(base + core, columns)
        index_ref[2 * step + 1] = lax.rem(base + 1 - core, columns)


def products(totals, left, planes, index, guard, groups, rows, first=0):
    flat = [tile for pair in planes for tile in pair]
    count = len(flat)
    width = left.shape[-1]
    carried = [] if totals is None else [totals[row] for row in rows]
    total = jax.ShapeDtypeStruct((2, width, width), jnp.float32)

    def kernel(*refs):
        product_kernel(groups, rows, bool(carried), first, *refs)

    return pl.pallas_call(
        kernel,
        in_specs=[SMEM, SMEM] + [ANY] * (1 + count) + [VMEM] * len(carried),
        out_specs=[VMEM] * len(rows),
        out_shape=[total] * len(rows),
        scratch_shapes=[
            pltpu.VMEM((count, len(rows), width, width), left.dtype),
            pltpu.VMEM((count, 2, width, width), left.dtype),
            pltpu.SemaphoreType.DMA((count, len(rows) + 1)),
        ],
        compiler_params=params(14),
        cost_estimate=pl.CostEstimate(
            flops=4 * len(rows) * count * width**3,
            bytes_accessed=8 * count * width**2,
            transcendentals=0,
        ),
    )(index, guard, left, *flat, *carried)


def square_kernel(kept_ref, mine_ref, other_ref, inflated_ref, sums_ref):
    for place in range(2):
        value = mine_ref[place] + other_ref[place]
        value = jnp.where(kept_ref[place] > 0, value * value, 0.0)
        inflated_ref[place] = value
        sums_ref[place : place + 1, :] = jnp.sum(value, axis=0, keepdims=True)


def blend_kernel(scale, own_ref, target_ref, tiles_ref, inflated_ref, parts_ref, out_ref):
    totals = jnp.sum(parts_ref[...], axis=0)
    for slot in range(2):
        tile = tiles_ref[slot].astype(jnp.float32)
        for place in range(2):
            @pl.when(own_ref[slot] == target_ref[place])
            def _():
                normed = inflated_ref[place] * scale / totals[place : place + 1, :]
                out_ref[slot] = 0.5 * tile + 0.5 * normed

        @pl.when(own_ref[slot] < 0)
        def _():
            out_ref[slot] = jnp.zeros_like(tile)


def on_device(flow_tiles, tile_cols, pairs):
    width = flow_tiles.shape[3]
    planes, cores = lax.axis_size("z"), lax.axis_size("core")
    columns = lax.axis_size(COLS)
    plane, core, column = lax.axis_index("z"), lax.axis_index("core"), lax.axis_index(COLS)
    targets = (column + columns * jnp.arange(2, dtype=jnp.int32)).astype(jnp.int32)
    own = tile_cols[0]
    tiles = flow_tiles[0]
    mine = pl.pallas_call(
        order_kernel,
        in_specs=[SMEM, SMEM, VMEM],
        out_specs=VMEM,
        out_shape=jax.ShapeDtypeStruct((2, width, width), tiles.dtype),
        compiler_params=params(4),
    )(own, targets, tiles)
    other = lax.ppermute(mine, "core", SWAP)

    half = planes // 2
    ring = [(2 * z, 2 * ((z + 1) % planes)) for z in range(planes)]
    back = [(2 * z + 1, 2 * ((z - 1) % planes) + 1) for z in range(planes)]
    held = [(mine, other)]
    for step in range(1, half + 1):
        perm = ring + back if step < half else back
        held.append(tuple(lax.ppermute(t, ROWS, perm) for t in held[-1]))

    low = lax.rem(column - 2 * (plane - half + 1) + 2 * columns, 2 * columns)
    place = jnp.where((low < columns) == (core == 0), 0, 1).astype(jnp.int32).reshape(1)
    sent = pl.pallas_call(
        spread_kernel,
        in_specs=[SMEM, VMEM, VMEM],
        out_specs=HBM,
        out_shape=jax.ShapeDtypeStruct((columns, 2, width, width), tiles.dtype),
        scratch_shapes=[pltpu.SemaphoreType.DMA((columns, 2))],
        compiler_params=params(4),
    )(place, mine, other)
    left = lax.all_to_all(sent, COLS, 0, 0, tiled=True)

    core_scalar = core.astype(jnp.int32).reshape(1)

    def fill(*refs):
        index_kernel(columns, *refs)

    index = pl.pallas_call(
        fill,
        in_specs=[SMEM, ANY],
        out_specs=SMEM,
        out_shape=jax.ShapeDtypeStruct((2 * half + 2,), jnp.int32),
        compiler_params=params(1),
        cost_estimate=pl.CostEstimate(flops=FLOPS, bytes_accessed=0, transcendentals=0),
    )(jnp.stack([plane, core]).astype(jnp.int32), held[half - 1][0])
    totals = products(
        None, left, held[:half], index, core_scalar,
        [([0], 0), ([1, 2], None), ([3, 4], None), ([5, 6], None), ([7], None)], (0, 1),
    )
    outward = products(totals, left, held[half:], index, core_scalar, [([0], 1)], (1,), 2 * half)[0]
    received = lax.ppermute(outward, "core", SWAP)
    total = products(totals, left, held[half:], index, core_scalar, [([0], 1)], (0,), 2 * half)[0]
    kept = jnp.any(own[None, :] == targets[:, None], axis=1).astype(jnp.int32)
    inflated, sums = pl.pallas_call(
        square_kernel,
        in_specs=[SMEM, VMEM, VMEM],
        out_specs=[VMEM, VMEM],
        out_shape=[
            jax.ShapeDtypeStruct((2, width, width), jnp.float32),
            jax.ShapeDtypeStruct((2, width), jnp.float32),
        ],
        compiler_params=params(6),
    )(kept, total, received)
    sums = lax.all_gather(sums, "core", axis=0).sum(axis=0)
    parts = lax.all_to_all(
        jnp.broadcast_to(sums[None], (planes, *sums.shape)), "z", 0, 0, tiled=True
    )
    scale = float(planes * cores * width)

    def blend(*refs):
        blend_kernel(scale, *refs)

    out = pl.pallas_call(
        blend,
        in_specs=[SMEM, SMEM, VMEM, VMEM, VMEM],
        out_specs=VMEM,
        out_shape=jax.ShapeDtypeStruct((2, width, width), jnp.float32),
        compiler_params=params(6),
    )(own, targets, tiles, inflated, parts)
    return out[None]


def solution(mesh):
    physical = Mesh(mesh.devices.reshape(16, 2, 4, 4), (*ROWS, *COLS))
    tiled = P(ROWS, COLS, None, None)
    return jax.shard_map(
        on_device,
        mesh=physical,
        in_specs=(tiled, P(ROWS, COLS), P((*ROWS, *COLS), None)),
        out_specs=tiled,
        check_vma=False,
    )
```

time: 135 us -> 135 us (level)
  starting transfers between devices: 85.8 us -> 77.1 us
  Pallas kernels: 13.2 us -> 18.1 us
  local copies, waits for them, and re-layouts: 4.18 us -> 8.57 us
  blocking collectives: 22.2 us -> 25.3 us
  other arithmetic: 2.38 us -> 0.28 us
    ppermute x16, starting transfers between devices: 67.7 us -> 59.4 us  [on_device(): held.append(tuple((lax.ppermute(t, ROWS, perm) for t in held[-1])))]
    pallas_call x2 -> x5, Pallas kernels: 7.38 us -> 15.4 us  [the longest x3 8.42 us: products(): pl.pallas_call(kernel, in_specs=[SMEM, SMEM] + [ANY] * (1 + count) + [VME...]
    unnamed x10 -> x22, local copies, waits for them, and re-layouts: 1.6 us -> 8.56 us
    all_to_all x1, blocking collectives: 20.2 us -> 23.6 us  [on_device(): lax.all_to_all(jnp.broadcast_to(sums[None], (planes, *sums.shape)), 'z',...]
    ppermute x2, starting transfers between devices: 13.5 us -> 10.8 us  [the longest x1 8.79 us: on_device(): other = lax.ppermute(mine, 'core', SWAP)]
    broadcast_in_dim x2 -> x1, local copies, waits for them, and re-layouts: 2.49 us -> 0.01 us  [on_device(): jnp.broadcast_to(sums[None], (planes, *sums.shape))]
    all_to_all x1, starting transfers between devices: 4.67 us -> 6.81 us  [on_device(): left = lax.all_to_all(sent, COLS, 0, 0, tiled=True)]
    pallas_call x1, Pallas kernels: 2.09 us -> 0.63 us  [on_device(): pl.pallas_call(square_kernel, in_specs=[SMEM, VMEM, VMEM], out_specs=[VME...]
  transfers between devices with their start and end apart: 19 -> 19, of which waited for: 9 -> 4; matrix products, arithmetic and copies ran while one was open for 1% -> 0% of each run, Pallas kernels for 3% -> 10%
where the time goes in v3:
time: 135 us; the launch traced here: 134 us
  starting transfers between devices  77.1 us (57%)
  blocking collectives  25.3 us (19%)
  Pallas kernels  18.1 us (13%)
  local copies, waits for them, and re-layouts  8.57 us (6%)
  waiting for transfers between devices  4.08 us (3%)
    ppermute x16, starting transfers between devices, on_device(): held.append(tuple((lax.ppermute(t, ROWS, perm) for t in held[-1])))  59.4 us
    all_to_all x1, blocking collectives, on_device(): lax.all_to_all(jnp.broadcast_to(sums[None], (planes, *sums.shape)), 'z',...  23.6 us
    ppermute x1, starting transfers between devices, on_device(): other = lax.ppermute(mine, 'core', SWAP)  8.79 us
    unnamed x22, local copies, waits for them, and re-layouts  8.56 us
    pallas_call x3, Pallas kernels, products(): pl.pallas_call(kernel, in_specs=[SMEM, SMEM] + [ANY] * (1 + count) + [VME...  8.42 us
    all_to_all x1, starting transfers between devices, on_device(): left = lax.all_to_all(sent, COLS, 0, 0, tiled=True)  6.81 us
    pallas_call x1, Pallas kernels, on_device(): pl.pallas_call(spread_kernel, in_specs=[SMEM, VMEM, VMEM], out_specs=HBM,...  5.75 us
    ppermute x16, waiting for transfers between devices, on_device(): held.append(tuple((lax.ppermute(t, ROWS, perm) for t in held[-1])))  4.07 us
  transfers between devices with their start and end apart: 19, of which 4 were waited for; matrix products, arithmetic and copies ran while one was open for 0% of the time, Pallas kernels for 10%

profile of v3, /device:TPU:1, one launch (start us, length us, event | category | flops | bytes accessed | tf_op | source)
XLA Modules:
  0.0 133.8 jit_solution(13927966474812989875)
XLA Ops:
  0.0 0.9 copy-done.1
  1.0 0.7 copy-done.9
  1.6 0.6 shard_map.28.mine_ref.refs_3_
  2.3 8.8 %collective-permute-start.7 = (bf16[2,256,256]{2,1,0:T(8,128)(2,1)S(1)}, bf16[2,256,256]{2,1,0:T(8,128)(2,1)S(1)}, u32[]{:S(2)}, u32[]{:S(2)}) collective-permute-start(bf16[2,256,256]{2,1,0:T(8,128)(2,1)S(1)} %shard_map.28.mine_ref.refs_3_), channel_id=1, source_target_pairs={{0,16},{16,0},{1,17},{17,1},{2,18},{18,2},{3,19},{19,3},{4,20},{20... | collective-permute-start | bytes 786440 | tf_op jit(solution)/shard_map/ppermute | solution.py:163
  11.1 5.7 %collective-permute-start = (bf16[2,256,256]{2,1,0:T(8,128)(2,1)S(1)}, bf16[2,256,256]{2,1,0:T(8,128)(2,1)S(1)}, u32[]{:S(2)}, u32[]{:S(2)}) collective-permute-start(bf16[2,256,256]{2,1,0:T(8,128)(2,1)S(1)} %shard_map.28.mine_ref.refs_3_), channel_id=1, source_target_pairs={{0,32},{32,64},{64,96},{96,128},{128,160},{160,192},{192,224},{224... | collective-permute-start | bytes 786440 | tf_op jit(solution)/shard_map/ppermute | solution.py:171
  16.8 0.0 collective-permute-done.7.other_ref.refs_4_
  16.8 2.6 %collective-permute-start.9 = (bf16[2,256,256]{2,1,0:T(8,128)(2,1)S(1)}, bf16[2,256,256]{2,1,0:T(8,128)(2,1)S(1)}, u32[]{:S(2)}, u32[]{:S(2)}) collective-permute-start(bf16[2,256,256]{2,1,0:T(8,128)(2,1)S(1)} %collective-permute-done.7.other_ref.refs_4_), channel_id=1, source_target_pairs={{0,32},{32,64},{64,96},{96,128},{128,160},{160,192},{192,224},{224... | collective-permute-start | bytes 786440 | tf_op jit(solution)/shard_map/ppermute | solution.py:171
  19.5 5.7 %shard_map.30 = bf16[16,2,256,256]{3,2,1,0:T(8,128)(2,1)S(1)} custom-call(s32[1]{0:T(128)} %bitcast.4.place_ref, bf16[2,256,256]{2,1,0:T(8,128)(2,1)S(1)} %shard_map.28.mine_ref.refs_3_, bf16[2,256,256]{2,1,0:T(8,128)(2,1)S(1)} %collective-permute-done.7.other_ref.refs_4_), custom_call_target="tpu_custom_call" | custom-call | tf_op jit(solution)/shard_map/pallas_call | solution.py:175
  25.2 0.0 copy-start
  25.3 2.0 %copy-done = bf16[16,2,256,256]{3,2,1,0:T(8,128)(2,1)} copy-done((bf16[16,2,256,256]{3,2,1,0:T(8,128)(2,1)}, bf16[16,2,256,256]{3,2,1,0:T(8,128)(2,1)S(1)}, u32[]{:S(2)}) %copy-start) | copy-done | bytes 4194328
  27.3 6.8 %all-to-all-start = ((bf16[16,2,256,256]{3,2,1,0:T(8,128)(2,1)}), bf16[16,2,256,256]{3,2,1,0:T(8,128)(2,1)}, u32[]{:S(2)}, u32[]{:S(2)}) async-start(bf16[16,2,256,256]{3,2,1,0:T(8,128)(2,1)} %copy-done), calls=%async_computation | async-start | bytes 8388608 | tf_op jit(solution)/shard_map/all_to_all | solution.py:183
  34.1 0.0 collective-permute-done.refs_5_
  34.1 2.6 %collective-permute-start.1 = (bf16[2,256,256]{2,1,0:T(8,128)(2,1)S(1)}, bf16[2,256,256]{2,1,0:T(8,128)(2,1)S(1)}, u32[]{:S(2)}, u32[]{:S(2)}) collective-permute-start(bf16[2,256,256]{2,1,0:T(8,128)(2,1)S(1)} %collective-permute-done.refs_5_), channel_id=1, source_target_pairs={{0,32},{32,64},{64,96},{96,128},{128,160},{160,192},{192,224},{224... | collective-permute-start | bytes 786440 | tf_op jit(solution)/shard_map/ppermute | solution.py:171
  36.7 0.0 collective-permute-done.9.refs_6_
  36.7 2.6 %collective-permute-start.10 = (bf16[2,256,256]{2,1,0:T(8,128)(2,1)S(1)}, bf16[2,256,256]{2,1,0:T(8,128)(2,1)S(1)}, u32[]{:S(2)}, u32[]{:S(2)}) collective-permute-start(bf16[2,256,256]{2,1,0:T(8,128)(2,1)S(1)} %collective-permute-done.9.refs_6_), channel_id=1, source_target_pairs={{0,32},{32,64},{64,96},{96,128},{128,160},{160,192},{192,224},{224... | collective-permute-start | bytes 786440 | tf_op jit(solution)/shard_map/ppermute | solution.py:171
  39.4 2.2 %collective-permute-done.1.refs_7_ = bf16[2,256,256]{2,1,0:T(8,128)(2,1)S(1)} collective-permute-done((bf16[2,256,256]{2,1,0:T(8,128)(2,1)S(1)}, bf16[2,256,256]{2,1,0:T(8,128)(2,1)S(1)}, u32[]{:S(2)}, u32[]{:S(2)}) %collective-permute-start.1) | collective-permute-done | bytes 262176 | tf_op jit(solution)/shard_map/ppermute | solution.py:171
  41.6 3.8 %collective-permute-start.2 = (bf16[2,256,256]{2,1,0:T(8,128)(2,1)S(1)}, bf16[2,256,256]{2,1,0:T(8,128)(2,1)S(1)}, u32[]{:S(2)}, u32[]{:S(2)}) collective-permute-start(bf16[2,256,256]{2,1,0:T(8,128)(2,1)S(1)} %collective-permute-done.1.refs_7_), channel_id=1, source_target_pairs={{0,32},{32,64},{64,96},{96,128},{128,160},{160,192},{192,224},{224... | collective-permute-start | bytes 786440 | tf_op jit(solution)/shard_map/ppermute | solution.py:171
  45.5 0.0 collective-permute-done.10.refs_8_
  45.5 2.8 %collective-permute-start.11 = (bf16[2,256,256]{2,1,0:T(8,128)(2,1)S(1)}, bf16[2,256,256]{2,1,0:T(8,128)(2,1)S(1)}, u32[]{:S(2)}, u32[]{:S(2)}) collective-permute-start(bf16[2,256,256]{2,1,0:T(8,128)(2,1)S(1)} %collective-permute-done.10.refs_8_), channel_id=1, source_target_pairs={{0,32},{32,64},{64,96},{96,128},{128,160},{160,192},{192,224},{224... | collective-permute-start | bytes 786440 | tf_op jit(solution)/shard_map/ppermute | solution.py:171
  48.3 0.9 collective-permute-done.2.refs_9_
  49.1 5.0 %collective-permute-start.3 = (bf16[2,256,256]{2,1,0:T(8,128)(2,1)S(1)}, bf16[2,256,256]{2,1,0:T(8,128)(2,1)S(1)}, u32[]{:S(2)}, u32[]{:S(2)}) collective-permute-start(bf16[2,256,256]{2,1,0:T(8,128)(2,1)S(1)} %collective-permute-done.2.refs_9_), channel_id=1, source_target_pairs={{0,32},{32,64},{64,96},{96,128},{128,160},{160,192},{192,224},{224... | collective-permute-start | bytes 786440 | tf_op jit(solution)/shard_map/ppermute | solution.py:171
  54.2 0.0 collective-permute-done.11.refs_10_
  54.2 2.8 %collective-permute-start.12 = (bf16[2,256,256]{2,1,0:T(8,128)(2,1)S(1)}, bf16[2,256,256]{2,1,0:T(8,128)(2,1)S(1)}, u32[]{:S(2)}, u32[]{:S(2)}) collective-permute-start(bf16[2,256,256]{2,1,0:T(8,128)(2,1)S(1)} %collective-permute-done.11.refs_10_), channel_id=1, source_target_pairs={{0,32},{32,64},{64,96},{96,128},{128,160},{160,192},{192,224},{224... | collective-permute-start | bytes 786440 | tf_op jit(solution)/shard_map/ppermute | solution.py:171
  57.0 0.5 collective-permute-done.3.refs_11_
  57.5 5.4 %collective-permute-start.4 = (bf16[2,256,256]{2,1,0:T(8,128)(2,1)S(1)}, bf16[2,256,256]{2,1,0:T(8,128)(2,1)S(1)}, u32[]{:S(2)}, u32[]{:S(2)}) collective-permute-start(bf16[2,256,256]{2,1,0:T(8,128)(2,1)S(1)} %collective-permute-done.3.refs_11_), channel_id=1, source_target_pairs={{0,32},{32,64},{64,96},{96,128},{128,160},{160,192},{192,224},{224... | collective-permute-start | bytes 786440 | tf_op jit(solution)/shard_map/ppermute | solution.py:171
  62.9 0.0 collective-permute-done.12.refs_12_
  62.9 2.8 %collective-permute-start.13 = (bf16[2,256,256]{2,1,0:T(8,128)(2,1)S(1)}, bf16[2,256,256]{2,1,0:T(8,128)(2,1)S(1)}, u32[]{:S(2)}, u32[]{:S(2)}) collective-permute-start(bf16[2,256,256]{2,1,0:T(8,128)(2,1)S(1)} %collective-permute-done.12.refs_12_), channel_id=1, source_target_pairs={{0,32},{32,64},{64,96},{96,128},{128,160},{160,192},{192,224},{224... | collective-permute-start | bytes 786440 | tf_op jit(solution)/shard_map/ppermute | solution.py:171
  65.7 0.5 collective-permute-done.4.refs_13_
  66.2 5.4 %collective-permute-start.5 = (bf16[2,256,256]{2,1,0:T(8,128)(2,1)S(1)}, bf16[2,256,256]{2,1,0:T(8,128)(2,1)S(1)}, u32[]{:S(2)}, u32[]{:S(2)}) collective-permute-start(bf16[2,256,256]{2,1,0:T(8,128)(2,1)S(1)} %collective-permute-done.4.refs_13_), channel_id=1, source_target_pairs={{0,32},{32,64},{64,96},{96,128},{128,160},{160,192},{192,224},{224... | collective-permute-start | bytes 786440 | tf_op jit(solution)/shard_map/ppermute | solution.py:171
  71.6 0.0 collective-permute-done.13.refs_14_
  71.6 2.8 %collective-permute-start.14 = (bf16[2,256,256]{2,1,0:T(8,128)(2,1)S(1)}, bf16[2,256,256]{2,1,0:T(8,128)(2,1)S(1)}, u32[]{:S(2)}, u32[]{:S(2)}) collective-permute-start(bf16[2,256,256]{2,1,0:T(8,128)(2,1)S(1)} %collective-permute-done.13.refs_14_), channel_id=1, source_target_pairs={{0,32},{32,64},{64,96},{96,128},{128,160},{160,192},{192,224},{224... | collective-permute-start | bytes 786440 | tf_op jit(solution)/shard_map/ppermute | solution.py:171
  74.4 0.0 copy-start.3
  74.4 0.7 copy-done.3
  75.1 0.0 collective-permute-done.5.refs_15_
  75.1 5.2 %collective-permute-start.6 = (bf16[2,256,256]{2,1,0:T(8,128)(2,1)S(1)}, bf16[2,256,256]{2,1,0:T(8,128)(2,1)}, u32[]{:S(2)}, u32[]{:S(2)}) collective-permute-start(bf16[2,256,256]{2,1,0:T(8,128)(2,1)S(1)} %collective-permute-done.5.refs_15_), channel_id=1, source_target_pairs={{0,32},{32,64},{64,96},{96,128},{128,160},{160,192},{192,224},{224... | collective-permute-start | bytes 786440 | tf_op jit(solution)/shard_map/ppermute | solution.py:171
  80.3 0.7 copy-done.5
  81.0 0.0 collective-permute-done.14.refs_16_
  81.0 2.1 %collective-permute-start.15 = (bf16[2,256,256]{2,1,0:T(8,128)(2,1)S(1)}, bf16[2,256,256]{2,1,0:T(8,128)(2,1)}, u32[]{:S(2)}, u32[]{:S(2)}) collective-permute-start(bf16[2,256,256]{2,1,0:T(8,128)(2,1)S(1)} %collective-permute-done.14.refs_16_), channel_id=1, source_target_pairs={{0,32},{32,64},{64,96},{96,128},{128,160},{160,192},{192,224},{224... | collective-permute-start | bytes 786440 | tf_op jit(solution)/shard_map/ppermute | solution.py:171
  83.1 0.7 copy-done.7
  83.8 0.1 pad_add_fusion.refs_0_
  83.9 0.0 collective-permute-done.6.refs_1_.refs_17_
  83.9 4.8 %collective-permute-start.8 = (bf16[2,256,256]{2,1,0:T(8,128)(2,1)}, bf16[2,256,256]{2,1,0:T(8,128)(2,1)S(1)}, u32[]{:S(2)}, u32[]{:S(2)}) collective-permute-start(bf16[2,256,256]{2,1,0:T(8,128)(2,1)} %collective-permute-done.6.refs_1_.refs_17_), channel_id=1, source_target_pairs={{16,496},{48,16},{80,48},{112,80},{144,112},{176,144},{208,176},{2... | collective-permute-start | bytes 786440 | tf_op jit(solution)/shard_map/ppermute | solution.py:171
  88.7 0.0 collective-permute-done.15.refs_18_
  88.7 2.8 %collective-permute-start.16 = (bf16[2,256,256]{2,1,0:T(8,128)(2,1)}, bf16[2,256,256]{2,1,0:T(8,128)(2,1)S(1)}, u32[]{:S(2)}, u32[]{:S(2)}) collective-permute-start(bf16[2,256,256]{2,1,0:T(8,128)(2,1)} %collective-permute-done.15.refs_18_), channel_id=1, source_target_pairs={{16,496},{48,16},{80,48},{112,80},{144,112},{176,144},{208,176},{2... | collective-permute-start | bytes 786440 | tf_op jit(solution)/shard_map/ppermute | solution.py:171
  91.5 1.2 shard_map.29.refs_0_
  92.7 0.0 all-to-all-done.refs_2_
  92.8 0.0 copy-start.4
  92.8 0.9 copy-done.4
  93.7 0.9 copy-done.6
  94.7 0.9 copy-done.8
  95.6 4.7 %shard_map.31 = (f32[2,256,256]{2,1,0:T(8,128)S(1)}, f32[2,256,256]{2,1,0:T(8,128)S(1)}) custom-call(s32[18]{0:T(128)S(1)} %shard_map.29.refs_0_, s32[1]{0:T(128)} %bitcast.3.refs_1_, bf16[16,2,256,256]{3,2,1,0:T(8,128)(2,1)} %all-to-all-done.refs_2_, bf16[2,256,256]{2,1,0:T(8,128)(2,1)S(1)} %shard_map.28.mine_ref.refs_3_, ...), custom_call_target="tpu_custom_call" | custom-call | flops 2147483648 | bytes 8388608 | tf_op jit(solution)/shard_map/pallas_call | solution.py:106
  100.3 0.0 copy-start.10
  100.3 0.0 collective-permute-done.8.refs_3_
  100.3 0.0 collective-permute-done.16.refs_4_
  100.4 1.9 %shard_map.33 = f32[2,256,256]{2,1,0:T(8,128)S(1)} custom-call(s32[18]{0:T(128)S(1)} %shard_map.29.refs_0_, s32[1]{0:T(128)} %bitcast.3.refs_1_, bf16[16,2,256,256]{3,2,1,0:T(8,128)(2,1)} %all-to-all-done.refs_2_, bf16[2,256,256]{2,1,0:T(8,128)(2,1)S(1)} %collective-permute-done.8.refs_3_, bf16[2,256,256]{2,1,0:T(8,128)(2,1)S(1)} %collective-permute-done.16.refs_4_, ...), custom_call_target="tpu_custom_call" | custom-call | flops 134217728 | bytes 1048576 | tf_op jit(solution)/shard_map/pallas_call | solution.py:106
  102.2 0.0 copy-start.2
  102.2 2.1 %collective-permute-start.17 = (f32[2,256,256]{2,1,0:T(8,128)S(1)}, f32[2,256,256]{2,1,0:T(8,128)S(1)}, u32[]{:S(2)}, u32[]{:S(2)}) collective-permute-start(f32[2,256,256]{2,1,0:T(8,128)S(1)} %shard_map.33), channel_id=1, source_target_pairs={{0,16},{16,0},{1,17},{17,1},{2,18},{18,2},{3,19},{19,3},{4,20},{20... | collective-permute-start | bytes 1572872 | tf_op jit(solution)/shard_map/ppermute | solution.py:203
  104.3 0.2 compare_reduce_fusion
  104.5 1.9 %shard_map.32.mine_ref = f32[2,256,256]{2,1,0:T(8,128)S(1)} custom-call(s32[18]{0:T(128)S(1)} %shard_map.29.refs_0_, s32[1]{0:T(128)} %bitcast.3.refs_1_, bf16[16,2,256,256]{3,2,1,0:T(8,128)(2,1)} %all-to-all-done.refs_2_, bf16[2,256,256]{2,1,0:T(8,128)(2,1)S(1)} %collective-permute-done.8.refs_3_, bf16[2,256,256]{2,1,0:T(8,128)(2,1)S(1)} %collective-permute-done.16.refs_4_, ...), custom_call_target="tpu_custom_call" | custom-call | flops 134217728 | bytes 1048576 | tf_op jit(solution)/shard_map/pallas_call | solution.py:106
  106.4 0.0 collective-permute-done.17.other_ref
  106.4 0.6 shard_map.34
  107.0 1.8 %all-gather.1 = f32[2,2,256]{2,1,0:T(2,128)S(1)} all-gather(f32[1,2,256]{2,1,0:T(2,128)S(1)} %bitcast.9), channel_id=2, replica_groups=mesh['z'=16,'core'=2,'y'=4,'x'=4] {'core'}, dimensions={0}, use_global_device_ids=true | all-gather | bytes 6144 | tf_op jit(solution)/shard_map/all_gather | solution.py:216
  108.8 23.6 %all_to_all.10.refs_4_ = f32[16,2,256]{2,1,0:T(2,128)S(1)} all-to-all(f32[16,2,256]{2,1,0:T(2,128)S(1)} %broadcast_in_dim.4), channel_id=1, replica_groups=mesh['z'=16,'core'=2,'y'=4,'x'=4] {'z'}, dimensions={0} | all-to-all | bytes 65536 | tf_op jit(solution)/shard_map/all_to_all | solution.py:217
  132.4 1.4 %shard_map.35 = f32[2,256,256]{2,1,0:T(8,128)} custom-call(s32[2]{0:T(128)S(1)} %bitcast.12, s32[2]{0:T(128)S(1)} %multiply_add_fusion.target_ref.refs_1_, bf16[2,256,256]{2,1,0:T(8,128)(2,1)S(1)} %bitcast.8, f32[2,256,256]{2,1,0:T(8,128)S(1)} %get-tuple-element.11.refs_3_, f32[16,2,256]{2,1,0:T(2,128)S(1)} %all_to_all.10.refs_4_), custom_call_target="tpu_custom_call" | custom-call | tf_op jit(solution)/shard_map/pallas_call | solution.py:225
  (12 shorter events, 0.1 us)
Async XLA Ops:
  0.0 0.9 copy-start.1
  1.0 0.7 copy-start.9
  2.3 14.6 %collective-permute-start.7 = (bf16[2,256,256]{2,1,0:T(8,128)(2,1)S(1)}, bf16[2,256,256]{2,1,0:T(8,128)(2,1)S(1)}, u32[]{:S(2)}, u32[]{:S(2)}) collective-permute-start(bf16[2,256,256]{2,1,0:T(8,128)(2,1)S(1)} %shard_map.28.mine_ref.refs_3_), channel_id=1, source_target_pairs={{0,16},{16,0},{1,17},{17,1},{2,18},{18,2},{3,19},{19,3},{4,20},{20... | collective-permute-start | bytes 786440 | tf_op jit(solution)/shard_map/ppermute | solution.py:163
  11.1 23.0 %collective-permute-start = (bf16[2,256,256]{2,1,0:T(8,128)(2,1)S(1)}, bf16[2,256,256]{2,1,0:T(8,128)(2,1)S(1)}, u32[]{:S(2)}, u32[]{:S(2)}) collective-permute-start(bf16[2,256,256]{2,1,0:T(8,128)(2,1)S(1)} %shard_map.28.mine_ref.refs_3_), channel_id=1, source_target_pairs={{0,32},{32,64},{64,96},{96,128},{128,160},{160,192},{192,224},{224... | collective-permute-start | bytes 786440 | tf_op jit(solution)/shard_map/ppermute | solution.py:171
  16.8 19.9 %collective-permute-start.9 = (bf16[2,256,256]{2,1,0:T(8,128)(2,1)S(1)}, bf16[2,256,256]{2,1,0:T(8,128)(2,1)S(1)}, u32[]{:S(2)}, u32[]{:S(2)}) collective-permute-start(bf16[2,256,256]{2,1,0:T(8,128)(2,1)S(1)} %collective-permute-done.7.other_ref.refs_4_), channel_id=1, source_target_pairs={{0,32},{32,64},{64,96},{96,128},{128,160},{160,192},{192,224},{224... | collective-permute-start | bytes 786440 | tf_op jit(solution)/shard_map/ppermute | solution.py:171
  25.2 2.0 %copy-start = (bf16[16,2,256,256]{3,2,1,0:T(8,128)(2,1)}, bf16[16,2,256,256]{3,2,1,0:T(8,128)(2,1)S(1)}, u32[]{:S(2)}) copy-start(bf16[16,2,256,256]{3,2,1,0:T(8,128)(2,1)S(1)} %shard_map.30) | copy-start | bytes 12582916
  27.3 65.5 %all-to-all-start = ((bf16[16,2,256,256]{3,2,1,0:T(8,128)(2,1)}), bf16[16,2,256,256]{3,2,1,0:T(8,128)(2,1)}, u32[]{:S(2)}, u32[]{:S(2)}) async-start(bf16[16,2,256,256]{3,2,1,0:T(8,128)(2,1)} %copy-done), calls=%async_computation | async-start | bytes 8388608 | tf_op jit(solution)/shard_map/all_to_all | solution.py:183
  34.1 7.5 %collective-permute-start.1 = (bf16[2,256,256]{2,1,0:T(8,128)(2,1)S(1)}, bf16[2,256,256]{2,1,0:T(8,128)(2,1)S(1)}, u32[]{:S(2)}, u32[]{:S(2)}) collective-permute-start(bf16[2,256,256]{2,1,0:T(8,128)(2,1)S(1)} %collective-permute-done.refs_5_), channel_id=1, source_target_pairs={{0,32},{32,64},{64,96},{96,128},{128,160},{160,192},{192,224},{224... | collective-permute-start | bytes 786440 | tf_op jit(solution)/shard_map/ppermute | solution.py:171
  36.7 8.7 %collective-permute-start.10 = (bf16[2,256,256]{2,1,0:T(8,128)(2,1)S(1)}, bf16[2,256,256]{2,1,0:T(8,128)(2,1)S(1)}, u32[]{:S(2)}, u32[]{:S(2)}) collective-permute-start(bf16[2,256,256]{2,1,0:T(8,128)(2,1)S(1)} %collective-permute-done.9.refs_6_), channel_id=1, source_target_pairs={{0,32},{32,64},{64,96},{96,128},{128,160},{160,192},{192,224},{224... | collective-permute-start | bytes 786440 | tf_op jit(solution)/shard_map/ppermute | solution.py:171
  41.6 7.5 %collective-permute-start.2 = (bf16[2,256,256]{2,1,0:T(8,128)(2,1)S(1)}, bf16[2,256,256]{2,1,0:T(8,128)(2,1)S(1)}, u32[]{:S(2)}, u32[]{:S(2)}) collective-permute-start(bf16[2,256,256]{2,1,0:T(8,128)(2,1)S(1)} %collective-permute-done.1.refs_7_), channel_id=1, source_target_pairs={{0,32},{32,64},{64,96},{96,128},{128,160},{160,192},{192,224},{224... | collective-permute-start | bytes 786440 | tf_op jit(solution)/shard_map/ppermute | solution.py:171
  45.5 8.7 %collective-permute-start.11 = (bf16[2,256,256]{2,1,0:T(8,128)(2,1)S(1)}, bf16[2,256,256]{2,1,0:T(8,128)(2,1)S(1)}, u32[]{:S(2)}, u32[]{:S(2)}) collective-permute-start(bf16[2,256,256]{2,1,0:T(8,128)(2,1)S(1)} %collective-permute-done.10.refs_8_), channel_id=1, source_target_pairs={{0,32},{32,64},{64,96},{96,128},{128,160},{160,192},{192,224},{224... | collective-permute-start | bytes 786440 | tf_op jit(solution)/shard_map/ppermute | solution.py:171
  49.1 8.3 %collective-permute-start.3 = (bf16[2,256,256]{2,1,0:T(8,128)(2,1)S(1)}, bf16[2,256,256]{2,1,0:T(8,128)(2,1)S(1)}, u32[]{:S(2)}, u32[]{:S(2)}) collective-permute-start(bf16[2,256,256]{2,1,0:T(8,128)(2,1)S(1)} %collective-permute-done.2.refs_9_), channel_id=1, source_target_pairs={{0,32},{32,64},{64,96},{96,128},{128,160},{160,192},{192,224},{224... | collective-permute-start | bytes 786440 | tf_op jit(solution)/shard_map/ppermute | solution.py:171
  54.2 8.7 %collective-permute-start.12 = (bf16[2,256,256]{2,1,0:T(8,128)(2,1)S(1)}, bf16[2,256,256]{2,1,0:T(8,128)(2,1)S(1)}, u32[]{:S(2)}, u32[]{:S(2)}) collective-permute-start(bf16[2,256,256]{2,1,0:T(8,128)(2,1)S(1)} %collective-permute-done.11.refs_10_), channel_id=1, source_target_pairs={{0,32},{32,64},{64,96},{96,128},{128,160},{160,192},{192,224},{224... | collective-permute-start | bytes 786440 | tf_op jit(solution)/shard_map/ppermute | solution.py:171
  57.5 8.7 %collective-permute-start.4 = (bf16[2,256,256]{2,1,0:T(8,128)(2,1)S(1)}, bf16[2,256,256]{2,1,0:T(8,128)(2,1)S(1)}, u32[]{:S(2)}, u32[]{:S(2)}) collective-permute-start(bf16[2,256,256]{2,1,0:T(8,128)(2,1)S(1)} %collective-permute-done.3.refs_11_), channel_id=1, source_target_pairs={{0,32},{32,64},{64,96},{96,128},{128,160},{160,192},{192,224},{224... | collective-permute-start | bytes 786440 | tf_op jit(solution)/shard_map/ppermute | solution.py:171
  62.9 8.7 %collective-permute-start.13 = (bf16[2,256,256]{2,1,0:T(8,128)(2,1)S(1)}, bf16[2,256,256]{2,1,0:T(8,128)(2,1)S(1)}, u32[]{:S(2)}, u32[]{:S(2)}) collective-permute-start(bf16[2,256,256]{2,1,0:T(8,128)(2,1)S(1)} %collective-permute-done.12.refs_12_), channel_id=1, source_target_pairs={{0,32},{32,64},{64,96},{96,128},{128,160},{160,192},{192,224},{224... | collective-permute-start | bytes 786440 | tf_op jit(solution)/shard_map/ppermute | solution.py:171
  66.2 8.9 %collective-permute-start.5 = (bf16[2,256,256]{2,1,0:T(8,128)(2,1)S(1)}, bf16[2,256,256]{2,1,0:T(8,128)(2,1)S(1)}, u32[]{:S(2)}, u32[]{:S(2)}) collective-permute-start(bf16[2,256,256]{2,1,0:T(8,128)(2,1)S(1)} %collective-permute-done.4.refs_13_), channel_id=1, source_target_pairs={{0,32},{32,64},{64,96},{96,128},{128,160},{160,192},{192,224},{224... | collective-permute-start | bytes 786440 | tf_op jit(solution)/shard_map/ppermute | solution.py:171
  71.6 9.4 %collective-permute-start.14 = (bf16[2,256,256]{2,1,0:T(8,128)(2,1)S(1)}, bf16[2,256,256]{2,1,0:T(8,128)(2,1)S(1)}, u32[]{:S(2)}, u32[]{:S(2)}) collective-permute-start(bf16[2,256,256]{2,1,0:T(8,128)(2,1)S(1)} %collective-permute-done.13.refs_14_), channel_id=1, source_target_pairs={{0,32},{32,64},{64,96},{96,128},{128,160},{160,192},{192,224},{224... | collective-permute-start | bytes 786440 | tf_op jit(solution)/shard_map/ppermute | solution.py:171
  74.4 0.7 copy-start.3
  75.1 8.8 %collective-permute-start.6 = (bf16[2,256,256]{2,1,0:T(8,128)(2,1)S(1)}, bf16[2,256,256]{2,1,0:T(8,128)(2,1)}, u32[]{:S(2)}, u32[]{:S(2)}) collective-permute-start(bf16[2,256,256]{2,1,0:T(8,128)(2,1)S(1)} %collective-permute-done.5.refs_15_), channel_id=1, source_target_pairs={{0,32},{32,64},{64,96},{96,128},{128,160},{160,192},{192,224},{224... | collective-permute-start | bytes 786440 | tf_op jit(solution)/shard_map/ppermute | solution.py:171
  80.3 0.7 copy-start.5
  81.0 7.7 %collective-permute-start.15 = (bf16[2,256,256]{2,1,0:T(8,128)(2,1)S(1)}, bf16[2,256,256]{2,1,0:T(8,128)(2,1)}, u32[]{:S(2)}, u32[]{:S(2)}) collective-permute-start(bf16[2,256,256]{2,1,0:T(8,128)(2,1)S(1)} %collective-permute-done.14.refs_16_), channel_id=1, source_target_pairs={{0,32},{32,64},{64,96},{96,128},{128,160},{160,192},{192,224},{224... | collective-permute-start | bytes 786440 | tf_op jit(solution)/shard_map/ppermute | solution.py:171
  83.1 0.7 copy-start.7
  83.9 16.4 %collective-permute-start.8 = (bf16[2,256,256]{2,1,0:T(8,128)(2,1)}, bf16[2,256,256]{2,1,0:T(8,128)(2,1)S(1)}, u32[]{:S(2)}, u32[]{:S(2)}) collective-permute-start(bf16[2,256,256]{2,1,0:T(8,128)(2,1)} %collective-permute-done.6.refs_1_.refs_17_), channel_id=1, source_target_pairs={{16,496},{48,16},{80,48},{112,80},{144,112},{176,144},{208,176},{2... | collective-permute-start | bytes 786440 | tf_op jit(solution)/shard_map/ppermute | solution.py:171
  88.7 11.6 %collective-permute-start.16 = (bf16[2,256,256]{2,1,0:T(8,128)(2,1)}, bf16[2,256,256]{2,1,0:T(8,128)(2,1)S(1)}, u32[]{:S(2)}, u32[]{:S(2)}) collective-permute-start(bf16[2,256,256]{2,1,0:T(8,128)(2,1)} %collective-permute-done.15.refs_18_), channel_id=1, source_target_pairs={{16,496},{48,16},{80,48},{112,80},{144,112},{176,144},{208,176},{2... | collective-permute-start | bytes 786440 | tf_op jit(solution)/shard_map/ppermute | solution.py:171
  92.8 1.0 copy-start.4
  93.7 0.9 copy-start.6
  94.7 0.9 copy-start.8
  100.3 4.0 %copy-start.10 = (s32[1,2]{1,0:T(1,128)S(1)}, s32[1,2]{1,0:T(1,128)}, u32[]{:S(2)}) copy-start(s32[1,2]{1,0:T(1,128)} %param.4) | copy-start | bytes 28
  102.2 30.1 %copy-start.2 = (bf16[1,2,256,256]{3,2,1,0:T(8,128)(2,1)S(1)}, bf16[1,2,256,256]{3,2,1,0:T(8,128)(2,1)}, u32[]{:S(2)}) copy-start(bf16[1,2,256,256]{3,2,1,0:T(8,128)(2,1)} %param.3) | copy-start | bytes 786436
  102.2 4.1 %collective-permute-start.17 = (f32[2,256,256]{2,1,0:T(8,128)S(1)}, f32[2,256,256]{2,1,0:T(8,128)S(1)}, u32[]{:S(2)}, u32[]{:S(2)}) collective-permute-start(f32[2,256,256]{2,1,0:T(8,128)S(1)} %shard_map.33), channel_id=1, source_target_pairs={{0,16},{16,0},{1,17},{17,1},{2,18},{18,2},{3,19},{19,3},{4,20},{20... | collective-permute-start | bytes 1572872 | tf_op jit(solution)/shard_map/ppermute | solution.py:203

commit v4 on v3

v4 whole, which is shorter than its diff:
```python
import functools

import jax
import jax.numpy as jnp
from jax import lax
from jax.experimental import pallas as pl
from jax.experimental.pallas import tpu as pltpu
from jax.sharding import Mesh, PartitionSpec as P

ROWS = ("z", "core")
COLS = ("y", "x")
SMEM = pl.BlockSpec(memory_space=pltpu.SMEM)
VMEM = pl.BlockSpec(memory_space=pltpu.VMEM)
ANY = pl.BlockSpec(memory_space=pl.ANY)
HBM = pl.BlockSpec(memory_space=pltpu.HBM)
MIB = 1024 * 1024
SWAP = [(0, 1), (1, 0)]
FLOPS = 26 * 10**9


def params(mib):
    return pltpu.CompilerParams(vmem_limit_bytes=mib * MIB)


def order_kernel(columns, own_ref, column_ref, tiles_ref, ordered_ref):
    for place in range(2):
        target = column_ref[0] + columns * place
        first = (own_ref[0] == target).astype(jnp.float32)
        second = (own_ref[1] == target).astype(jnp.float32)
        value = tiles_ref[0].astype(jnp.float32) * first + tiles_ref[1].astype(jnp.float32) * second
        ordered_ref[place] = value.astype(ordered_ref.dtype)


def settle_kernel(given_ref, same_ref):
    del given_ref, same_ref


def fetch(plan, guard_ref, start):
    for copies, guard in plan:
        def go(copies=copies):
            for copy in copies:
                copy.start() if start else copy.wait()

        if guard is None:
            go()
        else:
            pl.when(guard_ref[0] == guard)(go)


def product_kernel(planes, rows, groups, columns, plane_ref, core_ref, left_ref, *refs):
    count = 2 * len(planes)
    rights, refs = refs[:count], refs[count:]
    totals, (held, kept, sems) = refs[-3 - len(rows) : -3], refs[-3:]
    carried = len(refs) > 3 + len(rows)
    core = core_ref[0]
    plan = []
    for i, (distance, guard) in enumerate(planes):
        copies = []
        for j in range(2):
            inner = 2 * (plane_ref[0] + jnp.where(core == 0, -distance, distance))
            inner += jnp.where(core == 0, j, 1 - j)
            place = lax.rem(inner + 2 * columns, columns)
            for n, row in enumerate(rows):
                copies.append(
                    pltpu.make_async_copy(
                        left_ref.at[place, row], held.at[2 * i + j, n], sems.at[2 * i + j, n]
                    )
                )
            copies.append(
                pltpu.make_async_copy(
                    rights[2 * i + j], kept.at[2 * i + j], sems.at[2 * i + j, len(rows)]
                )
            )
        plan.append((copies, guard))
    for group in groups:
        fetch([plan[i] for i in group], core_ref, True)
    if not carried:
        for total in totals:
            total[...] = jnp.zeros_like(total)
    width = held.shape[-1]
    for group in groups:
        fetch([plan[i] for i in group], core_ref, False)

        def add(group=group):
            tiles = [2 * i + j for i in group for j in range(2)]
            left = jnp.concatenate(
                [held[i].reshape(len(rows) * width, width) for i in tiles], axis=1
            )
            for column in range(2):
                right = jnp.concatenate([kept[i, column] for i in tiles], axis=0)
                product = jnp.dot(left, right, preferred_element_type=jnp.float32)
                for n, total in enumerate(totals):
                    total[column] += product[n * width : (n + 1) * width]

        guard = planes[group[0]][1]
        if guard is None:
            add()
        else:
            pl.when(core == guard)(add)


def products(totals, rows, plane, core, left, held, planes, groups):
    width = left.shape[-1]
    tiles = [tile for distance, _ in planes for tile in held[distance]]
    if totals is None:
        tiles = [pltpu.with_memory_space_constraint(tile, pltpu.HBM) for tile in tiles]
    given = [] if totals is None else [totals[row] for row in rows]
    kernel = functools.partial(product_kernel, planes, rows, groups, left.shape[0])
    out = pl.pallas_call(
        kernel,
        in_specs=[SMEM, SMEM, HBM] + [HBM] * len(tiles) + [VMEM] * len(given),
        out_specs=[VMEM] * len(rows),
        out_shape=[jax.ShapeDtypeStruct((2, width, width), jnp.float32)] * len(rows),
        scratch_shapes=[
            pltpu.VMEM((len(tiles), len(rows), width, width), left.dtype),
            pltpu.VMEM((len(tiles), 2, width, width), left.dtype),
            pltpu.SemaphoreType.DMA((len(tiles), len(rows) + 1)),
        ],
        input_output_aliases={3 + len(tiles) + n: n for n in range(len(given))},
        compiler_params=params(10),
        cost_estimate=pl.CostEstimate(
            flops=4 * len(tiles) * len(rows) * width**3,
            bytes_accessed=4 * len(tiles) * (len(rows) + 2) * width**2,
            transcendentals=0,
        ),
    )(plane, core, left, *tiles, *given)
    return dict(zip(rows, out))


def square_kernel(columns, own_ref, column_ref, mine_ref, other_ref, inflated_ref, sums_ref):
    for place in range(2):
        target = column_ref[0] + columns * place
        kept = (own_ref[0] == target) | (own_ref[1] == target)
        value = mine_ref[place] + other_ref[place]
        value = jnp.where(kept, value * value, 0.0)
        inflated_ref[place] = value
        sums_ref[place : place + 1, :] = jnp.sum(value, axis=0, keepdims=True)


def blend_kernel(scale, columns, own_ref, column_ref, tiles_ref, inflated_ref, parts_ref, out_ref):
    totals = jnp.sum(parts_ref[...], axis=0)
    for slot in range(2):
        tile = tiles_ref[slot].astype(jnp.float32)
        for place in range(2):
            @pl.when(own_ref[slot] == column_ref[0] + columns * place)
            def _():
                normed = inflated_ref[place] * scale / totals[place : place + 1, :]
                out_ref[slot] = 0.5 * tile + 0.5 * normed

        @pl.when(own_ref[slot] < 0)
        def _():
            out_ref[slot] = jnp.zeros_like(tile)


def settle(value):
    return pl.pallas_call(
        settle_kernel,
        in_specs=[ANY],
        out_specs=ANY,
        out_shape=jax.ShapeDtypeStruct(value.shape, value.dtype),
        input_output_aliases={0: 0},
        compiler_params=params(1),
        cost_estimate=pl.CostEstimate(flops=FLOPS, bytes_accessed=0, transcendentals=0),
    )(value)


def on_device(flow_tiles, tile_cols, pairs):
    width = flow_tiles.shape[3]
    planes, cores = lax.axis_size("z"), lax.axis_size("core")
    columns = lax.axis_size(COLS)
    plane, core, column = lax.axis_index("z"), lax.axis_index("core"), lax.axis_index(COLS)
    plane_ref, core_ref, column_ref = (
        i.astype(jnp.int32).reshape(1) for i in (plane, core, column)
    )
    own = tile_cols[0]
    tiles = flow_tiles[0]
    mine = pl.pallas_call(
        functools.partial(order_kernel, columns),
        in_specs=[SMEM, SMEM, VMEM],
        out_specs=VMEM,
        out_shape=jax.ShapeDtypeStruct((2, width, width), tiles.dtype),
        compiler_params=params(4),
    )(own, column_ref, tiles)
    other = lax.ppermute(mine, "core", SWAP)

    half = planes // 2
    ring = [(2 * z, 2 * ((z + 1) % planes)) for z in range(planes)]
    back = [(2 * z + 1, 2 * ((z - 1) % planes) + 1) for z in range(planes)]
    held = [(mine, other)]
    for step in range(1, half + 1):
        perm = ring + back if step < half else back
        if step == half:
            held[-1] = (settle(held[-1][0]), held[-1][1])
        held.append(tuple(lax.ppermute(t, ROWS, perm) for t in held[-1]))

    low = lax.rem(column - 2 * (plane - half + 1) + 2 * columns, 2 * columns)
    place = jnp.where((low < columns) == (core == 0), 0, 1)
    sent = jnp.stack([jnp.where(place == 0, t[0], t[1]) for t in (mine, other)])
    sent = jnp.broadcast_to(sent[None], (columns, *sent.shape))
    left = lax.all_to_all(sent, COLS, 0, 0, tiled=True)

    known = (plane_ref, core_ref, left, held)
    early = [(0, 0)] + [(i, None) for i in range(1, half - 1)]
    totals = products(None, (0, 1), *known, early, [[1, 2], [3, 4], [5, 6], [0]])
    late = [(half - 1, None), (half, 1)]
    outward = products(totals, (1,), *known, late, [[0], [1]])[1]
    received = lax.ppermute(outward, "core", SWAP)
    total = products(totals, (0,), *known, late, [[0], [1]])[0]
    inflated, sums = pl.pallas_call(
        functools.partial(square_kernel, columns),
        in_specs=[SMEM, SMEM, VMEM, VMEM],
        out_specs=[VMEM, VMEM],
        out_shape=[
            jax.ShapeDtypeStruct((2, width, width), jnp.float32),
            jax.ShapeDtypeStruct((2, width), jnp.float32),
        ],
        compiler_params=params(6),
    )(own, column_ref, total, received)
    sums = lax.all_gather(sums, "core", axis=0).sum(axis=0)
    parts = lax.all_to_all(
        jnp.broadcast_to(sums[None], (planes, *sums.shape)), "z", 0, 0, tiled=True
    )
    scale = float(planes * cores * width)
    out = pl.pallas_call(
        functools.partial(blend_kernel, scale, columns),
        in_specs=[SMEM, SMEM, VMEM, VMEM, VMEM],
        out_specs=VMEM,
        out_shape=jax.ShapeDtypeStruct((2, width, width), jnp.float32),
        compiler_params=params(6),
    )(own, column_ref, tiles, inflated, parts)
    return out[None]


def solution(mesh):
    physical = Mesh(mesh.devices.reshape(16, 2, 4, 4), (*ROWS, *COLS))
    tiled = P(ROWS, COLS, None, None)
    return jax.shard_map(
        on_device,
        mesh=physical,
        in_specs=(tiled, P(ROWS, COLS), P((*ROWS, *COLS), None)),
        out_specs=tiled,
        check_vma=False,
    )
```

time: 135 us -> 131 us (0.970)
  waiting for transfers between devices: 4.08 us -> 16 us
  Pallas kernels: 18.1 us -> 9.97 us
  local copies, waits for them, and re-layouts: 8.57 us -> 4.19 us
  blocking collectives: 25.3 us -> 21.8 us
    all_to_all x1, waiting for transfers between devices: 0.01 us -> 8.66 us  [on_device(): left = lax.all_to_all(sent, COLS, 0, 0, tiled=True)]
    pallas_call x8 -> x7, Pallas kernels: 18.1 us -> 9.97 us  [the longest x3 7.28 us: products(): pl.pallas_call(kernel, in_specs=[SMEM, SMEM, HBM] + [HBM] * len(tiles) +...]
    unnamed x22 -> x36, local copies, waits for them, and re-layouts: 8.56 us -> 1.67 us
    all_to_all x1, blocking collectives: 23.6 us -> 20 us  [on_device(): lax.all_to_all(jnp.broadcast_to(sums[None], (planes, *sums.shape)), 'z',...]
    ppermute x16, waiting for transfers between devices: 4.07 us -> 7.14 us  [on_device(): held.append(tuple((lax.ppermute(t, ROWS, perm) for t in held[-1])))]
    broadcast_in_dim x0 -> x1, local copies, waits for them, and re-layouts: none -> 2.5 us  [on_device(): sent = jnp.broadcast_to(sent[None], (columns, *sent.shape))]
  transfers between devices with their start and end apart: 19 -> 19, of which waited for: 4 -> 9; matrix products, arithmetic and copies ran while one was open for 0% -> 2% of each run, Pallas kernels for 10% -> 4%
where the time goes in v4:
time: 131 us
  starting transfers between devices  78 us (60%)
  blocking collectives  21.8 us (17%)
  waiting for transfers between devices  16 us (12%)
  Pallas kernels  9.97 us (8%)
  local copies, waits for them, and re-layouts  4.19 us (3%)
    ppermute x16, starting transfers between devices, on_device(): held.append(tuple((lax.ppermute(t, ROWS, perm) for t in held[-1])))  60.3 us
    all_to_all x1, blocking collectives, on_device(): lax.all_to_all(jnp.broadcast_to(sums[None], (planes, *sums.shape)), 'z',...  20 us
    ppermute x1, starting transfers between devices, on_device(): other = lax.ppermute(mine, 'core', SWAP)  8.79 us
    all_to_all x1, waiting for transfers between devices, on_device(): left = lax.all_to_all(sent, COLS, 0, 0, tiled=True)  8.66 us
    pallas_call x3, Pallas kernels, products(): pl.pallas_call(kernel, in_specs=[SMEM, SMEM, HBM] + [HBM] * len(tiles) +...  7.28 us
    ppermute x16, waiting for transfers between devices, on_device(): held.append(tuple((lax.ppermute(t, ROWS, perm) for t in held[-1])))  7.14 us
    all_to_all x1, starting transfers between devices, on_device(): left = lax.all_to_all(sent, COLS, 0, 0, tiled=True)  6.81 us
  transfers between devices with their start and end apart: 19, of which 9 were waited for; matrix products, arithmetic and copies ran while one was open for 2% of the time, Pallas kernels for 4%

profile of v4, /device:TPU:1, one launch (start us, length us, event | category | flops | bytes accessed | tf_op | source)
XLA Modules:
  0.0 130.5 jit_solution(10118247607756224744)
XLA Ops:
  0.0 0.9 copy-done.1
  1.0 0.7 copy-done.3
  1.6 0.6 shard_map.28.refs_0_
  2.3 0.0 copy-start
  2.3 8.8 %collective-permute-start = (bf16[2,256,256]{2,1,0:T(8,128)(2,1)S(1)}, bf16[2,256,256]{2,1,0:T(8,128)(2,1)S(1)}, u32[]{:S(2)}, u32[]{:S(2)}) collective-permute-start(bf16[2,256,256]{2,1,0:T(8,128)(2,1)S(1)} %shard_map.28.refs_0_), channel_id=1, source_target_pairs={{0,16},{16,0},{1,17},{17,1},{2,18},{18,2},{3,19},{19,3},{4,20},{20... | collective-permute-start | bytes 786440 | tf_op jit(solution)/shard_map/ppermute | solution.py:184
  11.1 5.7 %collective-permute-start.1 = (bf16[2,256,256]{2,1,0:T(8,128)(2,1)S(1)}, bf16[2,256,256]{2,1,0:T(8,128)(2,1)S(1)}, u32[]{:S(2)}, u32[]{:S(2)}) collective-permute-start(bf16[2,256,256]{2,1,0:T(8,128)(2,1)S(1)} %shard_map.28.refs_0_), channel_id=1, source_target_pairs={{0,32},{32,64},{64,96},{96,128},{128,160},{160,192},{192,224},{224... | collective-permute-start | bytes 786440 | tf_op jit(solution)/shard_map/ppermute | solution.py:194
  16.9 0.0 collective-permute-done.refs_1_
  16.9 0.0 copy-start.5
  16.9 2.6 %collective-permute-start.8 = (bf16[2,256,256]{2,1,0:T(8,128)(2,1)S(1)}, bf16[2,256,256]{2,1,0:T(8,128)(2,1)S(1)}, u32[]{:S(2)}, u32[]{:S(2)}) collective-permute-start(bf16[2,256,256]{2,1,0:T(8,128)(2,1)S(1)} %collective-permute-done.refs_1_), channel_id=1, source_target_pairs={{0,32},{32,64},{64,96},{96,128},{128,160},{160,192},{192,224},{224... | collective-permute-start | bytes 786440 | tf_op jit(solution)/shard_map/ppermute | solution.py:194
  19.5 0.6 collective-permute-done.1.refs_2_
  20.1 5.0 %collective-permute-start.2 = (bf16[2,256,256]{2,1,0:T(8,128)(2,1)S(1)}, bf16[2,256,256]{2,1,0:T(8,128)(2,1)S(1)}, u32[]{:S(2)}, u32[]{:S(2)}) collective-permute-start(bf16[2,256,256]{2,1,0:T(8,128)(2,1)S(1)} %collective-permute-done.1.refs_2_), channel_id=1, source_target_pairs={{0,32},{32,64},{64,96},{96,128},{128,160},{160,192},{192,224},{224... | collective-permute-start | bytes 786440 | tf_op jit(solution)/shard_map/ppermute | solution.py:194
  25.2 2.5 %broadcast_in_dim.6 = bf16[16,2,256,256]{3,2,1,0:T(8,128)(2,1)} broadcast(bf16[2,256,256]{2,1,0:T(8,128)(2,1)S(1)} %pad_maximum_fusion), dimensions={1,2,3} | broadcast | bytes 4456448 | tf_op jit(solution)/shard_map/broadcast_in_dim | solution.py:199
  27.7 0.0 copy-done
  27.7 0.0 copy-done.5
  27.7 0.0 copy-done.6
  27.7 6.8 %all-to-all-start = ((bf16[16,2,256,256]{3,2,1,0:T(8,128)(2,1)}), bf16[16,2,256,256]{3,2,1,0:T(8,128)(2,1)}, u32[]{:S(2)}, u32[]{:S(2)}) async-start(bf16[16,2,256,256]{3,2,1,0:T(8,128)(2,1)} %broadcast_in_dim.6), calls=%async_computation | async-start | bytes 8388608 | tf_op jit(solution)/shard_map/all_to_all | solution.py:200
  34.5 0.0 collective-permute-done.8.refs_3_
  34.5 0.0 copy-start.7
  34.5 1.9 %collective-permute-start.9 = (bf16[2,256,256]{2,1,0:T(8,128)(2,1)S(1)}, bf16[2,256,256]{2,1,0:T(8,128)(2,1)S(1)}, u32[]{:S(2)}, u32[]{:S(2)}) collective-permute-start(bf16[2,256,256]{2,1,0:T(8,128)(2,1)S(1)} %collective-permute-done.8.refs_3_), channel_id=1, source_target_pairs={{0,32},{32,64},{64,96},{96,128},{128,160},{160,192},{192,224},{224... | collective-permute-start | bytes 786440 | tf_op jit(solution)/shard_map/ppermute | solution.py:194
  36.5 0.0 collective-permute-done.2.refs_4_
  36.5 0.0 copy-start.8
  36.5 2.4 %collective-permute-start.3 = (bf16[2,256,256]{2,1,0:T(8,128)(2,1)S(1)}, bf16[2,256,256]{2,1,0:T(8,128)(2,1)S(1)}, u32[]{:S(2)}, u32[]{:S(2)}) collective-permute-start(bf16[2,256,256]{2,1,0:T(8,128)(2,1)S(1)} %collective-permute-done.2.refs_4_), channel_id=1, source_target_pairs={{0,32},{32,64},{64,96},{96,128},{128,160},{160,192},{192,224},{224... | collective-permute-start | bytes 786440 | tf_op jit(solution)/shard_map/ppermute | solution.py:194
  38.9 3.1 %collective-permute-done.9.refs_5_ = bf16[2,256,256]{2,1,0:T(8,128)(2,1)S(1)} collective-permute-done((bf16[2,256,256]{2,1,0:T(8,128)(2,1)S(1)}, bf16[2,256,256]{2,1,0:T(8,128)(2,1)S(1)}, u32[]{:S(2)}, u32[]{:S(2)}) %collective-permute-start.9) | collective-permute-done | bytes 262176 | tf_op jit(solution)/shard_map/ppermute | solution.py:194
  42.1 3.1 %collective-permute-start.10 = (bf16[2,256,256]{2,1,0:T(8,128)(2,1)S(1)}, bf16[2,256,256]{2,1,0:T(8,128)(2,1)S(1)}, u32[]{:S(2)}, u32[]{:S(2)}) collective-permute-start(bf16[2,256,256]{2,1,0:T(8,128)(2,1)S(1)} %collective-permute-done.9.refs_5_), channel_id=1, source_target_pairs={{0,32},{32,64},{64,96},{96,128},{128,160},{160,192},{192,224},{224... | collective-permute-start | bytes 786440 | tf_op jit(solution)/shard_map/ppermute | solution.py:194
  45.2 0.0 collective-permute-done.3.refs_6_
  45.2 0.0 copy-start.10
  45.2 2.8 %collective-permute-start.4 = (bf16[2,256,256]{2,1,0:T(8,128)(2,1)S(1)}, bf16[2,256,256]{2,1,0:T(8,128)(2,1)S(1)}, u32[]{:S(2)}, u32[]{:S(2)}) collective-permute-start(bf16[2,256,256]{2,1,0:T(8,128)(2,1)S(1)} %collective-permute-done.3.refs_6_), channel_id=1, source_target_pairs={{0,32},{32,64},{64,96},{96,128},{128,160},{160,192},{192,224},{224... | collective-permute-start | bytes 786440 | tf_op jit(solution)/shard_map/ppermute | solution.py:194
  48.0 1.6 %collective-permute-done.10.refs_7_ = bf16[2,256,256]{2,1,0:T(8,128)(2,1)S(1)} collective-permute-done((bf16[2,256,256]{2,1,0:T(8,128)(2,1)S(1)}, bf16[2,256,256]{2,1,0:T(8,128)(2,1)S(1)}, u32[]{:S(2)}, u32[]{:S(2)}) %collective-permute-start.10) | collective-permute-done | bytes 262176 | tf_op jit(solution)/shard_map/ppermute | solution.py:194
  49.6 4.3 %collective-permute-start.11 = (bf16[2,256,256]{2,1,0:T(8,128)(2,1)S(1)}, bf16[2,256,256]{2,1,0:T(8,128)(2,1)S(1)}, u32[]{:S(2)}, u32[]{:S(2)}) collective-permute-start(bf16[2,256,256]{2,1,0:T(8,128)(2,1)S(1)} %collective-permute-done.10.refs_7_), channel_id=1, source_target_pairs={{0,32},{32,64},{64,96},{96,128},{128,160},{160,192},{192,224},{224... | collective-permute-start | bytes 786440 | tf_op jit(solution)/shard_map/ppermute | solution.py:194
  53.9 0.0 collective-permute-done.4.refs_8_
  53.9 0.0 copy-start.12
  53.9 2.8 %collective-permute-start.5 = (bf16[2,256,256]{2,1,0:T(8,128)(2,1)S(1)}, bf16[2,256,256]{2,1,0:T(8,128)(2,1)S(1)}, u32[]{:S(2)}, u32[]{:S(2)}) collective-permute-start(bf16[2,256,256]{2,1,0:T(8,128)(2,1)S(1)} %collective-permute-done.4.refs_8_), channel_id=1, source_target_pairs={{0,32},{32,64},{64,96},{96,128},{128,160},{160,192},{192,224},{224... | collective-permute-start | bytes 786440 | tf_op jit(solution)/shard_map/ppermute | solution.py:194
  56.7 0.5 collective-permute-done.11.refs_9_
  57.2 5.4 %collective-permute-start.12 = (bf16[2,256,256]{2,1,0:T(8,128)(2,1)S(1)}, bf16[2,256,256]{2,1,0:T(8,128)(2,1)S(1)}, u32[]{:S(2)}, u32[]{:S(2)}) collective-permute-start(bf16[2,256,256]{2,1,0:T(8,128)(2,1)S(1)} %collective-permute-done.11.refs_9_), channel_id=1, source_target_pairs={{0,32},{32,64},{64,96},{96,128},{128,160},{160,192},{192,224},{224... | collective-permute-start | bytes 786440 | tf_op jit(solution)/shard_map/ppermute | solution.py:194
  62.6 0.0 collective-permute-done.5.refs_10_
  62.6 0.0 copy-start.14
  62.6 2.8 %collective-permute-start.6 = (bf16[2,256,256]{2,1,0:T(8,128)(2,1)S(1)}, bf16[2,256,256]{2,1,0:T(8,128)(2,1)S(1)}, u32[]{:S(2)}, u32[]{:S(2)}) collective-permute-start(bf16[2,256,256]{2,1,0:T(8,128)(2,1)S(1)} %collective-permute-done.5.refs_10_), channel_id=1, source_target_pairs={{0,32},{32,64},{64,96},{96,128},{128,160},{160,192},{192,224},{224... | collective-permute-start | bytes 786440 | tf_op jit(solution)/shard_map/ppermute | solution.py:194
  65.4 0.5 collective-permute-done.12.refs_11_
  65.9 5.4 %collective-permute-start.13 = (bf16[2,256,256]{2,1,0:T(8,128)(2,1)S(1)}, bf16[2,256,256]{2,1,0:T(8,128)(2,1)S(1)}, u32[]{:S(2)}, u32[]{:S(2)}) collective-permute-start(bf16[2,256,256]{2,1,0:T(8,128)(2,1)S(1)} %collective-permute-done.12.refs_11_), channel_id=1, source_target_pairs={{0,32},{32,64},{64,96},{96,128},{128,160},{160,192},{192,224},{224... | collective-permute-start | bytes 786440 | tf_op jit(solution)/shard_map/ppermute | solution.py:194
  71.3 0.0 collective-permute-done.6.refs_12_
  71.4 0.0 copy-start.16
  71.4 2.8 %collective-permute-start.7 = (bf16[2,256,256]{2,1,0:T(8,128)(2,1)S(1)}, bf16[2,256,256]{2,1,0:T(8,128)(2,1)S(1)}, u32[]{:S(2)}, u32[]{:S(2)}) collective-permute-start(bf16[2,256,256]{2,1,0:T(8,128)(2,1)S(1)} %collective-permute-done.6.refs_12_), channel_id=1, source_target_pairs={{0,32},{32,64},{64,96},{96,128},{128,160},{160,192},{192,224},{224... | collective-permute-start | bytes 786440 | tf_op jit(solution)/shard_map/ppermute | solution.py:194
  74.2 0.0 copy-done.15
  74.2 0.5 collective-permute-done.13.refs_13_
  74.6 5.4 %collective-permute-start.14 = (bf16[2,256,256]{2,1,0:T(8,128)(2,1)S(1)}, bf16[2,256,256]{2,1,0:T(8,128)(2,1)S(1)}, u32[]{:S(2)}, u32[]{:S(2)}) collective-permute-start(bf16[2,256,256]{2,1,0:T(8,128)(2,1)S(1)} %collective-permute-done.13.refs_13_), channel_id=1, source_target_pairs={{0,32},{32,64},{64,96},{96,128},{128,160},{160,192},{192,224},{224... | collective-permute-start | bytes 786440 | tf_op jit(solution)/shard_map/ppermute | solution.py:194
  80.1 0.0 collective-permute-done.7.given_ref
  80.1 0.0 copy-done.16
  80.2 2.8 %collective-permute-start.15 = (bf16[2,256,256]{2,1,0:T(8,128)(2,1)S(1)}, bf16[2,256,256]{2,1,0:T(8,128)(2,1)S(1)}, u32[]{:S(2)}, u32[]{:S(2)}) collective-permute-start(bf16[2,256,256]{2,1,0:T(8,128)(2,1)S(1)} %shard_map.29.refs_0_), channel_id=1, source_target_pairs={{16,496},{48,16},{80,48},{112,80},{144,112},{176,144},{208,176},{2... | collective-permute-start | bytes 786440 | tf_op jit(solution)/shard_map/ppermute | solution.py:194
  83.0 0.4 collective-permute-done.14.refs_1_
  83.4 5.0 %collective-permute-start.16 = (bf16[2,256,256]{2,1,0:T(8,128)(2,1)S(1)}, bf16[2,256,256]{2,1,0:T(8,128)(2,1)S(1)}, u32[]{:S(2)}, u32[]{:S(2)}) collective-permute-start(bf16[2,256,256]{2,1,0:T(8,128)(2,1)S(1)} %collective-permute-done.14.refs_1_), channel_id=1, source_target_pairs={{16,496},{48,16},{80,48},{112,80},{144,112},{176,144},{208,176},{2... | collective-permute-start | bytes 786440 | tf_op jit(solution)/shard_map/ppermute | solution.py:194
  88.4 8.7 %all-to-all-done.left_ref = bf16[16,2,256,256]{3,2,1,0:T(8,128)(2,1)} async-done(((bf16[16,2,256,256]{3,2,1,0:T(8,128)(2,1)}), bf16[16,2,256,256]{3,2,1,0:T(8,128)(2,1)}, u32[]{:S(2)}, u32[]{:S(2)}) %all-to-all-start) | async-done | bytes 4194336 | tf_op jit(solution)/shard_map/all_to_all | solution.py:200
  97.0 3.9 %shard_map.30 = (f32[2,256,256]{2,1,0:T(8,128)S(1)}, f32[2,256,256]{2,1,0:T(8,128)S(1)}) custom-call(s32[1]{0:T(128)} %bitcast.3.plane_ref, s32[1]{0:T(128)} %bitcast.4.core_ref, bf16[16,2,256,256]{3,2,1,0:T(8,128)(2,1)} %all-to-all-done.left_ref, bf16[2,256,256]{2,1,0:T(8,128)(2,1)} %copy-done, bf16[2,256,256]{2,1,0:T(8,128)(2,1)} %copy-done.5, ...), custom_call_target="tpu_custom_call" | custom-call | flops 1879048192 | bytes 14680064 | tf_op jit(solution)/shard_map/pallas_call | solution.py:109
  101.0 0.0 collective-permute-done.15.refs_2_
  101.0 0.0 collective-permute-done.16.refs_3_
  101.0 1.7 %shard_map.32 = f32[2,256,256]{2,1,0:T(8,128)S(1)} custom-call(s32[1]{0:T(128)} %bitcast.3.plane_ref, s32[1]{0:T(128)} %bitcast.4.core_ref, bf16[16,2,256,256]{3,2,1,0:T(8,128)(2,1)} %all-to-all-done.left_ref, bf16[2,256,256]{2,1,0:T(8,128)(2,1)S(1)} %shard_map.29.refs_0_, ...), custom_call_target="tpu_custom_call", output_to_operand_aliasing={{}: (7, {})} | custom-call | flops 268435456 | bytes 3145728 | tf_op jit(solution)/shard_map/pallas_call | solution.py:109
  102.7 0.0 copy-start.4
  102.7 0.0 copy-start.2
  102.7 2.1 %collective-permute-start.17 = (f32[2,256,256]{2,1,0:T(8,128)S(1)}, f32[2,256,256]{2,1,0:T(8,128)S(1)}, u32[]{:S(2)}, u32[]{:S(2)}) collective-permute-start(f32[2,256,256]{2,1,0:T(8,128)S(1)} %shard_map.32), channel_id=1, source_target_pairs={{0,16},{16,0},{1,17},{17,1},{2,18},{18,2},{3,19},{19,3},{4,20},{20... | collective-permute-start | bytes 1572872 | tf_op jit(solution)/shard_map/ppermute | solution.py:207
  104.8 1.7 %shard_map.31.mine_ref = f32[2,256,256]{2,1,0:T(8,128)S(1)} custom-call(s32[1]{0:T(128)} %bitcast.3.plane_ref, s32[1]{0:T(128)} %bitcast.4.core_ref, bf16[16,2,256,256]{3,2,1,0:T(8,128)(2,1)} %all-to-all-done.left_ref, bf16[2,256,256]{2,1,0:T(8,128)(2,1)S(1)} %shard_map.29.refs_0_, ...), custom_call_target="tpu_custom_call", output_to_operand_aliasing={{}: (7, {})} | custom-call | flops 268435456 | bytes 3145728 | tf_op jit(solution)/shard_map/pallas_call | solution.py:109
  106.4 0.2 collective-permute-done.17.other_ref
  106.6 0.6 shard_map.33
  107.3 1.8 %all-gather.1 = f32[2,2,256]{2,1,0:T(2,128)S(1)} all-gather(f32[1,2,256]{2,1,0:T(2,128)S(1)} %bitcast.12), channel_id=2, replica_groups=mesh['z'=16,'core'=2,'y'=4,'x'=4] {'core'}, dimensions={0}, use_global_device_ids=true | all-gather | bytes 6144 | tf_op jit(solution)/shard_map/all_gather | solution.py:219
  109.1 20.0 %all_to_all.10.parts_ref = f32[16,2,256]{2,1,0:T(2,128)S(1)} all-to-all(f32[16,2,256]{2,1,0:T(2,128)S(1)} %broadcast_in_dim.7), channel_id=1, replica_groups=mesh['z'=16,'core'=2,'y'=4,'x'=4] {'z'}, dimensions={0} | all-to-all | bytes 65536 | tf_op jit(solution)/shard_map/all_to_all | solution.py:220
  129.1 1.4 %shard_map.34 = f32[2,256,256]{2,1,0:T(8,128)} custom-call(s32[2]{0:T(128)S(1)} %bitcast.11, s32[1]{0:T(128)} %bitcast.1.column_ref, bf16[2,256,256]{2,1,0:T(8,128)(2,1)S(1)} %bitcast.8, f32[2,256,256]{2,1,0:T(8,128)S(1)} %get-tuple-element.11.inflated_ref, f32[16,2,256]{2,1,0:T(2,128)S(1)} %all_to_all.10.parts_ref), custom_call_target="tpu_custom_call" | custom-call | tf_op jit(solution)/shard_map/pallas_call | solution.py:224
  (25 shorter events, 0.1 us)
Async XLA Ops:
  0.0 0.9 copy-start.1
  1.0 0.7 copy-start.3
  2.3 25.4 %copy-start = (bf16[2,256,256]{2,1,0:T(8,128)(2,1)}, bf16[2,256,256]{2,1,0:T(8,128)(2,1)S(1)}, u32[]{:S(2)}) copy-start(bf16[2,256,256]{2,1,0:T(8,128)(2,1)S(1)} %shard_map.28.refs_0_) | copy-start | bytes 786436
  2.3 14.6 %collective-permute-start = (bf16[2,256,256]{2,1,0:T(8,128)(2,1)S(1)}, bf16[2,256,256]{2,1,0:T(8,128)(2,1)S(1)}, u32[]{:S(2)}, u32[]{:S(2)}) collective-permute-start(bf16[2,256,256]{2,1,0:T(8,128)(2,1)S(1)} %shard_map.28.refs_0_), channel_id=1, source_target_pairs={{0,16},{16,0},{1,17},{17,1},{2,18},{18,2},{3,19},{19,3},{4,20},{20... | collective-permute-start | bytes 786440 | tf_op jit(solution)/shard_map/ppermute | solution.py:184
  11.1 9.1 %collective-permute-start.1 = (bf16[2,256,256]{2,1,0:T(8,128)(2,1)S(1)}, bf16[2,256,256]{2,1,0:T(8,128)(2,1)S(1)}, u32[]{:S(2)}, u32[]{:S(2)}) collective-permute-start(bf16[2,256,256]{2,1,0:T(8,128)(2,1)S(1)} %shard_map.28.refs_0_), channel_id=1, source_target_pairs={{0,32},{32,64},{64,96},{96,128},{128,160},{160,192},{192,224},{224... | collective-permute-start | bytes 786440 | tf_op jit(solution)/shard_map/ppermute | solution.py:194
  16.9 10.8 %copy-start.5 = (bf16[2,256,256]{2,1,0:T(8,128)(2,1)}, bf16[2,256,256]{2,1,0:T(8,128)(2,1)S(1)}, u32[]{:S(2)}) copy-start(bf16[2,256,256]{2,1,0:T(8,128)(2,1)S(1)} %collective-permute-done.refs_1_) | copy-start | bytes 786436
  16.9 17.6 %collective-permute-start.8 = (bf16[2,256,256]{2,1,0:T(8,128)(2,1)S(1)}, bf16[2,256,256]{2,1,0:T(8,128)(2,1)S(1)}, u32[]{:S(2)}, u32[]{:S(2)}) collective-permute-start(bf16[2,256,256]{2,1,0:T(8,128)(2,1)S(1)} %collective-permute-done.refs_1_), channel_id=1, source_target_pairs={{0,32},{32,64},{64,96},{96,128},{128,160},{160,192},{192,224},{224... | collective-permute-start | bytes 786440 | tf_op jit(solution)/shard_map/ppermute | solution.py:194
  20.1 7.6 %copy-start.6 = (bf16[2,256,256]{2,1,0:T(8,128)(2,1)}, bf16[2,256,256]{2,1,0:T(8,128)(2,1)S(1)}, u32[]{:S(2)}) copy-start(bf16[2,256,256]{2,1,0:T(8,128)(2,1)S(1)} %collective-permute-done.1.refs_2_) | copy-start | bytes 786436
  20.1 16.4 %collective-permute-start.2 = (bf16[2,256,256]{2,1,0:T(8,128)(2,1)S(1)}, bf16[2,256,256]{2,1,0:T(8,128)(2,1)S(1)}, u32[]{:S(2)}, u32[]{:S(2)}) collective-permute-start(bf16[2,256,256]{2,1,0:T(8,128)(2,1)S(1)} %collective-permute-done.1.refs_2_), channel_id=1, source_target_pairs={{0,32},{32,64},{64,96},{96,128},{128,160},{160,192},{192,224},{224... | collective-permute-start | bytes 786440 | tf_op jit(solution)/shard_map/ppermute | solution.py:194
  27.7 69.3 %all-to-all-start = ((bf16[16,2,256,256]{3,2,1,0:T(8,128)(2,1)}), bf16[16,2,256,256]{3,2,1,0:T(8,128)(2,1)}, u32[]{:S(2)}, u32[]{:S(2)}) async-start(bf16[16,2,256,256]{3,2,1,0:T(8,128)(2,1)} %broadcast_in_dim.6), calls=%async_computation | async-start | bytes 8388608 | tf_op jit(solution)/shard_map/all_to_all | solution.py:200
  34.5 45.6 %copy-start.7 = (bf16[2,256,256]{2,1,0:T(8,128)(2,1)}, bf16[2,256,256]{2,1,0:T(8,128)(2,1)S(1)}, u32[]{:S(2)}) copy-start(bf16[2,256,256]{2,1,0:T(8,128)(2,1)S(1)} %collective-permute-done.8.refs_3_) | copy-start | bytes 786436
  34.5 7.5 %collective-permute-start.9 = (bf16[2,256,256]{2,1,0:T(8,128)(2,1)S(1)}, bf16[2,256,256]{2,1,0:T(8,128)(2,1)S(1)}, u32[]{:S(2)}, u32[]{:S(2)}) collective-permute-start(bf16[2,256,256]{2,1,0:T(8,128)(2,1)S(1)} %collective-permute-done.8.refs_3_), channel_id=1, source_target_pairs={{0,32},{32,64},{64,96},{96,128},{128,160},{160,192},{192,224},{224... | collective-permute-start | bytes 786440 | tf_op jit(solution)/shard_map/ppermute | solution.py:194
  36.5 43.6 %copy-start.8 = (bf16[2,256,256]{2,1,0:T(8,128)(2,1)}, bf16[2,256,256]{2,1,0:T(8,128)(2,1)S(1)}, u32[]{:S(2)}) copy-start(bf16[2,256,256]{2,1,0:T(8,128)(2,1)S(1)} %collective-permute-done.2.refs_4_) | copy-start | bytes 786436
  36.5 8.7 %collective-permute-start.3 = (bf16[2,256,256]{2,1,0:T(8,128)(2,1)S(1)}, bf16[2,256,256]{2,1,0:T(8,128)(2,1)S(1)}, u32[]{:S(2)}, u32[]{:S(2)}) collective-permute-start(bf16[2,256,256]{2,1,0:T(8,128)(2,1)S(1)} %collective-permute-done.2.refs_4_), channel_id=1, source_target_pairs={{0,32},{32,64},{64,96},{96,128},{128,160},{160,192},{192,224},{224... | collective-permute-start | bytes 786440 | tf_op jit(solution)/shard_map/ppermute | solution.py:194
  42.1 38.1 %copy-start.9 = (bf16[2,256,256]{2,1,0:T(8,128)(2,1)}, bf16[2,256,256]{2,1,0:T(8,128)(2,1)S(1)}, u32[]{:S(2)}) copy-start(bf16[2,256,256]{2,1,0:T(8,128)(2,1)S(1)} %collective-permute-done.9.refs_5_) | copy-start | bytes 786436
  42.1 7.5 %collective-permute-start.10 = (bf16[2,256,256]{2,1,0:T(8,128)(2,1)S(1)}, bf16[2,256,256]{2,1,0:T(8,128)(2,1)S(1)}, u32[]{:S(2)}, u32[]{:S(2)}) collective-permute-start(bf16[2,256,256]{2,1,0:T(8,128)(2,1)S(1)} %collective-permute-done.9.refs_5_), channel_id=1, source_target_pairs={{0,32},{32,64},{64,96},{96,128},{128,160},{160,192},{192,224},{224... | collective-permute-start | bytes 786440 | tf_op jit(solution)/shard_map/ppermute | solution.py:194
  45.2 34.9 %copy-start.10 = (bf16[2,256,256]{2,1,0:T(8,128)(2,1)}, bf16[2,256,256]{2,1,0:T(8,128)(2,1)S(1)}, u32[]{:S(2)}) copy-start(bf16[2,256,256]{2,1,0:T(8,128)(2,1)S(1)} %collective-permute-done.3.refs_6_) | copy-start | bytes 786436
  45.2 8.7 %collective-permute-start.4 = (bf16[2,256,256]{2,1,0:T(8,128)(2,1)S(1)}, bf16[2,256,256]{2,1,0:T(8,128)(2,1)S(1)}, u32[]{:S(2)}, u32[]{:S(2)}) collective-permute-start(bf16[2,256,256]{2,1,0:T(8,128)(2,1)S(1)} %collective-permute-done.3.refs_6_), channel_id=1, source_target_pairs={{0,32},{32,64},{64,96},{96,128},{128,160},{160,192},{192,224},{224... | collective-permute-start | bytes 786440 | tf_op jit(solution)/shard_map/ppermute | solution.py:194
  49.6 30.6 %copy-start.11 = (bf16[2,256,256]{2,1,0:T(8,128)(2,1)}, bf16[2,256,256]{2,1,0:T(8,128)(2,1)S(1)}, u32[]{:S(2)}) copy-start(bf16[2,256,256]{2,1,0:T(8,128)(2,1)S(1)} %collective-permute-done.10.refs_7_) | copy-start | bytes 786436
  49.6 7.6 %collective-permute-start.11 = (bf16[2,256,256]{2,1,0:T(8,128)(2,1)S(1)}, bf16[2,256,256]{2,1,0:T(8,128)(2,1)S(1)}, u32[]{:S(2)}, u32[]{:S(2)}) collective-permute-start(bf16[2,256,256]{2,1,0:T(8,128)(2,1)S(1)} %collective-permute-done.10.refs_7_), channel_id=1, source_target_pairs={{0,32},{32,64},{64,96},{96,128},{128,160},{160,192},{192,224},{224... | collective-permute-start | bytes 786440 | tf_op jit(solution)/shard_map/ppermute | solution.py:194
  53.9 26.2 %copy-start.12 = (bf16[2,256,256]{2,1,0:T(8,128)(2,1)}, bf16[2,256,256]{2,1,0:T(8,128)(2,1)S(1)}, u32[]{:S(2)}) copy-start(bf16[2,256,256]{2,1,0:T(8,128)(2,1)S(1)} %collective-permute-done.4.refs_8_) | copy-start | bytes 786436
  53.9 8.7 %collective-permute-start.5 = (bf16[2,256,256]{2,1,0:T(8,128)(2,1)S(1)}, bf16[2,256,256]{2,1,0:T(8,128)(2,1)S(1)}, u32[]{:S(2)}, u32[]{:S(2)}) collective-permute-start(bf16[2,256,256]{2,1,0:T(8,128)(2,1)S(1)} %collective-permute-done.4.refs_8_), channel_id=1, source_target_pairs={{0,32},{32,64},{64,96},{96,128},{128,160},{160,192},{192,224},{224... | collective-permute-start | bytes 786440 | tf_op jit(solution)/shard_map/ppermute | solution.py:194
  57.2 23.0 %copy-start.13 = (bf16[2,256,256]{2,1,0:T(8,128)(2,1)}, bf16[2,256,256]{2,1,0:T(8,128)(2,1)S(1)}, u32[]{:S(2)}) copy-start(bf16[2,256,256]{2,1,0:T(8,128)(2,1)S(1)} %collective-permute-done.11.refs_9_) | copy-start | bytes 786436
  57.2 8.7 %collective-permute-start.12 = (bf16[2,256,256]{2,1,0:T(8,128)(2,1)S(1)}, bf16[2,256,256]{2,1,0:T(8,128)(2,1)S(1)}, u32[]{:S(2)}, u32[]{:S(2)}) collective-permute-start(bf16[2,256,256]{2,1,0:T(8,128)(2,1)S(1)} %collective-permute-done.11.refs_9_), channel_id=1, source_target_pairs={{0,32},{32,64},{64,96},{96,128},{128,160},{160,192},{192,224},{224... | collective-permute-start | bytes 786440 | tf_op jit(solution)/shard_map/ppermute | solution.py:194
  62.6 17.5 %copy-start.14 = (bf16[2,256,256]{2,1,0:T(8,128)(2,1)}, bf16[2,256,256]{2,1,0:T(8,128)(2,1)S(1)}, u32[]{:S(2)}) copy-start(bf16[2,256,256]{2,1,0:T(8,128)(2,1)S(1)} %collective-permute-done.5.refs_10_) | copy-start | bytes 786436
  62.6 8.7 %collective-permute-start.6 = (bf16[2,256,256]{2,1,0:T(8,128)(2,1)S(1)}, bf16[2,256,256]{2,1,0:T(8,128)(2,1)S(1)}, u32[]{:S(2)}, u32[]{:S(2)}) collective-permute-start(bf16[2,256,256]{2,1,0:T(8,128)(2,1)S(1)} %collective-permute-done.5.refs_10_), channel_id=1, source_target_pairs={{0,32},{32,64},{64,96},{96,128},{128,160},{160,192},{192,224},{224... | collective-permute-start | bytes 786440 | tf_op jit(solution)/shard_map/ppermute | solution.py:194
  65.9 8.2 %copy-start.15 = (bf16[2,256,256]{2,1,0:T(8,128)(2,1)}, bf16[2,256,256]{2,1,0:T(8,128)(2,1)S(1)}, u32[]{:S(2)}) copy-start(bf16[2,256,256]{2,1,0:T(8,128)(2,1)S(1)} %collective-permute-done.12.refs_11_) | copy-start | bytes 786436
  65.9 8.7 %collective-permute-start.13 = (bf16[2,256,256]{2,1,0:T(8,128)(2,1)S(1)}, bf16[2,256,256]{2,1,0:T(8,128)(2,1)S(1)}, u32[]{:S(2)}, u32[]{:S(2)}) collective-permute-start(bf16[2,256,256]{2,1,0:T(8,128)(2,1)S(1)} %collective-permute-done.12.refs_11_), channel_id=1, source_target_pairs={{0,32},{32,64},{64,96},{96,128},{128,160},{160,192},{192,224},{224... | collective-permute-start | bytes 786440 | tf_op jit(solution)/shard_map/ppermute | solution.py:194
  71.4 8.7 %copy-start.16 = (bf16[2,256,256]{2,1,0:T(8,128)(2,1)}, bf16[2,256,256]{2,1,0:T(8,128)(2,1)S(1)}, u32[]{:S(2)}) copy-start(bf16[2,256,256]{2,1,0:T(8,128)(2,1)S(1)} %collective-permute-done.6.refs_12_) | copy-start | bytes 786436
  71.4 8.7 %collective-permute-start.7 = (bf16[2,256,256]{2,1,0:T(8,128)(2,1)S(1)}, bf16[2,256,256]{2,1,0:T(8,128)(2,1)S(1)}, u32[]{:S(2)}, u32[]{:S(2)}) collective-permute-start(bf16[2,256,256]{2,1,0:T(8,128)(2,1)S(1)} %collective-permute-done.6.refs_12_), channel_id=1, source_target_pairs={{0,32},{32,64},{64,96},{96,128},{128,160},{160,192},{192,224},{224... | collective-permute-start | bytes 786440 | tf_op jit(solution)/shard_map/ppermute | solution.py:194
  74.6 5.5 %copy-start.17 = (bf16[2,256,256]{2,1,0:T(8,128)(2,1)}, bf16[2,256,256]{2,1,0:T(8,128)(2,1)S(1)}, u32[]{:S(2)}) copy-start(bf16[2,256,256]{2,1,0:T(8,128)(2,1)S(1)} %collective-permute-done.13.refs_13_) | copy-start | bytes 786436
  74.6 8.7 %collective-permute-start.14 = (bf16[2,256,256]{2,1,0:T(8,128)(2,1)S(1)}, bf16[2,256,256]{2,1,0:T(8,128)(2,1)S(1)}, u32[]{:S(2)}, u32[]{:S(2)}) collective-permute-start(bf16[2,256,256]{2,1,0:T(8,128)(2,1)S(1)} %collective-permute-done.13.refs_13_), channel_id=1, source_target_pairs={{0,32},{32,64},{64,96},{96,128},{128,160},{160,192},{192,224},{224... | collective-permute-start | bytes 786440 | tf_op jit(solution)/shard_map/ppermute | solution.py:194
  80.2 20.8 %collective-permute-start.15 = (bf16[2,256,256]{2,1,0:T(8,128)(2,1)S(1)}, bf16[2,256,256]{2,1,0:T(8,128)(2,1)S(1)}, u32[]{:S(2)}, u32[]{:S(2)}) collective-permute-start(bf16[2,256,256]{2,1,0:T(8,128)(2,1)S(1)} %shard_map.29.refs_0_), channel_id=1, source_target_pairs={{16,496},{48,16},{80,48},{112,80},{144,112},{176,144},{208,176},{2... | collective-permute-start | bytes 786440 | tf_op jit(solution)/shard_map/ppermute | solution.py:194
  83.4 17.6 %collective-permute-start.16 = (bf16[2,256,256]{2,1,0:T(8,128)(2,1)S(1)}, bf16[2,256,256]{2,1,0:T(8,128)(2,1)S(1)}, u32[]{:S(2)}, u32[]{:S(2)}) collective-permute-start(bf16[2,256,256]{2,1,0:T(8,128)(2,1)S(1)} %collective-permute-done.14.refs_1_), channel_id=1, source_target_pairs={{16,496},{48,16},{80,48},{112,80},{144,112},{176,144},{208,176},{2... | collective-permute-start | bytes 786440 | tf_op jit(solution)/shard_map/ppermute | solution.py:194
  102.7 4.0 %copy-start.4 = (s32[1,2]{1,0:T(1,128)S(1)}, s32[1,2]{1,0:T(1,128)}, u32[]{:S(2)}) copy-start(s32[1,2]{1,0:T(1,128)} %param.4) | copy-start | bytes 28
  102.7 26.4 %copy-start.2 = (bf16[1,2,256,256]{3,2,1,0:T(8,128)(2,1)S(1)}, bf16[1,2,256,256]{3,2,1,0:T(8,128)(2,1)}, u32[]{:S(2)}) copy-start(bf16[1,2,256,256]{3,2,1,0:T(8,128)(2,1)} %param.3) | copy-start | bytes 786436
  102.7 3.9 %collective-permute-start.17 = (f32[2,256,256]{2,1,0:T(8,128)S(1)}, f32[2,256,256]{2,1,0:T(8,128)S(1)}, u32[]{:S(2)}, u32[]{:S(2)}) collective-permute-start(f32[2,256,256]{2,1,0:T(8,128)S(1)} %shard_map.32), channel_id=1, source_target_pairs={{0,16},{16,0},{1,17},{17,1},{2,18},{18,2},{3,19},{19,3},{4,20},{20... | collective-permute-start | bytes 1572872 | tf_op jit(solution)/shard_map/ppermute | solution.py:207

commit v5 on v4

--- a/solution.py
+++ b/solution.py
@@ -15,7 +15,7 @@
 HBM = pl.BlockSpec(memory_space=pltpu.HBM)
 MIB = 1024 * 1024
 SWAP = [(0, 1), (1, 0)]
-FLOPS = 26 * 10**9
+FLOPS = 23 * 10**9
 
 
 def params(mib):
@@ -47,12 +47,14 @@
             pl.when(guard_ref[0] == guard)(go)
 
 
-def product_kernel(planes, rows, groups, columns, plane_ref, core_ref, left_ref, *refs):
+def product_kernel(planes, rows, groups, plane_ref, core_ref, left_ref, *refs):
     count = 2 * len(planes)
     rights, refs = refs[:count], refs[count:]
     totals, (held, kept, sems) = refs[-3 - len(rows) : -3], refs[-3:]
     carried = len(refs) > 3 + len(rows)
     core = core_ref[0]
+    breadth = left_ref.shape[0]
+    columns = breadth * breadth
     plan = []
     for i, (distance, guard) in enumerate(planes):
         copies = []
@@ -60,11 +62,12 @@
             inner = 2 * (plane_ref[0] + jnp.where(core == 0, -distance, distance))
             inner += jnp.where(core == 0, j, 1 - j)
             place = lax.rem(inner + 2 * columns, columns)
+            y, x = place // breadth, lax.rem(place, breadth)
+            outer, nested = jnp.where(core == 0, y, x), jnp.where(core == 0, x, y)
             for n, row in enumerate(rows):
+                source = left_ref.at[outer, nested, row]
                 copies.append(
-                    pltpu.make_async_copy(
-                        left_ref.at[place, row], held.at[2 * i + j, n], sems.at[2 * i + j, n]
-                    )
+                    pltpu.make_async_copy(source, held.at[2 * i + j, n], sems.at[2 * i + j, n])
                 )
             copies.append(
                 pltpu.make_async_copy(
@@ -105,7 +108,7 @@
     if totals is None:
         tiles = [pltpu.with_memory_space_constraint(tile, pltpu.HBM) for tile in tiles]
     given = [] if totals is None else [totals[row] for row in rows]
-    kernel = functools.partial(product_kernel, planes, rows, groups, left.shape[0])
+    kernel = functools.partial(product_kernel, planes, rows, groups)
     out = pl.pallas_call(
         kernel,
         in_specs=[SMEM, SMEM, HBM] + [HBM] * len(tiles) + [VMEM] * len(given),
@@ -195,9 +198,27 @@
 
     low = lax.rem(column - 2 * (plane - half + 1) + 2 * columns, 2 * columns)
     place = jnp.where((low < columns) == (core == 0), 0, 1)
+    height, breadth = lax.axis_size("y"), lax.axis_size("x")
+    assert height == breadth
+
+    def lines_of(phase):
+        lines = []
+        for c in range(cores):
+            for fixed in range(height):
+                along_x = [breadth * fixed + i for i in range(breadth)]
+                along_y = [breadth * i + fixed for i in range(height)]
+                line = along_x if phase == c else along_y
+                lines.append([columns * c + i for i in line])
+        return lines
+
+    def copy_for_each(value, lines):
+        spread = jnp.broadcast_to(value[None], (len(lines[0]), *value.shape))
+        return lax.all_to_all(
+            spread, ("core", *COLS), 0, 0, axis_index_groups=lines, tiled=True
+        )
+
     sent = jnp.stack([jnp.where(place == 0, t[0], t[1]) for t in (mine, other)])
-    sent = jnp.broadcast_to(sent[None], (columns, *sent.shape))
-    left = lax.all_to_all(sent, COLS, 0, 0, tiled=True)
+    left = copy_for_each(copy_for_each(sent, lines_of(0)), lines_of(1))
 
     known = (plane_ref, core_ref, left, held)
     early = [(0, 0)] + [(i, None) for i in range(1, half - 1)]

time: 131 us -> 125 us (0.954)
  waiting for transfers between devices: 16 us -> 8.8 us
  starting transfers between devices: 78 us -> 76 us
    all_to_all x1 -> x2, waiting for transfers between devices: 8.66 us -> 0.01 us  [copy_for_each(): lax.all_to_all(spread, ('core', *COLS), 0, 0, axis_index_groups=lines, ti...]
    ppermute x16, starting transfers between devices: 60.3 us -> 55.2 us  [on_device(): held.append(tuple((lax.ppermute(t, ROWS, perm) for t in held[-1])))]
    all_to_all x1 -> x2, starting transfers between devices: 6.81 us -> 9.04 us  [copy_for_each(): lax.all_to_all(spread, ('core', *COLS), 0, 0, axis_index_groups=lines, ti...]
    ppermute x16, waiting for transfers between devices: 7.14 us -> 8.79 us  [on_device(): held.append(tuple((lax.ppermute(t, ROWS, perm) for t in held[-1])))]
    broadcast_in_dim x1 -> x2, local copies, waits for them, and re-layouts: 2.5 us -> 3.56 us  [copy_for_each(): spread = jnp.broadcast_to(value[None], (len(lines[0]), *value.shape))]
  transfers between devices with their start and end apart: 19 -> 20, of which waited for: 9 -> 6; matrix products, arithmetic and copies ran while one was open for 2% -> 3% of each run, Pallas kernels for 4% -> 5%
where the time goes in v5:
time: 125 us; the launch traced here: 124 us
  starting transfers between devices  76 us (61%)
  blocking collectives  22.9 us (18%)
  Pallas kernels  10.1 us (8%)
  waiting for transfers between devices  8.8 us (7%)
  local copies, waits for them, and re-layouts  5.25 us (4%)
    ppermute x16, starting transfers between devices, on_device(): held.append(tuple((lax.ppermute(t, ROWS, perm) for t in held[-1])))  55.2 us
    all_to_all x1, blocking collectives, on_device(): lax.all_to_all(jnp.broadcast_to(sums[None], (planes, *sums.shape)), 'z',...  21.1 us
    all_to_all x2, starting transfers between devices, copy_for_each(): lax.all_to_all(spread, ('core', *COLS), 0, 0, axis_index_groups=lines, ti...  9.04 us
    ppermute x16, waiting for transfers between devices, on_device(): held.append(tuple((lax.ppermute(t, ROWS, perm) for t in held[-1])))  8.79 us
    ppermute x1, starting transfers between devices, on_device(): other = lax.ppermute(mine, 'core', SWAP)  8.79 us
    pallas_call x3, Pallas kernels, products(): pl.pallas_call(kernel, in_specs=[SMEM, SMEM, HBM] + [HBM] * len(tiles) +...  7.34 us
    broadcast_in_dim x2, local copies, waits for them, and re-layouts, copy_for_each(): spread = jnp.broadcast_to(value[None], (len(lines[0]), *value.shape))  3.56 us
    ppermute x1, starting transfers between devices, on_device(): received = lax.ppermute(outward, 'core', SWAP)  2.98 us
  transfers between devices with their start and end apart: 20, of which 6 were waited for; matrix products, arithmetic and copies ran while one was open for 3% of the time, Pallas kernels for 5%

profile of v5, /device:TPU:1, one launch (start us, length us, event | category | flops | bytes accessed | tf_op | source)
XLA Modules:
  0.0 123.7 jit_solution(9014260461557328611)
XLA Ops:
  0.0 0.9 copy-done.1
  1.0 0.7 copy-done.3
  1.6 0.6 shard_map.28.refs_0_
  2.3 0.0 copy-start
  2.3 8.8 %collective-permute-start = (bf16[2,256,256]{2,1,0:T(8,128)(2,1)S(1)}, bf16[2,256,256]{2,1,0:T(8,128)(2,1)S(1)}, u32[]{:S(2)}, u32[]{:S(2)}) collective-permute-start(bf16[2,256,256]{2,1,0:T(8,128)(2,1)S(1)} %shard_map.28.refs_0_), channel_id=1, source_target_pairs={{0,16},{16,0},{1,17},{17,1},{2,18},{18,2},{3,19},{19,3},{4,20},{20... | collective-permute-start | bytes 786440 | tf_op jit(solution)/shard_map/ppermute | solution.py:187
  11.1 5.7 %collective-permute-start.1 = (bf16[2,256,256]{2,1,0:T(8,128)(2,1)S(1)}, bf16[2,256,256]{2,1,0:T(8,128)(2,1)S(1)}, u32[]{:S(2)}, u32[]{:S(2)}) collective-permute-start(bf16[2,256,256]{2,1,0:T(8,128)(2,1)S(1)} %shard_map.28.refs_0_), channel_id=1, source_target_pairs={{0,32},{32,64},{64,96},{96,128},{128,160},{160,192},{192,224},{224... | collective-permute-start | bytes 786440 | tf_op jit(solution)/shard_map/ppermute | solution.py:197
  16.9 0.0 collective-permute-done.refs_1_
  16.9 0.0 copy-start.5
  16.9 1.0 broadcast_in_dim.8
  18.0 4.2 %all-to-all-start = ((bf16[4,2,256,256]{3,2,1,0:T(8,128)(2,1)}), bf16[4,2,256,256]{3,2,1,0:T(8,128)(2,1)S(1)}, u32[]{:S(2)}, u32[]{:S(2)}) async-start(bf16[4,2,256,256]{3,2,1,0:T(8,128)(2,1)} %broadcast_in_dim.8), calls=%async_computation | async-start | bytes 2097152 | tf_op jit(solution)/shard_map/all_to_all | solution.py:216
  22.2 2.6 %collective-permute-start.8 = (bf16[2,256,256]{2,1,0:T(8,128)(2,1)S(1)}, bf16[2,256,256]{2,1,0:T(8,128)(2,1)S(1)}, u32[]{:S(2)}, u32[]{:S(2)}) collective-permute-start(bf16[2,256,256]{2,1,0:T(8,128)(2,1)S(1)} %collective-permute-done.refs_1_), channel_id=1, source_target_pairs={{0,32},{32,64},{64,96},{96,128},{128,160},{160,192},{192,224},{224... | collective-permute-start | bytes 786440 | tf_op jit(solution)/shard_map/ppermute | solution.py:197
  24.8 0.0 collective-permute-done.1.refs_2_
  24.8 0.0 copy-start.6
  24.8 2.6 %collective-permute-start.2 = (bf16[2,256,256]{2,1,0:T(8,128)(2,1)S(1)}, bf16[2,256,256]{2,1,0:T(8,128)(2,1)S(1)}, u32[]{:S(2)}, u32[]{:S(2)}) collective-permute-start(bf16[2,256,256]{2,1,0:T(8,128)(2,1)S(1)} %collective-permute-done.1.refs_2_), channel_id=1, source_target_pairs={{0,32},{32,64},{64,96},{96,128},{128,160},{160,192},{192,224},{224... | collective-permute-start | bytes 786440 | tf_op jit(solution)/shard_map/ppermute | solution.py:197
  27.5 2.1 %collective-permute-done.8.refs_3_ = bf16[2,256,256]{2,1,0:T(8,128)(2,1)S(1)} collective-permute-done((bf16[2,256,256]{2,1,0:T(8,128)(2,1)S(1)}, bf16[2,256,256]{2,1,0:T(8,128)(2,1)S(1)}, u32[]{:S(2)}, u32[]{:S(2)}) %collective-permute-start.8) | collective-permute-done | bytes 262176 | tf_op jit(solution)/shard_map/ppermute | solution.py:197
  29.6 3.8 %collective-permute-start.9 = (bf16[2,256,256]{2,1,0:T(8,128)(2,1)S(1)}, bf16[2,256,256]{2,1,0:T(8,128)(2,1)S(1)}, u32[]{:S(2)}, u32[]{:S(2)}) collective-permute-start(bf16[2,256,256]{2,1,0:T(8,128)(2,1)S(1)} %collective-permute-done.8.refs_3_), channel_id=1, source_target_pairs={{0,32},{32,64},{64,96},{96,128},{128,160},{160,192},{192,224},{224... | collective-permute-start | bytes 786440 | tf_op jit(solution)/shard_map/ppermute | solution.py:197
  33.4 0.0 collective-permute-done.2.refs_4_
  33.4 0.0 copy-start.8
  33.4 2.5 %collective-permute-start.3 = (bf16[2,256,256]{2,1,0:T(8,128)(2,1)S(1)}, bf16[2,256,256]{2,1,0:T(8,128)(2,1)S(1)}, u32[]{:S(2)}, u32[]{:S(2)}) collective-permute-start(bf16[2,256,256]{2,1,0:T(8,128)(2,1)S(1)} %collective-permute-done.2.refs_4_), channel_id=1, source_target_pairs={{0,32},{32,64},{64,96},{96,128},{128,160},{160,192},{192,224},{224... | collective-permute-start | bytes 786440 | tf_op jit(solution)/shard_map/ppermute | solution.py:197
  35.9 1.0 collective-permute-done.9.refs_5_
  37.0 4.8 %collective-permute-start.10 = (bf16[2,256,256]{2,1,0:T(8,128)(2,1)S(1)}, bf16[2,256,256]{2,1,0:T(8,128)(2,1)S(1)}, u32[]{:S(2)}, u32[]{:S(2)}) collective-permute-start(bf16[2,256,256]{2,1,0:T(8,128)(2,1)S(1)} %collective-permute-done.9.refs_5_), channel_id=1, source_target_pairs={{0,32},{32,64},{64,96},{96,128},{128,160},{160,192},{192,224},{224... | collective-permute-start | bytes 786440 | tf_op jit(solution)/shard_map/ppermute | solution.py:197
  41.7 0.0 collective-permute-done.3.refs_6_
  41.8 0.0 copy-start.10
  41.8 2.8 %collective-permute-start.4 = (bf16[2,256,256]{2,1,0:T(8,128)(2,1)S(1)}, bf16[2,256,256]{2,1,0:T(8,128)(2,1)S(1)}, u32[]{:S(2)}, u32[]{:S(2)}) collective-permute-start(bf16[2,256,256]{2,1,0:T(8,128)(2,1)S(1)} %collective-permute-done.3.refs_6_), channel_id=1, source_target_pairs={{0,32},{32,64},{64,96},{96,128},{128,160},{160,192},{192,224},{224... | collective-permute-start | bytes 786440 | tf_op jit(solution)/shard_map/ppermute | solution.py:197
  44.6 0.0 all-to-all-done
  44.6 2.5 %broadcast_in_dim.9 = bf16[4,4,2,256,256]{4,3,2,1,0:T(8,128)(2,1)} broadcast(bf16[4,2,256,256]{3,2,1,0:T(8,128)(2,1)S(1)} %all-to-all-done), dimensions={1,2,3,4} | broadcast | bytes 5242880 | tf_op jit(solution)/shard_map/broadcast_in_dim | solution.py:215
  47.1 0.0 copy-done
  47.1 0.0 copy-done.5
  47.1 0.0 copy-done.6
  47.1 4.9 %all-to-all-start.1 = ((bf16[4,4,2,256,256]{4,3,2,1,0:T(8,128)(2,1)}), bf16[4,4,2,256,256]{4,3,2,1,0:T(8,128)(2,1)}, u32[]{:S(2)}, u32[]{:S(2)}) async-start(bf16[4,4,2,256,256]{4,3,2,1,0:T(8,128)(2,1)} %broadcast_in_dim.9), calls=%async_computation.1 | async-start | bytes 8388608 | tf_op jit(solution)/shard_map/all_to_all | solution.py:216
  52.0 0.0 collective-permute-done.10.refs_7_
  52.0 1.9 %collective-permute-start.11 = (bf16[2,256,256]{2,1,0:T(8,128)(2,1)S(1)}, bf16[2,256,256]{2,1,0:T(8,128)(2,1)S(1)}, u32[]{:S(2)}, u32[]{:S(2)}) collective-permute-start(bf16[2,256,256]{2,1,0:T(8,128)(2,1)S(1)} %collective-permute-done.10.refs_7_), channel_id=1, source_target_pairs={{0,32},{32,64},{64,96},{96,128},{128,160},{160,192},{192,224},{224... | collective-permute-start | bytes 786440 | tf_op jit(solution)/shard_map/ppermute | solution.py:197
  53.9 0.0 collective-permute-done.4.refs_8_
  54.0 2.3 %collective-permute-start.5 = (bf16[2,256,256]{2,1,0:T(8,128)(2,1)S(1)}, bf16[2,256,256]{2,1,0:T(8,128)(2,1)S(1)}, u32[]{:S(2)}, u32[]{:S(2)}) collective-permute-start(bf16[2,256,256]{2,1,0:T(8,128)(2,1)S(1)} %collective-permute-done.4.refs_8_), channel_id=1, source_target_pairs={{0,32},{32,64},{64,96},{96,128},{128,160},{160,192},{192,224},{224... | collective-permute-start | bytes 786440 | tf_op jit(solution)/shard_map/ppermute | solution.py:197
  56.3 3.3 %collective-permute-done.11.refs_9_ = bf16[2,256,256]{2,1,0:T(8,128)(2,1)S(1)} collective-permute-done((bf16[2,256,256]{2,1,0:T(8,128)(2,1)S(1)}, bf16[2,256,256]{2,1,0:T(8,128)(2,1)S(1)}, u32[]{:S(2)}, u32[]{:S(2)}) %collective-permute-start.11) | collective-permute-done | bytes 262176 | tf_op jit(solution)/shard_map/ppermute | solution.py:197
  59.5 3.1 %collective-permute-start.12 = (bf16[2,256,256]{2,1,0:T(8,128)(2,1)S(1)}, bf16[2,256,256]{2,1,0:T(8,128)(2,1)S(1)}, u32[]{:S(2)}, u32[]{:S(2)}) collective-permute-start(bf16[2,256,256]{2,1,0:T(8,128)(2,1)S(1)} %collective-permute-done.11.refs_9_), channel_id=1, source_target_pairs={{0,32},{32,64},{64,96},{96,128},{128,160},{160,192},{192,224},{224... | collective-permute-start | bytes 786440 | tf_op jit(solution)/shard_map/ppermute | solution.py:197
  62.7 0.0 collective-permute-done.5.refs_10_
  62.7 0.0 copy-start.14
  62.7 2.8 %collective-permute-start.6 = (bf16[2,256,256]{2,1,0:T(8,128)(2,1)S(1)}, bf16[2,256,256]{2,1,0:T(8,128)(2,1)S(1)}, u32[]{:S(2)}, u32[]{:S(2)}) collective-permute-start(bf16[2,256,256]{2,1,0:T(8,128)(2,1)S(1)} %collective-permute-done.5.refs_10_), channel_id=1, source_target_pairs={{0,32},{32,64},{64,96},{96,128},{128,160},{160,192},{192,224},{224... | collective-permute-start | bytes 786440 | tf_op jit(solution)/shard_map/ppermute | solution.py:197
  65.5 1.6 %collective-permute-done.12.refs_11_ = bf16[2,256,256]{2,1,0:T(8,128)(2,1)S(1)} collective-permute-done((bf16[2,256,256]{2,1,0:T(8,128)(2,1)S(1)}, bf16[2,256,256]{2,1,0:T(8,128)(2,1)S(1)}, u32[]{:S(2)}, u32[]{:S(2)}) %collective-permute-start.12) | collective-permute-done | bytes 262176 | tf_op jit(solution)/shard_map/ppermute | solution.py:197
  67.0 4.2 %collective-permute-start.13 = (bf16[2,256,256]{2,1,0:T(8,128)(2,1)S(1)}, bf16[2,256,256]{2,1,0:T(8,128)(2,1)S(1)}, u32[]{:S(2)}, u32[]{:S(2)}) collective-permute-start(bf16[2,256,256]{2,1,0:T(8,128)(2,1)S(1)} %collective-permute-done.12.refs_11_), channel_id=1, source_target_pairs={{0,32},{32,64},{64,96},{96,128},{128,160},{160,192},{192,224},{224... | collective-permute-start | bytes 786440 | tf_op jit(solution)/shard_map/ppermute | solution.py:197
  71.2 0.0 collective-permute-done.6.refs_12_
  71.2 0.0 copy-start.16
  71.2 3.0 %collective-permute-start.7 = (bf16[2,256,256]{2,1,0:T(8,128)(2,1)S(1)}, bf16[2,256,256]{2,1,0:T(8,128)(2,1)S(1)}, u32[]{:S(2)}, u32[]{:S(2)}) collective-permute-start(bf16[2,256,256]{2,1,0:T(8,128)(2,1)S(1)} %collective-permute-done.6.refs_12_), channel_id=1, source_target_pairs={{0,32},{32,64},{64,96},{96,128},{128,160},{160,192},{192,224},{224... | collective-permute-start | bytes 786440 | tf_op jit(solution)/shard_map/ppermute | solution.py:197
  74.2 0.4 collective-permute-done.13.refs_13_
  74.5 5.4 %collective-permute-start.14 = (bf16[2,256,256]{2,1,0:T(8,128)(2,1)S(1)}, bf16[2,256,256]{2,1,0:T(8,128)(2,1)S(1)}, u32[]{:S(2)}, u32[]{:S(2)}) collective-permute-start(bf16[2,256,256]{2,1,0:T(8,128)(2,1)S(1)} %collective-permute-done.13.refs_13_), channel_id=1, source_target_pairs={{0,32},{32,64},{64,96},{96,128},{128,160},{160,192},{192,224},{224... | collective-permute-start | bytes 786440 | tf_op jit(solution)/shard_map/ppermute | solution.py:197
  79.9 0.0 collective-permute-done.7.given_ref
  80.0 2.8 %collective-permute-start.15 = (bf16[2,256,256]{2,1,0:T(8,128)(2,1)S(1)}, bf16[2,256,256]{2,1,0:T(8,128)(2,1)S(1)}, u32[]{:S(2)}, u32[]{:S(2)}) collective-permute-start(bf16[2,256,256]{2,1,0:T(8,128)(2,1)S(1)} %shard_map.29.refs_0_), channel_id=1, source_target_pairs={{16,496},{48,16},{80,48},{112,80},{144,112},{176,144},{208,176},{2... | collective-permute-start | bytes 786440 | tf_op jit(solution)/shard_map/ppermute | solution.py:197
  82.8 0.4 collective-permute-done.14.refs_1_
  83.2 5.0 %collective-permute-start.16 = (bf16[2,256,256]{2,1,0:T(8,128)(2,1)S(1)}, bf16[2,256,256]{2,1,0:T(8,128)(2,1)S(1)}, u32[]{:S(2)}, u32[]{:S(2)}) collective-permute-start(bf16[2,256,256]{2,1,0:T(8,128)(2,1)S(1)} %collective-permute-done.14.refs_1_), channel_id=1, source_target_pairs={{16,496},{48,16},{80,48},{112,80},{144,112},{176,144},{208,176},{2... | collective-permute-start | bytes 786440 | tf_op jit(solution)/shard_map/ppermute | solution.py:197
  88.2 0.0 all-to-all-done.1.left_ref
  88.2 3.9 %shard_map.30 = (f32[2,256,256]{2,1,0:T(8,128)S(1)}, f32[2,256,256]{2,1,0:T(8,128)S(1)}) custom-call(s32[1]{0:T(128)} %bitcast.3.plane_ref, s32[1]{0:T(128)} %bitcast.4.core_ref, bf16[4,4,2,256,256]{4,3,2,1,0:T(8,128)(2,1)} %all-to-all-done.1.left_ref, bf16[2,256,256]{2,1,0:T(8,128)(2,1)} %copy-done, bf16[2,256,256]{2,1,0:T(8,128)(2,1)} %copy-done.5, ...), custom_call_target="tpu_custom_call" | custom-call | flops 1879048192 | bytes 14680064 | tf_op jit(solution)/shard_map/pallas_call | solution.py:112
  92.2 0.0 collective-permute-done.15.refs_2_
  92.2 0.0 collective-permute-done.16.refs_3_
  92.2 1.7 %shard_map.32 = f32[2,256,256]{2,1,0:T(8,128)S(1)} custom-call(s32[1]{0:T(128)} %bitcast.3.plane_ref, s32[1]{0:T(128)} %bitcast.4.core_ref, bf16[4,4,2,256,256]{4,3,2,1,0:T(8,128)(2,1)} %all-to-all-done.1.left_ref, bf16[2,256,256]{2,1,0:T(8,128)(2,1)S(1)} %shard_map.29.refs_0_, ...), custom_call_target="tpu_custom_call", output_to_operand_aliasing={{}: (7, {})} | custom-call | flops 268435456 | bytes 3145728 | tf_op jit(solution)/shard_map/pallas_call | solution.py:112
  93.9 0.0 copy-start.4
  93.9 0.0 copy-start.2
  93.9 3.0 %collective-permute-start.17 = (f32[2,256,256]{2,1,0:T(8,128)S(1)}, f32[2,256,256]{2,1,0:T(8,128)S(1)}, u32[]{:S(2)}, u32[]{:S(2)}) collective-permute-start(f32[2,256,256]{2,1,0:T(8,128)S(1)} %shard_map.32), channel_id=1, source_target_pairs={{0,16},{16,0},{1,17},{17,1},{2,18},{18,2},{3,19},{19,3},{4,20},{20... | collective-permute-start | bytes 1572872 | tf_op jit(solution)/shard_map/ppermute | solution.py:228
  96.9 1.7 %shard_map.31.mine_ref = f32[2,256,256]{2,1,0:T(8,128)S(1)} custom-call(s32[1]{0:T(128)} %bitcast.3.plane_ref, s32[1]{0:T(128)} %bitcast.4.core_ref, bf16[4,4,2,256,256]{4,3,2,1,0:T(8,128)(2,1)} %all-to-all-done.1.left_ref, bf16[2,256,256]{2,1,0:T(8,128)(2,1)S(1)} %shard_map.29.refs_0_, ...), custom_call_target="tpu_custom_call", output_to_operand_aliasing={{}: (7, {})} | custom-call | flops 268435456 | bytes 3145728 | tf_op jit(solution)/shard_map/pallas_call | solution.py:112
  98.6 0.0 collective-permute-done.17.other_ref
  98.7 0.6 shard_map.33
  99.3 1.8 %all-gather.1 = f32[2,2,256]{2,1,0:T(2,128)S(1)} all-gather(f32[1,2,256]{2,1,0:T(2,128)S(1)} %bitcast.12), channel_id=2, replica_groups=mesh['z'=16,'core'=2,'y'=4,'x'=4] {'core'}, dimensions={0}, use_global_device_ids=true | all-gather | bytes 6144 | tf_op jit(solution)/shard_map/all_gather | solution.py:240
  101.1 21.1 %all_to_all.15.parts_ref = f32[16,2,256]{2,1,0:T(2,128)S(1)} all-to-all(f32[16,2,256]{2,1,0:T(2,128)S(1)} %broadcast_in_dim.10), channel_id=1, replica_groups=mesh['z'=16,'core'=2,'y'=4,'x'=4] {'z'}, dimensions={0} | all-to-all | bytes 65536 | tf_op jit(solution)/shard_map/all_to_all | solution.py:241
  122.2 1.5 %shard_map.34 = f32[2,256,256]{2,1,0:T(8,128)} custom-call(s32[2]{0:T(128)S(1)} %bitcast.11, s32[1]{0:T(128)} %bitcast.1.column_ref, bf16[2,256,256]{2,1,0:T(8,128)(2,1)S(1)} %bitcast.8, f32[2,256,256]{2,1,0:T(8,128)S(1)} %get-tuple-element.11.inflated_ref, f32[16,2,256]{2,1,0:T(2,128)S(1)} %all_to_all.15.parts_ref), custom_call_target="tpu_custom_call" | custom-call | tf_op jit(solution)/shard_map/pallas_call | solution.py:245
  (28 shorter events, 0.1 us)
Async XLA Ops:
  0.0 0.9 copy-start.1
  1.0 0.7 copy-start.3
  2.3 44.8 %copy-start = (bf16[2,256,256]{2,1,0:T(8,128)(2,1)}, bf16[2,256,256]{2,1,0:T(8,128)(2,1)S(1)}, u32[]{:S(2)}) copy-start(bf16[2,256,256]{2,1,0:T(8,128)(2,1)S(1)} %shard_map.28.refs_0_) | copy-start | bytes 786436
  2.3 14.6 %collective-permute-start = (bf16[2,256,256]{2,1,0:T(8,128)(2,1)S(1)}, bf16[2,256,256]{2,1,0:T(8,128)(2,1)S(1)}, u32[]{:S(2)}, u32[]{:S(2)}) collective-permute-start(bf16[2,256,256]{2,1,0:T(8,128)(2,1)S(1)} %shard_map.28.refs_0_), channel_id=1, source_target_pairs={{0,16},{16,0},{1,17},{17,1},{2,18},{18,2},{3,19},{19,3},{4,20},{20... | collective-permute-start | bytes 786440 | tf_op jit(solution)/shard_map/ppermute | solution.py:187
  11.1 13.8 %collective-permute-start.1 = (bf16[2,256,256]{2,1,0:T(8,128)(2,1)S(1)}, bf16[2,256,256]{2,1,0:T(8,128)(2,1)S(1)}, u32[]{:S(2)}, u32[]{:S(2)}) collective-permute-start(bf16[2,256,256]{2,1,0:T(8,128)(2,1)S(1)} %shard_map.28.refs_0_), channel_id=1, source_target_pairs={{0,32},{32,64},{64,96},{96,128},{128,160},{160,192},{192,224},{224... | collective-permute-start | bytes 786440 | tf_op jit(solution)/shard_map/ppermute | solution.py:197
  16.9 30.2 %copy-start.5 = (bf16[2,256,256]{2,1,0:T(8,128)(2,1)}, bf16[2,256,256]{2,1,0:T(8,128)(2,1)S(1)}, u32[]{:S(2)}) copy-start(bf16[2,256,256]{2,1,0:T(8,128)(2,1)S(1)} %collective-permute-done.refs_1_) | copy-start | bytes 786436
  18.0 26.6 %all-to-all-start = ((bf16[4,2,256,256]{3,2,1,0:T(8,128)(2,1)}), bf16[4,2,256,256]{3,2,1,0:T(8,128)(2,1)S(1)}, u32[]{:S(2)}, u32[]{:S(2)}) async-start(bf16[4,2,256,256]{3,2,1,0:T(8,128)(2,1)} %broadcast_in_dim.8), calls=%async_computation | async-start | bytes 2097152 | tf_op jit(solution)/shard_map/all_to_all | solution.py:216
  22.2 7.4 %collective-permute-start.8 = (bf16[2,256,256]{2,1,0:T(8,128)(2,1)S(1)}, bf16[2,256,256]{2,1,0:T(8,128)(2,1)S(1)}, u32[]{:S(2)}, u32[]{:S(2)}) collective-permute-start(bf16[2,256,256]{2,1,0:T(8,128)(2,1)S(1)} %collective-permute-done.refs_1_), channel_id=1, source_target_pairs={{0,32},{32,64},{64,96},{96,128},{128,160},{160,192},{192,224},{224... | collective-permute-start | bytes 786440 | tf_op jit(solution)/shard_map/ppermute | solution.py:197
  24.8 22.3 %copy-start.6 = (bf16[2,256,256]{2,1,0:T(8,128)(2,1)}, bf16[2,256,256]{2,1,0:T(8,128)(2,1)S(1)}, u32[]{:S(2)}) copy-start(bf16[2,256,256]{2,1,0:T(8,128)(2,1)S(1)} %collective-permute-done.1.refs_2_) | copy-start | bytes 786436
  24.8 8.6 %collective-permute-start.2 = (bf16[2,256,256]{2,1,0:T(8,128)(2,1)S(1)}, bf16[2,256,256]{2,1,0:T(8,128)(2,1)S(1)}, u32[]{:S(2)}, u32[]{:S(2)}) collective-permute-start(bf16[2,256,256]{2,1,0:T(8,128)(2,1)S(1)} %collective-permute-done.1.refs_2_), channel_id=1, source_target_pairs={{0,32},{32,64},{64,96},{96,128},{128,160},{160,192},{192,224},{224... | collective-permute-start | bytes 786440 | tf_op jit(solution)/shard_map/ppermute | solution.py:197
  29.6 17.5 %copy-start.7 = (bf16[2,256,256]{2,1,0:T(8,128)(2,1)}, bf16[2,256,256]{2,1,0:T(8,128)(2,1)S(1)}, u32[]{:S(2)}) copy-start(bf16[2,256,256]{2,1,0:T(8,128)(2,1)S(1)} %collective-permute-done.8.refs_3_) | copy-start | bytes 786436
  29.6 7.4 %collective-permute-start.9 = (bf16[2,256,256]{2,1,0:T(8,128)(2,1)S(1)}, bf16[2,256,256]{2,1,0:T(8,128)(2,1)S(1)}, u32[]{:S(2)}, u32[]{:S(2)}) collective-permute-start(bf16[2,256,256]{2,1,0:T(8,128)(2,1)S(1)} %collective-permute-done.8.refs_3_), channel_id=1, source_target_pairs={{0,32},{32,64},{64,96},{96,128},{128,160},{160,192},{192,224},{224... | collective-permute-start | bytes 786440 | tf_op jit(solution)/shard_map/ppermute | solution.py:197
  33.4 13.7 %copy-start.8 = (bf16[2,256,256]{2,1,0:T(8,128)(2,1)}, bf16[2,256,256]{2,1,0:T(8,128)(2,1)S(1)}, u32[]{:S(2)}) copy-start(bf16[2,256,256]{2,1,0:T(8,128)(2,1)S(1)} %collective-permute-done.2.refs_4_) | copy-start | bytes 786436
  33.4 8.3 %collective-permute-start.3 = (bf16[2,256,256]{2,1,0:T(8,128)(2,1)S(1)}, bf16[2,256,256]{2,1,0:T(8,128)(2,1)S(1)}, u32[]{:S(2)}, u32[]{:S(2)}) collective-permute-start(bf16[2,256,256]{2,1,0:T(8,128)(2,1)S(1)} %collective-permute-done.2.refs_4_), channel_id=1, source_target_pairs={{0,32},{32,64},{64,96},{96,128},{128,160},{160,192},{192,224},{224... | collective-permute-start | bytes 786440 | tf_op jit(solution)/shard_map/ppermute | solution.py:197
  37.0 10.1 %copy-start.9 = (bf16[2,256,256]{2,1,0:T(8,128)(2,1)}, bf16[2,256,256]{2,1,0:T(8,128)(2,1)S(1)}, u32[]{:S(2)}) copy-start(bf16[2,256,256]{2,1,0:T(8,128)(2,1)S(1)} %collective-permute-done.9.refs_5_) | copy-start | bytes 786436
  37.0 15.0 %collective-permute-start.10 = (bf16[2,256,256]{2,1,0:T(8,128)(2,1)S(1)}, bf16[2,256,256]{2,1,0:T(8,128)(2,1)S(1)}, u32[]{:S(2)}, u32[]{:S(2)}) collective-permute-start(bf16[2,256,256]{2,1,0:T(8,128)(2,1)S(1)} %collective-permute-done.9.refs_5_), channel_id=1, source_target_pairs={{0,32},{32,64},{64,96},{96,128},{128,160},{160,192},{192,224},{224... | collective-permute-start | bytes 786440 | tf_op jit(solution)/shard_map/ppermute | solution.py:197
  41.8 5.4 %copy-start.10 = (bf16[2,256,256]{2,1,0:T(8,128)(2,1)}, bf16[2,256,256]{2,1,0:T(8,128)(2,1)S(1)}, u32[]{:S(2)}) copy-start(bf16[2,256,256]{2,1,0:T(8,128)(2,1)S(1)} %collective-permute-done.3.refs_6_) | copy-start | bytes 786436
  41.8 12.2 %collective-permute-start.4 = (bf16[2,256,256]{2,1,0:T(8,128)(2,1)S(1)}, bf16[2,256,256]{2,1,0:T(8,128)(2,1)S(1)}, u32[]{:S(2)}, u32[]{:S(2)}) collective-permute-start(bf16[2,256,256]{2,1,0:T(8,128)(2,1)S(1)} %collective-permute-done.3.refs_6_), channel_id=1, source_target_pairs={{0,32},{32,64},{64,96},{96,128},{128,160},{160,192},{192,224},{224... | collective-permute-start | bytes 786440 | tf_op jit(solution)/shard_map/ppermute | solution.py:197
  47.1 41.1 %all-to-all-start.1 = ((bf16[4,4,2,256,256]{4,3,2,1,0:T(8,128)(2,1)}), bf16[4,4,2,256,256]{4,3,2,1,0:T(8,128)(2,1)}, u32[]{:S(2)}, u32[]{:S(2)}) async-start(bf16[4,4,2,256,256]{4,3,2,1,0:T(8,128)(2,1)} %broadcast_in_dim.9), calls=%async_computation.1 | async-start | bytes 8388608 | tf_op jit(solution)/shard_map/all_to_all | solution.py:216
  52.0 27.9 %copy-start.11 = (bf16[2,256,256]{2,1,0:T(8,128)(2,1)}, bf16[2,256,256]{2,1,0:T(8,128)(2,1)S(1)}, u32[]{:S(2)}) copy-start(bf16[2,256,256]{2,1,0:T(8,128)(2,1)S(1)} %collective-permute-done.10.refs_7_) | copy-start | bytes 786436
  52.0 7.5 %collective-permute-start.11 = (bf16[2,256,256]{2,1,0:T(8,128)(2,1)S(1)}, bf16[2,256,256]{2,1,0:T(8,128)(2,1)S(1)}, u32[]{:S(2)}, u32[]{:S(2)}) collective-permute-start(bf16[2,256,256]{2,1,0:T(8,128)(2,1)S(1)} %collective-permute-done.10.refs_7_), channel_id=1, source_target_pairs={{0,32},{32,64},{64,96},{96,128},{128,160},{160,192},{192,224},{224... | collective-permute-start | bytes 786440 | tf_op jit(solution)/shard_map/ppermute | solution.py:197
  53.9 26.0 %copy-start.12 = (bf16[2,256,256]{2,1,0:T(8,128)(2,1)}, bf16[2,256,256]{2,1,0:T(8,128)(2,1)S(1)}, u32[]{:S(2)}) copy-start(bf16[2,256,256]{2,1,0:T(8,128)(2,1)S(1)} %collective-permute-done.4.refs_8_) | copy-start | bytes 786436
  54.0 8.7 %collective-permute-start.5 = (bf16[2,256,256]{2,1,0:T(8,128)(2,1)S(1)}, bf16[2,256,256]{2,1,0:T(8,128)(2,1)S(1)}, u32[]{:S(2)}, u32[]{:S(2)}) collective-permute-start(bf16[2,256,256]{2,1,0:T(8,128)(2,1)S(1)} %collective-permute-done.4.refs_8_), channel_id=1, source_target_pairs={{0,32},{32,64},{64,96},{96,128},{128,160},{160,192},{192,224},{224... | collective-permute-start | bytes 786440 | tf_op jit(solution)/shard_map/ppermute | solution.py:197
  59.5 20.4 %copy-start.13 = (bf16[2,256,256]{2,1,0:T(8,128)(2,1)}, bf16[2,256,256]{2,1,0:T(8,128)(2,1)S(1)}, u32[]{:S(2)}) copy-start(bf16[2,256,256]{2,1,0:T(8,128)(2,1)S(1)} %collective-permute-done.11.refs_9_) | copy-start | bytes 786436
  59.5 7.5 %collective-permute-start.12 = (bf16[2,256,256]{2,1,0:T(8,128)(2,1)S(1)}, bf16[2,256,256]{2,1,0:T(8,128)(2,1)S(1)}, u32[]{:S(2)}, u32[]{:S(2)}) collective-permute-start(bf16[2,256,256]{2,1,0:T(8,128)(2,1)S(1)} %collective-permute-done.11.refs_9_), channel_id=1, source_target_pairs={{0,32},{32,64},{64,96},{96,128},{128,160},{160,192},{192,224},{224... | collective-permute-start | bytes 786440 | tf_op jit(solution)/shard_map/ppermute | solution.py:197
  62.7 17.3 %copy-start.14 = (bf16[2,256,256]{2,1,0:T(8,128)(2,1)}, bf16[2,256,256]{2,1,0:T(8,128)(2,1)S(1)}, u32[]{:S(2)}) copy-start(bf16[2,256,256]{2,1,0:T(8,128)(2,1)S(1)} %collective-permute-done.5.refs_10_) | copy-start | bytes 786436
  62.7 8.5 %collective-permute-start.6 = (bf16[2,256,256]{2,1,0:T(8,128)(2,1)S(1)}, bf16[2,256,256]{2,1,0:T(8,128)(2,1)S(1)}, u32[]{:S(2)}, u32[]{:S(2)}) collective-permute-start(bf16[2,256,256]{2,1,0:T(8,128)(2,1)S(1)} %collective-permute-done.5.refs_10_), channel_id=1, source_target_pairs={{0,32},{32,64},{64,96},{96,128},{128,160},{160,192},{192,224},{224... | collective-permute-start | bytes 786440 | tf_op jit(solution)/shard_map/ppermute | solution.py:197
  67.0 12.9 %copy-start.15 = (bf16[2,256,256]{2,1,0:T(8,128)(2,1)}, bf16[2,256,256]{2,1,0:T(8,128)(2,1)S(1)}, u32[]{:S(2)}) copy-start(bf16[2,256,256]{2,1,0:T(8,128)(2,1)S(1)} %collective-permute-done.12.refs_11_) | copy-start | bytes 786436
  67.0 7.5 %collective-permute-start.13 = (bf16[2,256,256]{2,1,0:T(8,128)(2,1)S(1)}, bf16[2,256,256]{2,1,0:T(8,128)(2,1)S(1)}, u32[]{:S(2)}, u32[]{:S(2)}) collective-permute-start(bf16[2,256,256]{2,1,0:T(8,128)(2,1)S(1)} %collective-permute-done.12.refs_11_), channel_id=1, source_target_pairs={{0,32},{32,64},{64,96},{96,128},{128,160},{160,192},{192,224},{224... | collective-permute-start | bytes 786440 | tf_op jit(solution)/shard_map/ppermute | solution.py:197
  71.2 8.8 %copy-start.16 = (bf16[2,256,256]{2,1,0:T(8,128)(2,1)}, bf16[2,256,256]{2,1,0:T(8,128)(2,1)S(1)}, u32[]{:S(2)}) copy-start(bf16[2,256,256]{2,1,0:T(8,128)(2,1)S(1)} %collective-permute-done.6.refs_12_) | copy-start | bytes 786436
  71.2 8.7 %collective-permute-start.7 = (bf16[2,256,256]{2,1,0:T(8,128)(2,1)S(1)}, bf16[2,256,256]{2,1,0:T(8,128)(2,1)S(1)}, u32[]{:S(2)}, u32[]{:S(2)}) collective-permute-start(bf16[2,256,256]{2,1,0:T(8,128)(2,1)S(1)} %collective-permute-done.6.refs_12_), channel_id=1, source_target_pairs={{0,32},{32,64},{64,96},{96,128},{128,160},{160,192},{192,224},{224... | collective-permute-start | bytes 786440 | tf_op jit(solution)/shard_map/ppermute | solution.py:197
  74.5 5.5 %copy-start.17 = (bf16[2,256,256]{2,1,0:T(8,128)(2,1)}, bf16[2,256,256]{2,1,0:T(8,128)(2,1)S(1)}, u32[]{:S(2)}) copy-start(bf16[2,256,256]{2,1,0:T(8,128)(2,1)S(1)} %collective-permute-done.13.refs_13_) | copy-start | bytes 786436
  74.5 8.7 %collective-permute-start.14 = (bf16[2,256,256]{2,1,0:T(8,128)(2,1)S(1)}, bf16[2,256,256]{2,1,0:T(8,128)(2,1)S(1)}, u32[]{:S(2)}, u32[]{:S(2)}) collective-permute-start(bf16[2,256,256]{2,1,0:T(8,128)(2,1)S(1)} %collective-permute-done.13.refs_13_), channel_id=1, source_target_pairs={{0,32},{32,64},{64,96},{96,128},{128,160},{160,192},{192,224},{224... | collective-permute-start | bytes 786440 | tf_op jit(solution)/shard_map/ppermute | solution.py:197
  80.0 12.2 %collective-permute-start.15 = (bf16[2,256,256]{2,1,0:T(8,128)(2,1)S(1)}, bf16[2,256,256]{2,1,0:T(8,128)(2,1)S(1)}, u32[]{:S(2)}, u32[]{:S(2)}) collective-permute-start(bf16[2,256,256]{2,1,0:T(8,128)(2,1)S(1)} %shard_map.29.refs_0_), channel_id=1, source_target_pairs={{16,496},{48,16},{80,48},{112,80},{144,112},{176,144},{208,176},{2... | collective-permute-start | bytes 786440 | tf_op jit(solution)/shard_map/ppermute | solution.py:197
  83.2 9.0 %collective-permute-start.16 = (bf16[2,256,256]{2,1,0:T(8,128)(2,1)S(1)}, bf16[2,256,256]{2,1,0:T(8,128)(2,1)S(1)}, u32[]{:S(2)}, u32[]{:S(2)}) collective-permute-start(bf16[2,256,256]{2,1,0:T(8,128)(2,1)S(1)} %collective-permute-done.14.refs_1_), channel_id=1, source_target_pairs={{16,496},{48,16},{80,48},{112,80},{144,112},{176,144},{208,176},{2... | collective-permute-start | bytes 786440 | tf_op jit(solution)/shard_map/ppermute | solution.py:197
  93.9 4.7 %copy-start.4 = (s32[1,2]{1,0:T(1,128)S(1)}, s32[1,2]{1,0:T(1,128)}, u32[]{:S(2)}) copy-start(s32[1,2]{1,0:T(1,128)} %param.4) | copy-start | bytes 28
  93.9 28.3 %copy-start.2 = (bf16[1,2,256,256]{3,2,1,0:T(8,128)(2,1)S(1)}, bf16[1,2,256,256]{3,2,1,0:T(8,128)(2,1)}, u32[]{:S(2)}) copy-start(bf16[1,2,256,256]{3,2,1,0:T(8,128)(2,1)} %param.3) | copy-start | bytes 786436
  93.9 4.7 %collective-permute-start.17 = (f32[2,256,256]{2,1,0:T(8,128)S(1)}, f32[2,256,256]{2,1,0:T(8,128)S(1)}, u32[]{:S(2)}, u32[]{:S(2)}) collective-permute-start(f32[2,256,256]{2,1,0:T(8,128)S(1)} %shard_map.32), channel_id=1, source_target_pairs={{0,16},{16,0},{1,17},{17,1},{2,18},{18,2},{3,19},{19,3},{4,20},{20... | collective-permute-start | bytes 1572872 | tf_op jit(solution)/shard_map/ppermute | solution.py:228

commit v6 on v5

--- a/solution.py
+++ b/solution.py
@@ -15,7 +15,8 @@
 HBM = pl.BlockSpec(memory_space=pltpu.HBM)
 MIB = 1024 * 1024
 SWAP = [(0, 1), (1, 0)]
-FLOPS = 23 * 10**9
+SETTLE = 7
+FLOPS = 26 * 10**9
 
 
 def params(mib):
@@ -31,8 +32,8 @@
         ordered_ref[place] = value.astype(ordered_ref.dtype)
 
 
-def settle_kernel(given_ref, same_ref):
-    del given_ref, same_ref
+def settle_kernel(*refs):
+    del refs
 
 
 def fetch(plan, guard_ref, start):
@@ -155,16 +156,16 @@
             out_ref[slot] = jnp.zeros_like(tile)
 
 
-def settle(value):
+def settle(value, *after, flops=0):
     return pl.pallas_call(
         settle_kernel,
-        in_specs=[ANY],
+        in_specs=[ANY] * (1 + len(after)),
         out_specs=ANY,
         out_shape=jax.ShapeDtypeStruct(value.shape, value.dtype),
         input_output_aliases={0: 0},
         compiler_params=params(1),
-        cost_estimate=pl.CostEstimate(flops=FLOPS, bytes_accessed=0, transcendentals=0),
-    )(value)
+        cost_estimate=pl.CostEstimate(flops=flops, bytes_accessed=0, transcendentals=0),
+    )(value, *after)
 
 
 def on_device(flow_tiles, tile_cols, pairs):
@@ -189,13 +190,6 @@
     half = planes // 2
     ring = [(2 * z, 2 * ((z + 1) % planes)) for z in range(planes)]
     back = [(2 * z + 1, 2 * ((z - 1) % planes) + 1) for z in range(planes)]
-    held = [(mine, other)]
-    for step in range(1, half + 1):
-        perm = ring + back if step < half else back
-        if step == half:
-            held[-1] = (settle(held[-1][0]), held[-1][1])
-        held.append(tuple(lax.ppermute(t, ROWS, perm) for t in held[-1]))
-
     low = lax.rem(column - 2 * (plane - half + 1) + 2 * columns, 2 * columns)
     place = jnp.where((low < columns) == (core == 0), 0, 1)
     height, breadth = lax.axis_size("y"), lax.axis_size("x")
@@ -220,9 +214,20 @@
     sent = jnp.stack([jnp.where(place == 0, t[0], t[1]) for t in (mine, other)])
     left = copy_for_each(copy_for_each(sent, lines_of(0)), lines_of(1))
 
+    held = [(mine, other)]
+    totals = None
+    for step in range(1, half + 1):
+        if step == SETTLE:
+            held[-1] = (settle(held[-1][0], flops=FLOPS), held[-1][1])
+        if step == half:
+            early = [(0, 0)] + [(i, None) for i in range(1, half - 1)]
+            totals = products(
+                None, (0, 1), plane_ref, core_ref, left, held, early, [[1, 2], [3, 4], [5, 6], [0]]
+            )
+            held[-1] = (settle(held[-1][0], *totals.values()), held[-1][1])
+        perm = ring + back if step < half else back
+        held.append(tuple(lax.ppermute(t, ROWS, perm) for t in held[-1]))
     known = (plane_ref, core_ref, left, held)
-    early = [(0, 0)] + [(i, None) for i in range(1, half - 1)]
-    totals = products(None, (0, 1), *known, early, [[1, 2], [3, 4], [5, 6], [0]])
     late = [(half - 1, None), (half, 1)]
     outward = products(totals, (1,), *known, late, [[0], [1]])[1]
     received = lax.ppermute(outward, "core", SWAP)

time: 125 us -> 122 us (0.976)
  waiting for transfers between devices: 8.8 us -> 13.8 us
  blocking collectives: 22.9 us -> 18.4 us
  starting transfers between devices: 76 us -> 72.4 us
    ppermute x16, waiting for transfers between devices: 8.79 us -> 13.6 us  [on_device(): held.append(tuple((lax.ppermute(t, ROWS, perm) for t in held[-1])))]
    all_to_all x1, blocking collectives: 21.1 us -> 16.6 us  [on_device(): lax.all_to_all(jnp.broadcast_to(sums[None], (planes, *sums.shape)), 'z',...]
    ppermute x16, starting transfers between devices: 55.2 us -> 52.5 us  [on_device(): held.append(tuple((lax.ppermute(t, ROWS, perm) for t in held[-1])))]
  transfers between devices with their start and end apart: 20 -> 20, of which waited for: 6 -> 7; matrix products, arithmetic and copies ran while one was open for 3% -> 3% of each run, Pallas kernels for 5% -> 5%
where the time goes in v6:
time: 122 us; the launch traced here: 120 us
  starting transfers between devices  72.4 us (59%)
  blocking collectives  18.4 us (15%)
  waiting for transfers between devices  13.8 us (11%)
  Pallas kernels  10.1 us (8%)
  local copies, waits for them, and re-layouts  5.22 us (4%)
    ppermute x16, starting transfers between devices, on_device(): held.append(tuple((lax.ppermute(t, ROWS, perm) for t in held[-1])))  52.5 us
    all_to_all x1, blocking collectives, on_device(): lax.all_to_all(jnp.broadcast_to(sums[None], (planes, *sums.shape)), 'z',...  16.6 us
    ppermute x16, waiting for transfers between devices, on_device(): held.append(tuple((lax.ppermute(t, ROWS, perm) for t in held[-1])))  13.6 us
    all_to_all x2, starting transfers between devices, copy_for_each(): lax.all_to_all(spread, ('core', *COLS), 0, 0, axis_index_groups=lines, ti...  9.03 us
    ppermute x1, starting transfers between devices, on_device(): other = lax.ppermute(mine, 'core', SWAP)  8.79 us
    pallas_call x3, Pallas kernels, products(): pl.pallas_call(kernel, in_specs=[SMEM, SMEM, HBM] + [HBM] * len(tiles) +...  7.3 us
    broadcast_in_dim x2, local copies, waits for them, and re-layouts, copy_for_each(): spread = jnp.broadcast_to(value[None], (len(lines[0]), *value.shape))  3.53 us
  transfers between devices with their start and end apart: 20, of which 7 were waited for; matrix products, arithmetic and copies ran while one was open for 3% of the time, Pallas kernels for 5%

profile of v6, /device:TPU:1, one launch (start us, length us, event | category | flops | bytes accessed | tf_op | source)
XLA Modules:
  0.0 120.5 jit_solution(11446540938996327620)
XLA Ops:
  0.0 0.9 copy-done.1
  1.0 0.7 copy-done.4
  1.6 0.6 shard_map.28.refs_0_
  2.3 0.0 copy-start
  2.3 8.8 %collective-permute-start = (bf16[2,256,256]{2,1,0:T(8,128)(2,1)S(1)}, bf16[2,256,256]{2,1,0:T(8,128)(2,1)S(1)}, u32[]{:S(2)}, u32[]{:S(2)}) collective-permute-start(bf16[2,256,256]{2,1,0:T(8,128)(2,1)S(1)} %shard_map.28.refs_0_), channel_id=1, source_target_pairs={{0,16},{16,0},{1,17},{17,1},{2,18},{18,2},{3,19},{19,3},{4,20},{20... | collective-permute-start | bytes 786440 | tf_op jit(solution)/shard_map/ppermute | solution.py:188
  11.1 5.7 %collective-permute-start.1 = (bf16[2,256,256]{2,1,0:T(8,128)(2,1)S(1)}, bf16[2,256,256]{2,1,0:T(8,128)(2,1)S(1)}, u32[]{:S(2)}, u32[]{:S(2)}) collective-permute-start(bf16[2,256,256]{2,1,0:T(8,128)(2,1)S(1)} %shard_map.28.refs_0_), channel_id=1, source_target_pairs={{0,32},{32,64},{64,96},{96,128},{128,160},{160,192},{192,224},{224... | collective-permute-start | bytes 786440 | tf_op jit(solution)/shard_map/ppermute | solution.py:229
  16.9 0.0 collective-permute-done.refs_1_
  16.9 0.0 copy-start.6
  16.9 2.6 %collective-permute-start.8 = (bf16[2,256,256]{2,1,0:T(8,128)(2,1)S(1)}, bf16[2,256,256]{2,1,0:T(8,128)(2,1)S(1)}, u32[]{:S(2)}, u32[]{:S(2)}) collective-permute-start(bf16[2,256,256]{2,1,0:T(8,128)(2,1)S(1)} %collective-permute-done.refs_1_), channel_id=1, source_target_pairs={{0,32},{32,64},{64,96},{96,128},{128,160},{160,192},{192,224},{224... | collective-permute-start | bytes 786440 | tf_op jit(solution)/shard_map/ppermute | solution.py:229
  19.6 1.0 broadcast_in_dim.8
  20.6 4.2 %all-to-all-start = ((bf16[4,2,256,256]{3,2,1,0:T(8,128)(2,1)}), bf16[4,2,256,256]{3,2,1,0:T(8,128)(2,1)S(1)}, u32[]{:S(2)}, u32[]{:S(2)}) async-start(bf16[4,2,256,256]{3,2,1,0:T(8,128)(2,1)} %broadcast_in_dim.8), calls=%async_computation | async-start | bytes 2097152 | tf_op jit(solution)/shard_map/all_to_all | solution.py:210
  24.8 0.0 collective-permute-done.8.refs_3_
  24.8 3.1 %collective-permute-start.9 = (bf16[2,256,256]{2,1,0:T(8,128)(2,1)S(1)}, bf16[2,256,256]{2,1,0:T(8,128)(2,1)S(1)}, u32[]{:S(2)}, u32[]{:S(2)}) collective-permute-start(bf16[2,256,256]{2,1,0:T(8,128)(2,1)S(1)} %collective-permute-done.8.refs_3_), channel_id=1, source_target_pairs={{0,32},{32,64},{64,96},{96,128},{128,160},{160,192},{192,224},{224... | collective-permute-start | bytes 786440 | tf_op jit(solution)/shard_map/ppermute | solution.py:229
  27.9 0.0 collective-permute-done.1.refs_2_
  28.0 0.0 copy-start.7
  28.0 2.1 %collective-permute-start.2 = (bf16[2,256,256]{2,1,0:T(8,128)(2,1)S(1)}, bf16[2,256,256]{2,1,0:T(8,128)(2,1)S(1)}, u32[]{:S(2)}, u32[]{:S(2)}) collective-permute-start(bf16[2,256,256]{2,1,0:T(8,128)(2,1)S(1)} %collective-permute-done.1.refs_2_), channel_id=1, source_target_pairs={{0,32},{32,64},{64,96},{96,128},{128,160},{160,192},{192,224},{224... | collective-permute-start | bytes 786440 | tf_op jit(solution)/shard_map/ppermute | solution.py:229
  30.1 2.1 %collective-permute-done.9.refs_5_ = bf16[2,256,256]{2,1,0:T(8,128)(2,1)S(1)} collective-permute-done((bf16[2,256,256]{2,1,0:T(8,128)(2,1)S(1)}, bf16[2,256,256]{2,1,0:T(8,128)(2,1)S(1)}, u32[]{:S(2)}, u32[]{:S(2)}) %collective-permute-start.9) | collective-permute-done | bytes 262176 | tf_op jit(solution)/shard_map/ppermute | solution.py:229
  32.2 4.3 %collective-permute-start.10 = (bf16[2,256,256]{2,1,0:T(8,128)(2,1)S(1)}, bf16[2,256,256]{2,1,0:T(8,128)(2,1)S(1)}, u32[]{:S(2)}, u32[]{:S(2)}) collective-permute-start(bf16[2,256,256]{2,1,0:T(8,128)(2,1)S(1)} %collective-permute-done.9.refs_5_), channel_id=1, source_target_pairs={{0,32},{32,64},{64,96},{96,128},{128,160},{160,192},{192,224},{224... | collective-permute-start | bytes 786440 | tf_op jit(solution)/shard_map/ppermute | solution.py:229
  36.6 0.0 collective-permute-done.2.refs_4_
  36.6 0.0 copy-start.10
  36.6 2.5 %collective-permute-start.3 = (bf16[2,256,256]{2,1,0:T(8,128)(2,1)S(1)}, bf16[2,256,256]{2,1,0:T(8,128)(2,1)S(1)}, u32[]{:S(2)}, u32[]{:S(2)}) collective-permute-start(bf16[2,256,256]{2,1,0:T(8,128)(2,1)S(1)} %collective-permute-done.2.refs_4_), channel_id=1, source_target_pairs={{0,32},{32,64},{64,96},{96,128},{128,160},{160,192},{192,224},{224... | collective-permute-start | bytes 786440 | tf_op jit(solution)/shard_map/ppermute | solution.py:229
  39.1 0.8 collective-permute-done.10.refs_7_
  39.9 5.0 %collective-permute-start.11 = (bf16[2,256,256]{2,1,0:T(8,128)(2,1)S(1)}, bf16[2,256,256]{2,1,0:T(8,128)(2,1)S(1)}, u32[]{:S(2)}, u32[]{:S(2)}) collective-permute-start(bf16[2,256,256]{2,1,0:T(8,128)(2,1)S(1)} %collective-permute-done.10.refs_7_), channel_id=1, source_target_pairs={{0,32},{32,64},{64,96},{96,128},{128,160},{160,192},{192,224},{224... | collective-permute-start | bytes 786440 | tf_op jit(solution)/shard_map/ppermute | solution.py:229
  44.9 0.0 collective-permute-done.3.refs_6_
  44.9 0.0 copy-start.12
  44.9 2.8 %collective-permute-start.4 = (bf16[2,256,256]{2,1,0:T(8,128)(2,1)S(1)}, bf16[2,256,256]{2,1,0:T(8,128)(2,1)}, u32[]{:S(2)}, u32[]{:S(2)}) collective-permute-start(bf16[2,256,256]{2,1,0:T(8,128)(2,1)S(1)} %collective-permute-done.3.refs_6_), channel_id=1, source_target_pairs={{0,32},{32,64},{64,96},{96,128},{128,160},{160,192},{192,224},{224... | collective-permute-start | bytes 786440 | tf_op jit(solution)/shard_map/ppermute | solution.py:229
  47.7 0.0 all-to-all-done
  47.7 2.5 %broadcast_in_dim.9 = bf16[4,4,2,256,256]{4,3,2,1,0:T(8,128)(2,1)} broadcast(bf16[4,2,256,256]{3,2,1,0:T(8,128)(2,1)S(1)} %all-to-all-done), dimensions={1,2,3,4} | broadcast | bytes 5242880 | tf_op jit(solution)/shard_map/broadcast_in_dim | solution.py:209
  50.2 0.0 copy-done
  50.2 0.0 copy-done.8
  50.2 4.8 %all-to-all-start.1 = ((bf16[4,4,2,256,256]{4,3,2,1,0:T(8,128)(2,1)}), bf16[4,4,2,256,256]{4,3,2,1,0:T(8,128)(2,1)}, u32[]{:S(2)}, u32[]{:S(2)}) async-start(bf16[4,4,2,256,256]{4,3,2,1,0:T(8,128)(2,1)} %broadcast_in_dim.9), calls=%async_computation.1 | async-start | bytes 8388608 | tf_op jit(solution)/shard_map/all_to_all | solution.py:210
  55.1 0.0 collective-permute-done.11.refs_9_
  55.1 0.0 copy-start.13
  55.1 1.9 %collective-permute-start.12 = (bf16[2,256,256]{2,1,0:T(8,128)(2,1)S(1)}, bf16[2,256,256]{2,1,0:T(8,128)(2,1)S(1)}, u32[]{:S(2)}, u32[]{:S(2)}) collective-permute-start(bf16[2,256,256]{2,1,0:T(8,128)(2,1)S(1)} %collective-permute-done.11.refs_9_), channel_id=1, source_target_pairs={{0,32},{32,64},{64,96},{96,128},{128,160},{160,192},{192,224},{224... | collective-permute-start | bytes 786440 | tf_op jit(solution)/shard_map/ppermute | solution.py:229
  57.0 0.0 collective-permute-done.4.refs_8_
  57.1 2.0 %collective-permute-start.5 = (bf16[2,256,256]{2,1,0:T(8,128)(2,1)}, bf16[2,256,256]{2,1,0:T(8,128)(2,1)S(1)}, u32[]{:S(2)}, u32[]{:S(2)}) collective-permute-start(bf16[2,256,256]{2,1,0:T(8,128)(2,1)} %collective-permute-done.4.refs_8_), channel_id=1, source_target_pairs={{0,32},{32,64},{64,96},{96,128},{128,160},{160,192},{192,224},{224... | collective-permute-start | bytes 786440 | tf_op jit(solution)/shard_map/ppermute | solution.py:229
  59.1 3.5 %collective-permute-done.12.refs_11_ = bf16[2,256,256]{2,1,0:T(8,128)(2,1)S(1)} collective-permute-done((bf16[2,256,256]{2,1,0:T(8,128)(2,1)S(1)}, bf16[2,256,256]{2,1,0:T(8,128)(2,1)S(1)}, u32[]{:S(2)}, u32[]{:S(2)}) %collective-permute-start.12) | collective-permute-done | bytes 262176 | tf_op jit(solution)/shard_map/ppermute | solution.py:229
  62.6 3.1 %collective-permute-start.13 = (bf16[2,256,256]{2,1,0:T(8,128)(2,1)S(1)}, bf16[2,256,256]{2,1,0:T(8,128)(2,1)S(1)}, u32[]{:S(2)}, u32[]{:S(2)}) collective-permute-start(bf16[2,256,256]{2,1,0:T(8,128)(2,1)S(1)} %collective-permute-done.12.refs_11_), channel_id=1, source_target_pairs={{0,32},{32,64},{64,96},{96,128},{128,160},{160,192},{192,224},{224... | collective-permute-start | bytes 786440 | tf_op jit(solution)/shard_map/ppermute | solution.py:229
  65.8 0.0 collective-permute-done.5.refs_10_
  65.8 0.0 copy-start.15
  65.8 2.8 %collective-permute-start.6 = (bf16[2,256,256]{2,1,0:T(8,128)(2,1)S(1)}, bf16[2,256,256]{2,1,0:T(8,128)(2,1)S(1)}, u32[]{:S(2)}, u32[]{:S(2)}) collective-permute-start(bf16[2,256,256]{2,1,0:T(8,128)(2,1)S(1)} %collective-permute-done.5.refs_10_), channel_id=1, source_target_pairs={{0,32},{32,64},{64,96},{96,128},{128,160},{160,192},{192,224},{224... | collective-permute-start | bytes 786440 | tf_op jit(solution)/shard_map/ppermute | solution.py:229
  68.6 1.6 %collective-permute-done.13.refs_13_ = bf16[2,256,256]{2,1,0:T(8,128)(2,1)S(1)} collective-permute-done((bf16[2,256,256]{2,1,0:T(8,128)(2,1)S(1)}, bf16[2,256,256]{2,1,0:T(8,128)(2,1)S(1)}, u32[]{:S(2)}, u32[]{:S(2)}) %collective-permute-start.13) | collective-permute-done | bytes 262176 | tf_op jit(solution)/shard_map/ppermute | solution.py:229
  70.1 4.3 %collective-permute-start.14 = (bf16[2,256,256]{2,1,0:T(8,128)(2,1)S(1)}, bf16[2,256,256]{2,1,0:T(8,128)(2,1)S(1)}, u32[]{:S(2)}, u32[]{:S(2)}) collective-permute-start(bf16[2,256,256]{2,1,0:T(8,128)(2,1)S(1)} %collective-permute-done.13.refs_13_), channel_id=1, source_target_pairs={{0,32},{32,64},{64,96},{96,128},{128,160},{160,192},{192,224},{224... | collective-permute-start | bytes 786440 | tf_op jit(solution)/shard_map/ppermute | solution.py:229
  74.5 0.0 collective-permute-done.6.refs_0_
  74.6 2.8 %collective-permute-start.7 = (bf16[2,256,256]{2,1,0:T(8,128)(2,1)S(1)}, bf16[2,256,256]{2,1,0:T(8,128)(2,1)S(1)}, u32[]{:S(2)}, u32[]{:S(2)}) collective-permute-start(bf16[2,256,256]{2,1,0:T(8,128)(2,1)S(1)} %shard_map.29.refs_12_), channel_id=1, source_target_pairs={{0,32},{32,64},{64,96},{96,128},{128,160},{160,192},{192,224},{224... | collective-permute-start | bytes 786440 | tf_op jit(solution)/shard_map/ppermute | solution.py:229
  77.3 0.4 collective-permute-done.14.refs_1_
  77.8 5.4 %collective-permute-start.16 = (bf16[2,256,256]{2,1,0:T(8,128)(2,1)S(1)}, bf16[2,256,256]{2,1,0:T(8,128)(2,1)S(1)}, u32[]{:S(2)}, u32[]{:S(2)}) collective-permute-start(bf16[2,256,256]{2,1,0:T(8,128)(2,1)S(1)} %collective-permute-done.14.refs_1_), channel_id=1, source_target_pairs={{16,496},{48,16},{80,48},{112,80},{144,112},{176,144},{208,176},{2... | collective-permute-start | bytes 786440 | tf_op jit(solution)/shard_map/ppermute | solution.py:229
  83.2 0.0 all-to-all-done.1.left_ref
  83.2 3.9 %shard_map.30 = (f32[2,256,256]{2,1,0:T(8,128)S(1)}, f32[2,256,256]{2,1,0:T(8,128)S(1)}) custom-call(s32[1]{0:T(128)} %bitcast.3.plane_ref, s32[1]{0:T(128)} %bitcast.4.core_ref, bf16[4,4,2,256,256]{4,3,2,1,0:T(8,128)(2,1)} %all-to-all-done.1.left_ref, bf16[2,256,256]{2,1,0:T(8,128)(2,1)} %copy-done, bf16[2,256,256]{2,1,0:T(8,128)(2,1)} %copy-done.6, ...), custom_call_target="tpu_custom_call" | custom-call | flops 1879048192 | bytes 14680064 | tf_op jit(solution)/shard_map/pallas_call | solution.py:113
  87.2 0.0 collective-permute-done.7.refs_0_
  87.2 1.9 %collective-permute-start.15 = (bf16[2,256,256]{2,1,0:T(8,128)(2,1)S(1)}, bf16[2,256,256]{2,1,0:T(8,128)(2,1)S(1)}, u32[]{:S(2)}, u32[]{:S(2)}) collective-permute-start(bf16[2,256,256]{2,1,0:T(8,128)(2,1)S(1)} %shard_map.31.refs_0_), channel_id=1, source_target_pairs={{16,496},{48,16},{80,48},{112,80},{144,112},{176,144},{208,176},{2... | collective-permute-start | bytes 786440 | tf_op jit(solution)/shard_map/ppermute | solution.py:229
  89.1 0.0 collective-permute-done.16.refs_3_
  89.1 5.2 %collective-permute-done.15.refs_2_ = bf16[2,256,256]{2,1,0:T(8,128)(2,1)S(1)} collective-permute-done((bf16[2,256,256]{2,1,0:T(8,128)(2,1)S(1)}, bf16[2,256,256]{2,1,0:T(8,128)(2,1)S(1)}, u32[]{:S(2)}, u32[]{:S(2)}) %collective-permute-start.15) | collective-permute-done | bytes 262176 | tf_op jit(solution)/shard_map/ppermute | solution.py:229
  94.3 1.7 %shard_map.33 = f32[2,256,256]{2,1,0:T(8,128)S(1)} custom-call(s32[1]{0:T(128)} %bitcast.3.plane_ref, s32[1]{0:T(128)} %bitcast.4.core_ref, bf16[4,4,2,256,256]{4,3,2,1,0:T(8,128)(2,1)} %all-to-all-done.1.left_ref, bf16[2,256,256]{2,1,0:T(8,128)(2,1)S(1)} %shard_map.31.refs_0_, ...), custom_call_target="tpu_custom_call", output_to_operand_aliasing={{}: (7, {})} | custom-call | flops 268435456 | bytes 3145728 | tf_op jit(solution)/shard_map/pallas_call | solution.py:113
  96.0 0.0 copy-start.5
  96.0 0.0 copy-start.2
  96.0 2.1 %collective-permute-start.17 = (f32[2,256,256]{2,1,0:T(8,128)S(1)}, f32[2,256,256]{2,1,0:T(8,128)S(1)}, u32[]{:S(2)}, u32[]{:S(2)}) collective-permute-start(f32[2,256,256]{2,1,0:T(8,128)S(1)} %shard_map.33), channel_id=1, source_target_pairs={{0,16},{16,0},{1,17},{17,1},{2,18},{18,2},{3,19},{19,3},{4,20},{20... | collective-permute-start | bytes 1572872 | tf_op jit(solution)/shard_map/ppermute | solution.py:233
  98.1 1.7 %shard_map.32.mine_ref = f32[2,256,256]{2,1,0:T(8,128)S(1)} custom-call(s32[1]{0:T(128)} %bitcast.3.plane_ref, s32[1]{0:T(128)} %bitcast.4.core_ref, bf16[4,4,2,256,256]{4,3,2,1,0:T(8,128)(2,1)} %all-to-all-done.1.left_ref, bf16[2,256,256]{2,1,0:T(8,128)(2,1)S(1)} %shard_map.31.refs_0_, ...), custom_call_target="tpu_custom_call", output_to_operand_aliasing={{}: (7, {})} | custom-call | flops 268435456 | bytes 3145728 | tf_op jit(solution)/shard_map/pallas_call | solution.py:113
  99.8 0.2 collective-permute-done.17.other_ref
  99.9 0.6 shard_map.34
  100.6 1.8 %all-gather.1 = f32[2,2,256]{2,1,0:T(2,128)S(1)} all-gather(f32[1,2,256]{2,1,0:T(2,128)S(1)} %bitcast.12), channel_id=2, replica_groups=mesh['z'=16,'core'=2,'y'=4,'x'=4] {'core'}, dimensions={0}, use_global_device_ids=true | all-gather | bytes 6144 | tf_op jit(solution)/shard_map/all_gather | solution.py:245
  102.4 16.6 %all_to_all.15.parts_ref = f32[16,2,256]{2,1,0:T(2,128)S(1)} all-to-all(f32[16,2,256]{2,1,0:T(2,128)S(1)} %broadcast_in_dim.10), channel_id=1, replica_groups=mesh['z'=16,'core'=2,'y'=4,'x'=4] {'z'}, dimensions={0} | all-to-all | bytes 65536 | tf_op jit(solution)/shard_map/all_to_all | solution.py:246
  119.0 0.0 copy-done.2
  119.0 1.5 %shard_map.35 = f32[2,256,256]{2,1,0:T(8,128)} custom-call(s32[2]{0:T(128)S(1)} %bitcast.11, s32[1]{0:T(128)} %bitcast.1.column_ref, bf16[2,256,256]{2,1,0:T(8,128)(2,1)S(1)} %bitcast.8, f32[2,256,256]{2,1,0:T(8,128)S(1)} %get-tuple-element.11.inflated_ref, f32[16,2,256]{2,1,0:T(2,128)S(1)} %all_to_all.15.parts_ref), custom_call_target="tpu_custom_call" | custom-call | tf_op jit(solution)/shard_map/pallas_call | solution.py:250
  (27 shorter events, 0.1 us)
Async XLA Ops:
  0.0 0.9 copy-start.1
  1.0 0.7 copy-start.4
  2.3 47.9 %copy-start = (bf16[2,256,256]{2,1,0:T(8,128)(2,1)}, bf16[2,256,256]{2,1,0:T(8,128)(2,1)S(1)}, u32[]{:S(2)}) copy-start(bf16[2,256,256]{2,1,0:T(8,128)(2,1)S(1)} %shard_map.28.refs_0_) | copy-start | bytes 786436
  2.3 14.6 %collective-permute-start = (bf16[2,256,256]{2,1,0:T(8,128)(2,1)S(1)}, bf16[2,256,256]{2,1,0:T(8,128)(2,1)S(1)}, u32[]{:S(2)}, u32[]{:S(2)}) collective-permute-start(bf16[2,256,256]{2,1,0:T(8,128)(2,1)S(1)} %shard_map.28.refs_0_), channel_id=1, source_target_pairs={{0,16},{16,0},{1,17},{17,1},{2,18},{18,2},{3,19},{19,3},{4,20},{20... | collective-permute-start | bytes 786440 | tf_op jit(solution)/shard_map/ppermute | solution.py:188
  11.1 16.9 %collective-permute-start.1 = (bf16[2,256,256]{2,1,0:T(8,128)(2,1)S(1)}, bf16[2,256,256]{2,1,0:T(8,128)(2,1)S(1)}, u32[]{:S(2)}, u32[]{:S(2)}) collective-permute-start(bf16[2,256,256]{2,1,0:T(8,128)(2,1)S(1)} %shard_map.28.refs_0_), channel_id=1, source_target_pairs={{0,32},{32,64},{64,96},{96,128},{128,160},{160,192},{192,224},{224... | collective-permute-start | bytes 786440 | tf_op jit(solution)/shard_map/ppermute | solution.py:229
  16.9 33.3 %copy-start.6 = (bf16[2,256,256]{2,1,0:T(8,128)(2,1)}, bf16[2,256,256]{2,1,0:T(8,128)(2,1)S(1)}, u32[]{:S(2)}) copy-start(bf16[2,256,256]{2,1,0:T(8,128)(2,1)S(1)} %collective-permute-done.refs_1_) | copy-start | bytes 786436
  16.9 7.9 %collective-permute-start.8 = (bf16[2,256,256]{2,1,0:T(8,128)(2,1)S(1)}, bf16[2,256,256]{2,1,0:T(8,128)(2,1)S(1)}, u32[]{:S(2)}, u32[]{:S(2)}) collective-permute-start(bf16[2,256,256]{2,1,0:T(8,128)(2,1)S(1)} %collective-permute-done.refs_1_), channel_id=1, source_target_pairs={{0,32},{32,64},{64,96},{96,128},{128,160},{160,192},{192,224},{224... | collective-permute-start | bytes 786440 | tf_op jit(solution)/shard_map/ppermute | solution.py:229
  20.6 27.1 %all-to-all-start = ((bf16[4,2,256,256]{3,2,1,0:T(8,128)(2,1)}), bf16[4,2,256,256]{3,2,1,0:T(8,128)(2,1)S(1)}, u32[]{:S(2)}, u32[]{:S(2)}) async-start(bf16[4,2,256,256]{3,2,1,0:T(8,128)(2,1)} %broadcast_in_dim.8), calls=%async_computation | async-start | bytes 2097152 | tf_op jit(solution)/shard_map/all_to_all | solution.py:210
  24.8 25.4 %copy-start.8 = (bf16[2,256,256]{2,1,0:T(8,128)(2,1)}, bf16[2,256,256]{2,1,0:T(8,128)(2,1)S(1)}, u32[]{:S(2)}) copy-start(bf16[2,256,256]{2,1,0:T(8,128)(2,1)S(1)} %collective-permute-done.8.refs_3_) | copy-start | bytes 786436
  24.8 7.4 %collective-permute-start.9 = (bf16[2,256,256]{2,1,0:T(8,128)(2,1)S(1)}, bf16[2,256,256]{2,1,0:T(8,128)(2,1)S(1)}, u32[]{:S(2)}, u32[]{:S(2)}) collective-permute-start(bf16[2,256,256]{2,1,0:T(8,128)(2,1)S(1)} %collective-permute-done.8.refs_3_), channel_id=1, source_target_pairs={{0,32},{32,64},{64,96},{96,128},{128,160},{160,192},{192,224},{224... | collective-permute-start | bytes 786440 | tf_op jit(solution)/shard_map/ppermute | solution.py:229
  28.0 22.2 %copy-start.7 = (bf16[2,256,256]{2,1,0:T(8,128)(2,1)}, bf16[2,256,256]{2,1,0:T(8,128)(2,1)S(1)}, u32[]{:S(2)}) copy-start(bf16[2,256,256]{2,1,0:T(8,128)(2,1)S(1)} %collective-permute-done.1.refs_2_) | copy-start | bytes 786436
  28.0 8.6 %collective-permute-start.2 = (bf16[2,256,256]{2,1,0:T(8,128)(2,1)S(1)}, bf16[2,256,256]{2,1,0:T(8,128)(2,1)S(1)}, u32[]{:S(2)}, u32[]{:S(2)}) collective-permute-start(bf16[2,256,256]{2,1,0:T(8,128)(2,1)S(1)} %collective-permute-done.1.refs_2_), channel_id=1, source_target_pairs={{0,32},{32,64},{64,96},{96,128},{128,160},{160,192},{192,224},{224... | collective-permute-start | bytes 786440 | tf_op jit(solution)/shard_map/ppermute | solution.py:229
  32.2 18.0 %copy-start.9 = (bf16[2,256,256]{2,1,0:T(8,128)(2,1)}, bf16[2,256,256]{2,1,0:T(8,128)(2,1)S(1)}, u32[]{:S(2)}) copy-start(bf16[2,256,256]{2,1,0:T(8,128)(2,1)S(1)} %collective-permute-done.9.refs_5_) | copy-start | bytes 786436
  32.2 7.6 %collective-permute-start.10 = (bf16[2,256,256]{2,1,0:T(8,128)(2,1)S(1)}, bf16[2,256,256]{2,1,0:T(8,128)(2,1)S(1)}, u32[]{:S(2)}, u32[]{:S(2)}) collective-permute-start(bf16[2,256,256]{2,1,0:T(8,128)(2,1)S(1)} %collective-permute-done.9.refs_5_), channel_id=1, source_target_pairs={{0,32},{32,64},{64,96},{96,128},{128,160},{160,192},{192,224},{224... | collective-permute-start | bytes 786440 | tf_op jit(solution)/shard_map/ppermute | solution.py:229
  36.6 13.6 %copy-start.10 = (bf16[2,256,256]{2,1,0:T(8,128)(2,1)}, bf16[2,256,256]{2,1,0:T(8,128)(2,1)S(1)}, u32[]{:S(2)}) copy-start(bf16[2,256,256]{2,1,0:T(8,128)(2,1)S(1)} %collective-permute-done.2.refs_4_) | copy-start | bytes 786436
  36.6 8.3 %collective-permute-start.3 = (bf16[2,256,256]{2,1,0:T(8,128)(2,1)S(1)}, bf16[2,256,256]{2,1,0:T(8,128)(2,1)S(1)}, u32[]{:S(2)}, u32[]{:S(2)}) collective-permute-start(bf16[2,256,256]{2,1,0:T(8,128)(2,1)S(1)} %collective-permute-done.2.refs_4_), channel_id=1, source_target_pairs={{0,32},{32,64},{64,96},{96,128},{128,160},{160,192},{192,224},{224... | collective-permute-start | bytes 786440 | tf_op jit(solution)/shard_map/ppermute | solution.py:229
  39.9 10.4 %copy-start.11 = (bf16[2,256,256]{2,1,0:T(8,128)(2,1)}, bf16[2,256,256]{2,1,0:T(8,128)(2,1)S(1)}, u32[]{:S(2)}) copy-start(bf16[2,256,256]{2,1,0:T(8,128)(2,1)S(1)} %collective-permute-done.10.refs_7_) | copy-start | bytes 786436
  39.9 15.2 %collective-permute-start.11 = (bf16[2,256,256]{2,1,0:T(8,128)(2,1)S(1)}, bf16[2,256,256]{2,1,0:T(8,128)(2,1)S(1)}, u32[]{:S(2)}, u32[]{:S(2)}) collective-permute-start(bf16[2,256,256]{2,1,0:T(8,128)(2,1)S(1)} %collective-permute-done.10.refs_7_), channel_id=1, source_target_pairs={{0,32},{32,64},{64,96},{96,128},{128,160},{160,192},{192,224},{224... | collective-permute-start | bytes 786440 | tf_op jit(solution)/shard_map/ppermute | solution.py:229
  44.9 5.4 %copy-start.12 = (bf16[2,256,256]{2,1,0:T(8,128)(2,1)}, bf16[2,256,256]{2,1,0:T(8,128)(2,1)S(1)}, u32[]{:S(2)}) copy-start(bf16[2,256,256]{2,1,0:T(8,128)(2,1)S(1)} %collective-permute-done.3.refs_6_) | copy-start | bytes 786436
  44.9 12.2 %collective-permute-start.4 = (bf16[2,256,256]{2,1,0:T(8,128)(2,1)S(1)}, bf16[2,256,256]{2,1,0:T(8,128)(2,1)}, u32[]{:S(2)}, u32[]{:S(2)}) collective-permute-start(bf16[2,256,256]{2,1,0:T(8,128)(2,1)S(1)} %collective-permute-done.3.refs_6_), channel_id=1, source_target_pairs={{0,32},{32,64},{64,96},{96,128},{128,160},{160,192},{192,224},{224... | collective-permute-start | bytes 786440 | tf_op jit(solution)/shard_map/ppermute | solution.py:229
  50.2 33.0 %all-to-all-start.1 = ((bf16[4,4,2,256,256]{4,3,2,1,0:T(8,128)(2,1)}), bf16[4,4,2,256,256]{4,3,2,1,0:T(8,128)(2,1)}, u32[]{:S(2)}, u32[]{:S(2)}) async-start(bf16[4,4,2,256,256]{4,3,2,1,0:T(8,128)(2,1)} %broadcast_in_dim.9), calls=%async_computation.1 | async-start | bytes 8388608 | tf_op jit(solution)/shard_map/all_to_all | solution.py:210
  55.1 19.4 %copy-start.13 = (bf16[2,256,256]{2,1,0:T(8,128)(2,1)}, bf16[2,256,256]{2,1,0:T(8,128)(2,1)S(1)}, u32[]{:S(2)}) copy-start(bf16[2,256,256]{2,1,0:T(8,128)(2,1)S(1)} %collective-permute-done.11.refs_9_) | copy-start | bytes 786436
  55.1 7.5 %collective-permute-start.12 = (bf16[2,256,256]{2,1,0:T(8,128)(2,1)S(1)}, bf16[2,256,256]{2,1,0:T(8,128)(2,1)S(1)}, u32[]{:S(2)}, u32[]{:S(2)}) collective-permute-start(bf16[2,256,256]{2,1,0:T(8,128)(2,1)S(1)} %collective-permute-done.11.refs_9_), channel_id=1, source_target_pairs={{0,32},{32,64},{64,96},{96,128},{128,160},{160,192},{192,224},{224... | collective-permute-start | bytes 786440 | tf_op jit(solution)/shard_map/ppermute | solution.py:229
  57.1 8.7 %collective-permute-start.5 = (bf16[2,256,256]{2,1,0:T(8,128)(2,1)}, bf16[2,256,256]{2,1,0:T(8,128)(2,1)S(1)}, u32[]{:S(2)}, u32[]{:S(2)}) collective-permute-start(bf16[2,256,256]{2,1,0:T(8,128)(2,1)} %collective-permute-done.4.refs_8_), channel_id=1, source_target_pairs={{0,32},{32,64},{64,96},{96,128},{128,160},{160,192},{192,224},{224... | collective-permute-start | bytes 786440 | tf_op jit(solution)/shard_map/ppermute | solution.py:229
  62.6 11.9 %copy-start.14 = (bf16[2,256,256]{2,1,0:T(8,128)(2,1)}, bf16[2,256,256]{2,1,0:T(8,128)(2,1)S(1)}, u32[]{:S(2)}) copy-start(bf16[2,256,256]{2,1,0:T(8,128)(2,1)S(1)} %collective-permute-done.12.refs_11_) | copy-start | bytes 786436
  62.6 7.5 %collective-permute-start.13 = (bf16[2,256,256]{2,1,0:T(8,128)(2,1)S(1)}, bf16[2,256,256]{2,1,0:T(8,128)(2,1)S(1)}, u32[]{:S(2)}, u32[]{:S(2)}) collective-permute-start(bf16[2,256,256]{2,1,0:T(8,128)(2,1)S(1)} %collective-permute-done.12.refs_11_), channel_id=1, source_target_pairs={{0,32},{32,64},{64,96},{96,128},{128,160},{160,192},{192,224},{224... | collective-permute-start | bytes 786440 | tf_op jit(solution)/shard_map/ppermute | solution.py:229
  65.8 8.8 %copy-start.15 = (bf16[2,256,256]{2,1,0:T(8,128)(2,1)}, bf16[2,256,256]{2,1,0:T(8,128)(2,1)S(1)}, u32[]{:S(2)}) copy-start(bf16[2,256,256]{2,1,0:T(8,128)(2,1)S(1)} %collective-permute-done.5.refs_10_) | copy-start | bytes 786436
  65.8 8.7 %collective-permute-start.6 = (bf16[2,256,256]{2,1,0:T(8,128)(2,1)S(1)}, bf16[2,256,256]{2,1,0:T(8,128)(2,1)S(1)}, u32[]{:S(2)}, u32[]{:S(2)}) collective-permute-start(bf16[2,256,256]{2,1,0:T(8,128)(2,1)S(1)} %collective-permute-done.5.refs_10_), channel_id=1, source_target_pairs={{0,32},{32,64},{64,96},{96,128},{128,160},{160,192},{192,224},{224... | collective-permute-start | bytes 786440 | tf_op jit(solution)/shard_map/ppermute | solution.py:229
  70.1 4.4 %copy-start.16 = (bf16[2,256,256]{2,1,0:T(8,128)(2,1)}, bf16[2,256,256]{2,1,0:T(8,128)(2,1)S(1)}, u32[]{:S(2)}) copy-start(bf16[2,256,256]{2,1,0:T(8,128)(2,1)S(1)} %collective-permute-done.13.refs_13_) | copy-start | bytes 786436
  70.1 7.6 %collective-permute-start.14 = (bf16[2,256,256]{2,1,0:T(8,128)(2,1)S(1)}, bf16[2,256,256]{2,1,0:T(8,128)(2,1)S(1)}, u32[]{:S(2)}, u32[]{:S(2)}) collective-permute-start(bf16[2,256,256]{2,1,0:T(8,128)(2,1)S(1)} %collective-permute-done.13.refs_13_), channel_id=1, source_target_pairs={{0,32},{32,64},{64,96},{96,128},{128,160},{160,192},{192,224},{224... | collective-permute-start | bytes 786440 | tf_op jit(solution)/shard_map/ppermute | solution.py:229
  74.5 8.7 %copy-start.3 = (bf16[2,256,256]{2,1,0:T(8,128)(2,1)}, bf16[2,256,256]{2,1,0:T(8,128)(2,1)S(1)}, u32[]{:S(2)}) copy-start(bf16[2,256,256]{2,1,0:T(8,128)(2,1)S(1)} %shard_map.29.refs_12_) | copy-start | bytes 786436
  74.6 12.6 %collective-permute-start.7 = (bf16[2,256,256]{2,1,0:T(8,128)(2,1)S(1)}, bf16[2,256,256]{2,1,0:T(8,128)(2,1)S(1)}, u32[]{:S(2)}, u32[]{:S(2)}) collective-permute-start(bf16[2,256,256]{2,1,0:T(8,128)(2,1)S(1)} %shard_map.29.refs_12_), channel_id=1, source_target_pairs={{0,32},{32,64},{64,96},{96,128},{128,160},{160,192},{192,224},{224... | collective-permute-start | bytes 786440 | tf_op jit(solution)/shard_map/ppermute | solution.py:229
  77.8 11.3 %collective-permute-start.16 = (bf16[2,256,256]{2,1,0:T(8,128)(2,1)S(1)}, bf16[2,256,256]{2,1,0:T(8,128)(2,1)S(1)}, u32[]{:S(2)}, u32[]{:S(2)}) collective-permute-start(bf16[2,256,256]{2,1,0:T(8,128)(2,1)S(1)} %collective-permute-done.14.refs_1_), channel_id=1, source_target_pairs={{16,496},{48,16},{80,48},{112,80},{144,112},{176,144},{208,176},{2... | collective-permute-start | bytes 786440 | tf_op jit(solution)/shard_map/ppermute | solution.py:229
  87.2 7.1 %collective-permute-start.15 = (bf16[2,256,256]{2,1,0:T(8,128)(2,1)S(1)}, bf16[2,256,256]{2,1,0:T(8,128)(2,1)S(1)}, u32[]{:S(2)}, u32[]{:S(2)}) collective-permute-start(bf16[2,256,256]{2,1,0:T(8,128)(2,1)S(1)} %shard_map.31.refs_0_), channel_id=1, source_target_pairs={{16,496},{48,16},{80,48},{112,80},{144,112},{176,144},{208,176},{2... | collective-permute-start | bytes 786440 | tf_op jit(solution)/shard_map/ppermute | solution.py:229
  96.0 4.0 %copy-start.5 = (s32[1,2]{1,0:T(1,128)S(1)}, s32[1,2]{1,0:T(1,128)}, u32[]{:S(2)}) copy-start(s32[1,2]{1,0:T(1,128)} %param.4) | copy-start | bytes 28
  96.0 23.0 %copy-start.2 = (bf16[1,2,256,256]{3,2,1,0:T(8,128)(2,1)S(1)}, bf16[1,2,256,256]{3,2,1,0:T(8,128)(2,1)}, u32[]{:S(2)}) copy-start(bf16[1,2,256,256]{3,2,1,0:T(8,128)(2,1)} %param.3) | copy-start | bytes 786436
  96.0 3.9 %collective-permute-start.17 = (f32[2,256,256]{2,1,0:T(8,128)S(1)}, f32[2,256,256]{2,1,0:T(8,128)S(1)}, u32[]{:S(2)}, u32[]{:S(2)}) collective-permute-start(f32[2,256,256]{2,1,0:T(8,128)S(1)} %shard_map.33), channel_id=1, source_target_pairs={{0,16},{16,0},{1,17},{17,1},{2,18},{18,2},{3,19},{19,3},{4,20},{20... | collective-permute-start | bytes 1572872 | tf_op jit(solution)/shard_map/ppermute | solution.py:233

commit v7 on v6

--- a/solution.py
+++ b/solution.py
@@ -15,8 +15,9 @@
 HBM = pl.BlockSpec(memory_space=pltpu.HBM)
 MIB = 1024 * 1024
 SWAP = [(0, 1), (1, 0)]
-SETTLE = 7
-FLOPS = 26 * 10**9
+SETTLE = 8
+CHAIN = 1
+FLOPS = 23 * 10**9
 
 
 def params(mib):
@@ -107,7 +108,8 @@
     width = left.shape[-1]
     tiles = [tile for distance, _ in planes for tile in held[distance]]
     if totals is None:
-        tiles = [pltpu.with_memory_space_constraint(tile, pltpu.HBM) for tile in tiles]
+        early = [pltpu.with_memory_space_constraint(tile, pltpu.HBM) for tile in tiles[:-2]]
+        tiles = early + tiles[-2:]
     given = [] if totals is None else [totals[row] for row in rows]
     kernel = functools.partial(product_kernel, planes, rows, groups)
     out = pl.pallas_call(
@@ -156,16 +158,16 @@
             out_ref[slot] = jnp.zeros_like(tile)
 
 
-def settle(value, *after, flops=0):
+def settle(value, flops):
     return pl.pallas_call(
         settle_kernel,
-        in_specs=[ANY] * (1 + len(after)),
+        in_specs=[ANY],
         out_specs=ANY,
         out_shape=jax.ShapeDtypeStruct(value.shape, value.dtype),
         input_output_aliases={0: 0},
         compiler_params=params(1),
         cost_estimate=pl.CostEstimate(flops=flops, bytes_accessed=0, transcendentals=0),
-    )(value, *after)
+    )(value)
 
 
 def on_device(flow_tiles, tile_cols, pairs):
@@ -215,23 +217,20 @@
     left = copy_for_each(copy_for_each(sent, lines_of(0)), lines_of(1))
 
     held = [(mine, other)]
-    totals = None
     for step in range(1, half + 1):
         if step == SETTLE:
-            held[-1] = (settle(held[-1][0], flops=FLOPS), held[-1][1])
-        if step == half:
-            early = [(0, 0)] + [(i, None) for i in range(1, half - 1)]
-            totals = products(
-                None, (0, 1), plane_ref, core_ref, left, held, early, [[1, 2], [3, 4], [5, 6], [0]]
-            )
-            held[-1] = (settle(held[-1][0], *totals.values()), held[-1][1])
+            moved = list(held[-1])
+            moved[CHAIN] = settle(moved[CHAIN], flops=FLOPS)
+            held[-1] = tuple(moved)
         perm = ring + back if step < half else back
         held.append(tuple(lax.ppermute(t, ROWS, perm) for t in held[-1]))
     known = (plane_ref, core_ref, left, held)
-    late = [(half - 1, None), (half, 1)]
-    outward = products(totals, (1,), *known, late, [[0], [1]])[1]
+    early = [(0, 0)] + [(i, None) for i in range(1, half)]
+    totals = products(None, (0, 1), *known, early, [[1, 2], [3, 4], [5, 6], [7], [0]])
+    late = [(half, 1)]
+    outward = products(totals, (1,), *known, late, [[0]])[1]
     received = lax.ppermute(outward, "core", SWAP)
-    total = products(totals, (0,), *known, late, [[0], [1]])[0]
+    total = products(totals, (0,), *known, late, [[0]])[0]
     inflated, sums = pl.pallas_call(
         functools.partial(square_kernel, columns),
         in_specs=[SMEM, SMEM, VMEM, VMEM],

time: 122 us -> 121 us (level)
  waiting for transfers between devices: 13.8 us -> 9.26 us
  blocking collectives: 18.4 us -> 21.6 us
    ppermute x16, waiting for transfers between devices: 13.6 us -> 8.72 us  [on_device(): held.append(tuple((lax.ppermute(t, ROWS, perm) for t in held[-1])))]
    all_to_all x1, blocking collectives: 16.6 us -> 19.8 us  [on_device(): lax.all_to_all(jnp.broadcast_to(sums[None], (planes, *sums.shape)), 'z',...]
where the time goes in v7:
time: 121 us; the launch traced here: 119 us
  starting transfers between devices  72.5 us (60%)
  blocking collectives  21.6 us (18%)
  Pallas kernels  9.76 us (8%)
  waiting for transfers between devices  9.26 us (8%)
  local copies, waits for them, and re-layouts  5.22 us (4%)
    ppermute x16, starting transfers between devices, on_device(): held.append(tuple((lax.ppermute(t, ROWS, perm) for t in held[-1])))  52.7 us
    all_to_all x1, blocking collectives, on_device(): lax.all_to_all(jnp.broadcast_to(sums[None], (planes, *sums.shape)), 'z',...  19.8 us
    all_to_all x2, starting transfers between devices, copy_for_each(): lax.all_to_all(spread, ('core', *COLS), 0, 0, axis_index_groups=lines, ti...  9.03 us
    ppermute x1, starting transfers between devices, on_device(): other = lax.ppermute(mine, 'core', SWAP)  8.79 us
    ppermute x16, waiting for transfers between devices, on_device(): held.append(tuple((lax.ppermute(t, ROWS, perm) for t in held[-1])))  8.72 us
    pallas_call x3, Pallas kernels, products(): pl.pallas_call(kernel, in_specs=[SMEM, SMEM, HBM] + [HBM] * len(tiles) +...  7 us
    broadcast_in_dim x2, local copies, waits for them, and re-layouts, copy_for_each(): spread = jnp.broadcast_to(value[None], (len(lines[0]), *value.shape))  3.53 us
  transfers between devices with their start and end apart: 20, of which 7 were waited for; matrix products, arithmetic and copies ran while one was open for 3% of the time, Pallas kernels for 5%

profile of v7, /device:TPU:1, one launch (start us, length us, event | category | flops | bytes accessed | tf_op | source)
XLA Modules:
  0.0 118.9 jit_solution(334989049988477148)
XLA Ops:
  0.0 0.9 copy-done.1
  1.0 0.7 copy-done.3
  1.6 0.6 shard_map.28.refs_0_
  2.3 0.0 copy-start
  2.3 8.8 %collective-permute-start = (bf16[2,256,256]{2,1,0:T(8,128)(2,1)S(1)}, bf16[2,256,256]{2,1,0:T(8,128)(2,1)S(1)}, u32[]{:S(2)}, u32[]{:S(2)}) collective-permute-start(bf16[2,256,256]{2,1,0:T(8,128)(2,1)S(1)} %shard_map.28.refs_0_), channel_id=1, source_target_pairs={{0,16},{16,0},{1,17},{17,1},{2,18},{18,2},{3,19},{19,3},{4,20},{20... | collective-permute-start | bytes 786440 | tf_op jit(solution)/shard_map/ppermute | solution.py:190
  11.1 5.7 %collective-permute-start.1 = (bf16[2,256,256]{2,1,0:T(8,128)(2,1)S(1)}, bf16[2,256,256]{2,1,0:T(8,128)(2,1)S(1)}, u32[]{:S(2)}, u32[]{:S(2)}) collective-permute-start(bf16[2,256,256]{2,1,0:T(8,128)(2,1)S(1)} %shard_map.28.refs_0_), channel_id=1, source_target_pairs={{0,32},{32,64},{64,96},{96,128},{128,160},{160,192},{192,224},{224... | collective-permute-start | bytes 786440 | tf_op jit(solution)/shard_map/ppermute | solution.py:226
  16.9 0.0 collective-permute-done.refs_1_
  16.9 0.0 copy-start.5
  16.9 2.6 %collective-permute-start.9 = (bf16[2,256,256]{2,1,0:T(8,128)(2,1)S(1)}, bf16[2,256,256]{2,1,0:T(8,128)(2,1)S(1)}, u32[]{:S(2)}, u32[]{:S(2)}) collective-permute-start(bf16[2,256,256]{2,1,0:T(8,128)(2,1)S(1)} %collective-permute-done.refs_1_), channel_id=1, source_target_pairs={{0,32},{32,64},{64,96},{96,128},{128,160},{160,192},{192,224},{224... | collective-permute-start | bytes 786440 | tf_op jit(solution)/shard_map/ppermute | solution.py:226
  19.6 1.0 broadcast_in_dim.8
  20.6 4.2 %all-to-all-start = ((bf16[4,2,256,256]{3,2,1,0:T(8,128)(2,1)}), bf16[4,2,256,256]{3,2,1,0:T(8,128)(2,1)S(1)}, u32[]{:S(2)}, u32[]{:S(2)}) async-start(bf16[4,2,256,256]{3,2,1,0:T(8,128)(2,1)} %broadcast_in_dim.8), calls=%async_computation | async-start | bytes 2097152 | tf_op jit(solution)/shard_map/all_to_all | solution.py:212
  24.8 0.0 collective-permute-done.1.refs_2_
  24.8 2.6 %collective-permute-start.2 = (bf16[2,256,256]{2,1,0:T(8,128)(2,1)S(1)}, bf16[2,256,256]{2,1,0:T(8,128)(2,1)S(1)}, u32[]{:S(2)}, u32[]{:S(2)}) collective-permute-start(bf16[2,256,256]{2,1,0:T(8,128)(2,1)S(1)} %collective-permute-done.1.refs_2_), channel_id=1, source_target_pairs={{0,32},{32,64},{64,96},{96,128},{128,160},{160,192},{192,224},{224... | collective-permute-start | bytes 786440 | tf_op jit(solution)/shard_map/ppermute | solution.py:226
  27.5 0.0 collective-permute-done.9.refs_3_
  27.5 0.0 copy-start.7
  27.5 2.6 %collective-permute-start.10 = (bf16[2,256,256]{2,1,0:T(8,128)(2,1)S(1)}, bf16[2,256,256]{2,1,0:T(8,128)(2,1)S(1)}, u32[]{:S(2)}, u32[]{:S(2)}) collective-permute-start(bf16[2,256,256]{2,1,0:T(8,128)(2,1)S(1)} %collective-permute-done.9.refs_3_), channel_id=1, source_target_pairs={{0,32},{32,64},{64,96},{96,128},{128,160},{160,192},{192,224},{224... | collective-permute-start | bytes 786440 | tf_op jit(solution)/shard_map/ppermute | solution.py:226
  30.1 2.1 %collective-permute-done.2.refs_4_ = bf16[2,256,256]{2,1,0:T(8,128)(2,1)S(1)} collective-permute-done((bf16[2,256,256]{2,1,0:T(8,128)(2,1)S(1)}, bf16[2,256,256]{2,1,0:T(8,128)(2,1)S(1)}, u32[]{:S(2)}, u32[]{:S(2)}) %collective-permute-start.2) | collective-permute-done | bytes 262176 | tf_op jit(solution)/shard_map/ppermute | solution.py:226
  32.2 3.8 %collective-permute-start.3 = (bf16[2,256,256]{2,1,0:T(8,128)(2,1)S(1)}, bf16[2,256,256]{2,1,0:T(8,128)(2,1)S(1)}, u32[]{:S(2)}, u32[]{:S(2)}) collective-permute-start(bf16[2,256,256]{2,1,0:T(8,128)(2,1)S(1)} %collective-permute-done.2.refs_4_), channel_id=1, source_target_pairs={{0,32},{32,64},{64,96},{96,128},{128,160},{160,192},{192,224},{224... | collective-permute-start | bytes 786440 | tf_op jit(solution)/shard_map/ppermute | solution.py:226
  36.1 0.0 collective-permute-done.10.refs_5_
  36.1 0.0 copy-start.9
  36.1 2.5 %collective-permute-start.11 = (bf16[2,256,256]{2,1,0:T(8,128)(2,1)S(1)}, bf16[2,256,256]{2,1,0:T(8,128)(2,1)S(1)}, u32[]{:S(2)}, u32[]{:S(2)}) collective-permute-start(bf16[2,256,256]{2,1,0:T(8,128)(2,1)S(1)} %collective-permute-done.10.refs_5_), channel_id=1, source_target_pairs={{0,32},{32,64},{64,96},{96,128},{128,160},{160,192},{192,224},{224... | collective-permute-start | bytes 786440 | tf_op jit(solution)/shard_map/ppermute | solution.py:226
  38.6 1.0 collective-permute-done.3.refs_6_
  39.6 4.8 %collective-permute-start.4 = (bf16[2,256,256]{2,1,0:T(8,128)(2,1)S(1)}, bf16[2,256,256]{2,1,0:T(8,128)(2,1)S(1)}, u32[]{:S(2)}, u32[]{:S(2)}) collective-permute-start(bf16[2,256,256]{2,1,0:T(8,128)(2,1)S(1)} %collective-permute-done.3.refs_6_), channel_id=1, source_target_pairs={{0,32},{32,64},{64,96},{96,128},{128,160},{160,192},{192,224},{224... | collective-permute-start | bytes 786440 | tf_op jit(solution)/shard_map/ppermute | solution.py:226
  44.4 0.0 collective-permute-done.11.refs_7_
  44.4 0.0 copy-start.11
  44.4 2.8 %collective-permute-start.12 = (bf16[2,256,256]{2,1,0:T(8,128)(2,1)S(1)}, bf16[2,256,256]{2,1,0:T(8,128)(2,1)}, u32[]{:S(2)}, u32[]{:S(2)}) collective-permute-start(bf16[2,256,256]{2,1,0:T(8,128)(2,1)S(1)} %collective-permute-done.11.refs_7_), channel_id=1, source_target_pairs={{0,32},{32,64},{64,96},{96,128},{128,160},{160,192},{192,224},{224... | collective-permute-start | bytes 786440 | tf_op jit(solution)/shard_map/ppermute | solution.py:226
  47.2 0.0 all-to-all-done
  47.2 2.5 %broadcast_in_dim.9 = bf16[4,4,2,256,256]{4,3,2,1,0:T(8,128)(2,1)} broadcast(bf16[4,2,256,256]{3,2,1,0:T(8,128)(2,1)S(1)} %all-to-all-done), dimensions={1,2,3,4} | broadcast | bytes 5242880 | tf_op jit(solution)/shard_map/broadcast_in_dim | solution.py:211
  49.7 0.0 copy-done
  49.7 0.0 copy-done.5
  49.7 0.0 copy-done.6
  49.7 0.0 copy-done.7
  49.8 4.8 %all-to-all-start.1 = ((bf16[4,4,2,256,256]{4,3,2,1,0:T(8,128)(2,1)}), bf16[4,4,2,256,256]{4,3,2,1,0:T(8,128)(2,1)}, u32[]{:S(2)}, u32[]{:S(2)}) async-start(bf16[4,4,2,256,256]{4,3,2,1,0:T(8,128)(2,1)} %broadcast_in_dim.9), calls=%async_computation.1 | async-start | bytes 8388608 | tf_op jit(solution)/shard_map/all_to_all | solution.py:212
  54.6 0.0 collective-permute-done.4.refs_8_
  54.6 1.9 %collective-permute-start.5 = (bf16[2,256,256]{2,1,0:T(8,128)(2,1)S(1)}, bf16[2,256,256]{2,1,0:T(8,128)(2,1)S(1)}, u32[]{:S(2)}, u32[]{:S(2)}) collective-permute-start(bf16[2,256,256]{2,1,0:T(8,128)(2,1)S(1)} %collective-permute-done.4.refs_8_), channel_id=1, source_target_pairs={{0,32},{32,64},{64,96},{96,128},{128,160},{160,192},{192,224},{224... | collective-permute-start | bytes 786440 | tf_op jit(solution)/shard_map/ppermute | solution.py:226
  56.6 0.0 collective-permute-done.12.refs_9_
  56.6 2.4 %collective-permute-start.13 = (bf16[2,256,256]{2,1,0:T(8,128)(2,1)}, bf16[2,256,256]{2,1,0:T(8,128)(2,1)S(1)}, u32[]{:S(2)}, u32[]{:S(2)}) collective-permute-start(bf16[2,256,256]{2,1,0:T(8,128)(2,1)} %collective-permute-done.12.refs_9_), channel_id=1, source_target_pairs={{0,32},{32,64},{64,96},{96,128},{128,160},{160,192},{192,224},{224... | collective-permute-start | bytes 786440 | tf_op jit(solution)/shard_map/ppermute | solution.py:226
  59.0 3.1 %collective-permute-done.5.refs_10_ = bf16[2,256,256]{2,1,0:T(8,128)(2,1)S(1)} collective-permute-done((bf16[2,256,256]{2,1,0:T(8,128)(2,1)S(1)}, bf16[2,256,256]{2,1,0:T(8,128)(2,1)S(1)}, u32[]{:S(2)}, u32[]{:S(2)}) %collective-permute-start.5) | collective-permute-done | bytes 262176 | tf_op jit(solution)/shard_map/ppermute | solution.py:226
  62.2 3.1 %collective-permute-start.6 = (bf16[2,256,256]{2,1,0:T(8,128)(2,1)S(1)}, bf16[2,256,256]{2,1,0:T(8,128)(2,1)S(1)}, u32[]{:S(2)}, u32[]{:S(2)}) collective-permute-start(bf16[2,256,256]{2,1,0:T(8,128)(2,1)S(1)} %collective-permute-done.5.refs_10_), channel_id=1, source_target_pairs={{0,32},{32,64},{64,96},{96,128},{128,160},{160,192},{192,224},{224... | collective-permute-start | bytes 786440 | tf_op jit(solution)/shard_map/ppermute | solution.py:226
  65.3 0.0 collective-permute-done.13.refs_11_
  65.3 2.8 %collective-permute-start.14 = (bf16[2,256,256]{2,1,0:T(8,128)(2,1)S(1)}, bf16[2,256,256]{2,1,0:T(8,128)(2,1)S(1)}, u32[]{:S(2)}, u32[]{:S(2)}) collective-permute-start(bf16[2,256,256]{2,1,0:T(8,128)(2,1)S(1)} %collective-permute-done.13.refs_11_), channel_id=1, source_target_pairs={{0,32},{32,64},{64,96},{96,128},{128,160},{160,192},{192,224},{224... | collective-permute-start | bytes 786440 | tf_op jit(solution)/shard_map/ppermute | solution.py:226
  68.1 1.6 %collective-permute-done.6.refs_12_ = bf16[2,256,256]{2,1,0:T(8,128)(2,1)S(1)} collective-permute-done((bf16[2,256,256]{2,1,0:T(8,128)(2,1)S(1)}, bf16[2,256,256]{2,1,0:T(8,128)(2,1)S(1)}, u32[]{:S(2)}, u32[]{:S(2)}) %collective-permute-start.6) | collective-permute-done | bytes 262176 | tf_op jit(solution)/shard_map/ppermute | solution.py:226
  69.7 4.3 %collective-permute-start.7 = (bf16[2,256,256]{2,1,0:T(8,128)(2,1)S(1)}, bf16[2,256,256]{2,1,0:T(8,128)(2,1)S(1)}, u32[]{:S(2)}, u32[]{:S(2)}) collective-permute-start(bf16[2,256,256]{2,1,0:T(8,128)(2,1)S(1)} %collective-permute-done.6.refs_12_), channel_id=1, source_target_pairs={{0,32},{32,64},{64,96},{96,128},{128,160},{160,192},{192,224},{224... | collective-permute-start | bytes 786440 | tf_op jit(solution)/shard_map/ppermute | solution.py:226
  74.0 0.0 collective-permute-done.14.refs_13_
  74.0 2.8 %collective-permute-start.15 = (bf16[2,256,256]{2,1,0:T(8,128)(2,1)S(1)}, bf16[2,256,256]{2,1,0:T(8,128)(2,1)S(1)}, u32[]{:S(2)}, u32[]{:S(2)}) collective-permute-start(bf16[2,256,256]{2,1,0:T(8,128)(2,1)S(1)} %collective-permute-done.14.refs_13_), channel_id=1, source_target_pairs={{0,32},{32,64},{64,96},{96,128},{128,160},{160,192},{192,224},{224... | collective-permute-start | bytes 786440 | tf_op jit(solution)/shard_map/ppermute | solution.py:226
  76.8 0.5 collective-permute-done.7.refs_14_
  77.3 5.4 %collective-permute-start.8 = (bf16[2,256,256]{2,1,0:T(8,128)(2,1)S(1)}, bf16[2,256,256]{2,1,0:T(8,128)(2,1)S(1)}, u32[]{:S(2)}, u32[]{:S(2)}) collective-permute-start(bf16[2,256,256]{2,1,0:T(8,128)(2,1)S(1)} %collective-permute-done.7.refs_14_), channel_id=1, source_target_pairs={{16,496},{48,16},{80,48},{112,80},{144,112},{176,144},{208,176},{2... | collective-permute-start | bytes 786440 | tf_op jit(solution)/shard_map/ppermute | solution.py:226
  82.7 0.0 collective-permute-done.15.refs_0_
  82.8 2.4 %collective-permute-start.16 = (bf16[2,256,256]{2,1,0:T(8,128)(2,1)S(1)}, bf16[2,256,256]{2,1,0:T(8,128)(2,1)S(1)}, u32[]{:S(2)}, u32[]{:S(2)}) collective-permute-start(bf16[2,256,256]{2,1,0:T(8,128)(2,1)S(1)} %shard_map.29.refs_15_), channel_id=1, source_target_pairs={{16,496},{48,16},{80,48},{112,80},{144,112},{176,144},{208,176},{2... | collective-permute-start | bytes 786440 | tf_op jit(solution)/shard_map/ppermute | solution.py:226
  85.2 0.0 all-to-all-done.1.left_ref
  85.2 4.3 %shard_map.30 = (f32[2,256,256]{2,1,0:T(8,128)S(1)}, f32[2,256,256]{2,1,0:T(8,128)S(1)}) custom-call(s32[1]{0:T(128)} %bitcast.3.plane_ref, s32[1]{0:T(128)} %bitcast.4.core_ref, bf16[4,4,2,256,256]{4,3,2,1,0:T(8,128)(2,1)} %all-to-all-done.1.left_ref, bf16[2,256,256]{2,1,0:T(8,128)(2,1)} %copy-done, bf16[2,256,256]{2,1,0:T(8,128)(2,1)} %copy-done.5, ...), custom_call_target="tpu_custom_call" | custom-call | flops 2147483648 | bytes 16777216 | tf_op jit(solution)/shard_map/pallas_call | solution.py:115
  89.5 0.0 collective-permute-done.8.refs_0_
  89.5 0.4 collective-permute-done.16.refs_1_
  89.9 1.3 %shard_map.32 = f32[2,256,256]{2,1,0:T(8,128)S(1)} custom-call(s32[1]{0:T(128)} %bitcast.3.plane_ref, s32[1]{0:T(128)} %bitcast.4.core_ref, bf16[4,4,2,256,256]{4,3,2,1,0:T(8,128)(2,1)} %all-to-all-done.1.left_ref, bf16[2,256,256]{2,1,0:T(8,128)(2,1)S(1)} %collective-permute-done.8.refs_0_, ...), custom_call_target="tpu_custom_call", output_to_operand_aliasing={{}: (5, {})} | custom-call | flops 134217728 | bytes 1572864 | tf_op jit(solution)/shard_map/pallas_call | solution.py:115
  91.2 0.0 copy-start.4
  91.2 0.0 copy-start.2
  91.2 2.1 %collective-permute-start.17 = (f32[2,256,256]{2,1,0:T(8,128)S(1)}, f32[2,256,256]{2,1,0:T(8,128)S(1)}, u32[]{:S(2)}, u32[]{:S(2)}) collective-permute-start(f32[2,256,256]{2,1,0:T(8,128)S(1)} %shard_map.32), channel_id=1, source_target_pairs={{0,16},{16,0},{1,17},{17,1},{2,18},{18,2},{3,19},{19,3},{4,20},{20... | collective-permute-start | bytes 1572872 | tf_op jit(solution)/shard_map/ppermute | solution.py:232
  93.3 1.3 %shard_map.31.mine_ref = f32[2,256,256]{2,1,0:T(8,128)S(1)} custom-call(s32[1]{0:T(128)} %bitcast.3.plane_ref, s32[1]{0:T(128)} %bitcast.4.core_ref, bf16[4,4,2,256,256]{4,3,2,1,0:T(8,128)(2,1)} %all-to-all-done.1.left_ref, bf16[2,256,256]{2,1,0:T(8,128)(2,1)S(1)} %collective-permute-done.8.refs_0_, ...), custom_call_target="tpu_custom_call", output_to_operand_aliasing={{}: (5, {})} | custom-call | flops 134217728 | bytes 1572864 | tf_op jit(solution)/shard_map/pallas_call | solution.py:115
  94.7 0.5 collective-permute-done.17.other_ref
  95.2 0.0 copy-done.4
  95.2 0.6 shard_map.33
  95.8 1.8 %all-gather.1 = f32[2,2,256]{2,1,0:T(2,128)S(1)} all-gather(f32[1,2,256]{2,1,0:T(2,128)S(1)} %bitcast.12), channel_id=2, replica_groups=mesh['z'=16,'core'=2,'y'=4,'x'=4] {'core'}, dimensions={0}, use_global_device_ids=true | all-gather | bytes 6144 | tf_op jit(solution)/shard_map/all_gather | solution.py:244
  97.6 19.8 %all_to_all.15.parts_ref = f32[16,2,256]{2,1,0:T(2,128)S(1)} all-to-all(f32[16,2,256]{2,1,0:T(2,128)S(1)} %broadcast_in_dim.10), channel_id=1, replica_groups=mesh['z'=16,'core'=2,'y'=4,'x'=4] {'z'}, dimensions={0} | all-to-all | bytes 65536 | tf_op jit(solution)/shard_map/all_to_all | solution.py:245
  117.4 1.5 %shard_map.34 = f32[2,256,256]{2,1,0:T(8,128)} custom-call(s32[2]{0:T(128)S(1)} %bitcast.11, s32[1]{0:T(128)} %bitcast.1.column_ref, bf16[2,256,256]{2,1,0:T(8,128)(2,1)S(1)} %bitcast.8, f32[2,256,256]{2,1,0:T(8,128)S(1)} %get-tuple-element.11.inflated_ref, f32[16,2,256]{2,1,0:T(2,128)S(1)} %all_to_all.15.parts_ref), custom_call_target="tpu_custom_call" | custom-call | tf_op jit(solution)/shard_map/pallas_call | solution.py:249
  (26 shorter events, 0.1 us)
Async XLA Ops:
  0.0 0.9 copy-start.1
  1.0 0.7 copy-start.3
  2.3 47.5 %copy-start = (bf16[2,256,256]{2,1,0:T(8,128)(2,1)}, bf16[2,256,256]{2,1,0:T(8,128)(2,1)S(1)}, u32[]{:S(2)}) copy-start(bf16[2,256,256]{2,1,0:T(8,128)(2,1)S(1)} %shard_map.28.refs_0_) | copy-start | bytes 786436
  2.3 14.6 %collective-permute-start = (bf16[2,256,256]{2,1,0:T(8,128)(2,1)S(1)}, bf16[2,256,256]{2,1,0:T(8,128)(2,1)S(1)}, u32[]{:S(2)}, u32[]{:S(2)}) collective-permute-start(bf16[2,256,256]{2,1,0:T(8,128)(2,1)S(1)} %shard_map.28.refs_0_), channel_id=1, source_target_pairs={{0,16},{16,0},{1,17},{17,1},{2,18},{18,2},{3,19},{19,3},{4,20},{20... | collective-permute-start | bytes 786440 | tf_op jit(solution)/shard_map/ppermute | solution.py:190
  11.1 13.8 %collective-permute-start.1 = (bf16[2,256,256]{2,1,0:T(8,128)(2,1)S(1)}, bf16[2,256,256]{2,1,0:T(8,128)(2,1)S(1)}, u32[]{:S(2)}, u32[]{:S(2)}) collective-permute-start(bf16[2,256,256]{2,1,0:T(8,128)(2,1)S(1)} %shard_map.28.refs_0_), channel_id=1, source_target_pairs={{0,32},{32,64},{64,96},{96,128},{128,160},{160,192},{192,224},{224... | collective-permute-start | bytes 786440 | tf_op jit(solution)/shard_map/ppermute | solution.py:226
  16.9 32.8 %copy-start.5 = (bf16[2,256,256]{2,1,0:T(8,128)(2,1)}, bf16[2,256,256]{2,1,0:T(8,128)(2,1)S(1)}, u32[]{:S(2)}) copy-start(bf16[2,256,256]{2,1,0:T(8,128)(2,1)S(1)} %collective-permute-done.refs_1_) | copy-start | bytes 786436
  16.9 10.6 %collective-permute-start.9 = (bf16[2,256,256]{2,1,0:T(8,128)(2,1)S(1)}, bf16[2,256,256]{2,1,0:T(8,128)(2,1)S(1)}, u32[]{:S(2)}, u32[]{:S(2)}) collective-permute-start(bf16[2,256,256]{2,1,0:T(8,128)(2,1)S(1)} %collective-permute-done.refs_1_), channel_id=1, source_target_pairs={{0,32},{32,64},{64,96},{96,128},{128,160},{160,192},{192,224},{224... | collective-permute-start | bytes 786440 | tf_op jit(solution)/shard_map/ppermute | solution.py:226
  20.6 26.6 %all-to-all-start = ((bf16[4,2,256,256]{3,2,1,0:T(8,128)(2,1)}), bf16[4,2,256,256]{3,2,1,0:T(8,128)(2,1)S(1)}, u32[]{:S(2)}, u32[]{:S(2)}) async-start(bf16[4,2,256,256]{3,2,1,0:T(8,128)(2,1)} %broadcast_in_dim.8), calls=%async_computation | async-start | bytes 2097152 | tf_op jit(solution)/shard_map/all_to_all | solution.py:212
  24.8 24.9 %copy-start.6 = (bf16[2,256,256]{2,1,0:T(8,128)(2,1)}, bf16[2,256,256]{2,1,0:T(8,128)(2,1)S(1)}, u32[]{:S(2)}) copy-start(bf16[2,256,256]{2,1,0:T(8,128)(2,1)S(1)} %collective-permute-done.1.refs_2_) | copy-start | bytes 786436
  24.8 7.4 %collective-permute-start.2 = (bf16[2,256,256]{2,1,0:T(8,128)(2,1)S(1)}, bf16[2,256,256]{2,1,0:T(8,128)(2,1)S(1)}, u32[]{:S(2)}, u32[]{:S(2)}) collective-permute-start(bf16[2,256,256]{2,1,0:T(8,128)(2,1)S(1)} %collective-permute-done.1.refs_2_), channel_id=1, source_target_pairs={{0,32},{32,64},{64,96},{96,128},{128,160},{160,192},{192,224},{224... | collective-permute-start | bytes 786440 | tf_op jit(solution)/shard_map/ppermute | solution.py:226
  27.5 22.2 %copy-start.7 = (bf16[2,256,256]{2,1,0:T(8,128)(2,1)}, bf16[2,256,256]{2,1,0:T(8,128)(2,1)S(1)}, u32[]{:S(2)}) copy-start(bf16[2,256,256]{2,1,0:T(8,128)(2,1)S(1)} %collective-permute-done.9.refs_3_) | copy-start | bytes 786436
  27.5 8.6 %collective-permute-start.10 = (bf16[2,256,256]{2,1,0:T(8,128)(2,1)S(1)}, bf16[2,256,256]{2,1,0:T(8,128)(2,1)S(1)}, u32[]{:S(2)}, u32[]{:S(2)}) collective-permute-start(bf16[2,256,256]{2,1,0:T(8,128)(2,1)S(1)} %collective-permute-done.9.refs_3_), channel_id=1, source_target_pairs={{0,32},{32,64},{64,96},{96,128},{128,160},{160,192},{192,224},{224... | collective-permute-start | bytes 786440 | tf_op jit(solution)/shard_map/ppermute | solution.py:226
  32.2 17.5 %copy-start.8 = (bf16[2,256,256]{2,1,0:T(8,128)(2,1)}, bf16[2,256,256]{2,1,0:T(8,128)(2,1)S(1)}, u32[]{:S(2)}) copy-start(bf16[2,256,256]{2,1,0:T(8,128)(2,1)S(1)} %collective-permute-done.2.refs_4_) | copy-start | bytes 786436
  32.2 7.4 %collective-permute-start.3 = (bf16[2,256,256]{2,1,0:T(8,128)(2,1)S(1)}, bf16[2,256,256]{2,1,0:T(8,128)(2,1)S(1)}, u32[]{:S(2)}, u32[]{:S(2)}) collective-permute-start(bf16[2,256,256]{2,1,0:T(8,128)(2,1)S(1)} %collective-permute-done.2.refs_4_), channel_id=1, source_target_pairs={{0,32},{32,64},{64,96},{96,128},{128,160},{160,192},{192,224},{224... | collective-permute-start | bytes 786440 | tf_op jit(solution)/shard_map/ppermute | solution.py:226
  36.1 13.6 %copy-start.9 = (bf16[2,256,256]{2,1,0:T(8,128)(2,1)}, bf16[2,256,256]{2,1,0:T(8,128)(2,1)S(1)}, u32[]{:S(2)}) copy-start(bf16[2,256,256]{2,1,0:T(8,128)(2,1)S(1)} %collective-permute-done.10.refs_5_) | copy-start | bytes 786436
  36.1 8.3 %collective-permute-start.11 = (bf16[2,256,256]{2,1,0:T(8,128)(2,1)S(1)}, bf16[2,256,256]{2,1,0:T(8,128)(2,1)S(1)}, u32[]{:S(2)}, u32[]{:S(2)}) collective-permute-start(bf16[2,256,256]{2,1,0:T(8,128)(2,1)S(1)} %collective-permute-done.10.refs_5_), channel_id=1, source_target_pairs={{0,32},{32,64},{64,96},{96,128},{128,160},{160,192},{192,224},{224... | collective-permute-start | bytes 786440 | tf_op jit(solution)/shard_map/ppermute | solution.py:226
  39.6 10.1 %copy-start.10 = (bf16[2,256,256]{2,1,0:T(8,128)(2,1)}, bf16[2,256,256]{2,1,0:T(8,128)(2,1)S(1)}, u32[]{:S(2)}) copy-start(bf16[2,256,256]{2,1,0:T(8,128)(2,1)S(1)} %collective-permute-done.3.refs_6_) | copy-start | bytes 786436
  39.6 15.0 %collective-permute-start.4 = (bf16[2,256,256]{2,1,0:T(8,128)(2,1)S(1)}, bf16[2,256,256]{2,1,0:T(8,128)(2,1)S(1)}, u32[]{:S(2)}, u32[]{:S(2)}) collective-permute-start(bf16[2,256,256]{2,1,0:T(8,128)(2,1)S(1)} %collective-permute-done.3.refs_6_), channel_id=1, source_target_pairs={{0,32},{32,64},{64,96},{96,128},{128,160},{160,192},{192,224},{224... | collective-permute-start | bytes 786440 | tf_op jit(solution)/shard_map/ppermute | solution.py:226
  44.4 5.4 %copy-start.11 = (bf16[2,256,256]{2,1,0:T(8,128)(2,1)}, bf16[2,256,256]{2,1,0:T(8,128)(2,1)S(1)}, u32[]{:S(2)}) copy-start(bf16[2,256,256]{2,1,0:T(8,128)(2,1)S(1)} %collective-permute-done.11.refs_7_) | copy-start | bytes 786436
  44.4 12.2 %collective-permute-start.12 = (bf16[2,256,256]{2,1,0:T(8,128)(2,1)S(1)}, bf16[2,256,256]{2,1,0:T(8,128)(2,1)}, u32[]{:S(2)}, u32[]{:S(2)}) collective-permute-start(bf16[2,256,256]{2,1,0:T(8,128)(2,1)S(1)} %collective-permute-done.11.refs_7_), channel_id=1, source_target_pairs={{0,32},{32,64},{64,96},{96,128},{128,160},{160,192},{192,224},{224... | collective-permute-start | bytes 786440 | tf_op jit(solution)/shard_map/ppermute | solution.py:226
  49.8 35.4 %all-to-all-start.1 = ((bf16[4,4,2,256,256]{4,3,2,1,0:T(8,128)(2,1)}), bf16[4,4,2,256,256]{4,3,2,1,0:T(8,128)(2,1)}, u32[]{:S(2)}, u32[]{:S(2)}) async-start(bf16[4,4,2,256,256]{4,3,2,1,0:T(8,128)(2,1)} %broadcast_in_dim.9), calls=%async_computation.1 | async-start | bytes 8388608 | tf_op jit(solution)/shard_map/all_to_all | solution.py:212
  54.6 28.1 %copy-start.12 = (bf16[2,256,256]{2,1,0:T(8,128)(2,1)}, bf16[2,256,256]{2,1,0:T(8,128)(2,1)S(1)}, u32[]{:S(2)}) copy-start(bf16[2,256,256]{2,1,0:T(8,128)(2,1)S(1)} %collective-permute-done.4.refs_8_) | copy-start | bytes 786436
  54.6 7.5 %collective-permute-start.5 = (bf16[2,256,256]{2,1,0:T(8,128)(2,1)S(1)}, bf16[2,256,256]{2,1,0:T(8,128)(2,1)S(1)}, u32[]{:S(2)}, u32[]{:S(2)}) collective-permute-start(bf16[2,256,256]{2,1,0:T(8,128)(2,1)S(1)} %collective-permute-done.4.refs_8_), channel_id=1, source_target_pairs={{0,32},{32,64},{64,96},{96,128},{128,160},{160,192},{192,224},{224... | collective-permute-start | bytes 786440 | tf_op jit(solution)/shard_map/ppermute | solution.py:226
  56.6 8.7 %collective-permute-start.13 = (bf16[2,256,256]{2,1,0:T(8,128)(2,1)}, bf16[2,256,256]{2,1,0:T(8,128)(2,1)S(1)}, u32[]{:S(2)}, u32[]{:S(2)}) collective-permute-start(bf16[2,256,256]{2,1,0:T(8,128)(2,1)} %collective-permute-done.12.refs_9_), channel_id=1, source_target_pairs={{0,32},{32,64},{64,96},{96,128},{128,160},{160,192},{192,224},{224... | collective-permute-start | bytes 786440 | tf_op jit(solution)/shard_map/ppermute | solution.py:226
  62.2 20.6 %copy-start.13 = (bf16[2,256,256]{2,1,0:T(8,128)(2,1)}, bf16[2,256,256]{2,1,0:T(8,128)(2,1)S(1)}, u32[]{:S(2)}) copy-start(bf16[2,256,256]{2,1,0:T(8,128)(2,1)S(1)} %collective-permute-done.5.refs_10_) | copy-start | bytes 786436
  62.2 7.5 %collective-permute-start.6 = (bf16[2,256,256]{2,1,0:T(8,128)(2,1)S(1)}, bf16[2,256,256]{2,1,0:T(8,128)(2,1)S(1)}, u32[]{:S(2)}, u32[]{:S(2)}) collective-permute-start(bf16[2,256,256]{2,1,0:T(8,128)(2,1)S(1)} %collective-permute-done.5.refs_10_), channel_id=1, source_target_pairs={{0,32},{32,64},{64,96},{96,128},{128,160},{160,192},{192,224},{224... | collective-permute-start | bytes 786440 | tf_op jit(solution)/shard_map/ppermute | solution.py:226
  65.3 17.5 %copy-start.14 = (bf16[2,256,256]{2,1,0:T(8,128)(2,1)}, bf16[2,256,256]{2,1,0:T(8,128)(2,1)S(1)}, u32[]{:S(2)}) copy-start(bf16[2,256,256]{2,1,0:T(8,128)(2,1)S(1)} %collective-permute-done.13.refs_11_) | copy-start | bytes 786436
  65.3 8.7 %collective-permute-start.14 = (bf16[2,256,256]{2,1,0:T(8,128)(2,1)S(1)}, bf16[2,256,256]{2,1,0:T(8,128)(2,1)S(1)}, u32[]{:S(2)}, u32[]{:S(2)}) collective-permute-start(bf16[2,256,256]{2,1,0:T(8,128)(2,1)S(1)} %collective-permute-done.13.refs_11_), channel_id=1, source_target_pairs={{0,32},{32,64},{64,96},{96,128},{128,160},{160,192},{192,224},{224... | collective-permute-start | bytes 786440 | tf_op jit(solution)/shard_map/ppermute | solution.py:226
  69.7 13.1 %copy-start.15 = (bf16[2,256,256]{2,1,0:T(8,128)(2,1)}, bf16[2,256,256]{2,1,0:T(8,128)(2,1)S(1)}, u32[]{:S(2)}) copy-start(bf16[2,256,256]{2,1,0:T(8,128)(2,1)S(1)} %collective-permute-done.6.refs_12_) | copy-start | bytes 786436
  69.7 7.6 %collective-permute-start.7 = (bf16[2,256,256]{2,1,0:T(8,128)(2,1)S(1)}, bf16[2,256,256]{2,1,0:T(8,128)(2,1)S(1)}, u32[]{:S(2)}, u32[]{:S(2)}) collective-permute-start(bf16[2,256,256]{2,1,0:T(8,128)(2,1)S(1)} %collective-permute-done.6.refs_12_), channel_id=1, source_target_pairs={{0,32},{32,64},{64,96},{96,128},{128,160},{160,192},{192,224},{224... | collective-permute-start | bytes 786440 | tf_op jit(solution)/shard_map/ppermute | solution.py:226
  74.0 8.8 %copy-start.16 = (bf16[2,256,256]{2,1,0:T(8,128)(2,1)}, bf16[2,256,256]{2,1,0:T(8,128)(2,1)S(1)}, u32[]{:S(2)}) copy-start(bf16[2,256,256]{2,1,0:T(8,128)(2,1)S(1)} %collective-permute-done.14.refs_13_) | copy-start | bytes 786436
  74.0 8.7 %collective-permute-start.15 = (bf16[2,256,256]{2,1,0:T(8,128)(2,1)S(1)}, bf16[2,256,256]{2,1,0:T(8,128)(2,1)S(1)}, u32[]{:S(2)}, u32[]{:S(2)}) collective-permute-start(bf16[2,256,256]{2,1,0:T(8,128)(2,1)S(1)} %collective-permute-done.14.refs_13_), channel_id=1, source_target_pairs={{0,32},{32,64},{64,96},{96,128},{128,160},{160,192},{192,224},{224... | collective-permute-start | bytes 786440 | tf_op jit(solution)/shard_map/ppermute | solution.py:226
  77.3 12.2 %collective-permute-start.8 = (bf16[2,256,256]{2,1,0:T(8,128)(2,1)S(1)}, bf16[2,256,256]{2,1,0:T(8,128)(2,1)S(1)}, u32[]{:S(2)}, u32[]{:S(2)}) collective-permute-start(bf16[2,256,256]{2,1,0:T(8,128)(2,1)S(1)} %collective-permute-done.7.refs_14_), channel_id=1, source_target_pairs={{16,496},{48,16},{80,48},{112,80},{144,112},{176,144},{208,176},{2... | collective-permute-start | bytes 786440 | tf_op jit(solution)/shard_map/ppermute | solution.py:226
  82.8 7.1 %collective-permute-start.16 = (bf16[2,256,256]{2,1,0:T(8,128)(2,1)S(1)}, bf16[2,256,256]{2,1,0:T(8,128)(2,1)S(1)}, u32[]{:S(2)}, u32[]{:S(2)}) collective-permute-start(bf16[2,256,256]{2,1,0:T(8,128)(2,1)S(1)} %shard_map.29.refs_15_), channel_id=1, source_target_pairs={{16,496},{48,16},{80,48},{112,80},{144,112},{176,144},{208,176},{2... | collective-permute-start | bytes 786440 | tf_op jit(solution)/shard_map/ppermute | solution.py:226
  91.2 4.0 %copy-start.4 = (s32[1,2]{1,0:T(1,128)S(1)}, s32[1,2]{1,0:T(1,128)}, u32[]{:S(2)}) copy-start(s32[1,2]{1,0:T(1,128)} %param.4) | copy-start | bytes 28
  91.2 26.2 %copy-start.2 = (bf16[1,2,256,256]{3,2,1,0:T(8,128)(2,1)S(1)}, bf16[1,2,256,256]{3,2,1,0:T(8,128)(2,1)}, u32[]{:S(2)}) copy-start(bf16[1,2,256,256]{3,2,1,0:T(8,128)(2,1)} %param.3) | copy-start | bytes 786436
  91.2 3.9 %collective-permute-start.17 = (f32[2,256,256]{2,1,0:T(8,128)S(1)}, f32[2,256,256]{2,1,0:T(8,128)S(1)}, u32[]{:S(2)}, u32[]{:S(2)}) collective-permute-start(f32[2,256,256]{2,1,0:T(8,128)S(1)} %shard_map.32), channel_id=1, source_target_pairs={{0,16},{16,0},{1,17},{17,1},{2,18},{18,2},{3,19},{19,3},{4,20},{20... | collective-permute-start | bytes 1572872 | tf_op jit(solution)/shard_map/ppermute | solution.py:232

commit v8 on v6

--- a/solution.py
+++ b/solution.py
@@ -15,7 +15,6 @@
 HBM = pl.BlockSpec(memory_space=pltpu.HBM)
 MIB = 1024 * 1024
 SWAP = [(0, 1), (1, 0)]
-SETTLE = 7
 FLOPS = 26 * 10**9
 
 
@@ -106,7 +105,7 @@
 def products(totals, rows, plane, core, left, held, planes, groups):
     width = left.shape[-1]
     tiles = [tile for distance, _ in planes for tile in held[distance]]
-    if totals is None:
+    if len(planes) > 1:
         tiles = [pltpu.with_memory_space_constraint(tile, pltpu.HBM) for tile in tiles]
     given = [] if totals is None else [totals[row] for row in rows]
     kernel = functools.partial(product_kernel, planes, rows, groups)
@@ -156,7 +155,7 @@
             out_ref[slot] = jnp.zeros_like(tile)
 
 
-def settle(value, *after, flops=0):
+def settle(value, after, flops):
     return pl.pallas_call(
         settle_kernel,
         in_specs=[ANY] * (1 + len(after)),
@@ -176,7 +175,7 @@
     plane_ref, core_ref, column_ref = (
         i.astype(jnp.int32).reshape(1) for i in (plane, core, column)
     )
-    own = tile_cols[0]
+    own = pltpu.with_memory_space_constraint(tile_cols[0], pltpu.HBM)
     tiles = flow_tiles[0]
     mine = pl.pallas_call(
         functools.partial(order_kernel, columns),
@@ -184,7 +183,7 @@
         out_specs=VMEM,
         out_shape=jax.ShapeDtypeStruct((2, width, width), tiles.dtype),
         compiler_params=params(4),
-    )(own, column_ref, tiles)
+    )(own, column_ref, pltpu.with_memory_space_constraint(tiles, pltpu.HBM))
     other = lax.ppermute(mine, "core", SWAP)
 
     half = planes // 2
@@ -215,23 +214,22 @@
     left = copy_for_each(copy_for_each(sent, lines_of(0)), lines_of(1))
 
     held = [(mine, other)]
-    totals = None
     for step in range(1, half + 1):
-        if step == SETTLE:
-            held[-1] = (settle(held[-1][0], flops=FLOPS), held[-1][1])
         if step == half:
-            early = [(0, 0)] + [(i, None) for i in range(1, half - 1)]
-            totals = products(
-                None, (0, 1), plane_ref, core_ref, left, held, early, [[1, 2], [3, 4], [5, 6], [0]]
-            )
-            held[-1] = (settle(held[-1][0], *totals.values()), held[-1][1])
+            known = (plane_ref, core_ref, left, held)
+            early = [(i, 0) for i in range(half - 1)]
+            totals = products(None, (0, 1), *known, early, [[0, 1], [2, 3], [4, 5], [6]])
+            held[-1] = (held[-1][0], settle(held[-1][1], totals.values(), 0))
+        elif step == half - 1:
+            held[-1] = (held[-1][0], settle(held[-1][1], (), FLOPS))
         perm = ring + back if step < half else back
         held.append(tuple(lax.ppermute(t, ROWS, perm) for t in held[-1]))
-    known = (plane_ref, core_ref, left, held)
-    late = [(half - 1, None), (half, 1)]
-    outward = products(totals, (1,), *known, late, [[0], [1]])[1]
+    rest = [(i, 1) for i in range(1, half - 1)] + [(half - 1, None)]
+    totals = products(totals, (0, 1), *known, rest, [[0, 1], [2, 3], [4, 5], [6]])
+    late = [(half, 1)]
+    outward = products(totals, (1,), *known, late, [[0]])[1]
     received = lax.ppermute(outward, "core", SWAP)
-    total = products(totals, (0,), *known, late, [[0], [1]])[0]
+    total = products(totals, (0,), *known, late, [[0]])[0]
     inflated, sums = pl.pallas_call(
         functools.partial(square_kernel, columns),
         in_specs=[SMEM, SMEM, VMEM, VMEM],

time: 122 us -> 120 us (0.984)
  waiting for transfers between devices: 13.8 us -> 9.4 us
  blocking collectives: 18.4 us -> 20.8 us
  local copies, waits for them, and re-layouts: 5.22 us -> 3.65 us
    ppermute x16, waiting for transfers between devices: 13.6 us -> 8.86 us  [on_device(): held.append(tuple((lax.ppermute(t, ROWS, perm) for t in held[-1])))]
    all_to_all x1, blocking collectives: 16.6 us -> 19 us  [on_device(): lax.all_to_all(jnp.broadcast_to(sums[None], (planes, *sums.shape)), 'z',...]
    unnamed x34, local copies, waits for them, and re-layouts: 1.67 us -> 0.07 us
    pallas_call x3 -> x4, Pallas kernels: 7.3 us -> 7.95 us  [products(): pl.pallas_call(kernel, in_specs=[SMEM, SMEM, HBM] + [HBM] * len(tiles) +...]
  transfers between devices with their start and end apart: 20 -> 20, of which waited for: 7 -> 7; matrix products, arithmetic and copies ran while one was open for 3% -> 3% of each run, Pallas kernels for 5% -> 6%
where the time goes in v8:
time: 120 us; the launch traced here: 118 us
  starting transfers between devices  72.1 us (60%)
  blocking collectives  20.8 us (17%)
  Pallas kernels  11.3 us (9%)
  waiting for transfers between devices  9.4 us (8%)
  local copies, waits for them, and re-layouts  3.65 us (3%)
    ppermute x16, starting transfers between devices, on_device(): held.append(tuple((lax.ppermute(t, ROWS, perm) for t in held[-1])))  52.2 us
    all_to_all x1, blocking collectives, on_device(): lax.all_to_all(jnp.broadcast_to(sums[None], (planes, *sums.shape)), 'z',...  19 us
    all_to_all x2, starting transfers between devices, copy_for_each(): lax.all_to_all(spread, ('core', *COLS), 0, 0, axis_index_groups=lines, ti...  9.04 us
    ppermute x16, waiting for transfers between devices, on_device(): held.append(tuple((lax.ppermute(t, ROWS, perm) for t in held[-1])))  8.86 us
    ppermute x1, starting transfers between devices, on_device(): other = lax.ppermute(mine, 'core', SWAP)  8.79 us
    pallas_call x4, Pallas kernels, products(): pl.pallas_call(kernel, in_specs=[SMEM, SMEM, HBM] + [HBM] * len(tiles) +...  7.95 us
    broadcast_in_dim x2, local copies, waits for them, and re-layouts, copy_for_each(): spread = jnp.broadcast_to(value[None], (len(lines[0]), *value.shape))  3.56 us
  transfers between devices with their start and end apart: 20, of which 7 were waited for; matrix products, arithmetic and copies ran while one was open for 3% of the time, Pallas kernels for 6%

profile of v8, /device:TPU:1, one launch (start us, length us, event | category | flops | bytes accessed | tf_op | source)
XLA Modules:
  0.0 117.9 jit_solution(262991690905643505)
XLA Ops:
  0.0 1.1 shard_map.28.refs_0_
  1.1 0.0 copy-start
  1.1 8.8 %collective-permute-start = (bf16[2,256,256]{2,1,0:T(8,128)(2,1)S(1)}, bf16[2,256,256]{2,1,0:T(8,128)(2,1)S(1)}, u32[]{:S(2)}, u32[]{:S(2)}) collective-permute-start(bf16[2,256,256]{2,1,0:T(8,128)(2,1)S(1)} %shard_map.28.refs_0_), channel_id=1, source_target_pairs={{0,16},{16,0},{1,17},{17,1},{2,18},{18,2},{3,19},{19,3},{4,20},{20... | collective-permute-start | bytes 786440 | tf_op jit(solution)/shard_map/ppermute | solution.py:187
  9.9 5.7 %collective-permute-start.1 = (bf16[2,256,256]{2,1,0:T(8,128)(2,1)S(1)}, bf16[2,256,256]{2,1,0:T(8,128)(2,1)S(1)}, u32[]{:S(2)}, u32[]{:S(2)}) collective-permute-start(bf16[2,256,256]{2,1,0:T(8,128)(2,1)S(1)} %shard_map.28.refs_0_), channel_id=1, source_target_pairs={{0,32},{32,64},{64,96},{96,128},{128,160},{160,192},{192,224},{224... | collective-permute-start | bytes 786440 | tf_op jit(solution)/shard_map/ppermute | solution.py:226
  15.7 0.0 collective-permute-done.refs_1_
  15.7 0.0 copy-start.15
  15.7 2.6 %collective-permute-start.9 = (bf16[2,256,256]{2,1,0:T(8,128)(2,1)S(1)}, bf16[2,256,256]{2,1,0:T(8,128)(2,1)S(1)}, u32[]{:S(2)}, u32[]{:S(2)}) collective-permute-start(bf16[2,256,256]{2,1,0:T(8,128)(2,1)S(1)} %collective-permute-done.refs_1_), channel_id=1, source_target_pairs={{0,32},{32,64},{64,96},{96,128},{128,160},{160,192},{192,224},{224... | collective-permute-start | bytes 786440 | tf_op jit(solution)/shard_map/ppermute | solution.py:226
  18.4 1.0 broadcast_in_dim.8
  19.5 4.2 %all-to-all-start = ((bf16[4,2,256,256]{3,2,1,0:T(8,128)(2,1)}), bf16[4,2,256,256]{3,2,1,0:T(8,128)(2,1)S(1)}, u32[]{:S(2)}, u32[]{:S(2)}) async-start(bf16[4,2,256,256]{3,2,1,0:T(8,128)(2,1)} %broadcast_in_dim.8), calls=%async_computation | async-start | bytes 2097152 | tf_op jit(solution)/shard_map/all_to_all | solution.py:209
  23.6 0.0 collective-permute-done.1.refs_2_.refs_0_
  23.6 2.6 %collective-permute-start.2 = (bf16[2,256,256]{2,1,0:T(8,128)(2,1)S(1)}, bf16[2,256,256]{2,1,0:T(8,128)(2,1)S(1)}, u32[]{:S(2)}, u32[]{:S(2)}) collective-permute-start(bf16[2,256,256]{2,1,0:T(8,128)(2,1)S(1)} %collective-permute-done.1.refs_2_.refs_0_), channel_id=1, source_target_pairs={{0,32},{32,64},{64,96},{96,128},{128,160},{160,192},{192,224},{224... | collective-permute-start | bytes 786440 | tf_op jit(solution)/shard_map/ppermute | solution.py:226
  26.3 0.0 copy-done.15
  26.3 0.0 collective-permute-done.9.refs_3_.refs_1_
  26.3 0.0 copy-start.5
  26.3 2.6 %collective-permute-start.10 = (bf16[2,256,256]{2,1,0:T(8,128)(2,1)S(1)}, bf16[2,256,256]{2,1,0:T(8,128)(2,1)S(1)}, u32[]{:S(2)}, u32[]{:S(2)}) collective-permute-start(bf16[2,256,256]{2,1,0:T(8,128)(2,1)S(1)} %collective-permute-done.9.refs_3_.refs_1_), channel_id=1, source_target_pairs={{0,32},{32,64},{64,96},{96,128},{128,160},{160,192},{192,224},{224... | collective-permute-start | bytes 786440 | tf_op jit(solution)/shard_map/ppermute | solution.py:226
  29.0 2.1 %collective-permute-done.2.refs_4_.refs_2_ = bf16[2,256,256]{2,1,0:T(8,128)(2,1)S(1)} collective-permute-done((bf16[2,256,256]{2,1,0:T(8,128)(2,1)S(1)}, bf16[2,256,256]{2,1,0:T(8,128)(2,1)S(1)}, u32[]{:S(2)}, u32[]{:S(2)}) %collective-permute-start.2) | collective-permute-done | bytes 262176 | tf_op jit(solution)/shard_map/ppermute | solution.py:226
  31.1 3.8 %collective-permute-start.3 = (bf16[2,256,256]{2,1,0:T(8,128)(2,1)S(1)}, bf16[2,256,256]{2,1,0:T(8,128)(2,1)S(1)}, u32[]{:S(2)}, u32[]{:S(2)}) collective-permute-start(bf16[2,256,256]{2,1,0:T(8,128)(2,1)S(1)} %collective-permute-done.2.refs_4_.refs_2_), channel_id=1, source_target_pairs={{0,32},{32,64},{64,96},{96,128},{128,160},{160,192},{192,224},{224... | collective-permute-start | bytes 786440 | tf_op jit(solution)/shard_map/ppermute | solution.py:226
  34.9 0.0 collective-permute-done.10.refs_5_.refs_3_
  34.9 0.0 copy-start.7
  34.9 2.5 %collective-permute-start.11 = (bf16[2,256,256]{2,1,0:T(8,128)(2,1)S(1)}, bf16[2,256,256]{2,1,0:T(8,128)(2,1)S(1)}, u32[]{:S(2)}, u32[]{:S(2)}) collective-permute-start(bf16[2,256,256]{2,1,0:T(8,128)(2,1)S(1)} %collective-permute-done.10.refs_5_.refs_3_), channel_id=1, source_target_pairs={{0,32},{32,64},{64,96},{96,128},{128,160},{160,192},{192,224},{224... | collective-permute-start | bytes 786440 | tf_op jit(solution)/shard_map/ppermute | solution.py:226
  37.4 1.0 collective-permute-done.3.refs_6_.refs_4_
  38.5 4.8 %collective-permute-start.4 = (bf16[2,256,256]{2,1,0:T(8,128)(2,1)S(1)}, bf16[2,256,256]{2,1,0:T(8,128)(2,1)S(1)}, u32[]{:S(2)}, u32[]{:S(2)}) collective-permute-start(bf16[2,256,256]{2,1,0:T(8,128)(2,1)S(1)} %collective-permute-done.3.refs_6_.refs_4_), channel_id=1, source_target_pairs={{0,32},{32,64},{64,96},{96,128},{128,160},{160,192},{192,224},{224... | collective-permute-start | bytes 786440 | tf_op jit(solution)/shard_map/ppermute | solution.py:226
  43.2 0.0 collective-permute-done.11.refs_7_.refs_5_
  43.2 0.0 copy-start.9
  43.2 2.8 %collective-permute-start.12 = (bf16[2,256,256]{2,1,0:T(8,128)(2,1)S(1)}, bf16[2,256,256]{2,1,0:T(8,128)(2,1)S(1)}, u32[]{:S(2)}, u32[]{:S(2)}) collective-permute-start(bf16[2,256,256]{2,1,0:T(8,128)(2,1)S(1)} %collective-permute-done.11.refs_7_.refs_5_), channel_id=1, source_target_pairs={{0,32},{32,64},{64,96},{96,128},{128,160},{160,192},{192,224},{224... | collective-permute-start | bytes 786440 | tf_op jit(solution)/shard_map/ppermute | solution.py:226
  46.0 0.0 all-to-all-done
  46.0 2.5 %broadcast_in_dim.9 = bf16[4,4,2,256,256]{4,3,2,1,0:T(8,128)(2,1)} broadcast(bf16[4,2,256,256]{3,2,1,0:T(8,128)(2,1)S(1)} %all-to-all-done), dimensions={1,2,3,4} | broadcast | bytes 5242880 | tf_op jit(solution)/shard_map/broadcast_in_dim | solution.py:208
  48.5 0.0 copy-done
  48.5 0.0 copy-done.4
  48.5 0.0 copy-done.5
  48.6 0.0 copy-done.6
  48.6 4.9 %all-to-all-start.1 = ((bf16[4,4,2,256,256]{4,3,2,1,0:T(8,128)(2,1)}), bf16[4,4,2,256,256]{4,3,2,1,0:T(8,128)(2,1)}, u32[]{:S(2)}, u32[]{:S(2)}) async-start(bf16[4,4,2,256,256]{4,3,2,1,0:T(8,128)(2,1)} %broadcast_in_dim.9), calls=%async_computation.1 | async-start | bytes 8388608 | tf_op jit(solution)/shard_map/all_to_all | solution.py:209
  53.5 0.0 collective-permute-done.4.refs_8_.refs_6_
  53.5 1.9 %collective-permute-start.5 = (bf16[2,256,256]{2,1,0:T(8,128)(2,1)S(1)}, bf16[2,256,256]{2,1,0:T(8,128)(2,1)S(1)}, u32[]{:S(2)}, u32[]{:S(2)}) collective-permute-start(bf16[2,256,256]{2,1,0:T(8,128)(2,1)S(1)} %collective-permute-done.4.refs_8_.refs_6_), channel_id=1, source_target_pairs={{0,32},{32,64},{64,96},{96,128},{128,160},{160,192},{192,224},{224... | collective-permute-start | bytes 786440 | tf_op jit(solution)/shard_map/ppermute | solution.py:226
  55.4 0.0 collective-permute-done.12.refs_9_.refs_7_
  55.4 2.4 %collective-permute-start.13 = (bf16[2,256,256]{2,1,0:T(8,128)(2,1)S(1)}, bf16[2,256,256]{2,1,0:T(8,128)(2,1)S(1)}, u32[]{:S(2)}, u32[]{:S(2)}) collective-permute-start(bf16[2,256,256]{2,1,0:T(8,128)(2,1)S(1)} %collective-permute-done.12.refs_9_.refs_7_), channel_id=1, source_target_pairs={{0,32},{32,64},{64,96},{96,128},{128,160},{160,192},{192,224},{224... | collective-permute-start | bytes 786440 | tf_op jit(solution)/shard_map/ppermute | solution.py:226
  57.9 3.1 %collective-permute-done.5.refs_10_.refs_8_ = bf16[2,256,256]{2,1,0:T(8,128)(2,1)S(1)} collective-permute-done((bf16[2,256,256]{2,1,0:T(8,128)(2,1)S(1)}, bf16[2,256,256]{2,1,0:T(8,128)(2,1)S(1)}, u32[]{:S(2)}, u32[]{:S(2)}) %collective-permute-start.5) | collective-permute-done | bytes 262176 | tf_op jit(solution)/shard_map/ppermute | solution.py:226
  61.0 3.1 %collective-permute-start.6 = (bf16[2,256,256]{2,1,0:T(8,128)(2,1)S(1)}, bf16[2,256,256]{2,1,0:T(8,128)(2,1)S(1)}, u32[]{:S(2)}, u32[]{:S(2)}) collective-permute-start(bf16[2,256,256]{2,1,0:T(8,128)(2,1)S(1)} %collective-permute-done.5.refs_10_.refs_8_), channel_id=1, source_target_pairs={{0,32},{32,64},{64,96},{96,128},{128,160},{160,192},{192,224},{224... | collective-permute-start | bytes 786440 | tf_op jit(solution)/shard_map/ppermute | solution.py:226
  64.1 0.0 collective-permute-done.13.refs_11_.refs_9_
  64.1 0.0 copy-start.13
  64.1 2.8 %collective-permute-start.14 = (bf16[2,256,256]{2,1,0:T(8,128)(2,1)S(1)}, bf16[2,256,256]{2,1,0:T(8,128)(2,1)S(1)}, u32[]{:S(2)}, u32[]{:S(2)}) collective-permute-start(bf16[2,256,256]{2,1,0:T(8,128)(2,1)S(1)} %collective-permute-done.13.refs_11_.refs_9_), channel_id=1, source_target_pairs={{0,32},{32,64},{64,96},{96,128},{128,160},{160,192},{192,224},{224... | collective-permute-start | bytes 786440 | tf_op jit(solution)/shard_map/ppermute | solution.py:226
  66.9 1.6 %collective-permute-done.6.refs_12_.refs_10_ = bf16[2,256,256]{2,1,0:T(8,128)(2,1)S(1)} collective-permute-done((bf16[2,256,256]{2,1,0:T(8,128)(2,1)S(1)}, bf16[2,256,256]{2,1,0:T(8,128)(2,1)S(1)}, u32[]{:S(2)}, u32[]{:S(2)}) %collective-permute-start.6) | collective-permute-done | bytes 262176 | tf_op jit(solution)/shard_map/ppermute | solution.py:226
  68.5 4.3 %collective-permute-start.7 = (bf16[2,256,256]{2,1,0:T(8,128)(2,1)S(1)}, bf16[2,256,256]{2,1,0:T(8,128)(2,1)S(1)}, u32[]{:S(2)}, u32[]{:S(2)}) collective-permute-start(bf16[2,256,256]{2,1,0:T(8,128)(2,1)S(1)} %collective-permute-done.6.refs_12_.refs_10_), channel_id=1, source_target_pairs={{0,32},{32,64},{64,96},{96,128},{128,160},{160,192},{192,224},{224... | collective-permute-start | bytes 786440 | tf_op jit(solution)/shard_map/ppermute | solution.py:226
  72.8 0.0 collective-permute-done.14.refs_0_
  72.9 2.8 %collective-permute-start.15 = (bf16[2,256,256]{2,1,0:T(8,128)(2,1)S(1)}, bf16[2,256,256]{2,1,0:T(8,128)(2,1)S(1)}, u32[]{:S(2)}, u32[]{:S(2)}) collective-permute-start(bf16[2,256,256]{2,1,0:T(8,128)(2,1)S(1)} %shard_map.29.refs_13_.refs_11_), channel_id=1, source_target_pairs={{0,32},{32,64},{64,96},{96,128},{128,160},{160,192},{192,224},{224... | collective-permute-start | bytes 786440 | tf_op jit(solution)/shard_map/ppermute | solution.py:226
  75.7 0.4 collective-permute-done.7.refs_12_
  76.1 5.4 %collective-permute-start.8 = (bf16[2,256,256]{2,1,0:T(8,128)(2,1)S(1)}, bf16[2,256,256]{2,1,0:T(8,128)(2,1)S(1)}, u32[]{:S(2)}, u32[]{:S(2)}) collective-permute-start(bf16[2,256,256]{2,1,0:T(8,128)(2,1)S(1)} %collective-permute-done.7.refs_12_), channel_id=1, source_target_pairs={{16,496},{48,16},{80,48},{112,80},{144,112},{176,144},{208,176},{2... | collective-permute-start | bytes 786440 | tf_op jit(solution)/shard_map/ppermute | solution.py:226
  81.6 0.0 all-to-all-done.1.left_ref
  81.6 0.7 shard_map.30
  82.3 0.0 collective-permute-done.15.refs_0_
  82.3 0.0 copy-start.2
  82.3 1.9 %collective-permute-start.16 = (bf16[2,256,256]{2,1,0:T(8,128)(2,1)S(1)}, bf16[2,256,256]{2,1,0:T(8,128)(2,1)S(1)}, u32[]{:S(2)}, u32[]{:S(2)}) collective-permute-start(bf16[2,256,256]{2,1,0:T(8,128)(2,1)S(1)} %shard_map.31.refs_13_), channel_id=1, source_target_pairs={{16,496},{48,16},{80,48},{112,80},{144,112},{176,144},{208,176},{2... | collective-permute-start | bytes 786440 | tf_op jit(solution)/shard_map/ppermute | solution.py:226
  84.3 4.6 %shard_map.32 = (f32[2,256,256]{2,1,0:T(8,128)S(1)}, f32[2,256,256]{2,1,0:T(8,128)S(1)}) custom-call(s32[1]{0:T(128)} %bitcast.3.plane_ref, s32[1]{0:T(128)} %bitcast.4.core_ref, bf16[4,4,2,256,256]{4,3,2,1,0:T(8,128)(2,1)} %all-to-all-done.1.left_ref, bf16[2,256,256]{2,1,0:T(8,128)(2,1)} %copy-done.4, ...), custom_call_target="tpu_custom_call", output_to_operand_aliasing={{0}: (17, {}), {1}: (18, {})} | custom-call | flops 1879048192 | bytes 14680064 | tf_op jit(solution)/shard_map/pallas_call | solution.py:112
  88.9 0.0 collective-permute-done.8.refs_0_
  88.9 0.6 collective-permute-done.16.refs_1_
  89.5 1.3 %shard_map.34 = f32[2,256,256]{2,1,0:T(8,128)S(1)} custom-call(s32[1]{0:T(128)} %bitcast.3.plane_ref, s32[1]{0:T(128)} %bitcast.4.core_ref, bf16[4,4,2,256,256]{4,3,2,1,0:T(8,128)(2,1)} %all-to-all-done.1.left_ref, bf16[2,256,256]{2,1,0:T(8,128)(2,1)S(1)} %collective-permute-done.8.refs_0_, ...), custom_call_target="tpu_custom_call", output_to_operand_aliasing={{}: (5, {})} | custom-call | flops 134217728 | bytes 1572864 | tf_op jit(solution)/shard_map/pallas_call | solution.py:112
  90.8 0.0 copy-start.3
  90.8 2.1 %collective-permute-start.17 = (f32[2,256,256]{2,1,0:T(8,128)S(1)}, f32[2,256,256]{2,1,0:T(8,128)S(1)}, u32[]{:S(2)}, u32[]{:S(2)}) collective-permute-start(f32[2,256,256]{2,1,0:T(8,128)S(1)} %shard_map.34), channel_id=1, source_target_pairs={{0,16},{16,0},{1,17},{17,1},{2,18},{18,2},{3,19},{19,3},{4,20},{20... | collective-permute-start | bytes 1572872 | tf_op jit(solution)/shard_map/ppermute | solution.py:231
  92.8 1.3 %shard_map.33.mine_ref = f32[2,256,256]{2,1,0:T(8,128)S(1)} custom-call(s32[1]{0:T(128)} %bitcast.3.plane_ref, s32[1]{0:T(128)} %bitcast.4.core_ref, bf16[4,4,2,256,256]{4,3,2,1,0:T(8,128)(2,1)} %all-to-all-done.1.left_ref, bf16[2,256,256]{2,1,0:T(8,128)(2,1)S(1)} %collective-permute-done.8.refs_0_, ...), custom_call_target="tpu_custom_call", output_to_operand_aliasing={{}: (5, {})} | custom-call | flops 134217728 | bytes 1572864 | tf_op jit(solution)/shard_map/pallas_call | solution.py:112
  94.2 0.5 collective-permute-done.17.other_ref
  94.7 0.7 shard_map.35
  95.5 1.8 %all-gather.1 = f32[2,2,256]{2,1,0:T(2,128)S(1)} all-gather(f32[1,2,256]{2,1,0:T(2,128)S(1)} %bitcast.9), channel_id=2, replica_groups=mesh['z'=16,'core'=2,'y'=4,'x'=4] {'core'}, dimensions={0}, use_global_device_ids=true | all-gather | bytes 6144 | tf_op jit(solution)/shard_map/all_gather | solution.py:243
  97.3 19.0 %all_to_all.15.parts_ref = f32[16,2,256]{2,1,0:T(2,128)S(1)} all-to-all(f32[16,2,256]{2,1,0:T(2,128)S(1)} %broadcast_in_dim.10), channel_id=1, replica_groups=mesh['z'=16,'core'=2,'y'=4,'x'=4] {'z'}, dimensions={0} | all-to-all | bytes 65536 | tf_op jit(solution)/shard_map/all_to_all | solution.py:244
  116.3 1.6 %shard_map.36 = f32[2,256,256]{2,1,0:T(8,128)} custom-call(s32[2]{0:T(128)} %bitcast.12, s32[1]{0:T(128)} %bitcast.1.column_ref, bf16[2,256,256]{2,1,0:T(8,128)(2,1)S(1)} %bitcast.8, f32[2,256,256]{2,1,0:T(8,128)S(1)} %get-tuple-element.15.inflated_ref, f32[16,2,256]{2,1,0:T(2,128)S(1)} %all_to_all.15.parts_ref), custom_call_target="tpu_custom_call" | custom-call | tf_op jit(solution)/shard_map/pallas_call | solution.py:248
  (28 shorter events, 0.1 us)
Async XLA Ops:
  1.1 47.5 %copy-start = (bf16[2,256,256]{2,1,0:T(8,128)(2,1)}, bf16[2,256,256]{2,1,0:T(8,128)(2,1)S(1)}, u32[]{:S(2)}) copy-start(bf16[2,256,256]{2,1,0:T(8,128)(2,1)S(1)} %shard_map.28.refs_0_) | copy-start | bytes 786436
  1.1 14.6 %collective-permute-start = (bf16[2,256,256]{2,1,0:T(8,128)(2,1)S(1)}, bf16[2,256,256]{2,1,0:T(8,128)(2,1)S(1)}, u32[]{:S(2)}, u32[]{:S(2)}) collective-permute-start(bf16[2,256,256]{2,1,0:T(8,128)(2,1)S(1)} %shard_map.28.refs_0_), channel_id=1, source_target_pairs={{0,16},{16,0},{1,17},{17,1},{2,18},{18,2},{3,19},{19,3},{4,20},{20... | collective-permute-start | bytes 786440 | tf_op jit(solution)/shard_map/ppermute | solution.py:187
  9.9 13.8 %collective-permute-start.1 = (bf16[2,256,256]{2,1,0:T(8,128)(2,1)S(1)}, bf16[2,256,256]{2,1,0:T(8,128)(2,1)S(1)}, u32[]{:S(2)}, u32[]{:S(2)}) collective-permute-start(bf16[2,256,256]{2,1,0:T(8,128)(2,1)S(1)} %shard_map.28.refs_0_), channel_id=1, source_target_pairs={{0,32},{32,64},{64,96},{96,128},{128,160},{160,192},{192,224},{224... | collective-permute-start | bytes 786440 | tf_op jit(solution)/shard_map/ppermute | solution.py:226
  15.7 10.6 %copy-start.15 = (bf16[2,256,256]{2,1,0:T(8,128)(2,1)}, bf16[2,256,256]{2,1,0:T(8,128)(2,1)S(1)}, u32[]{:S(2)}) copy-start(bf16[2,256,256]{2,1,0:T(8,128)(2,1)S(1)} %collective-permute-done.refs_1_) | copy-start | bytes 786436
  15.7 10.6 %collective-permute-start.9 = (bf16[2,256,256]{2,1,0:T(8,128)(2,1)S(1)}, bf16[2,256,256]{2,1,0:T(8,128)(2,1)S(1)}, u32[]{:S(2)}, u32[]{:S(2)}) collective-permute-start(bf16[2,256,256]{2,1,0:T(8,128)(2,1)S(1)} %collective-permute-done.refs_1_), channel_id=1, source_target_pairs={{0,32},{32,64},{64,96},{96,128},{128,160},{160,192},{192,224},{224... | collective-permute-start | bytes 786440 | tf_op jit(solution)/shard_map/ppermute | solution.py:226
  19.5 26.6 %all-to-all-start = ((bf16[4,2,256,256]{3,2,1,0:T(8,128)(2,1)}), bf16[4,2,256,256]{3,2,1,0:T(8,128)(2,1)S(1)}, u32[]{:S(2)}, u32[]{:S(2)}) async-start(bf16[4,2,256,256]{3,2,1,0:T(8,128)(2,1)} %broadcast_in_dim.8), calls=%async_computation | async-start | bytes 2097152 | tf_op jit(solution)/shard_map/all_to_all | solution.py:209
  23.6 24.9 %copy-start.4 = (bf16[2,256,256]{2,1,0:T(8,128)(2,1)}, bf16[2,256,256]{2,1,0:T(8,128)(2,1)S(1)}, u32[]{:S(2)}) copy-start(bf16[2,256,256]{2,1,0:T(8,128)(2,1)S(1)} %collective-permute-done.1.refs_2_.refs_0_) | copy-start | bytes 786436
  23.6 7.4 %collective-permute-start.2 = (bf16[2,256,256]{2,1,0:T(8,128)(2,1)S(1)}, bf16[2,256,256]{2,1,0:T(8,128)(2,1)S(1)}, u32[]{:S(2)}, u32[]{:S(2)}) collective-permute-start(bf16[2,256,256]{2,1,0:T(8,128)(2,1)S(1)} %collective-permute-done.1.refs_2_.refs_0_), channel_id=1, source_target_pairs={{0,32},{32,64},{64,96},{96,128},{128,160},{160,192},{192,224},{224... | collective-permute-start | bytes 786440 | tf_op jit(solution)/shard_map/ppermute | solution.py:226
  26.3 22.2 %copy-start.5 = (bf16[2,256,256]{2,1,0:T(8,128)(2,1)}, bf16[2,256,256]{2,1,0:T(8,128)(2,1)S(1)}, u32[]{:S(2)}) copy-start(bf16[2,256,256]{2,1,0:T(8,128)(2,1)S(1)} %collective-permute-done.9.refs_3_.refs_1_) | copy-start | bytes 786436
  26.3 8.6 %collective-permute-start.10 = (bf16[2,256,256]{2,1,0:T(8,128)(2,1)S(1)}, bf16[2,256,256]{2,1,0:T(8,128)(2,1)S(1)}, u32[]{:S(2)}, u32[]{:S(2)}) collective-permute-start(bf16[2,256,256]{2,1,0:T(8,128)(2,1)S(1)} %collective-permute-done.9.refs_3_.refs_1_), channel_id=1, source_target_pairs={{0,32},{32,64},{64,96},{96,128},{128,160},{160,192},{192,224},{224... | collective-permute-start | bytes 786440 | tf_op jit(solution)/shard_map/ppermute | solution.py:226
  31.1 17.5 %copy-start.6 = (bf16[2,256,256]{2,1,0:T(8,128)(2,1)}, bf16[2,256,256]{2,1,0:T(8,128)(2,1)S(1)}, u32[]{:S(2)}) copy-start(bf16[2,256,256]{2,1,0:T(8,128)(2,1)S(1)} %collective-permute-done.2.refs_4_.refs_2_) | copy-start | bytes 786436
  31.1 7.4 %collective-permute-start.3 = (bf16[2,256,256]{2,1,0:T(8,128)(2,1)S(1)}, bf16[2,256,256]{2,1,0:T(8,128)(2,1)S(1)}, u32[]{:S(2)}, u32[]{:S(2)}) collective-permute-start(bf16[2,256,256]{2,1,0:T(8,128)(2,1)S(1)} %collective-permute-done.2.refs_4_.refs_2_), channel_id=1, source_target_pairs={{0,32},{32,64},{64,96},{96,128},{128,160},{160,192},{192,224},{224... | collective-permute-start | bytes 786440 | tf_op jit(solution)/shard_map/ppermute | solution.py:226
  34.9 13.7 %copy-start.7 = (bf16[2,256,256]{2,1,0:T(8,128)(2,1)}, bf16[2,256,256]{2,1,0:T(8,128)(2,1)S(1)}, u32[]{:S(2)}) copy-start(bf16[2,256,256]{2,1,0:T(8,128)(2,1)S(1)} %collective-permute-done.10.refs_5_.refs_3_) | copy-start | bytes 786436
  34.9 8.3 %collective-permute-start.11 = (bf16[2,256,256]{2,1,0:T(8,128)(2,1)S(1)}, bf16[2,256,256]{2,1,0:T(8,128)(2,1)S(1)}, u32[]{:S(2)}, u32[]{:S(2)}) collective-permute-start(bf16[2,256,256]{2,1,0:T(8,128)(2,1)S(1)} %collective-permute-done.10.refs_5_.refs_3_), channel_id=1, source_target_pairs={{0,32},{32,64},{64,96},{96,128},{128,160},{160,192},{192,224},{224... | collective-permute-start | bytes 786440 | tf_op jit(solution)/shard_map/ppermute | solution.py:226
  38.5 10.1 %copy-start.8 = (bf16[2,256,256]{2,1,0:T(8,128)(2,1)}, bf16[2,256,256]{2,1,0:T(8,128)(2,1)S(1)}, u32[]{:S(2)}) copy-start(bf16[2,256,256]{2,1,0:T(8,128)(2,1)S(1)} %collective-permute-done.3.refs_6_.refs_4_) | copy-start | bytes 786436
  38.5 15.0 %collective-permute-start.4 = (bf16[2,256,256]{2,1,0:T(8,128)(2,1)S(1)}, bf16[2,256,256]{2,1,0:T(8,128)(2,1)S(1)}, u32[]{:S(2)}, u32[]{:S(2)}) collective-permute-start(bf16[2,256,256]{2,1,0:T(8,128)(2,1)S(1)} %collective-permute-done.3.refs_6_.refs_4_), channel_id=1, source_target_pairs={{0,32},{32,64},{64,96},{96,128},{128,160},{160,192},{192,224},{224... | collective-permute-start | bytes 786440 | tf_op jit(solution)/shard_map/ppermute | solution.py:226
  43.2 5.4 %copy-start.9 = (bf16[2,256,256]{2,1,0:T(8,128)(2,1)}, bf16[2,256,256]{2,1,0:T(8,128)(2,1)S(1)}, u32[]{:S(2)}) copy-start(bf16[2,256,256]{2,1,0:T(8,128)(2,1)S(1)} %collective-permute-done.11.refs_7_.refs_5_) | copy-start | bytes 786436
  43.2 12.2 %collective-permute-start.12 = (bf16[2,256,256]{2,1,0:T(8,128)(2,1)S(1)}, bf16[2,256,256]{2,1,0:T(8,128)(2,1)S(1)}, u32[]{:S(2)}, u32[]{:S(2)}) collective-permute-start(bf16[2,256,256]{2,1,0:T(8,128)(2,1)S(1)} %collective-permute-done.11.refs_7_.refs_5_), channel_id=1, source_target_pairs={{0,32},{32,64},{64,96},{96,128},{128,160},{160,192},{192,224},{224... | collective-permute-start | bytes 786440 | tf_op jit(solution)/shard_map/ppermute | solution.py:226
  48.6 33.0 %all-to-all-start.1 = ((bf16[4,4,2,256,256]{4,3,2,1,0:T(8,128)(2,1)}), bf16[4,4,2,256,256]{4,3,2,1,0:T(8,128)(2,1)}, u32[]{:S(2)}, u32[]{:S(2)}) async-start(bf16[4,4,2,256,256]{4,3,2,1,0:T(8,128)(2,1)} %broadcast_in_dim.9), calls=%async_computation.1 | async-start | bytes 8388608 | tf_op jit(solution)/shard_map/all_to_all | solution.py:209
  53.5 19.4 %copy-start.10 = (bf16[2,256,256]{2,1,0:T(8,128)(2,1)}, bf16[2,256,256]{2,1,0:T(8,128)(2,1)S(1)}, u32[]{:S(2)}) copy-start(bf16[2,256,256]{2,1,0:T(8,128)(2,1)S(1)} %collective-permute-done.4.refs_8_.refs_6_) | copy-start | bytes 786436
  53.5 7.5 %collective-permute-start.5 = (bf16[2,256,256]{2,1,0:T(8,128)(2,1)S(1)}, bf16[2,256,256]{2,1,0:T(8,128)(2,1)S(1)}, u32[]{:S(2)}, u32[]{:S(2)}) collective-permute-start(bf16[2,256,256]{2,1,0:T(8,128)(2,1)S(1)} %collective-permute-done.4.refs_8_.refs_6_), channel_id=1, source_target_pairs={{0,32},{32,64},{64,96},{96,128},{128,160},{160,192},{192,224},{224... | collective-permute-start | bytes 786440 | tf_op jit(solution)/shard_map/ppermute | solution.py:226
  55.4 17.5 %copy-start.11 = (bf16[2,256,256]{2,1,0:T(8,128)(2,1)}, bf16[2,256,256]{2,1,0:T(8,128)(2,1)S(1)}, u32[]{:S(2)}) copy-start(bf16[2,256,256]{2,1,0:T(8,128)(2,1)S(1)} %collective-permute-done.12.refs_9_.refs_7_) | copy-start | bytes 786436
  55.4 8.7 %collective-permute-start.13 = (bf16[2,256,256]{2,1,0:T(8,128)(2,1)S(1)}, bf16[2,256,256]{2,1,0:T(8,128)(2,1)S(1)}, u32[]{:S(2)}, u32[]{:S(2)}) collective-permute-start(bf16[2,256,256]{2,1,0:T(8,128)(2,1)S(1)} %collective-permute-done.12.refs_9_.refs_7_), channel_id=1, source_target_pairs={{0,32},{32,64},{64,96},{96,128},{128,160},{160,192},{192,224},{224... | collective-permute-start | bytes 786440 | tf_op jit(solution)/shard_map/ppermute | solution.py:226
  61.0 11.9 %copy-start.12 = (bf16[2,256,256]{2,1,0:T(8,128)(2,1)}, bf16[2,256,256]{2,1,0:T(8,128)(2,1)S(1)}, u32[]{:S(2)}) copy-start(bf16[2,256,256]{2,1,0:T(8,128)(2,1)S(1)} %collective-permute-done.5.refs_10_.refs_8_) | copy-start | bytes 786436
  61.0 7.5 %collective-permute-start.6 = (bf16[2,256,256]{2,1,0:T(8,128)(2,1)S(1)}, bf16[2,256,256]{2,1,0:T(8,128)(2,1)S(1)}, u32[]{:S(2)}, u32[]{:S(2)}) collective-permute-start(bf16[2,256,256]{2,1,0:T(8,128)(2,1)S(1)} %collective-permute-done.5.refs_10_.refs_8_), channel_id=1, source_target_pairs={{0,32},{32,64},{64,96},{96,128},{128,160},{160,192},{192,224},{224... | collective-permute-start | bytes 786440 | tf_op jit(solution)/shard_map/ppermute | solution.py:226
  64.1 8.8 %copy-start.13 = (bf16[2,256,256]{2,1,0:T(8,128)(2,1)}, bf16[2,256,256]{2,1,0:T(8,128)(2,1)S(1)}, u32[]{:S(2)}) copy-start(bf16[2,256,256]{2,1,0:T(8,128)(2,1)S(1)} %collective-permute-done.13.refs_11_.refs_9_) | copy-start | bytes 786436
  64.1 8.7 %collective-permute-start.14 = (bf16[2,256,256]{2,1,0:T(8,128)(2,1)S(1)}, bf16[2,256,256]{2,1,0:T(8,128)(2,1)S(1)}, u32[]{:S(2)}, u32[]{:S(2)}) collective-permute-start(bf16[2,256,256]{2,1,0:T(8,128)(2,1)S(1)} %collective-permute-done.13.refs_11_.refs_9_), channel_id=1, source_target_pairs={{0,32},{32,64},{64,96},{96,128},{128,160},{160,192},{192,224},{224... | collective-permute-start | bytes 786440 | tf_op jit(solution)/shard_map/ppermute | solution.py:226
  68.5 4.4 %copy-start.14 = (bf16[2,256,256]{2,1,0:T(8,128)(2,1)}, bf16[2,256,256]{2,1,0:T(8,128)(2,1)S(1)}, u32[]{:S(2)}) copy-start(bf16[2,256,256]{2,1,0:T(8,128)(2,1)S(1)} %collective-permute-done.6.refs_12_.refs_10_) | copy-start | bytes 786436
  68.5 7.6 %collective-permute-start.7 = (bf16[2,256,256]{2,1,0:T(8,128)(2,1)S(1)}, bf16[2,256,256]{2,1,0:T(8,128)(2,1)S(1)}, u32[]{:S(2)}, u32[]{:S(2)}) collective-permute-start(bf16[2,256,256]{2,1,0:T(8,128)(2,1)S(1)} %collective-permute-done.6.refs_12_.refs_10_), channel_id=1, source_target_pairs={{0,32},{32,64},{64,96},{96,128},{128,160},{160,192},{192,224},{224... | collective-permute-start | bytes 786440 | tf_op jit(solution)/shard_map/ppermute | solution.py:226
  72.9 8.7 %copy-start.1 = (bf16[2,256,256]{2,1,0:T(8,128)(2,1)}, bf16[2,256,256]{2,1,0:T(8,128)(2,1)S(1)}, u32[]{:S(2)}) copy-start(bf16[2,256,256]{2,1,0:T(8,128)(2,1)S(1)} %shard_map.29.refs_13_.refs_11_) | copy-start | bytes 786436
  72.9 9.4 %collective-permute-start.15 = (bf16[2,256,256]{2,1,0:T(8,128)(2,1)S(1)}, bf16[2,256,256]{2,1,0:T(8,128)(2,1)S(1)}, u32[]{:S(2)}, u32[]{:S(2)}) collective-permute-start(bf16[2,256,256]{2,1,0:T(8,128)(2,1)S(1)} %shard_map.29.refs_13_.refs_11_), channel_id=1, source_target_pairs={{0,32},{32,64},{64,96},{96,128},{128,160},{160,192},{192,224},{224... | collective-permute-start | bytes 786440 | tf_op jit(solution)/shard_map/ppermute | solution.py:226
  76.1 6.2 %copy-start.16 = (bf16[2,256,256]{2,1,0:T(8,128)(2,1)}, bf16[2,256,256]{2,1,0:T(8,128)(2,1)S(1)}, u32[]{:S(2)}) copy-start(bf16[2,256,256]{2,1,0:T(8,128)(2,1)S(1)} %collective-permute-done.7.refs_12_) | copy-start | bytes 786436
  76.1 12.7 %collective-permute-start.8 = (bf16[2,256,256]{2,1,0:T(8,128)(2,1)S(1)}, bf16[2,256,256]{2,1,0:T(8,128)(2,1)S(1)}, u32[]{:S(2)}, u32[]{:S(2)}) collective-permute-start(bf16[2,256,256]{2,1,0:T(8,128)(2,1)S(1)} %collective-permute-done.7.refs_12_), channel_id=1, source_target_pairs={{16,496},{48,16},{80,48},{112,80},{144,112},{176,144},{208,176},{2... | collective-permute-start | bytes 786440 | tf_op jit(solution)/shard_map/ppermute | solution.py:226
  82.3 1.9 %copy-start.2 = (bf16[2,256,256]{2,1,0:T(8,128)(2,1)}, bf16[2,256,256]{2,1,0:T(8,128)(2,1)S(1)}, u32[]{:S(2)}) copy-start(bf16[2,256,256]{2,1,0:T(8,128)(2,1)S(1)} %shard_map.31.refs_13_) | copy-start | bytes 786436
  82.3 7.1 %collective-permute-start.16 = (bf16[2,256,256]{2,1,0:T(8,128)(2,1)S(1)}, bf16[2,256,256]{2,1,0:T(8,128)(2,1)S(1)}, u32[]{:S(2)}, u32[]{:S(2)}) collective-permute-start(bf16[2,256,256]{2,1,0:T(8,128)(2,1)S(1)} %shard_map.31.refs_13_), channel_id=1, source_target_pairs={{16,496},{48,16},{80,48},{112,80},{144,112},{176,144},{208,176},{2... | collective-permute-start | bytes 786440 | tf_op jit(solution)/shard_map/ppermute | solution.py:226
  90.8 25.6 %copy-start.3 = (bf16[1,2,256,256]{3,2,1,0:T(8,128)(2,1)S(1)}, bf16[1,2,256,256]{3,2,1,0:T(8,128)(2,1)}, u32[]{:S(2)}) copy-start(bf16[1,2,256,256]{3,2,1,0:T(8,128)(2,1)} %param.3) | copy-start | bytes 786436
  90.8 3.9 %collective-permute-start.17 = (f32[2,256,256]{2,1,0:T(8,128)S(1)}, f32[2,256,256]{2,1,0:T(8,128)S(1)}, u32[]{:S(2)}, u32[]{:S(2)}) collective-permute-start(f32[2,256,256]{2,1,0:T(8,128)S(1)} %shard_map.34), channel_id=1, source_target_pairs={{0,16},{16,0},{1,17},{17,1},{2,18},{18,2},{3,19},{19,3},{4,20},{20... | collective-permute-start | bytes 1572872 | tf_op jit(solution)/shard_map/ppermute | solution.py:231

commit v9 on v8

--- a/solution.py
+++ b/solution.py
@@ -240,9 +240,8 @@
         ],
         compiler_params=params(6),
     )(own, column_ref, total, received)
-    sums = lax.all_gather(sums, "core", axis=0).sum(axis=0)
     parts = lax.all_to_all(
-        jnp.broadcast_to(sums[None], (planes, *sums.shape)), "z", 0, 0, tiled=True
+        jnp.broadcast_to(sums[None], (planes * cores, *sums.shape)), ROWS, 0, 0, tiled=True
     )
     scale = float(planes * cores * width)
     out = pl.pallas_call(

time: 120 us -> 120 us (level)
    all_to_all x1, blocking collectives: 19 us -> 21.3 us  [on_device(): lax.all_to_all(jnp.broadcast_to(sums[None], (planes * cores, *sums.shape)...]
    all_gather x1 -> x0, blocking collectives: 1.78 us -> none  [on_device(): sums = lax.all_gather(sums, 'core', axis=0).sum(axis=0)]
where the time goes in v9:
time: 120 us; the launch traced here: 118 us
  starting transfers between devices  72.1 us (60%)
  blocking collectives  21.3 us (18%)
  Pallas kernels  11.4 us (10%)
  waiting for transfers between devices  9.4 us (8%)
  local copies, waits for them, and re-layouts  3.67 us (3%)
    ppermute x16, starting transfers between devices, on_device(): held.append(tuple((lax.ppermute(t, ROWS, perm) for t in held[-1])))  52.2 us
    all_to_all x1, blocking collectives, on_device(): lax.all_to_all(jnp.broadcast_to(sums[None], (planes * cores, *sums.shape)...  21.3 us
    all_to_all x2, starting transfers between devices, copy_for_each(): lax.all_to_all(spread, ('core', *COLS), 0, 0, axis_index_groups=lines, ti...  9.05 us
    ppermute x16, waiting for transfers between devices, on_device(): held.append(tuple((lax.ppermute(t, ROWS, perm) for t in held[-1])))  8.86 us
    ppermute x1, starting transfers between devices, on_device(): other = lax.ppermute(mine, 'core', SWAP)  8.79 us
    pallas_call x4, Pallas kernels, products(): pl.pallas_call(kernel, in_specs=[SMEM, SMEM, HBM] + [HBM] * len(tiles) +...  7.95 us
    broadcast_in_dim x2, local copies, waits for them, and re-layouts, copy_for_each(): spread = jnp.broadcast_to(value[None], (len(lines[0]), *value.shape))  3.57 us
  transfers between devices with their start and end apart: 20, of which 7 were waited for; matrix products, arithmetic and copies ran while one was open for 3% of the time, Pallas kernels for 6%

profile of v9, /device:TPU:1, one launch (start us, length us, event | category | flops | bytes accessed | tf_op | source)
XLA Modules:
  0.0 118.4 jit_solution(2097780251286283453)
XLA Ops:
  0.0 1.1 shard_map.28.refs_0_
  1.1 0.0 copy-start
  1.1 8.8 %collective-permute-start = (bf16[2,256,256]{2,1,0:T(8,128)(2,1)S(1)}, bf16[2,256,256]{2,1,0:T(8,128)(2,1)S(1)}, u32[]{:S(2)}, u32[]{:S(2)}) collective-permute-start(bf16[2,256,256]{2,1,0:T(8,128)(2,1)S(1)} %shard_map.28.refs_0_), channel_id=1, source_target_pairs={{0,16},{16,0},{1,17},{17,1},{2,18},{18,2},{3,19},{19,3},{4,20},{20... | collective-permute-start | bytes 786440 | tf_op jit(solution)/shard_map/ppermute | solution.py:187
  9.9 5.7 %collective-permute-start.1 = (bf16[2,256,256]{2,1,0:T(8,128)(2,1)S(1)}, bf16[2,256,256]{2,1,0:T(8,128)(2,1)S(1)}, u32[]{:S(2)}, u32[]{:S(2)}) collective-permute-start(bf16[2,256,256]{2,1,0:T(8,128)(2,1)S(1)} %shard_map.28.refs_0_), channel_id=1, source_target_pairs={{0,32},{32,64},{64,96},{96,128},{128,160},{160,192},{192,224},{224... | collective-permute-start | bytes 786440 | tf_op jit(solution)/shard_map/ppermute | solution.py:226
  15.7 0.0 collective-permute-done.refs_1_
  15.7 0.0 copy-start.15
  15.7 2.6 %collective-permute-start.9 = (bf16[2,256,256]{2,1,0:T(8,128)(2,1)S(1)}, bf16[2,256,256]{2,1,0:T(8,128)(2,1)S(1)}, u32[]{:S(2)}, u32[]{:S(2)}) collective-permute-start(bf16[2,256,256]{2,1,0:T(8,128)(2,1)S(1)} %collective-permute-done.refs_1_), channel_id=1, source_target_pairs={{0,32},{32,64},{64,96},{96,128},{128,160},{160,192},{192,224},{224... | collective-permute-start | bytes 786440 | tf_op jit(solution)/shard_map/ppermute | solution.py:226
  18.4 1.1 broadcast_in_dim.8
  19.5 4.2 %all-to-all-start = ((bf16[4,2,256,256]{3,2,1,0:T(8,128)(2,1)}), bf16[4,2,256,256]{3,2,1,0:T(8,128)(2,1)S(1)}, u32[]{:S(2)}, u32[]{:S(2)}) async-start(bf16[4,2,256,256]{3,2,1,0:T(8,128)(2,1)} %broadcast_in_dim.8), calls=%async_computation | async-start | bytes 2097152 | tf_op jit(solution)/shard_map/all_to_all | solution.py:209
  23.6 0.0 collective-permute-done.1.refs_2_.refs_0_
  23.7 2.6 %collective-permute-start.2 = (bf16[2,256,256]{2,1,0:T(8,128)(2,1)S(1)}, bf16[2,256,256]{2,1,0:T(8,128)(2,1)S(1)}, u32[]{:S(2)}, u32[]{:S(2)}) collective-permute-start(bf16[2,256,256]{2,1,0:T(8,128)(2,1)S(1)} %collective-permute-done.1.refs_2_.refs_0_), channel_id=1, source_target_pairs={{0,32},{32,64},{64,96},{96,128},{128,160},{160,192},{192,224},{224... | collective-permute-start | bytes 786440 | tf_op jit(solution)/shard_map/ppermute | solution.py:226
  26.3 0.0 copy-done.15
  26.3 0.0 collective-permute-done.9.refs_3_.refs_1_
  26.3 0.0 copy-start.5
  26.3 2.6 %collective-permute-start.10 = (bf16[2,256,256]{2,1,0:T(8,128)(2,1)S(1)}, bf16[2,256,256]{2,1,0:T(8,128)(2,1)S(1)}, u32[]{:S(2)}, u32[]{:S(2)}) collective-permute-start(bf16[2,256,256]{2,1,0:T(8,128)(2,1)S(1)} %collective-permute-done.9.refs_3_.refs_1_), channel_id=1, source_target_pairs={{0,32},{32,64},{64,96},{96,128},{128,160},{160,192},{192,224},{224... | collective-permute-start | bytes 786440 | tf_op jit(solution)/shard_map/ppermute | solution.py:226
  29.0 2.1 %collective-permute-done.2.refs_4_.refs_2_ = bf16[2,256,256]{2,1,0:T(8,128)(2,1)S(1)} collective-permute-done((bf16[2,256,256]{2,1,0:T(8,128)(2,1)S(1)}, bf16[2,256,256]{2,1,0:T(8,128)(2,1)S(1)}, u32[]{:S(2)}, u32[]{:S(2)}) %collective-permute-start.2) | collective-permute-done | bytes 262176 | tf_op jit(solution)/shard_map/ppermute | solution.py:226
  31.1 3.8 %collective-permute-start.3 = (bf16[2,256,256]{2,1,0:T(8,128)(2,1)S(1)}, bf16[2,256,256]{2,1,0:T(8,128)(2,1)S(1)}, u32[]{:S(2)}, u32[]{:S(2)}) collective-permute-start(bf16[2,256,256]{2,1,0:T(8,128)(2,1)S(1)} %collective-permute-done.2.refs_4_.refs_2_), channel_id=1, source_target_pairs={{0,32},{32,64},{64,96},{96,128},{128,160},{160,192},{192,224},{224... | collective-permute-start | bytes 786440 | tf_op jit(solution)/shard_map/ppermute | solution.py:226
  34.9 0.0 collective-permute-done.10.refs_5_.refs_3_
  34.9 0.0 copy-start.7
  34.9 2.5 %collective-permute-start.11 = (bf16[2,256,256]{2,1,0:T(8,128)(2,1)S(1)}, bf16[2,256,256]{2,1,0:T(8,128)(2,1)S(1)}, u32[]{:S(2)}, u32[]{:S(2)}) collective-permute-start(bf16[2,256,256]{2,1,0:T(8,128)(2,1)S(1)} %collective-permute-done.10.refs_5_.refs_3_), channel_id=1, source_target_pairs={{0,32},{32,64},{64,96},{96,128},{128,160},{160,192},{192,224},{224... | collective-permute-start | bytes 786440 | tf_op jit(solution)/shard_map/ppermute | solution.py:226
  37.4 1.0 collective-permute-done.3.refs_6_.refs_4_
  38.5 4.8 %collective-permute-start.4 = (bf16[2,256,256]{2,1,0:T(8,128)(2,1)S(1)}, bf16[2,256,256]{2,1,0:T(8,128)(2,1)S(1)}, u32[]{:S(2)}, u32[]{:S(2)}) collective-permute-start(bf16[2,256,256]{2,1,0:T(8,128)(2,1)S(1)} %collective-permute-done.3.refs_6_.refs_4_), channel_id=1, source_target_pairs={{0,32},{32,64},{64,96},{96,128},{128,160},{160,192},{192,224},{224... | collective-permute-start | bytes 786440 | tf_op jit(solution)/shard_map/ppermute | solution.py:226
  43.2 0.0 collective-permute-done.11.refs_7_.refs_5_
  43.2 0.0 copy-start.9
  43.2 2.8 %collective-permute-start.12 = (bf16[2,256,256]{2,1,0:T(8,128)(2,1)S(1)}, bf16[2,256,256]{2,1,0:T(8,128)(2,1)S(1)}, u32[]{:S(2)}, u32[]{:S(2)}) collective-permute-start(bf16[2,256,256]{2,1,0:T(8,128)(2,1)S(1)} %collective-permute-done.11.refs_7_.refs_5_), channel_id=1, source_target_pairs={{0,32},{32,64},{64,96},{96,128},{128,160},{160,192},{192,224},{224... | collective-permute-start | bytes 786440 | tf_op jit(solution)/shard_map/ppermute | solution.py:226
  46.0 0.0 all-to-all-done
  46.0 2.5 %broadcast_in_dim.9 = bf16[4,4,2,256,256]{4,3,2,1,0:T(8,128)(2,1)} broadcast(bf16[4,2,256,256]{3,2,1,0:T(8,128)(2,1)S(1)} %all-to-all-done), dimensions={1,2,3,4} | broadcast | bytes 5242880 | tf_op jit(solution)/shard_map/broadcast_in_dim | solution.py:208
  48.6 0.0 copy-done
  48.6 0.0 copy-done.7
  48.6 0.0 copy-done.8
  48.6 0.0 copy-done.9
  48.6 4.9 %all-to-all-start.1 = ((bf16[4,4,2,256,256]{4,3,2,1,0:T(8,128)(2,1)}), bf16[4,4,2,256,256]{4,3,2,1,0:T(8,128)(2,1)}, u32[]{:S(2)}, u32[]{:S(2)}) async-start(bf16[4,4,2,256,256]{4,3,2,1,0:T(8,128)(2,1)} %broadcast_in_dim.9), calls=%async_computation.1 | async-start | bytes 8388608 | tf_op jit(solution)/shard_map/all_to_all | solution.py:209
  53.5 0.0 collective-permute-done.4.refs_8_.refs_6_
  53.5 0.0 copy-start.10
  53.5 1.9 %collective-permute-start.5 = (bf16[2,256,256]{2,1,0:T(8,128)(2,1)S(1)}, bf16[2,256,256]{2,1,0:T(8,128)(2,1)S(1)}, u32[]{:S(2)}, u32[]{:S(2)}) collective-permute-start(bf16[2,256,256]{2,1,0:T(8,128)(2,1)S(1)} %collective-permute-done.4.refs_8_.refs_6_), channel_id=1, source_target_pairs={{0,32},{32,64},{64,96},{96,128},{128,160},{160,192},{192,224},{224... | collective-permute-start | bytes 786440 | tf_op jit(solution)/shard_map/ppermute | solution.py:226
  55.4 0.0 collective-permute-done.12.refs_9_.refs_7_
  55.4 2.4 %collective-permute-start.13 = (bf16[2,256,256]{2,1,0:T(8,128)(2,1)S(1)}, bf16[2,256,256]{2,1,0:T(8,128)(2,1)S(1)}, u32[]{:S(2)}, u32[]{:S(2)}) collective-permute-start(bf16[2,256,256]{2,1,0:T(8,128)(2,1)S(1)} %collective-permute-done.12.refs_9_.refs_7_), channel_id=1, source_target_pairs={{0,32},{32,64},{64,96},{96,128},{128,160},{160,192},{192,224},{224... | collective-permute-start | bytes 786440 | tf_op jit(solution)/shard_map/ppermute | solution.py:226
  57.9 3.1 %collective-permute-done.5.refs_10_.refs_8_ = bf16[2,256,256]{2,1,0:T(8,128)(2,1)S(1)} collective-permute-done((bf16[2,256,256]{2,1,0:T(8,128)(2,1)S(1)}, bf16[2,256,256]{2,1,0:T(8,128)(2,1)S(1)}, u32[]{:S(2)}, u32[]{:S(2)}) %collective-permute-start.5) | collective-permute-done | bytes 262176 | tf_op jit(solution)/shard_map/ppermute | solution.py:226
  61.0 3.1 %collective-permute-start.6 = (bf16[2,256,256]{2,1,0:T(8,128)(2,1)S(1)}, bf16[2,256,256]{2,1,0:T(8,128)(2,1)S(1)}, u32[]{:S(2)}, u32[]{:S(2)}) collective-permute-start(bf16[2,256,256]{2,1,0:T(8,128)(2,1)S(1)} %collective-permute-done.5.refs_10_.refs_8_), channel_id=1, source_target_pairs={{0,32},{32,64},{64,96},{96,128},{128,160},{160,192},{192,224},{224... | collective-permute-start | bytes 786440 | tf_op jit(solution)/shard_map/ppermute | solution.py:226
  64.1 0.0 collective-permute-done.13.refs_11_.refs_9_
  64.2 0.0 copy-start.13
  64.2 2.8 %collective-permute-start.14 = (bf16[2,256,256]{2,1,0:T(8,128)(2,1)S(1)}, bf16[2,256,256]{2,1,0:T(8,128)(2,1)S(1)}, u32[]{:S(2)}, u32[]{:S(2)}) collective-permute-start(bf16[2,256,256]{2,1,0:T(8,128)(2,1)S(1)} %collective-permute-done.13.refs_11_.refs_9_), channel_id=1, source_target_pairs={{0,32},{32,64},{64,96},{96,128},{128,160},{160,192},{192,224},{224... | collective-permute-start | bytes 786440 | tf_op jit(solution)/shard_map/ppermute | solution.py:226
  67.0 1.6 %collective-permute-done.6.refs_12_.refs_10_ = bf16[2,256,256]{2,1,0:T(8,128)(2,1)S(1)} collective-permute-done((bf16[2,256,256]{2,1,0:T(8,128)(2,1)S(1)}, bf16[2,256,256]{2,1,0:T(8,128)(2,1)S(1)}, u32[]{:S(2)}, u32[]{:S(2)}) %collective-permute-start.6) | collective-permute-done | bytes 262176 | tf_op jit(solution)/shard_map/ppermute | solution.py:226
  68.5 4.3 %collective-permute-start.7 = (bf16[2,256,256]{2,1,0:T(8,128)(2,1)S(1)}, bf16[2,256,256]{2,1,0:T(8,128)(2,1)S(1)}, u32[]{:S(2)}, u32[]{:S(2)}) collective-permute-start(bf16[2,256,256]{2,1,0:T(8,128)(2,1)S(1)} %collective-permute-done.6.refs_12_.refs_10_), channel_id=1, source_target_pairs={{0,32},{32,64},{64,96},{96,128},{128,160},{160,192},{192,224},{224... | collective-permute-start | bytes 786440 | tf_op jit(solution)/shard_map/ppermute | solution.py:226
  72.9 0.0 collective-permute-done.14.refs_0_
  72.9 2.8 %collective-permute-start.15 = (bf16[2,256,256]{2,1,0:T(8,128)(2,1)S(1)}, bf16[2,256,256]{2,1,0:T(8,128)(2,1)S(1)}, u32[]{:S(2)}, u32[]{:S(2)}) collective-permute-start(bf16[2,256,256]{2,1,0:T(8,128)(2,1)S(1)} %shard_map.29.refs_13_.refs_11_), channel_id=1, source_target_pairs={{0,32},{32,64},{64,96},{96,128},{128,160},{160,192},{192,224},{224... | collective-permute-start | bytes 786440 | tf_op jit(solution)/shard_map/ppermute | solution.py:226
  75.7 0.4 collective-permute-done.7.refs_12_
  76.2 5.4 %collective-permute-start.8 = (bf16[2,256,256]{2,1,0:T(8,128)(2,1)S(1)}, bf16[2,256,256]{2,1,0:T(8,128)(2,1)S(1)}, u32[]{:S(2)}, u32[]{:S(2)}) collective-permute-start(bf16[2,256,256]{2,1,0:T(8,128)(2,1)S(1)} %collective-permute-done.7.refs_12_), channel_id=1, source_target_pairs={{16,496},{48,16},{80,48},{112,80},{144,112},{176,144},{208,176},{2... | collective-permute-start | bytes 786440 | tf_op jit(solution)/shard_map/ppermute | solution.py:226
  81.6 0.0 all-to-all-done.1.left_ref
  81.6 0.7 shard_map.30
  82.3 0.0 collective-permute-done.15.refs_0_
  82.4 0.0 copy-start.2
  82.4 1.9 %collective-permute-start.16 = (bf16[2,256,256]{2,1,0:T(8,128)(2,1)S(1)}, bf16[2,256,256]{2,1,0:T(8,128)(2,1)S(1)}, u32[]{:S(2)}, u32[]{:S(2)}) collective-permute-start(bf16[2,256,256]{2,1,0:T(8,128)(2,1)S(1)} %shard_map.31.refs_13_), channel_id=1, source_target_pairs={{16,496},{48,16},{80,48},{112,80},{144,112},{176,144},{208,176},{2... | collective-permute-start | bytes 786440 | tf_op jit(solution)/shard_map/ppermute | solution.py:226
  84.3 4.6 %shard_map.32 = (f32[2,256,256]{2,1,0:T(8,128)S(1)}, f32[2,256,256]{2,1,0:T(8,128)S(1)}) custom-call(s32[1]{0:T(128)} %bitcast.3.plane_ref, s32[1]{0:T(128)} %bitcast.4.core_ref, bf16[4,4,2,256,256]{4,3,2,1,0:T(8,128)(2,1)} %all-to-all-done.1.left_ref, bf16[2,256,256]{2,1,0:T(8,128)(2,1)} %copy-done.4, ...), custom_call_target="tpu_custom_call", output_to_operand_aliasing={{0}: (17, {}), {1}: (18, {})} | custom-call | flops 1879048192 | bytes 14680064 | tf_op jit(solution)/shard_map/pallas_call | solution.py:112
  88.9 0.0 collective-permute-done.8.refs_0_
  88.9 0.6 collective-permute-done.16.refs_1_
  89.5 1.3 %shard_map.34 = f32[2,256,256]{2,1,0:T(8,128)S(1)} custom-call(s32[1]{0:T(128)} %bitcast.3.plane_ref, s32[1]{0:T(128)} %bitcast.4.core_ref, bf16[4,4,2,256,256]{4,3,2,1,0:T(8,128)(2,1)} %all-to-all-done.1.left_ref, bf16[2,256,256]{2,1,0:T(8,128)(2,1)S(1)} %collective-permute-done.8.refs_0_, ...), custom_call_target="tpu_custom_call", output_to_operand_aliasing={{}: (5, {})} | custom-call | flops 134217728 | bytes 1572864 | tf_op jit(solution)/shard_map/pallas_call | solution.py:112
  90.8 0.0 copy-start.3
  90.8 2.1 %collective-permute-start.17 = (f32[2,256,256]{2,1,0:T(8,128)S(1)}, f32[2,256,256]{2,1,0:T(8,128)S(1)}, u32[]{:S(2)}, u32[]{:S(2)}) collective-permute-start(f32[2,256,256]{2,1,0:T(8,128)S(1)} %shard_map.34), channel_id=1, source_target_pairs={{0,16},{16,0},{1,17},{17,1},{2,18},{18,2},{3,19},{19,3},{4,20},{20... | collective-permute-start | bytes 1572872 | tf_op jit(solution)/shard_map/ppermute | solution.py:231
  92.9 1.3 %shard_map.33.mine_ref = f32[2,256,256]{2,1,0:T(8,128)S(1)} custom-call(s32[1]{0:T(128)} %bitcast.3.plane_ref, s32[1]{0:T(128)} %bitcast.4.core_ref, bf16[4,4,2,256,256]{4,3,2,1,0:T(8,128)(2,1)} %all-to-all-done.1.left_ref, bf16[2,256,256]{2,1,0:T(8,128)(2,1)S(1)} %collective-permute-done.8.refs_0_, ...), custom_call_target="tpu_custom_call", output_to_operand_aliasing={{}: (5, {})} | custom-call | flops 134217728 | bytes 1572864 | tf_op jit(solution)/shard_map/pallas_call | solution.py:112
  94.2 0.5 collective-permute-done.17.other_ref
  94.8 0.7 shard_map.35
  95.5 21.3 %all_to_all.15.parts_ref = f32[32,2,256]{2,1,0:T(2,128)S(1)} all-to-all(f32[32,2,256]{2,1,0:T(2,128)S(1)} %broadcast_in_dim.10), channel_id=1, replica_groups=mesh['z'=16,'core'=2,'y'=4,'x'=4] {'z','core'}, dimensions={0} | all-to-all | bytes 131072 | tf_op jit(solution)/shard_map/all_to_all | solution.py:243
  116.8 1.6 %shard_map.36 = f32[2,256,256]{2,1,0:T(8,128)} custom-call(s32[2]{0:T(128)} %bitcast.10, s32[1]{0:T(128)} %bitcast.1.column_ref, bf16[2,256,256]{2,1,0:T(8,128)(2,1)S(1)} %bitcast.7, f32[2,256,256]{2,1,0:T(8,128)S(1)} %get-tuple-element.15.inflated_ref, f32[32,2,256]{2,1,0:T(2,128)S(1)} %all_to_all.15.parts_ref), custom_call_target="tpu_custom_call" | custom-call | tf_op jit(solution)/shard_map/pallas_call | solution.py:247
  (26 shorter events, 0.1 us)
Async XLA Ops:
  1.1 47.5 %copy-start = (bf16[2,256,256]{2,1,0:T(8,128)(2,1)}, bf16[2,256,256]{2,1,0:T(8,128)(2,1)S(1)}, u32[]{:S(2)}) copy-start(bf16[2,256,256]{2,1,0:T(8,128)(2,1)S(1)} %shard_map.28.refs_0_) | copy-start | bytes 786436
  1.1 14.6 %collective-permute-start = (bf16[2,256,256]{2,1,0:T(8,128)(2,1)S(1)}, bf16[2,256,256]{2,1,0:T(8,128)(2,1)S(1)}, u32[]{:S(2)}, u32[]{:S(2)}) collective-permute-start(bf16[2,256,256]{2,1,0:T(8,128)(2,1)S(1)} %shard_map.28.refs_0_), channel_id=1, source_target_pairs={{0,16},{16,0},{1,17},{17,1},{2,18},{18,2},{3,19},{19,3},{4,20},{20... | collective-permute-start | bytes 786440 | tf_op jit(solution)/shard_map/ppermute | solution.py:187
  9.9 13.8 %collective-permute-start.1 = (bf16[2,256,256]{2,1,0:T(8,128)(2,1)S(1)}, bf16[2,256,256]{2,1,0:T(8,128)(2,1)S(1)}, u32[]{:S(2)}, u32[]{:S(2)}) collective-permute-start(bf16[2,256,256]{2,1,0:T(8,128)(2,1)S(1)} %shard_map.28.refs_0_), channel_id=1, source_target_pairs={{0,32},{32,64},{64,96},{96,128},{128,160},{160,192},{192,224},{224... | collective-permute-start | bytes 786440 | tf_op jit(solution)/shard_map/ppermute | solution.py:226
  15.7 10.6 %copy-start.15 = (bf16[2,256,256]{2,1,0:T(8,128)(2,1)}, bf16[2,256,256]{2,1,0:T(8,128)(2,1)S(1)}, u32[]{:S(2)}) copy-start(bf16[2,256,256]{2,1,0:T(8,128)(2,1)S(1)} %collective-permute-done.refs_1_) | copy-start | bytes 786436
  15.7 10.6 %collective-permute-start.9 = (bf16[2,256,256]{2,1,0:T(8,128)(2,1)S(1)}, bf16[2,256,256]{2,1,0:T(8,128)(2,1)S(1)}, u32[]{:S(2)}, u32[]{:S(2)}) collective-permute-start(bf16[2,256,256]{2,1,0:T(8,128)(2,1)S(1)} %collective-permute-done.refs_1_), channel_id=1, source_target_pairs={{0,32},{32,64},{64,96},{96,128},{128,160},{160,192},{192,224},{224... | collective-permute-start | bytes 786440 | tf_op jit(solution)/shard_map/ppermute | solution.py:226
  19.5 26.6 %all-to-all-start = ((bf16[4,2,256,256]{3,2,1,0:T(8,128)(2,1)}), bf16[4,2,256,256]{3,2,1,0:T(8,128)(2,1)S(1)}, u32[]{:S(2)}, u32[]{:S(2)}) async-start(bf16[4,2,256,256]{3,2,1,0:T(8,128)(2,1)} %broadcast_in_dim.8), calls=%async_computation | async-start | bytes 2097152 | tf_op jit(solution)/shard_map/all_to_all | solution.py:209
  23.7 24.9 %copy-start.4 = (bf16[2,256,256]{2,1,0:T(8,128)(2,1)}, bf16[2,256,256]{2,1,0:T(8,128)(2,1)S(1)}, u32[]{:S(2)}) copy-start(bf16[2,256,256]{2,1,0:T(8,128)(2,1)S(1)} %collective-permute-done.1.refs_2_.refs_0_) | copy-start | bytes 786436
  23.7 7.4 %collective-permute-start.2 = (bf16[2,256,256]{2,1,0:T(8,128)(2,1)S(1)}, bf16[2,256,256]{2,1,0:T(8,128)(2,1)S(1)}, u32[]{:S(2)}, u32[]{:S(2)}) collective-permute-start(bf16[2,256,256]{2,1,0:T(8,128)(2,1)S(1)} %collective-permute-done.1.refs_2_.refs_0_), channel_id=1, source_target_pairs={{0,32},{32,64},{64,96},{96,128},{128,160},{160,192},{192,224},{224... | collective-permute-start | bytes 786440 | tf_op jit(solution)/shard_map/ppermute | solution.py:226
  26.3 22.3 %copy-start.5 = (bf16[2,256,256]{2,1,0:T(8,128)(2,1)}, bf16[2,256,256]{2,1,0:T(8,128)(2,1)S(1)}, u32[]{:S(2)}) copy-start(bf16[2,256,256]{2,1,0:T(8,128)(2,1)S(1)} %collective-permute-done.9.refs_3_.refs_1_) | copy-start | bytes 786436
  26.3 8.6 %collective-permute-start.10 = (bf16[2,256,256]{2,1,0:T(8,128)(2,1)S(1)}, bf16[2,256,256]{2,1,0:T(8,128)(2,1)S(1)}, u32[]{:S(2)}, u32[]{:S(2)}) collective-permute-start(bf16[2,256,256]{2,1,0:T(8,128)(2,1)S(1)} %collective-permute-done.9.refs_3_.refs_1_), channel_id=1, source_target_pairs={{0,32},{32,64},{64,96},{96,128},{128,160},{160,192},{192,224},{224... | collective-permute-start | bytes 786440 | tf_op jit(solution)/shard_map/ppermute | solution.py:226
  31.1 17.5 %copy-start.6 = (bf16[2,256,256]{2,1,0:T(8,128)(2,1)}, bf16[2,256,256]{2,1,0:T(8,128)(2,1)S(1)}, u32[]{:S(2)}) copy-start(bf16[2,256,256]{2,1,0:T(8,128)(2,1)S(1)} %collective-permute-done.2.refs_4_.refs_2_) | copy-start | bytes 786436
  31.1 7.4 %collective-permute-start.3 = (bf16[2,256,256]{2,1,0:T(8,128)(2,1)S(1)}, bf16[2,256,256]{2,1,0:T(8,128)(2,1)S(1)}, u32[]{:S(2)}, u32[]{:S(2)}) collective-permute-start(bf16[2,256,256]{2,1,0:T(8,128)(2,1)S(1)} %collective-permute-done.2.refs_4_.refs_2_), channel_id=1, source_target_pairs={{0,32},{32,64},{64,96},{96,128},{128,160},{160,192},{192,224},{224... | collective-permute-start | bytes 786440 | tf_op jit(solution)/shard_map/ppermute | solution.py:226
  34.9 13.7 %copy-start.7 = (bf16[2,256,256]{2,1,0:T(8,128)(2,1)}, bf16[2,256,256]{2,1,0:T(8,128)(2,1)S(1)}, u32[]{:S(2)}) copy-start(bf16[2,256,256]{2,1,0:T(8,128)(2,1)S(1)} %collective-permute-done.10.refs_5_.refs_3_) | copy-start | bytes 786436
  34.9 8.3 %collective-permute-start.11 = (bf16[2,256,256]{2,1,0:T(8,128)(2,1)S(1)}, bf16[2,256,256]{2,1,0:T(8,128)(2,1)S(1)}, u32[]{:S(2)}, u32[]{:S(2)}) collective-permute-start(bf16[2,256,256]{2,1,0:T(8,128)(2,1)S(1)} %collective-permute-done.10.refs_5_.refs_3_), channel_id=1, source_target_pairs={{0,32},{32,64},{64,96},{96,128},{128,160},{160,192},{192,224},{224... | collective-permute-start | bytes 786440 | tf_op jit(solution)/shard_map/ppermute | solution.py:226
  38.5 10.1 %copy-start.8 = (bf16[2,256,256]{2,1,0:T(8,128)(2,1)}, bf16[2,256,256]{2,1,0:T(8,128)(2,1)S(1)}, u32[]{:S(2)}) copy-start(bf16[2,256,256]{2,1,0:T(8,128)(2,1)S(1)} %collective-permute-done.3.refs_6_.refs_4_) | copy-start | bytes 786436
  38.5 15.0 %collective-permute-start.4 = (bf16[2,256,256]{2,1,0:T(8,128)(2,1)S(1)}, bf16[2,256,256]{2,1,0:T(8,128)(2,1)S(1)}, u32[]{:S(2)}, u32[]{:S(2)}) collective-permute-start(bf16[2,256,256]{2,1,0:T(8,128)(2,1)S(1)} %collective-permute-done.3.refs_6_.refs_4_), channel_id=1, source_target_pairs={{0,32},{32,64},{64,96},{96,128},{128,160},{160,192},{192,224},{224... | collective-permute-start | bytes 786440 | tf_op jit(solution)/shard_map/ppermute | solution.py:226
  43.2 5.4 %copy-start.9 = (bf16[2,256,256]{2,1,0:T(8,128)(2,1)}, bf16[2,256,256]{2,1,0:T(8,128)(2,1)S(1)}, u32[]{:S(2)}) copy-start(bf16[2,256,256]{2,1,0:T(8,128)(2,1)S(1)} %collective-permute-done.11.refs_7_.refs_5_) | copy-start | bytes 786436
  43.2 12.2 %collective-permute-start.12 = (bf16[2,256,256]{2,1,0:T(8,128)(2,1)S(1)}, bf16[2,256,256]{2,1,0:T(8,128)(2,1)S(1)}, u32[]{:S(2)}, u32[]{:S(2)}) collective-permute-start(bf16[2,256,256]{2,1,0:T(8,128)(2,1)S(1)} %collective-permute-done.11.refs_7_.refs_5_), channel_id=1, source_target_pairs={{0,32},{32,64},{64,96},{96,128},{128,160},{160,192},{192,224},{224... | collective-permute-start | bytes 786440 | tf_op jit(solution)/shard_map/ppermute | solution.py:226
  48.6 33.0 %all-to-all-start.1 = ((bf16[4,4,2,256,256]{4,3,2,1,0:T(8,128)(2,1)}), bf16[4,4,2,256,256]{4,3,2,1,0:T(8,128)(2,1)}, u32[]{:S(2)}, u32[]{:S(2)}) async-start(bf16[4,4,2,256,256]{4,3,2,1,0:T(8,128)(2,1)} %broadcast_in_dim.9), calls=%async_computation.1 | async-start | bytes 8388608 | tf_op jit(solution)/shard_map/all_to_all | solution.py:209
  53.5 19.4 %copy-start.10 = (bf16[2,256,256]{2,1,0:T(8,128)(2,1)}, bf16[2,256,256]{2,1,0:T(8,128)(2,1)S(1)}, u32[]{:S(2)}) copy-start(bf16[2,256,256]{2,1,0:T(8,128)(2,1)S(1)} %collective-permute-done.4.refs_8_.refs_6_) | copy-start | bytes 786436
  53.5 7.5 %collective-permute-start.5 = (bf16[2,256,256]{2,1,0:T(8,128)(2,1)S(1)}, bf16[2,256,256]{2,1,0:T(8,128)(2,1)S(1)}, u32[]{:S(2)}, u32[]{:S(2)}) collective-permute-start(bf16[2,256,256]{2,1,0:T(8,128)(2,1)S(1)} %collective-permute-done.4.refs_8_.refs_6_), channel_id=1, source_target_pairs={{0,32},{32,64},{64,96},{96,128},{128,160},{160,192},{192,224},{224... | collective-permute-start | bytes 786440 | tf_op jit(solution)/shard_map/ppermute | solution.py:226
  55.4 17.5 %copy-start.11 = (bf16[2,256,256]{2,1,0:T(8,128)(2,1)}, bf16[2,256,256]{2,1,0:T(8,128)(2,1)S(1)}, u32[]{:S(2)}) copy-start(bf16[2,256,256]{2,1,0:T(8,128)(2,1)S(1)} %collective-permute-done.12.refs_9_.refs_7_) | copy-start | bytes 786436
  55.4 8.7 %collective-permute-start.13 = (bf16[2,256,256]{2,1,0:T(8,128)(2,1)S(1)}, bf16[2,256,256]{2,1,0:T(8,128)(2,1)S(1)}, u32[]{:S(2)}, u32[]{:S(2)}) collective-permute-start(bf16[2,256,256]{2,1,0:T(8,128)(2,1)S(1)} %collective-permute-done.12.refs_9_.refs_7_), channel_id=1, source_target_pairs={{0,32},{32,64},{64,96},{96,128},{128,160},{160,192},{192,224},{224... | collective-permute-start | bytes 786440 | tf_op jit(solution)/shard_map/ppermute | solution.py:226
  61.0 11.9 %copy-start.12 = (bf16[2,256,256]{2,1,0:T(8,128)(2,1)}, bf16[2,256,256]{2,1,0:T(8,128)(2,1)S(1)}, u32[]{:S(2)}) copy-start(bf16[2,256,256]{2,1,0:T(8,128)(2,1)S(1)} %collective-permute-done.5.refs_10_.refs_8_) | copy-start | bytes 786436
  61.0 7.5 %collective-permute-start.6 = (bf16[2,256,256]{2,1,0:T(8,128)(2,1)S(1)}, bf16[2,256,256]{2,1,0:T(8,128)(2,1)S(1)}, u32[]{:S(2)}, u32[]{:S(2)}) collective-permute-start(bf16[2,256,256]{2,1,0:T(8,128)(2,1)S(1)} %collective-permute-done.5.refs_10_.refs_8_), channel_id=1, source_target_pairs={{0,32},{32,64},{64,96},{96,128},{128,160},{160,192},{192,224},{224... | collective-permute-start | bytes 786440 | tf_op jit(solution)/shard_map/ppermute | solution.py:226
  64.2 8.8 %copy-start.13 = (bf16[2,256,256]{2,1,0:T(8,128)(2,1)}, bf16[2,256,256]{2,1,0:T(8,128)(2,1)S(1)}, u32[]{:S(2)}) copy-start(bf16[2,256,256]{2,1,0:T(8,128)(2,1)S(1)} %collective-permute-done.13.refs_11_.refs_9_) | copy-start | bytes 786436
  64.2 8.7 %collective-permute-start.14 = (bf16[2,256,256]{2,1,0:T(8,128)(2,1)S(1)}, bf16[2,256,256]{2,1,0:T(8,128)(2,1)S(1)}, u32[]{:S(2)}, u32[]{:S(2)}) collective-permute-start(bf16[2,256,256]{2,1,0:T(8,128)(2,1)S(1)} %collective-permute-done.13.refs_11_.refs_9_), channel_id=1, source_target_pairs={{0,32},{32,64},{64,96},{96,128},{128,160},{160,192},{192,224},{224... | collective-permute-start | bytes 786440 | tf_op jit(solution)/shard_map/ppermute | solution.py:226
  68.5 4.4 %copy-start.14 = (bf16[2,256,256]{2,1,0:T(8,128)(2,1)}, bf16[2,256,256]{2,1,0:T(8,128)(2,1)S(1)}, u32[]{:S(2)}) copy-start(bf16[2,256,256]{2,1,0:T(8,128)(2,1)S(1)} %collective-permute-done.6.refs_12_.refs_10_) | copy-start | bytes 786436
  68.5 7.6 %collective-permute-start.7 = (bf16[2,256,256]{2,1,0:T(8,128)(2,1)S(1)}, bf16[2,256,256]{2,1,0:T(8,128)(2,1)S(1)}, u32[]{:S(2)}, u32[]{:S(2)}) collective-permute-start(bf16[2,256,256]{2,1,0:T(8,128)(2,1)S(1)} %collective-permute-done.6.refs_12_.refs_10_), channel_id=1, source_target_pairs={{0,32},{32,64},{64,96},{96,128},{128,160},{160,192},{192,224},{224... | collective-permute-start | bytes 786440 | tf_op jit(solution)/shard_map/ppermute | solution.py:226
  72.9 8.7 %copy-start.1 = (bf16[2,256,256]{2,1,0:T(8,128)(2,1)}, bf16[2,256,256]{2,1,0:T(8,128)(2,1)S(1)}, u32[]{:S(2)}) copy-start(bf16[2,256,256]{2,1,0:T(8,128)(2,1)S(1)} %shard_map.29.refs_13_.refs_11_) | copy-start | bytes 786436
  72.9 9.4 %collective-permute-start.15 = (bf16[2,256,256]{2,1,0:T(8,128)(2,1)S(1)}, bf16[2,256,256]{2,1,0:T(8,128)(2,1)S(1)}, u32[]{:S(2)}, u32[]{:S(2)}) collective-permute-start(bf16[2,256,256]{2,1,0:T(8,128)(2,1)S(1)} %shard_map.29.refs_13_.refs_11_), channel_id=1, source_target_pairs={{0,32},{32,64},{64,96},{96,128},{128,160},{160,192},{192,224},{224... | collective-permute-start | bytes 786440 | tf_op jit(solution)/shard_map/ppermute | solution.py:226
  76.2 6.2 %copy-start.16 = (bf16[2,256,256]{2,1,0:T(8,128)(2,1)}, bf16[2,256,256]{2,1,0:T(8,128)(2,1)S(1)}, u32[]{:S(2)}) copy-start(bf16[2,256,256]{2,1,0:T(8,128)(2,1)S(1)} %collective-permute-done.7.refs_12_) | copy-start | bytes 786436
  76.2 12.7 %collective-permute-start.8 = (bf16[2,256,256]{2,1,0:T(8,128)(2,1)S(1)}, bf16[2,256,256]{2,1,0:T(8,128)(2,1)S(1)}, u32[]{:S(2)}, u32[]{:S(2)}) collective-permute-start(bf16[2,256,256]{2,1,0:T(8,128)(2,1)S(1)} %collective-permute-done.7.refs_12_), channel_id=1, source_target_pairs={{16,496},{48,16},{80,48},{112,80},{144,112},{176,144},{208,176},{2... | collective-permute-start | bytes 786440 | tf_op jit(solution)/shard_map/ppermute | solution.py:226
  82.4 1.9 %copy-start.2 = (bf16[2,256,256]{2,1,0:T(8,128)(2,1)}, bf16[2,256,256]{2,1,0:T(8,128)(2,1)S(1)}, u32[]{:S(2)}) copy-start(bf16[2,256,256]{2,1,0:T(8,128)(2,1)S(1)} %shard_map.31.refs_13_) | copy-start | bytes 786436
  82.4 7.1 %collective-permute-start.16 = (bf16[2,256,256]{2,1,0:T(8,128)(2,1)S(1)}, bf16[2,256,256]{2,1,0:T(8,128)(2,1)S(1)}, u32[]{:S(2)}, u32[]{:S(2)}) collective-permute-start(bf16[2,256,256]{2,1,0:T(8,128)(2,1)S(1)} %shard_map.31.refs_13_), channel_id=1, source_target_pairs={{16,496},{48,16},{80,48},{112,80},{144,112},{176,144},{208,176},{2... | collective-permute-start | bytes 786440 | tf_op jit(solution)/shard_map/ppermute | solution.py:226
  90.8 26.0 %copy-start.3 = (bf16[1,2,256,256]{3,2,1,0:T(8,128)(2,1)S(1)}, bf16[1,2,256,256]{3,2,1,0:T(8,128)(2,1)}, u32[]{:S(2)}) copy-start(bf16[1,2,256,256]{3,2,1,0:T(8,128)(2,1)} %param.3) | copy-start | bytes 786436
  90.8 3.9 %collective-permute-start.17 = (f32[2,256,256]{2,1,0:T(8,128)S(1)}, f32[2,256,256]{2,1,0:T(8,128)S(1)}, u32[]{:S(2)}, u32[]{:S(2)}) collective-permute-start(f32[2,256,256]{2,1,0:T(8,128)S(1)} %shard_map.34), channel_id=1, source_target_pairs={{0,16},{16,0},{1,17},{17,1},{2,18},{18,2},{3,19},{19,3},{4,20},{20... | collective-permute-start | bytes 1572872 | tf_op jit(solution)/shard_map/ppermute | solution.py:231

commit v10 on v9

--- a/solution.py
+++ b/solution.py
@@ -240,8 +240,14 @@
         ],
         compiler_params=params(6),
     )(own, column_ref, total, received)
+    far = [(i + planes * cores // 2) % (planes * cores) for i in range(planes * cores)]
     parts = lax.all_to_all(
-        jnp.broadcast_to(sums[None], (planes * cores, *sums.shape)), ROWS, 0, 0, tiled=True
+        jnp.broadcast_to(sums[None], (planes * cores, *sums.shape)),
+        ROWS,
+        0,
+        0,
+        axis_index_groups=[far],
+        tiled=True,
     )
     scale = float(planes * cores * width)
     out = pl.pallas_call(

time: 120 us -> 114 us (0.950)
  blocking collectives: 21.3 us -> 16.1 us
    all_to_all x1, blocking collectives: 21.3 us -> 16.1 us  [on_device(): lax.all_to_all(jnp.broadcast_to(sums[None], (planes * cores, *sums.shape)...]
where the time goes in v10:
time: 114 us; the launch traced here: 113 us
  starting transfers between devices  72.1 us (63%)
  blocking collectives  16.1 us (14%)
  Pallas kernels  11.4 us (10%)
  waiting for transfers between devices  9.4 us (8%)
  local copies, waits for them, and re-layouts  3.67 us (3%)
    ppermute x16, starting transfers between devices, on_device(): held.append(tuple((lax.ppermute(t, ROWS, perm) for t in held[-1])))  52.2 us
    all_to_all x1, blocking collectives, on_device(): lax.all_to_all(jnp.broadcast_to(sums[None], (planes * cores, *sums.shape)...  16.1 us
    all_to_all x2, starting transfers between devices, copy_for_each(): lax.all_to_all(spread, ('core', *COLS), 0, 0, axis_index_groups=lines, ti...  9.05 us
    ppermute x16, waiting for transfers between devices, on_device(): held.append(tuple((lax.ppermute(t, ROWS, perm) for t in held[-1])))  8.86 us
    ppermute x1, starting transfers between devices, on_device(): other = lax.ppermute(mine, 'core', SWAP)  8.79 us
    pallas_call x4, Pallas kernels, products(): pl.pallas_call(kernel, in_specs=[SMEM, SMEM, HBM] + [HBM] * len(tiles) +...  7.95 us
    broadcast_in_dim x2, local copies, waits for them, and re-layouts, copy_for_each(): spread = jnp.broadcast_to(value[None], (len(lines[0]), *value.shape))  3.57 us
  transfers between devices with their start and end apart: 20, of which 7 were waited for; matrix products, arithmetic and copies ran while one was open for 3% of the time, Pallas kernels for 6%

profile of v10, /device:TPU:1, one launch (start us, length us, event | category | flops | bytes accessed | tf_op | source)
XLA Modules:
  0.0 113.3 jit_solution(17823773586480796358)
XLA Ops:
  0.0 1.1 shard_map.28.refs_0_
  1.1 0.0 copy-start
  1.1 8.8 %collective-permute-start = (bf16[2,256,256]{2,1,0:T(8,128)(2,1)S(1)}, bf16[2,256,256]{2,1,0:T(8,128)(2,1)S(1)}, u32[]{:S(2)}, u32[]{:S(2)}) collective-permute-start(bf16[2,256,256]{2,1,0:T(8,128)(2,1)S(1)} %shard_map.28.refs_0_), channel_id=1, source_target_pairs={{0,16},{16,0},{1,17},{17,1},{2,18},{18,2},{3,19},{19,3},{4,20},{20... | collective-permute-start | bytes 786440 | tf_op jit(solution)/shard_map/ppermute | solution.py:187
  9.9 5.7 %collective-permute-start.1 = (bf16[2,256,256]{2,1,0:T(8,128)(2,1)S(1)}, bf16[2,256,256]{2,1,0:T(8,128)(2,1)S(1)}, u32[]{:S(2)}, u32[]{:S(2)}) collective-permute-start(bf16[2,256,256]{2,1,0:T(8,128)(2,1)S(1)} %shard_map.28.refs_0_), channel_id=1, source_target_pairs={{0,32},{32,64},{64,96},{96,128},{128,160},{160,192},{192,224},{224... | collective-permute-start | bytes 786440 | tf_op jit(solution)/shard_map/ppermute | solution.py:226
  15.7 0.0 collective-permute-done.refs_1_
  15.7 0.0 copy-start.15
  15.7 2.6 %collective-permute-start.9 = (bf16[2,256,256]{2,1,0:T(8,128)(2,1)S(1)}, bf16[2,256,256]{2,1,0:T(8,128)(2,1)S(1)}, u32[]{:S(2)}, u32[]{:S(2)}) collective-permute-start(bf16[2,256,256]{2,1,0:T(8,128)(2,1)S(1)} %collective-permute-done.refs_1_), channel_id=1, source_target_pairs={{0,32},{32,64},{64,96},{96,128},{128,160},{160,192},{192,224},{224... | collective-permute-start | bytes 786440 | tf_op jit(solution)/shard_map/ppermute | solution.py:226
  18.4 1.1 broadcast_in_dim.8
  19.5 4.2 %all-to-all-start = ((bf16[4,2,256,256]{3,2,1,0:T(8,128)(2,1)}), bf16[4,2,256,256]{3,2,1,0:T(8,128)(2,1)S(1)}, u32[]{:S(2)}, u32[]{:S(2)}) async-start(bf16[4,2,256,256]{3,2,1,0:T(8,128)(2,1)} %broadcast_in_dim.8), calls=%async_computation | async-start | bytes 2097152 | tf_op jit(solution)/shard_map/all_to_all | solution.py:209
  23.6 0.0 collective-permute-done.1.refs_2_.refs_0_
  23.7 2.6 %collective-permute-start.2 = (bf16[2,256,256]{2,1,0:T(8,128)(2,1)S(1)}, bf16[2,256,256]{2,1,0:T(8,128)(2,1)S(1)}, u32[]{:S(2)}, u32[]{:S(2)}) collective-permute-start(bf16[2,256,256]{2,1,0:T(8,128)(2,1)S(1)} %collective-permute-done.1.refs_2_.refs_0_), channel_id=1, source_target_pairs={{0,32},{32,64},{64,96},{96,128},{128,160},{160,192},{192,224},{224... | collective-permute-start | bytes 786440 | tf_op jit(solution)/shard_map/ppermute | solution.py:226
  26.3 0.0 copy-done.15
  26.3 0.0 collective-permute-done.9.refs_3_.refs_1_
  26.3 0.0 copy-start.5
  26.3 2.6 %collective-permute-start.10 = (bf16[2,256,256]{2,1,0:T(8,128)(2,1)S(1)}, bf16[2,256,256]{2,1,0:T(8,128)(2,1)S(1)}, u32[]{:S(2)}, u32[]{:S(2)}) collective-permute-start(bf16[2,256,256]{2,1,0:T(8,128)(2,1)S(1)} %collective-permute-done.9.refs_3_.refs_1_), channel_id=1, source_target_pairs={{0,32},{32,64},{64,96},{96,128},{128,160},{160,192},{192,224},{224... | collective-permute-start | bytes 786440 | tf_op jit(solution)/shard_map/ppermute | solution.py:226
  29.0 2.1 %collective-permute-done.2.refs_4_.refs_2_ = bf16[2,256,256]{2,1,0:T(8,128)(2,1)S(1)} collective-permute-done((bf16[2,256,256]{2,1,0:T(8,128)(2,1)S(1)}, bf16[2,256,256]{2,1,0:T(8,128)(2,1)S(1)}, u32[]{:S(2)}, u32[]{:S(2)}) %collective-permute-start.2) | collective-permute-done | bytes 262176 | tf_op jit(solution)/shard_map/ppermute | solution.py:226
  31.1 3.8 %collective-permute-start.3 = (bf16[2,256,256]{2,1,0:T(8,128)(2,1)S(1)}, bf16[2,256,256]{2,1,0:T(8,128)(2,1)S(1)}, u32[]{:S(2)}, u32[]{:S(2)}) collective-permute-start(bf16[2,256,256]{2,1,0:T(8,128)(2,1)S(1)} %collective-permute-done.2.refs_4_.refs_2_), channel_id=1, source_target_pairs={{0,32},{32,64},{64,96},{96,128},{128,160},{160,192},{192,224},{224... | collective-permute-start | bytes 786440 | tf_op jit(solution)/shard_map/ppermute | solution.py:226
  34.9 0.0 collective-permute-done.10.refs_5_.refs_3_
  34.9 0.0 copy-start.7
  34.9 2.5 %collective-permute-start.11 = (bf16[2,256,256]{2,1,0:T(8,128)(2,1)S(1)}, bf16[2,256,256]{2,1,0:T(8,128)(2,1)S(1)}, u32[]{:S(2)}, u32[]{:S(2)}) collective-permute-start(bf16[2,256,256]{2,1,0:T(8,128)(2,1)S(1)} %collective-permute-done.10.refs_5_.refs_3_), channel_id=1, source_target_pairs={{0,32},{32,64},{64,96},{96,128},{128,160},{160,192},{192,224},{224... | collective-permute-start | bytes 786440 | tf_op jit(solution)/shard_map/ppermute | solution.py:226
  37.4 1.0 collective-permute-done.3.refs_6_.refs_4_
  38.5 4.8 %collective-permute-start.4 = (bf16[2,256,256]{2,1,0:T(8,128)(2,1)S(1)}, bf16[2,256,256]{2,1,0:T(8,128)(2,1)S(1)}, u32[]{:S(2)}, u32[]{:S(2)}) collective-permute-start(bf16[2,256,256]{2,1,0:T(8,128)(2,1)S(1)} %collective-permute-done.3.refs_6_.refs_4_), channel_id=1, source_target_pairs={{0,32},{32,64},{64,96},{96,128},{128,160},{160,192},{192,224},{224... | collective-permute-start | bytes 786440 | tf_op jit(solution)/shard_map/ppermute | solution.py:226
  43.2 0.0 collective-permute-done.11.refs_7_.refs_5_
  43.2 0.0 copy-start.9
  43.2 2.8 %collective-permute-start.12 = (bf16[2,256,256]{2,1,0:T(8,128)(2,1)S(1)}, bf16[2,256,256]{2,1,0:T(8,128)(2,1)S(1)}, u32[]{:S(2)}, u32[]{:S(2)}) collective-permute-start(bf16[2,256,256]{2,1,0:T(8,128)(2,1)S(1)} %collective-permute-done.11.refs_7_.refs_5_), channel_id=1, source_target_pairs={{0,32},{32,64},{64,96},{96,128},{128,160},{160,192},{192,224},{224... | collective-permute-start | bytes 786440 | tf_op jit(solution)/shard_map/ppermute | solution.py:226
  46.0 0.0 all-to-all-done
  46.0 2.5 %broadcast_in_dim.9 = bf16[4,4,2,256,256]{4,3,2,1,0:T(8,128)(2,1)} broadcast(bf16[4,2,256,256]{3,2,1,0:T(8,128)(2,1)S(1)} %all-to-all-done), dimensions={1,2,3,4} | broadcast | bytes 5242880 | tf_op jit(solution)/shard_map/broadcast_in_dim | solution.py:208
  48.6 0.0 copy-done
  48.6 0.0 copy-done.7
  48.6 0.0 copy-done.8
  48.6 0.0 copy-done.9
  48.6 4.9 %all-to-all-start.1 = ((bf16[4,4,2,256,256]{4,3,2,1,0:T(8,128)(2,1)}), bf16[4,4,2,256,256]{4,3,2,1,0:T(8,128)(2,1)}, u32[]{:S(2)}, u32[]{:S(2)}) async-start(bf16[4,4,2,256,256]{4,3,2,1,0:T(8,128)(2,1)} %broadcast_in_dim.9), calls=%async_computation.1 | async-start | bytes 8388608 | tf_op jit(solution)/shard_map/all_to_all | solution.py:209
  53.5 0.0 collective-permute-done.4.refs_8_.refs_6_
  53.5 0.0 copy-start.10
  53.5 1.9 %collective-permute-start.5 = (bf16[2,256,256]{2,1,0:T(8,128)(2,1)S(1)}, bf16[2,256,256]{2,1,0:T(8,128)(2,1)S(1)}, u32[]{:S(2)}, u32[]{:S(2)}) collective-permute-start(bf16[2,256,256]{2,1,0:T(8,128)(2,1)S(1)} %collective-permute-done.4.refs_8_.refs_6_), channel_id=1, source_target_pairs={{0,32},{32,64},{64,96},{96,128},{128,160},{160,192},{192,224},{224... | collective-permute-start | bytes 786440 | tf_op jit(solution)/shard_map/ppermute | solution.py:226
  55.4 0.0 collective-permute-done.12.refs_9_.refs_7_
  55.4 2.4 %collective-permute-start.13 = (bf16[2,256,256]{2,1,0:T(8,128)(2,1)S(1)}, bf16[2,256,256]{2,1,0:T(8,128)(2,1)S(1)}, u32[]{:S(2)}, u32[]{:S(2)}) collective-permute-start(bf16[2,256,256]{2,1,0:T(8,128)(2,1)S(1)} %collective-permute-done.12.refs_9_.refs_7_), channel_id=1, source_target_pairs={{0,32},{32,64},{64,96},{96,128},{128,160},{160,192},{192,224},{224... | collective-permute-start | bytes 786440 | tf_op jit(solution)/shard_map/ppermute | solution.py:226
  57.9 3.1 %collective-permute-done.5.refs_10_.refs_8_ = bf16[2,256,256]{2,1,0:T(8,128)(2,1)S(1)} collective-permute-done((bf16[2,256,256]{2,1,0:T(8,128)(2,1)S(1)}, bf16[2,256,256]{2,1,0:T(8,128)(2,1)S(1)}, u32[]{:S(2)}, u32[]{:S(2)}) %collective-permute-start.5) | collective-permute-done | bytes 262176 | tf_op jit(solution)/shard_map/ppermute | solution.py:226
  61.0 3.1 %collective-permute-start.6 = (bf16[2,256,256]{2,1,0:T(8,128)(2,1)S(1)}, bf16[2,256,256]{2,1,0:T(8,128)(2,1)S(1)}, u32[]{:S(2)}, u32[]{:S(2)}) collective-permute-start(bf16[2,256,256]{2,1,0:T(8,128)(2,1)S(1)} %collective-permute-done.5.refs_10_.refs_8_), channel_id=1, source_target_pairs={{0,32},{32,64},{64,96},{96,128},{128,160},{160,192},{192,224},{224... | collective-permute-start | bytes 786440 | tf_op jit(solution)/shard_map/ppermute | solution.py:226
  64.1 0.0 collective-permute-done.13.refs_11_.refs_9_
  64.2 0.0 copy-start.13
  64.2 2.8 %collective-permute-start.14 = (bf16[2,256,256]{2,1,0:T(8,128)(2,1)S(1)}, bf16[2,256,256]{2,1,0:T(8,128)(2,1)S(1)}, u32[]{:S(2)}, u32[]{:S(2)}) collective-permute-start(bf16[2,256,256]{2,1,0:T(8,128)(2,1)S(1)} %collective-permute-done.13.refs_11_.refs_9_), channel_id=1, source_target_pairs={{0,32},{32,64},{64,96},{96,128},{128,160},{160,192},{192,224},{224... | collective-permute-start | bytes 786440 | tf_op jit(solution)/shard_map/ppermute | solution.py:226
  67.0 1.6 %collective-permute-done.6.refs_12_.refs_10_ = bf16[2,256,256]{2,1,0:T(8,128)(2,1)S(1)} collective-permute-done((bf16[2,256,256]{2,1,0:T(8,128)(2,1)S(1)}, bf16[2,256,256]{2,1,0:T(8,128)(2,1)S(1)}, u32[]{:S(2)}, u32[]{:S(2)}) %collective-permute-start.6) | collective-permute-done | bytes 262176 | tf_op jit(solution)/shard_map/ppermute | solution.py:226
  68.5 4.3 %collective-permute-start.7 = (bf16[2,256,256]{2,1,0:T(8,128)(2,1)S(1)}, bf16[2,256,256]{2,1,0:T(8,128)(2,1)S(1)}, u32[]{:S(2)}, u32[]{:S(2)}) collective-permute-start(bf16[2,256,256]{2,1,0:T(8,128)(2,1)S(1)} %collective-permute-done.6.refs_12_.refs_10_), channel_id=1, source_target_pairs={{0,32},{32,64},{64,96},{96,128},{128,160},{160,192},{192,224},{224... | collective-permute-start | bytes 786440 | tf_op jit(solution)/shard_map/ppermute | solution.py:226
  72.9 0.0 collective-permute-done.14.refs_0_
  72.9 2.8 %collective-permute-start.15 = (bf16[2,256,256]{2,1,0:T(8,128)(2,1)S(1)}, bf16[2,256,256]{2,1,0:T(8,128)(2,1)S(1)}, u32[]{:S(2)}, u32[]{:S(2)}) collective-permute-start(bf16[2,256,256]{2,1,0:T(8,128)(2,1)S(1)} %shard_map.29.refs_13_.refs_11_), channel_id=1, source_target_pairs={{0,32},{32,64},{64,96},{96,128},{128,160},{160,192},{192,224},{224... | collective-permute-start | bytes 786440 | tf_op jit(solution)/shard_map/ppermute | solution.py:226
  75.7 0.4 collective-permute-done.7.refs_12_
  76.2 5.4 %collective-permute-start.8 = (bf16[2,256,256]{2,1,0:T(8,128)(2,1)S(1)}, bf16[2,256,256]{2,1,0:T(8,128)(2,1)S(1)}, u32[]{:S(2)}, u32[]{:S(2)}) collective-permute-start(bf16[2,256,256]{2,1,0:T(8,128)(2,1)S(1)} %collective-permute-done.7.refs_12_), channel_id=1, source_target_pairs={{16,496},{48,16},{80,48},{112,80},{144,112},{176,144},{208,176},{2... | collective-permute-start | bytes 786440 | tf_op jit(solution)/shard_map/ppermute | solution.py:226
  81.6 0.0 all-to-all-done.1.left_ref
  81.6 0.7 shard_map.30
  82.3 0.0 collective-permute-done.15.refs_0_
  82.4 0.0 copy-start.2
  82.4 1.9 %collective-permute-start.16 = (bf16[2,256,256]{2,1,0:T(8,128)(2,1)S(1)}, bf16[2,256,256]{2,1,0:T(8,128)(2,1)S(1)}, u32[]{:S(2)}, u32[]{:S(2)}) collective-permute-start(bf16[2,256,256]{2,1,0:T(8,128)(2,1)S(1)} %shard_map.31.refs_13_), channel_id=1, source_target_pairs={{16,496},{48,16},{80,48},{112,80},{144,112},{176,144},{208,176},{2... | collective-permute-start | bytes 786440 | tf_op jit(solution)/shard_map/ppermute | solution.py:226
  84.3 4.6 %shard_map.32 = (f32[2,256,256]{2,1,0:T(8,128)S(1)}, f32[2,256,256]{2,1,0:T(8,128)S(1)}) custom-call(s32[1]{0:T(128)} %bitcast.3.plane_ref, s32[1]{0:T(128)} %bitcast.4.core_ref, bf16[4,4,2,256,256]{4,3,2,1,0:T(8,128)(2,1)} %all-to-all-done.1.left_ref, bf16[2,256,256]{2,1,0:T(8,128)(2,1)} %copy-done.4, ...), custom_call_target="tpu_custom_call", output_to_operand_aliasing={{0}: (17, {}), {1}: (18, {})} | custom-call | flops 1879048192 | bytes 14680064 | tf_op jit(solution)/shard_map/pallas_call | solution.py:112
  88.9 0.0 collective-permute-done.8.refs_0_
  88.9 0.6 collective-permute-done.16.refs_1_
  89.5 1.3 %shard_map.34 = f32[2,256,256]{2,1,0:T(8,128)S(1)} custom-call(s32[1]{0:T(128)} %bitcast.3.plane_ref, s32[1]{0:T(128)} %bitcast.4.core_ref, bf16[4,4,2,256,256]{4,3,2,1,0:T(8,128)(2,1)} %all-to-all-done.1.left_ref, bf16[2,256,256]{2,1,0:T(8,128)(2,1)S(1)} %collective-permute-done.8.refs_0_, ...), custom_call_target="tpu_custom_call", output_to_operand_aliasing={{}: (5, {})} | custom-call | flops 134217728 | bytes 1572864 | tf_op jit(solution)/shard_map/pallas_call | solution.py:112
  90.8 0.0 copy-start.3
  90.8 2.1 %collective-permute-start.17 = (f32[2,256,256]{2,1,0:T(8,128)S(1)}, f32[2,256,256]{2,1,0:T(8,128)S(1)}, u32[]{:S(2)}, u32[]{:S(2)}) collective-permute-start(f32[2,256,256]{2,1,0:T(8,128)S(1)} %shard_map.34), channel_id=1, source_target_pairs={{0,16},{16,0},{1,17},{17,1},{2,18},{18,2},{3,19},{19,3},{4,20},{20... | collective-permute-start | bytes 1572872 | tf_op jit(solution)/shard_map/ppermute | solution.py:231
  92.9 1.3 %shard_map.33.mine_ref = f32[2,256,256]{2,1,0:T(8,128)S(1)} custom-call(s32[1]{0:T(128)} %bitcast.3.plane_ref, s32[1]{0:T(128)} %bitcast.4.core_ref, bf16[4,4,2,256,256]{4,3,2,1,0:T(8,128)(2,1)} %all-to-all-done.1.left_ref, bf16[2,256,256]{2,1,0:T(8,128)(2,1)S(1)} %collective-permute-done.8.refs_0_, ...), custom_call_target="tpu_custom_call", output_to_operand_aliasing={{}: (5, {})} | custom-call | flops 134217728 | bytes 1572864 | tf_op jit(solution)/shard_map/pallas_call | solution.py:112
  94.2 0.5 collective-permute-done.17.other_ref
  94.8 0.7 shard_map.35
  95.5 16.1 %all_to_all.15.parts_ref = f32[32,2,256]{2,1,0:T(2,128)S(1)} all-to-all(f32[32,2,256]{2,1,0:T(2,128)S(1)} %broadcast_in_dim.10), channel_id=1, replica_groups={{256,272,288,304,320,336,352,368,384,400,416,432,448,464,480,496,0,16,3..., dimensions={0} | all-to-all | bytes 131072 | tf_op jit(solution)/shard_map/all_to_all | solution.py:244
  111.6 1.6 %shard_map.36 = f32[2,256,256]{2,1,0:T(8,128)} custom-call(s32[2]{0:T(128)} %bitcast.10, s32[1]{0:T(128)} %bitcast.1.column_ref, bf16[2,256,256]{2,1,0:T(8,128)(2,1)S(1)} %bitcast.7, f32[2,256,256]{2,1,0:T(8,128)S(1)} %get-tuple-element.15.inflated_ref, f32[32,2,256]{2,1,0:T(2,128)S(1)} %all_to_all.15.parts_ref), custom_call_target="tpu_custom_call" | custom-call | tf_op jit(solution)/shard_map/pallas_call | solution.py:253
  (26 shorter events, 0.1 us)
Async XLA Ops:
  1.1 47.5 %copy-start = (bf16[2,256,256]{2,1,0:T(8,128)(2,1)}, bf16[2,256,256]{2,1,0:T(8,128)(2,1)S(1)}, u32[]{:S(2)}) copy-start(bf16[2,256,256]{2,1,0:T(8,128)(2,1)S(1)} %shard_map.28.refs_0_) | copy-start | bytes 786436
  1.1 14.6 %collective-permute-start = (bf16[2,256,256]{2,1,0:T(8,128)(2,1)S(1)}, bf16[2,256,256]{2,1,0:T(8,128)(2,1)S(1)}, u32[]{:S(2)}, u32[]{:S(2)}) collective-permute-start(bf16[2,256,256]{2,1,0:T(8,128)(2,1)S(1)} %shard_map.28.refs_0_), channel_id=1, source_target_pairs={{0,16},{16,0},{1,17},{17,1},{2,18},{18,2},{3,19},{19,3},{4,20},{20... | collective-permute-start | bytes 786440 | tf_op jit(solution)/shard_map/ppermute | solution.py:187
  9.9 13.8 %collective-permute-start.1 = (bf16[2,256,256]{2,1,0:T(8,128)(2,1)S(1)}, bf16[2,256,256]{2,1,0:T(8,128)(2,1)S(1)}, u32[]{:S(2)}, u32[]{:S(2)}) collective-permute-start(bf16[2,256,256]{2,1,0:T(8,128)(2,1)S(1)} %shard_map.28.refs_0_), channel_id=1, source_target_pairs={{0,32},{32,64},{64,96},{96,128},{128,160},{160,192},{192,224},{224... | collective-permute-start | bytes 786440 | tf_op jit(solution)/shard_map/ppermute | solution.py:226
  15.7 10.6 %copy-start.15 = (bf16[2,256,256]{2,1,0:T(8,128)(2,1)}, bf16[2,256,256]{2,1,0:T(8,128)(2,1)S(1)}, u32[]{:S(2)}) copy-start(bf16[2,256,256]{2,1,0:T(8,128)(2,1)S(1)} %collective-permute-done.refs_1_) | copy-start | bytes 786436
  15.7 10.6 %collective-permute-start.9 = (bf16[2,256,256]{2,1,0:T(8,128)(2,1)S(1)}, bf16[2,256,256]{2,1,0:T(8,128)(2,1)S(1)}, u32[]{:S(2)}, u32[]{:S(2)}) collective-permute-start(bf16[2,256,256]{2,1,0:T(8,128)(2,1)S(1)} %collective-permute-done.refs_1_), channel_id=1, source_target_pairs={{0,32},{32,64},{64,96},{96,128},{128,160},{160,192},{192,224},{224... | collective-permute-start | bytes 786440 | tf_op jit(solution)/shard_map/ppermute | solution.py:226
  19.5 26.6 %all-to-all-start = ((bf16[4,2,256,256]{3,2,1,0:T(8,128)(2,1)}), bf16[4,2,256,256]{3,2,1,0:T(8,128)(2,1)S(1)}, u32[]{:S(2)}, u32[]{:S(2)}) async-start(bf16[4,2,256,256]{3,2,1,0:T(8,128)(2,1)} %broadcast_in_dim.8), calls=%async_computation | async-start | bytes 2097152 | tf_op jit(solution)/shard_map/all_to_all | solution.py:209
  23.7 24.9 %copy-start.4 = (bf16[2,256,256]{2,1,0:T(8,128)(2,1)}, bf16[2,256,256]{2,1,0:T(8,128)(2,1)S(1)}, u32[]{:S(2)}) copy-start(bf16[2,256,256]{2,1,0:T(8,128)(2,1)S(1)} %collective-permute-done.1.refs_2_.refs_0_) | copy-start | bytes 786436
  23.7 7.4 %collective-permute-start.2 = (bf16[2,256,256]{2,1,0:T(8,128)(2,1)S(1)}, bf16[2,256,256]{2,1,0:T(8,128)(2,1)S(1)}, u32[]{:S(2)}, u32[]{:S(2)}) collective-permute-start(bf16[2,256,256]{2,1,0:T(8,128)(2,1)S(1)} %collective-permute-done.1.refs_2_.refs_0_), channel_id=1, source_target_pairs={{0,32},{32,64},{64,96},{96,128},{128,160},{160,192},{192,224},{224... | collective-permute-start | bytes 786440 | tf_op jit(solution)/shard_map/ppermute | solution.py:226
  26.3 22.3 %copy-start.5 = (bf16[2,256,256]{2,1,0:T(8,128)(2,1)}, bf16[2,256,256]{2,1,0:T(8,128)(2,1)S(1)}, u32[]{:S(2)}) copy-start(bf16[2,256,256]{2,1,0:T(8,128)(2,1)S(1)} %collective-permute-done.9.refs_3_.refs_1_) | copy-start | bytes 786436
  26.3 8.6 %collective-permute-start.10 = (bf16[2,256,256]{2,1,0:T(8,128)(2,1)S(1)}, bf16[2,256,256]{2,1,0:T(8,128)(2,1)S(1)}, u32[]{:S(2)}, u32[]{:S(2)}) collective-permute-start(bf16[2,256,256]{2,1,0:T(8,128)(2,1)S(1)} %collective-permute-done.9.refs_3_.refs_1_), channel_id=1, source_target_pairs={{0,32},{32,64},{64,96},{96,128},{128,160},{160,192},{192,224},{224... | collective-permute-start | bytes 786440 | tf_op jit(solution)/shard_map/ppermute | solution.py:226
  31.1 17.5 %copy-start.6 = (bf16[2,256,256]{2,1,0:T(8,128)(2,1)}, bf16[2,256,256]{2,1,0:T(8,128)(2,1)S(1)}, u32[]{:S(2)}) copy-start(bf16[2,256,256]{2,1,0:T(8,128)(2,1)S(1)} %collective-permute-done.2.refs_4_.refs_2_) | copy-start | bytes 786436
  31.1 7.4 %collective-permute-start.3 = (bf16[2,256,256]{2,1,0:T(8,128)(2,1)S(1)}, bf16[2,256,256]{2,1,0:T(8,128)(2,1)S(1)}, u32[]{:S(2)}, u32[]{:S(2)}) collective-permute-start(bf16[2,256,256]{2,1,0:T(8,128)(2,1)S(1)} %collective-permute-done.2.refs_4_.refs_2_), channel_id=1, source_target_pairs={{0,32},{32,64},{64,96},{96,128},{128,160},{160,192},{192,224},{224... | collective-permute-start | bytes 786440 | tf_op jit(solution)/shard_map/ppermute | solution.py:226
  34.9 13.7 %copy-start.7 = (bf16[2,256,256]{2,1,0:T(8,128)(2,1)}, bf16[2,256,256]{2,1,0:T(8,128)(2,1)S(1)}, u32[]{:S(2)}) copy-start(bf16[2,256,256]{2,1,0:T(8,128)(2,1)S(1)} %collective-permute-done.10.refs_5_.refs_3_) | copy-start | bytes 786436
  34.9 8.3 %collective-permute-start.11 = (bf16[2,256,256]{2,1,0:T(8,128)(2,1)S(1)}, bf16[2,256,256]{2,1,0:T(8,128)(2,1)S(1)}, u32[]{:S(2)}, u32[]{:S(2)}) collective-permute-start(bf16[2,256,256]{2,1,0:T(8,128)(2,1)S(1)} %collective-permute-done.10.refs_5_.refs_3_), channel_id=1, source_target_pairs={{0,32},{32,64},{64,96},{96,128},{128,160},{160,192},{192,224},{224... | collective-permute-start | bytes 786440 | tf_op jit(solution)/shard_map/ppermute | solution.py:226
  38.5 10.1 %copy-start.8 = (bf16[2,256,256]{2,1,0:T(8,128)(2,1)}, bf16[2,256,256]{2,1,0:T(8,128)(2,1)S(1)}, u32[]{:S(2)}) copy-start(bf16[2,256,256]{2,1,0:T(8,128)(2,1)S(1)} %collective-permute-done.3.refs_6_.refs_4_) | copy-start | bytes 786436
  38.5 15.0 %collective-permute-start.4 = (bf16[2,256,256]{2,1,0:T(8,128)(2,1)S(1)}, bf16[2,256,256]{2,1,0:T(8,128)(2,1)S(1)}, u32[]{:S(2)}, u32[]{:S(2)}) collective-permute-start(bf16[2,256,256]{2,1,0:T(8,128)(2,1)S(1)} %collective-permute-done.3.refs_6_.refs_4_), channel_id=1, source_target_pairs={{0,32},{32,64},{64,96},{96,128},{128,160},{160,192},{192,224},{224... | collective-permute-start | bytes 786440 | tf_op jit(solution)/shard_map/ppermute | solution.py:226
  43.2 5.4 %copy-start.9 = (bf16[2,256,256]{2,1,0:T(8,128)(2,1)}, bf16[2,256,256]{2,1,0:T(8,128)(2,1)S(1)}, u32[]{:S(2)}) copy-start(bf16[2,256,256]{2,1,0:T(8,128)(2,1)S(1)} %collective-permute-done.11.refs_7_.refs_5_) | copy-start | bytes 786436
  43.2 12.2 %collective-permute-start.12 = (bf16[2,256,256]{2,1,0:T(8,128)(2,1)S(1)}, bf16[2,256,256]{2,1,0:T(8,128)(2,1)S(1)}, u32[]{:S(2)}, u32[]{:S(2)}) collective-permute-start(bf16[2,256,256]{2,1,0:T(8,128)(2,1)S(1)} %collective-permute-done.11.refs_7_.refs_5_), channel_id=1, source_target_pairs={{0,32},{32,64},{64,96},{96,128},{128,160},{160,192},{192,224},{224... | collective-permute-start | bytes 786440 | tf_op jit(solution)/shard_map/ppermute | solution.py:226
  48.6 33.0 %all-to-all-start.1 = ((bf16[4,4,2,256,256]{4,3,2,1,0:T(8,128)(2,1)}), bf16[4,4,2,256,256]{4,3,2,1,0:T(8,128)(2,1)}, u32[]{:S(2)}, u32[]{:S(2)}) async-start(bf16[4,4,2,256,256]{4,3,2,1,0:T(8,128)(2,1)} %broadcast_in_dim.9), calls=%async_computation.1 | async-start | bytes 8388608 | tf_op jit(solution)/shard_map/all_to_all | solution.py:209
  53.5 19.4 %copy-start.10 = (bf16[2,256,256]{2,1,0:T(8,128)(2,1)}, bf16[2,256,256]{2,1,0:T(8,128)(2,1)S(1)}, u32[]{:S(2)}) copy-start(bf16[2,256,256]{2,1,0:T(8,128)(2,1)S(1)} %collective-permute-done.4.refs_8_.refs_6_) | copy-start | bytes 786436
  53.5 7.5 %collective-permute-start.5 = (bf16[2,256,256]{2,1,0:T(8,128)(2,1)S(1)}, bf16[2,256,256]{2,1,0:T(8,128)(2,1)S(1)}, u32[]{:S(2)}, u32[]{:S(2)}) collective-permute-start(bf16[2,256,256]{2,1,0:T(8,128)(2,1)S(1)} %collective-permute-done.4.refs_8_.refs_6_), channel_id=1, source_target_pairs={{0,32},{32,64},{64,96},{96,128},{128,160},{160,192},{192,224},{224... | collective-permute-start | bytes 786440 | tf_op jit(solution)/shard_map/ppermute | solution.py:226
  55.4 17.5 %copy-start.11 = (bf16[2,256,256]{2,1,0:T(8,128)(2,1)}, bf16[2,256,256]{2,1,0:T(8,128)(2,1)S(1)}, u32[]{:S(2)}) copy-start(bf16[2,256,256]{2,1,0:T(8,128)(2,1)S(1)} %collective-permute-done.12.refs_9_.refs_7_) | copy-start | bytes 786436
  55.4 8.7 %collective-permute-start.13 = (bf16[2,256,256]{2,1,0:T(8,128)(2,1)S(1)}, bf16[2,256,256]{2,1,0:T(8,128)(2,1)S(1)}, u32[]{:S(2)}, u32[]{:S(2)}) collective-permute-start(bf16[2,256,256]{2,1,0:T(8,128)(2,1)S(1)} %collective-permute-done.12.refs_9_.refs_7_), channel_id=1, source_target_pairs={{0,32},{32,64},{64,96},{96,128},{128,160},{160,192},{192,224},{224... | collective-permute-start | bytes 786440 | tf_op jit(solution)/shard_map/ppermute | solution.py:226
  61.0 11.9 %copy-start.12 = (bf16[2,256,256]{2,1,0:T(8,128)(2,1)}, bf16[2,256,256]{2,1,0:T(8,128)(2,1)S(1)}, u32[]{:S(2)}) copy-start(bf16[2,256,256]{2,1,0:T(8,128)(2,1)S(1)} %collective-permute-done.5.refs_10_.refs_8_) | copy-start | bytes 786436
  61.0 7.5 %collective-permute-start.6 = (bf16[2,256,256]{2,1,0:T(8,128)(2,1)S(1)}, bf16[2,256,256]{2,1,0:T(8,128)(2,1)S(1)}, u32[]{:S(2)}, u32[]{:S(2)}) collective-permute-start(bf16[2,256,256]{2,1,0:T(8,128)(2,1)S(1)} %collective-permute-done.5.refs_10_.refs_8_), channel_id=1, source_target_pairs={{0,32},{32,64},{64,96},{96,128},{128,160},{160,192},{192,224},{224... | collective-permute-start | bytes 786440 | tf_op jit(solution)/shard_map/ppermute | solution.py:226
  64.2 8.8 %copy-start.13 = (bf16[2,256,256]{2,1,0:T(8,128)(2,1)}, bf16[2,256,256]{2,1,0:T(8,128)(2,1)S(1)}, u32[]{:S(2)}) copy-start(bf16[2,256,256]{2,1,0:T(8,128)(2,1)S(1)} %collective-permute-done.13.refs_11_.refs_9_) | copy-start | bytes 786436
  64.2 8.7 %collective-permute-start.14 = (bf16[2,256,256]{2,1,0:T(8,128)(2,1)S(1)}, bf16[2,256,256]{2,1,0:T(8,128)(2,1)S(1)}, u32[]{:S(2)}, u32[]{:S(2)}) collective-permute-start(bf16[2,256,256]{2,1,0:T(8,128)(2,1)S(1)} %collective-permute-done.13.refs_11_.refs_9_), channel_id=1, source_target_pairs={{0,32},{32,64},{64,96},{96,128},{128,160},{160,192},{192,224},{224... | collective-permute-start | bytes 786440 | tf_op jit(solution)/shard_map/ppermute | solution.py:226
  68.5 4.4 %copy-start.14 = (bf16[2,256,256]{2,1,0:T(8,128)(2,1)}, bf16[2,256,256]{2,1,0:T(8,128)(2,1)S(1)}, u32[]{:S(2)}) copy-start(bf16[2,256,256]{2,1,0:T(8,128)(2,1)S(1)} %collective-permute-done.6.refs_12_.refs_10_) | copy-start | bytes 786436
  68.5 7.6 %collective-permute-start.7 = (bf16[2,256,256]{2,1,0:T(8,128)(2,1)S(1)}, bf16[2,256,256]{2,1,0:T(8,128)(2,1)S(1)}, u32[]{:S(2)}, u32[]{:S(2)}) collective-permute-start(bf16[2,256,256]{2,1,0:T(8,128)(2,1)S(1)} %collective-permute-done.6.refs_12_.refs_10_), channel_id=1, source_target_pairs={{0,32},{32,64},{64,96},{96,128},{128,160},{160,192},{192,224},{224... | collective-permute-start | bytes 786440 | tf_op jit(solution)/shard_map/ppermute | solution.py:226
  72.9 8.7 %copy-start.1 = (bf16[2,256,256]{2,1,0:T(8,128)(2,1)}, bf16[2,256,256]{2,1,0:T(8,128)(2,1)S(1)}, u32[]{:S(2)}) copy-start(bf16[2,256,256]{2,1,0:T(8,128)(2,1)S(1)} %shard_map.29.refs_13_.refs_11_) | copy-start | bytes 786436
  72.9 9.4 %collective-permute-start.15 = (bf16[2,256,256]{2,1,0:T(8,128)(2,1)S(1)}, bf16[2,256,256]{2,1,0:T(8,128)(2,1)S(1)}, u32[]{:S(2)}, u32[]{:S(2)}) collective-permute-start(bf16[2,256,256]{2,1,0:T(8,128)(2,1)S(1)} %shard_map.29.refs_13_.refs_11_), channel_id=1, source_target_pairs={{0,32},{32,64},{64,96},{96,128},{128,160},{160,192},{192,224},{224... | collective-permute-start | bytes 786440 | tf_op jit(solution)/shard_map/ppermute | solution.py:226
  76.2 6.2 %copy-start.16 = (bf16[2,256,256]{2,1,0:T(8,128)(2,1)}, bf16[2,256,256]{2,1,0:T(8,128)(2,1)S(1)}, u32[]{:S(2)}) copy-start(bf16[2,256,256]{2,1,0:T(8,128)(2,1)S(1)} %collective-permute-done.7.refs_12_) | copy-start | bytes 786436
  76.2 12.7 %collective-permute-start.8 = (bf16[2,256,256]{2,1,0:T(8,128)(2,1)S(1)}, bf16[2,256,256]{2,1,0:T(8,128)(2,1)S(1)}, u32[]{:S(2)}, u32[]{:S(2)}) collective-permute-start(bf16[2,256,256]{2,1,0:T(8,128)(2,1)S(1)} %collective-permute-done.7.refs_12_), channel_id=1, source_target_pairs={{16,496},{48,16},{80,48},{112,80},{144,112},{176,144},{208,176},{2... | collective-permute-start | bytes 786440 | tf_op jit(solution)/shard_map/ppermute | solution.py:226
  82.4 1.9 %copy-start.2 = (bf16[2,256,256]{2,1,0:T(8,128)(2,1)}, bf16[2,256,256]{2,1,0:T(8,128)(2,1)S(1)}, u32[]{:S(2)}) copy-start(bf16[2,256,256]{2,1,0:T(8,128)(2,1)S(1)} %shard_map.31.refs_13_) | copy-start | bytes 786436
  82.4 7.1 %collective-permute-start.16 = (bf16[2,256,256]{2,1,0:T(8,128)(2,1)S(1)}, bf16[2,256,256]{2,1,0:T(8,128)(2,1)S(1)}, u32[]{:S(2)}, u32[]{:S(2)}) collective-permute-start(bf16[2,256,256]{2,1,0:T(8,128)(2,1)S(1)} %shard_map.31.refs_13_), channel_id=1, source_target_pairs={{16,496},{48,16},{80,48},{112,80},{144,112},{176,144},{208,176},{2... | collective-permute-start | bytes 786440 | tf_op jit(solution)/shard_map/ppermute | solution.py:226
  90.8 20.8 %copy-start.3 = (bf16[1,2,256,256]{3,2,1,0:T(8,128)(2,1)S(1)}, bf16[1,2,256,256]{3,2,1,0:T(8,128)(2,1)}, u32[]{:S(2)}) copy-start(bf16[1,2,256,256]{3,2,1,0:T(8,128)(2,1)} %param.3) | copy-start | bytes 786436
  90.8 3.9 %collective-permute-start.17 = (f32[2,256,256]{2,1,0:T(8,128)S(1)}, f32[2,256,256]{2,1,0:T(8,128)S(1)}, u32[]{:S(2)}, u32[]{:S(2)}) collective-permute-start(f32[2,256,256]{2,1,0:T(8,128)S(1)} %shard_map.34), channel_id=1, source_target_pairs={{0,16},{16,0},{1,17},{17,1},{2,18},{18,2},{3,19},{19,3},{4,20},{20... | collective-permute-start | bytes 1572872 | tf_op jit(solution)/shard_map/ppermute | solution.py:231

commit v11 on v10

--- a/solution.py
+++ b/solution.py
@@ -240,7 +240,8 @@
         ],
         compiler_params=params(6),
     )(own, column_ref, total, received)
-    far = [(i + planes * cores // 2) % (planes * cores) for i in range(planes * cores)]
+    order = sorted(range(planes), key=lambda z: min(z, planes - z))
+    far = [cores * z + c for z in order[-1:] + order[:-1] for c in range(cores)]
     parts = lax.all_to_all(
         jnp.broadcast_to(sums[None], (planes * cores, *sums.shape)),
         ROWS,

time: 114 us -> 114 us (level)
  no operation moved by 1% of the time
where the time goes in v11:
time: 114 us; the launch traced here: 113 us
  starting transfers between devices  72.1 us (63%)
  blocking collectives  16 us (14%)
  Pallas kernels  11.4 us (10%)
  waiting for transfers between devices  9.4 us (8%)
  local copies, waits for them, and re-layouts  3.67 us (3%)
    ppermute x16, starting transfers between devices, on_device(): held.append(tuple((lax.ppermute(t, ROWS, perm) for t in held[-1])))  52.2 us
    all_to_all x1, blocking collectives, on_device(): lax.all_to_all(jnp.broadcast_to(sums[None], (planes * cores, *sums.shape)...  16 us
    all_to_all x2, starting transfers between devices, copy_for_each(): lax.all_to_all(spread, ('core', *COLS), 0, 0, axis_index_groups=lines, ti...  9.05 us
    ppermute x16, waiting for transfers between devices, on_device(): held.append(tuple((lax.ppermute(t, ROWS, perm) for t in held[-1])))  8.86 us
    ppermute x1, starting transfers between devices, on_device(): other = lax.ppermute(mine, 'core', SWAP)  8.79 us
    pallas_call x4, Pallas kernels, products(): pl.pallas_call(kernel, in_specs=[SMEM, SMEM, HBM] + [HBM] * len(tiles) +...  7.95 us
    broadcast_in_dim x2, local copies, waits for them, and re-layouts, copy_for_each(): spread = jnp.broadcast_to(value[None], (len(lines[0]), *value.shape))  3.57 us
  transfers between devices with their start and end apart: 20, of which 7 were waited for; matrix products, arithmetic and copies ran while one was open for 3% of the time, Pallas kernels for 6%

profile of v11, /device:TPU:1, one launch (start us, length us, event | category | flops | bytes accessed | tf_op | source)
XLA Modules:
  0.0 113.2 jit_solution(1334637901771264642)
XLA Ops:
  0.0 1.1 shard_map.28.refs_0_
  1.1 0.0 copy-start
  1.1 8.8 %collective-permute-start = (bf16[2,256,256]{2,1,0:T(8,128)(2,1)S(1)}, bf16[2,256,256]{2,1,0:T(8,128)(2,1)S(1)}, u32[]{:S(2)}, u32[]{:S(2)}) collective-permute-start(bf16[2,256,256]{2,1,0:T(8,128)(2,1)S(1)} %shard_map.28.refs_0_), channel_id=1, source_target_pairs={{0,16},{16,0},{1,17},{17,1},{2,18},{18,2},{3,19},{19,3},{4,20},{20... | collective-permute-start | bytes 786440 | tf_op jit(solution)/shard_map/ppermute | solution.py:187
  9.9 5.7 %collective-permute-start.1 = (bf16[2,256,256]{2,1,0:T(8,128)(2,1)S(1)}, bf16[2,256,256]{2,1,0:T(8,128)(2,1)S(1)}, u32[]{:S(2)}, u32[]{:S(2)}) collective-permute-start(bf16[2,256,256]{2,1,0:T(8,128)(2,1)S(1)} %shard_map.28.refs_0_), channel_id=1, source_target_pairs={{0,32},{32,64},{64,96},{96,128},{128,160},{160,192},{192,224},{224... | collective-permute-start | bytes 786440 | tf_op jit(solution)/shard_map/ppermute | solution.py:226
  15.7 0.0 collective-permute-done.refs_1_
  15.7 0.0 copy-start.15
  15.7 2.6 %collective-permute-start.9 = (bf16[2,256,256]{2,1,0:T(8,128)(2,1)S(1)}, bf16[2,256,256]{2,1,0:T(8,128)(2,1)S(1)}, u32[]{:S(2)}, u32[]{:S(2)}) collective-permute-start(bf16[2,256,256]{2,1,0:T(8,128)(2,1)S(1)} %collective-permute-done.refs_1_), channel_id=1, source_target_pairs={{0,32},{32,64},{64,96},{96,128},{128,160},{160,192},{192,224},{224... | collective-permute-start | bytes 786440 | tf_op jit(solution)/shard_map/ppermute | solution.py:226
  18.4 1.1 broadcast_in_dim.8
  19.5 4.2 %all-to-all-start = ((bf16[4,2,256,256]{3,2,1,0:T(8,128)(2,1)}), bf16[4,2,256,256]{3,2,1,0:T(8,128)(2,1)S(1)}, u32[]{:S(2)}, u32[]{:S(2)}) async-start(bf16[4,2,256,256]{3,2,1,0:T(8,128)(2,1)} %broadcast_in_dim.8), calls=%async_computation | async-start | bytes 2097152 | tf_op jit(solution)/shard_map/all_to_all | solution.py:209
  23.6 0.0 collective-permute-done.1.refs_2_.refs_0_
  23.7 2.6 %collective-permute-start.2 = (bf16[2,256,256]{2,1,0:T(8,128)(2,1)S(1)}, bf16[2,256,256]{2,1,0:T(8,128)(2,1)S(1)}, u32[]{:S(2)}, u32[]{:S(2)}) collective-permute-start(bf16[2,256,256]{2,1,0:T(8,128)(2,1)S(1)} %collective-permute-done.1.refs_2_.refs_0_), channel_id=1, source_target_pairs={{0,32},{32,64},{64,96},{96,128},{128,160},{160,192},{192,224},{224... | collective-permute-start | bytes 786440 | tf_op jit(solution)/shard_map/ppermute | solution.py:226
  26.3 0.0 copy-done.15
  26.3 0.0 collective-permute-done.9.refs_3_.refs_1_
  26.3 0.0 copy-start.5
  26.3 2.6 %collective-permute-start.10 = (bf16[2,256,256]{2,1,0:T(8,128)(2,1)S(1)}, bf16[2,256,256]{2,1,0:T(8,128)(2,1)S(1)}, u32[]{:S(2)}, u32[]{:S(2)}) collective-permute-start(bf16[2,256,256]{2,1,0:T(8,128)(2,1)S(1)} %collective-permute-done.9.refs_3_.refs_1_), channel_id=1, source_target_pairs={{0,32},{32,64},{64,96},{96,128},{128,160},{160,192},{192,224},{224... | collective-permute-start | bytes 786440 | tf_op jit(solution)/shard_map/ppermute | solution.py:226
  29.0 2.1 %collective-permute-done.2.refs_4_.refs_2_ = bf16[2,256,256]{2,1,0:T(8,128)(2,1)S(1)} collective-permute-done((bf16[2,256,256]{2,1,0:T(8,128)(2,1)S(1)}, bf16[2,256,256]{2,1,0:T(8,128)(2,1)S(1)}, u32[]{:S(2)}, u32[]{:S(2)}) %collective-permute-start.2) | collective-permute-done | bytes 262176 | tf_op jit(solution)/shard_map/ppermute | solution.py:226
  31.1 3.8 %collective-permute-start.3 = (bf16[2,256,256]{2,1,0:T(8,128)(2,1)S(1)}, bf16[2,256,256]{2,1,0:T(8,128)(2,1)S(1)}, u32[]{:S(2)}, u32[]{:S(2)}) collective-permute-start(bf16[2,256,256]{2,1,0:T(8,128)(2,1)S(1)} %collective-permute-done.2.refs_4_.refs_2_), channel_id=1, source_target_pairs={{0,32},{32,64},{64,96},{96,128},{128,160},{160,192},{192,224},{224... | collective-permute-start | bytes 786440 | tf_op jit(solution)/shard_map/ppermute | solution.py:226
  34.9 0.0 collective-permute-done.10.refs_5_.refs_3_
  34.9 0.0 copy-start.7
  34.9 2.5 %collective-permute-start.11 = (bf16[2,256,256]{2,1,0:T(8,128)(2,1)S(1)}, bf16[2,256,256]{2,1,0:T(8,128)(2,1)S(1)}, u32[]{:S(2)}, u32[]{:S(2)}) collective-permute-start(bf16[2,256,256]{2,1,0:T(8,128)(2,1)S(1)} %collective-permute-done.10.refs_5_.refs_3_), channel_id=1, source_target_pairs={{0,32},{32,64},{64,96},{96,128},{128,160},{160,192},{192,224},{224... | collective-permute-start | bytes 786440 | tf_op jit(solution)/shard_map/ppermute | solution.py:226
  37.4 1.0 collective-permute-done.3.refs_6_.refs_4_
  38.5 4.8 %collective-permute-start.4 = (bf16[2,256,256]{2,1,0:T(8,128)(2,1)S(1)}, bf16[2,256,256]{2,1,0:T(8,128)(2,1)S(1)}, u32[]{:S(2)}, u32[]{:S(2)}) collective-permute-start(bf16[2,256,256]{2,1,0:T(8,128)(2,1)S(1)} %collective-permute-done.3.refs_6_.refs_4_), channel_id=1, source_target_pairs={{0,32},{32,64},{64,96},{96,128},{128,160},{160,192},{192,224},{224... | collective-permute-start | bytes 786440 | tf_op jit(solution)/shard_map/ppermute | solution.py:226
  43.2 0.0 collective-permute-done.11.refs_7_.refs_5_
  43.2 0.0 copy-start.9
  43.2 2.8 %collective-permute-start.12 = (bf16[2,256,256]{2,1,0:T(8,128)(2,1)S(1)}, bf16[2,256,256]{2,1,0:T(8,128)(2,1)S(1)}, u32[]{:S(2)}, u32[]{:S(2)}) collective-permute-start(bf16[2,256,256]{2,1,0:T(8,128)(2,1)S(1)} %collective-permute-done.11.refs_7_.refs_5_), channel_id=1, source_target_pairs={{0,32},{32,64},{64,96},{96,128},{128,160},{160,192},{192,224},{224... | collective-permute-start | bytes 786440 | tf_op jit(solution)/shard_map/ppermute | solution.py:226
  46.0 0.0 all-to-all-done
  46.0 2.5 %broadcast_in_dim.9 = bf16[4,4,2,256,256]{4,3,2,1,0:T(8,128)(2,1)} broadcast(bf16[4,2,256,256]{3,2,1,0:T(8,128)(2,1)S(1)} %all-to-all-done), dimensions={1,2,3,4} | broadcast | bytes 5242880 | tf_op jit(solution)/shard_map/broadcast_in_dim | solution.py:208
  48.6 0.0 copy-done
  48.6 0.0 copy-done.7
  48.6 0.0 copy-done.8
  48.6 0.0 copy-done.9
  48.6 4.9 %all-to-all-start.1 = ((bf16[4,4,2,256,256]{4,3,2,1,0:T(8,128)(2,1)}), bf16[4,4,2,256,256]{4,3,2,1,0:T(8,128)(2,1)}, u32[]{:S(2)}, u32[]{:S(2)}) async-start(bf16[4,4,2,256,256]{4,3,2,1,0:T(8,128)(2,1)} %broadcast_in_dim.9), calls=%async_computation.1 | async-start | bytes 8388608 | tf_op jit(solution)/shard_map/all_to_all | solution.py:209
  53.5 0.0 collective-permute-done.4.refs_8_.refs_6_
  53.5 0.0 copy-start.10
  53.5 1.9 %collective-permute-start.5 = (bf16[2,256,256]{2,1,0:T(8,128)(2,1)S(1)}, bf16[2,256,256]{2,1,0:T(8,128)(2,1)S(1)}, u32[]{:S(2)}, u32[]{:S(2)}) collective-permute-start(bf16[2,256,256]{2,1,0:T(8,128)(2,1)S(1)} %collective-permute-done.4.refs_8_.refs_6_), channel_id=1, source_target_pairs={{0,32},{32,64},{64,96},{96,128},{128,160},{160,192},{192,224},{224... | collective-permute-start | bytes 786440 | tf_op jit(solution)/shard_map/ppermute | solution.py:226
  55.4 0.0 collective-permute-done.12.refs_9_.refs_7_
  55.4 2.4 %collective-permute-start.13 = (bf16[2,256,256]{2,1,0:T(8,128)(2,1)S(1)}, bf16[2,256,256]{2,1,0:T(8,128)(2,1)S(1)}, u32[]{:S(2)}, u32[]{:S(2)}) collective-permute-start(bf16[2,256,256]{2,1,0:T(8,128)(2,1)S(1)} %collective-permute-done.12.refs_9_.refs_7_), channel_id=1, source_target_pairs={{0,32},{32,64},{64,96},{96,128},{128,160},{160,192},{192,224},{224... | collective-permute-start | bytes 786440 | tf_op jit(solution)/shard_map/ppermute | solution.py:226
  57.9 3.1 %collective-permute-done.5.refs_10_.refs_8_ = bf16[2,256,256]{2,1,0:T(8,128)(2,1)S(1)} collective-permute-done((bf16[2,256,256]{2,1,0:T(8,128)(2,1)S(1)}, bf16[2,256,256]{2,1,0:T(8,128)(2,1)S(1)}, u32[]{:S(2)}, u32[]{:S(2)}) %collective-permute-start.5) | collective-permute-done | bytes 262176 | tf_op jit(solution)/shard_map/ppermute | solution.py:226
  61.0 3.1 %collective-permute-start.6 = (bf16[2,256,256]{2,1,0:T(8,128)(2,1)S(1)}, bf16[2,256,256]{2,1,0:T(8,128)(2,1)S(1)}, u32[]{:S(2)}, u32[]{:S(2)}) collective-permute-start(bf16[2,256,256]{2,1,0:T(8,128)(2,1)S(1)} %collective-permute-done.5.refs_10_.refs_8_), channel_id=1, source_target_pairs={{0,32},{32,64},{64,96},{96,128},{128,160},{160,192},{192,224},{224... | collective-permute-start | bytes 786440 | tf_op jit(solution)/shard_map/ppermute | solution.py:226
  64.1 0.0 collective-permute-done.13.refs_11_.refs_9_
  64.2 0.0 copy-start.13
  64.2 2.8 %collective-permute-start.14 = (bf16[2,256,256]{2,1,0:T(8,128)(2,1)S(1)}, bf16[2,256,256]{2,1,0:T(8,128)(2,1)S(1)}, u32[]{:S(2)}, u32[]{:S(2)}) collective-permute-start(bf16[2,256,256]{2,1,0:T(8,128)(2,1)S(1)} %collective-permute-done.13.refs_11_.refs_9_), channel_id=1, source_target_pairs={{0,32},{32,64},{64,96},{96,128},{128,160},{160,192},{192,224},{224... | collective-permute-start | bytes 786440 | tf_op jit(solution)/shard_map/ppermute | solution.py:226
  67.0 1.6 %collective-permute-done.6.refs_12_.refs_10_ = bf16[2,256,256]{2,1,0:T(8,128)(2,1)S(1)} collective-permute-done((bf16[2,256,256]{2,1,0:T(8,128)(2,1)S(1)}, bf16[2,256,256]{2,1,0:T(8,128)(2,1)S(1)}, u32[]{:S(2)}, u32[]{:S(2)}) %collective-permute-start.6) | collective-permute-done | bytes 262176 | tf_op jit(solution)/shard_map/ppermute | solution.py:226
  68.5 4.3 %collective-permute-start.7 = (bf16[2,256,256]{2,1,0:T(8,128)(2,1)S(1)}, bf16[2,256,256]{2,1,0:T(8,128)(2,1)S(1)}, u32[]{:S(2)}, u32[]{:S(2)}) collective-permute-start(bf16[2,256,256]{2,1,0:T(8,128)(2,1)S(1)} %collective-permute-done.6.refs_12_.refs_10_), channel_id=1, source_target_pairs={{0,32},{32,64},{64,96},{96,128},{128,160},{160,192},{192,224},{224... | collective-permute-start | bytes 786440 | tf_op jit(solution)/shard_map/ppermute | solution.py:226
  72.9 0.0 collective-permute-done.14.refs_0_
  72.9 2.8 %collective-permute-start.15 = (bf16[2,256,256]{2,1,0:T(8,128)(2,1)S(1)}, bf16[2,256,256]{2,1,0:T(8,128)(2,1)S(1)}, u32[]{:S(2)}, u32[]{:S(2)}) collective-permute-start(bf16[2,256,256]{2,1,0:T(8,128)(2,1)S(1)} %shard_map.29.refs_13_.refs_11_), channel_id=1, source_target_pairs={{0,32},{32,64},{64,96},{96,128},{128,160},{160,192},{192,224},{224... | collective-permute-start | bytes 786440 | tf_op jit(solution)/shard_map/ppermute | solution.py:226
  75.7 0.4 collective-permute-done.7.refs_12_
  76.2 5.4 %collective-permute-start.8 = (bf16[2,256,256]{2,1,0:T(8,128)(2,1)S(1)}, bf16[2,256,256]{2,1,0:T(8,128)(2,1)S(1)}, u32[]{:S(2)}, u32[]{:S(2)}) collective-permute-start(bf16[2,256,256]{2,1,0:T(8,128)(2,1)S(1)} %collective-permute-done.7.refs_12_), channel_id=1, source_target_pairs={{16,496},{48,16},{80,48},{112,80},{144,112},{176,144},{208,176},{2... | collective-permute-start | bytes 786440 | tf_op jit(solution)/shard_map/ppermute | solution.py:226
  81.6 0.0 all-to-all-done.1.left_ref
  81.6 0.7 shard_map.30
  82.3 0.0 collective-permute-done.15.refs_0_
  82.4 0.0 copy-start.2
  82.4 1.9 %collective-permute-start.16 = (bf16[2,256,256]{2,1,0:T(8,128)(2,1)S(1)}, bf16[2,256,256]{2,1,0:T(8,128)(2,1)S(1)}, u32[]{:S(2)}, u32[]{:S(2)}) collective-permute-start(bf16[2,256,256]{2,1,0:T(8,128)(2,1)S(1)} %shard_map.31.refs_13_), channel_id=1, source_target_pairs={{16,496},{48,16},{80,48},{112,80},{144,112},{176,144},{208,176},{2... | collective-permute-start | bytes 786440 | tf_op jit(solution)/shard_map/ppermute | solution.py:226
  84.3 4.6 %shard_map.32 = (f32[2,256,256]{2,1,0:T(8,128)S(1)}, f32[2,256,256]{2,1,0:T(8,128)S(1)}) custom-call(s32[1]{0:T(128)} %bitcast.3.plane_ref, s32[1]{0:T(128)} %bitcast.4.core_ref, bf16[4,4,2,256,256]{4,3,2,1,0:T(8,128)(2,1)} %all-to-all-done.1.left_ref, bf16[2,256,256]{2,1,0:T(8,128)(2,1)} %copy-done.4, ...), custom_call_target="tpu_custom_call", output_to_operand_aliasing={{0}: (17, {}), {1}: (18, {})} | custom-call | flops 1879048192 | bytes 14680064 | tf_op jit(solution)/shard_map/pallas_call | solution.py:112
  88.9 0.0 collective-permute-done.8.refs_0_
  88.9 0.6 collective-permute-done.16.refs_1_
  89.5 1.3 %shard_map.34 = f32[2,256,256]{2,1,0:T(8,128)S(1)} custom-call(s32[1]{0:T(128)} %bitcast.3.plane_ref, s32[1]{0:T(128)} %bitcast.4.core_ref, bf16[4,4,2,256,256]{4,3,2,1,0:T(8,128)(2,1)} %all-to-all-done.1.left_ref, bf16[2,256,256]{2,1,0:T(8,128)(2,1)S(1)} %collective-permute-done.8.refs_0_, ...), custom_call_target="tpu_custom_call", output_to_operand_aliasing={{}: (5, {})} | custom-call | flops 134217728 | bytes 1572864 | tf_op jit(solution)/shard_map/pallas_call | solution.py:112
  90.8 0.0 copy-start.3
  90.8 2.1 %collective-permute-start.17 = (f32[2,256,256]{2,1,0:T(8,128)S(1)}, f32[2,256,256]{2,1,0:T(8,128)S(1)}, u32[]{:S(2)}, u32[]{:S(2)}) collective-permute-start(f32[2,256,256]{2,1,0:T(8,128)S(1)} %shard_map.34), channel_id=1, source_target_pairs={{0,16},{16,0},{1,17},{17,1},{2,18},{18,2},{3,19},{19,3},{4,20},{20... | collective-permute-start | bytes 1572872 | tf_op jit(solution)/shard_map/ppermute | solution.py:231
  92.9 1.3 %shard_map.33.mine_ref = f32[2,256,256]{2,1,0:T(8,128)S(1)} custom-call(s32[1]{0:T(128)} %bitcast.3.plane_ref, s32[1]{0:T(128)} %bitcast.4.core_ref, bf16[4,4,2,256,256]{4,3,2,1,0:T(8,128)(2,1)} %all-to-all-done.1.left_ref, bf16[2,256,256]{2,1,0:T(8,128)(2,1)S(1)} %collective-permute-done.8.refs_0_, ...), custom_call_target="tpu_custom_call", output_to_operand_aliasing={{}: (5, {})} | custom-call | flops 134217728 | bytes 1572864 | tf_op jit(solution)/shard_map/pallas_call | solution.py:112
  94.2 0.5 collective-permute-done.17.other_ref
  94.8 0.7 shard_map.35
  95.5 16.0 %all_to_all.15.parts_ref = f32[32,2,256]{2,1,0:T(2,128)S(1)} all-to-all(f32[32,2,256]{2,1,0:T(2,128)S(1)} %broadcast_in_dim.10), channel_id=1, replica_groups={{256,272,0,16,32,48,480,496,64,80,448,464,96,112,416,432,128,144,384,40..., dimensions={0} | all-to-all | bytes 131072 | tf_op jit(solution)/shard_map/all_to_all | solution.py:245
  111.6 1.6 %shard_map.36 = f32[2,256,256]{2,1,0:T(8,128)} custom-call(s32[2]{0:T(128)} %bitcast.10, s32[1]{0:T(128)} %bitcast.1.column_ref, bf16[2,256,256]{2,1,0:T(8,128)(2,1)S(1)} %bitcast.7, f32[2,256,256]{2,1,0:T(8,128)S(1)} %get-tuple-element.15.inflated_ref, f32[32,2,256]{2,1,0:T(2,128)S(1)} %all_to_all.15.parts_ref), custom_call_target="tpu_custom_call" | custom-call | tf_op jit(solution)/shard_map/pallas_call | solution.py:254
  (26 shorter events, 0.1 us)
Async XLA Ops:
  1.1 47.5 %copy-start = (bf16[2,256,256]{2,1,0:T(8,128)(2,1)}, bf16[2,256,256]{2,1,0:T(8,128)(2,1)S(1)}, u32[]{:S(2)}) copy-start(bf16[2,256,256]{2,1,0:T(8,128)(2,1)S(1)} %shard_map.28.refs_0_) | copy-start | bytes 786436
  1.1 14.6 %collective-permute-start = (bf16[2,256,256]{2,1,0:T(8,128)(2,1)S(1)}, bf16[2,256,256]{2,1,0:T(8,128)(2,1)S(1)}, u32[]{:S(2)}, u32[]{:S(2)}) collective-permute-start(bf16[2,256,256]{2,1,0:T(8,128)(2,1)S(1)} %shard_map.28.refs_0_), channel_id=1, source_target_pairs={{0,16},{16,0},{1,17},{17,1},{2,18},{18,2},{3,19},{19,3},{4,20},{20... | collective-permute-start | bytes 786440 | tf_op jit(solution)/shard_map/ppermute | solution.py:187
  9.9 13.8 %collective-permute-start.1 = (bf16[2,256,256]{2,1,0:T(8,128)(2,1)S(1)}, bf16[2,256,256]{2,1,0:T(8,128)(2,1)S(1)}, u32[]{:S(2)}, u32[]{:S(2)}) collective-permute-start(bf16[2,256,256]{2,1,0:T(8,128)(2,1)S(1)} %shard_map.28.refs_0_), channel_id=1, source_target_pairs={{0,32},{32,64},{64,96},{96,128},{128,160},{160,192},{192,224},{224... | collective-permute-start | bytes 786440 | tf_op jit(solution)/shard_map/ppermute | solution.py:226
  15.7 10.6 %copy-start.15 = (bf16[2,256,256]{2,1,0:T(8,128)(2,1)}, bf16[2,256,256]{2,1,0:T(8,128)(2,1)S(1)}, u32[]{:S(2)}) copy-start(bf16[2,256,256]{2,1,0:T(8,128)(2,1)S(1)} %collective-permute-done.refs_1_) | copy-start | bytes 786436
  15.7 10.6 %collective-permute-start.9 = (bf16[2,256,256]{2,1,0:T(8,128)(2,1)S(1)}, bf16[2,256,256]{2,1,0:T(8,128)(2,1)S(1)}, u32[]{:S(2)}, u32[]{:S(2)}) collective-permute-start(bf16[2,256,256]{2,1,0:T(8,128)(2,1)S(1)} %collective-permute-done.refs_1_), channel_id=1, source_target_pairs={{0,32},{32,64},{64,96},{96,128},{128,160},{160,192},{192,224},{224... | collective-permute-start | bytes 786440 | tf_op jit(solution)/shard_map/ppermute | solution.py:226
  19.5 26.6 %all-to-all-start = ((bf16[4,2,256,256]{3,2,1,0:T(8,128)(2,1)}), bf16[4,2,256,256]{3,2,1,0:T(8,128)(2,1)S(1)}, u32[]{:S(2)}, u32[]{:S(2)}) async-start(bf16[4,2,256,256]{3,2,1,0:T(8,128)(2,1)} %broadcast_in_dim.8), calls=%async_computation | async-start | bytes 2097152 | tf_op jit(solution)/shard_map/all_to_all | solution.py:209
  23.7 24.9 %copy-start.4 = (bf16[2,256,256]{2,1,0:T(8,128)(2,1)}, bf16[2,256,256]{2,1,0:T(8,128)(2,1)S(1)}, u32[]{:S(2)}) copy-start(bf16[2,256,256]{2,1,0:T(8,128)(2,1)S(1)} %collective-permute-done.1.refs_2_.refs_0_) | copy-start | bytes 786436
  23.7 7.4 %collective-permute-start.2 = (bf16[2,256,256]{2,1,0:T(8,128)(2,1)S(1)}, bf16[2,256,256]{2,1,0:T(8,128)(2,1)S(1)}, u32[]{:S(2)}, u32[]{:S(2)}) collective-permute-start(bf16[2,256,256]{2,1,0:T(8,128)(2,1)S(1)} %collective-permute-done.1.refs_2_.refs_0_), channel_id=1, source_target_pairs={{0,32},{32,64},{64,96},{96,128},{128,160},{160,192},{192,224},{224... | collective-permute-start | bytes 786440 | tf_op jit(solution)/shard_map/ppermute | solution.py:226
  26.3 22.3 %copy-start.5 = (bf16[2,256,256]{2,1,0:T(8,128)(2,1)}, bf16[2,256,256]{2,1,0:T(8,128)(2,1)S(1)}, u32[]{:S(2)}) copy-start(bf16[2,256,256]{2,1,0:T(8,128)(2,1)S(1)} %collective-permute-done.9.refs_3_.refs_1_) | copy-start | bytes 786436
  26.3 8.6 %collective-permute-start.10 = (bf16[2,256,256]{2,1,0:T(8,128)(2,1)S(1)}, bf16[2,256,256]{2,1,0:T(8,128)(2,1)S(1)}, u32[]{:S(2)}, u32[]{:S(2)}) collective-permute-start(bf16[2,256,256]{2,1,0:T(8,128)(2,1)S(1)} %collective-permute-done.9.refs_3_.refs_1_), channel_id=1, source_target_pairs={{0,32},{32,64},{64,96},{96,128},{128,160},{160,192},{192,224},{224... | collective-permute-start | bytes 786440 | tf_op jit(solution)/shard_map/ppermute | solution.py:226
  31.1 17.5 %copy-start.6 = (bf16[2,256,256]{2,1,0:T(8,128)(2,1)}, bf16[2,256,256]{2,1,0:T(8,128)(2,1)S(1)}, u32[]{:S(2)}) copy-start(bf16[2,256,256]{2,1,0:T(8,128)(2,1)S(1)} %collective-permute-done.2.refs_4_.refs_2_) | copy-start | bytes 786436
  31.1 7.4 %collective-permute-start.3 = (bf16[2,256,256]{2,1,0:T(8,128)(2,1)S(1)}, bf16[2,256,256]{2,1,0:T(8,128)(2,1)S(1)}, u32[]{:S(2)}, u32[]{:S(2)}) collective-permute-start(bf16[2,256,256]{2,1,0:T(8,128)(2,1)S(1)} %collective-permute-done.2.refs_4_.refs_2_), channel_id=1, source_target_pairs={{0,32},{32,64},{64,96},{96,128},{128,160},{160,192},{192,224},{224... | collective-permute-start | bytes 786440 | tf_op jit(solution)/shard_map/ppermute | solution.py:226
  34.9 13.7 %copy-start.7 = (bf16[2,256,256]{2,1,0:T(8,128)(2,1)}, bf16[2,256,256]{2,1,0:T(8,128)(2,1)S(1)}, u32[]{:S(2)}) copy-start(bf16[2,256,256]{2,1,0:T(8,128)(2,1)S(1)} %collective-permute-done.10.refs_5_.refs_3_) | copy-start | bytes 786436
  34.9 8.3 %collective-permute-start.11 = (bf16[2,256,256]{2,1,0:T(8,128)(2,1)S(1)}, bf16[2,256,256]{2,1,0:T(8,128)(2,1)S(1)}, u32[]{:S(2)}, u32[]{:S(2)}) collective-permute-start(bf16[2,256,256]{2,1,0:T(8,128)(2,1)S(1)} %collective-permute-done.10.refs_5_.refs_3_), channel_id=1, source_target_pairs={{0,32},{32,64},{64,96},{96,128},{128,160},{160,192},{192,224},{224... | collective-permute-start | bytes 786440 | tf_op jit(solution)/shard_map/ppermute | solution.py:226
  38.5 10.1 %copy-start.8 = (bf16[2,256,256]{2,1,0:T(8,128)(2,1)}, bf16[2,256,256]{2,1,0:T(8,128)(2,1)S(1)}, u32[]{:S(2)}) copy-start(bf16[2,256,256]{2,1,0:T(8,128)(2,1)S(1)} %collective-permute-done.3.refs_6_.refs_4_) | copy-start | bytes 786436
  38.5 15.0 %collective-permute-start.4 = (bf16[2,256,256]{2,1,0:T(8,128)(2,1)S(1)}, bf16[2,256,256]{2,1,0:T(8,128)(2,1)S(1)}, u32[]{:S(2)}, u32[]{:S(2)}) collective-permute-start(bf16[2,256,256]{2,1,0:T(8,128)(2,1)S(1)} %collective-permute-done.3.refs_6_.refs_4_), channel_id=1, source_target_pairs={{0,32},{32,64},{64,96},{96,128},{128,160},{160,192},{192,224},{224... | collective-permute-start | bytes 786440 | tf_op jit(solution)/shard_map/ppermute | solution.py:226
  43.2 5.4 %copy-start.9 = (bf16[2,256,256]{2,1,0:T(8,128)(2,1)}, bf16[2,256,256]{2,1,0:T(8,128)(2,1)S(1)}, u32[]{:S(2)}) copy-start(bf16[2,256,256]{2,1,0:T(8,128)(2,1)S(1)} %collective-permute-done.11.refs_7_.refs_5_) | copy-start | bytes 786436
  43.2 12.2 %collective-permute-start.12 = (bf16[2,256,256]{2,1,0:T(8,128)(2,1)S(1)}, bf16[2,256,256]{2,1,0:T(8,128)(2,1)S(1)}, u32[]{:S(2)}, u32[]{:S(2)}) collective-permute-start(bf16[2,256,256]{2,1,0:T(8,128)(2,1)S(1)} %collective-permute-done.11.refs_7_.refs_5_), channel_id=1, source_target_pairs={{0,32},{32,64},{64,96},{96,128},{128,160},{160,192},{192,224},{224... | collective-permute-start | bytes 786440 | tf_op jit(solution)/shard_map/ppermute | solution.py:226
  48.6 33.0 %all-to-all-start.1 = ((bf16[4,4,2,256,256]{4,3,2,1,0:T(8,128)(2,1)}), bf16[4,4,2,256,256]{4,3,2,1,0:T(8,128)(2,1)}, u32[]{:S(2)}, u32[]{:S(2)}) async-start(bf16[4,4,2,256,256]{4,3,2,1,0:T(8,128)(2,1)} %broadcast_in_dim.9), calls=%async_computation.1 | async-start | bytes 8388608 | tf_op jit(solution)/shard_map/all_to_all | solution.py:209
  53.5 19.4 %copy-start.10 = (bf16[2,256,256]{2,1,0:T(8,128)(2,1)}, bf16[2,256,256]{2,1,0:T(8,128)(2,1)S(1)}, u32[]{:S(2)}) copy-start(bf16[2,256,256]{2,1,0:T(8,128)(2,1)S(1)} %collective-permute-done.4.refs_8_.refs_6_) | copy-start | bytes 786436
  53.5 7.5 %collective-permute-start.5 = (bf16[2,256,256]{2,1,0:T(8,128)(2,1)S(1)}, bf16[2,256,256]{2,1,0:T(8,128)(2,1)S(1)}, u32[]{:S(2)}, u32[]{:S(2)}) collective-permute-start(bf16[2,256,256]{2,1,0:T(8,128)(2,1)S(1)} %collective-permute-done.4.refs_8_.refs_6_), channel_id=1, source_target_pairs={{0,32},{32,64},{64,96},{96,128},{128,160},{160,192},{192,224},{224... | collective-permute-start | bytes 786440 | tf_op jit(solution)/shard_map/ppermute | solution.py:226
  55.4 17.5 %copy-start.11 = (bf16[2,256,256]{2,1,0:T(8,128)(2,1)}, bf16[2,256,256]{2,1,0:T(8,128)(2,1)S(1)}, u32[]{:S(2)}) copy-start(bf16[2,256,256]{2,1,0:T(8,128)(2,1)S(1)} %collective-permute-done.12.refs_9_.refs_7_) | copy-start | bytes 786436
  55.4 8.7 %collective-permute-start.13 = (bf16[2,256,256]{2,1,0:T(8,128)(2,1)S(1)}, bf16[2,256,256]{2,1,0:T(8,128)(2,1)S(1)}, u32[]{:S(2)}, u32[]{:S(2)}) collective-permute-start(bf16[2,256,256]{2,1,0:T(8,128)(2,1)S(1)} %collective-permute-done.12.refs_9_.refs_7_), channel_id=1, source_target_pairs={{0,32},{32,64},{64,96},{96,128},{128,160},{160,192},{192,224},{224... | collective-permute-start | bytes 786440 | tf_op jit(solution)/shard_map/ppermute | solution.py:226
  61.0 11.9 %copy-start.12 = (bf16[2,256,256]{2,1,0:T(8,128)(2,1)}, bf16[2,256,256]{2,1,0:T(8,128)(2,1)S(1)}, u32[]{:S(2)}) copy-start(bf16[2,256,256]{2,1,0:T(8,128)(2,1)S(1)} %collective-permute-done.5.refs_10_.refs_8_) | copy-start | bytes 786436
  61.0 7.5 %collective-permute-start.6 = (bf16[2,256,256]{2,1,0:T(8,128)(2,1)S(1)}, bf16[2,256,256]{2,1,0:T(8,128)(2,1)S(1)}, u32[]{:S(2)}, u32[]{:S(2)}) collective-permute-start(bf16[2,256,256]{2,1,0:T(8,128)(2,1)S(1)} %collective-permute-done.5.refs_10_.refs_8_), channel_id=1, source_target_pairs={{0,32},{32,64},{64,96},{96,128},{128,160},{160,192},{192,224},{224... | collective-permute-start | bytes 786440 | tf_op jit(solution)/shard_map/ppermute | solution.py:226
  64.2 8.8 %copy-start.13 = (bf16[2,256,256]{2,1,0:T(8,128)(2,1)}, bf16[2,256,256]{2,1,0:T(8,128)(2,1)S(1)}, u32[]{:S(2)}) copy-start(bf16[2,256,256]{2,1,0:T(8,128)(2,1)S(1)} %collective-permute-done.13.refs_11_.refs_9_) | copy-start | bytes 786436
  64.2 8.7 %collective-permute-start.14 = (bf16[2,256,256]{2,1,0:T(8,128)(2,1)S(1)}, bf16[2,256,256]{2,1,0:T(8,128)(2,1)S(1)}, u32[]{:S(2)}, u32[]{:S(2)}) collective-permute-start(bf16[2,256,256]{2,1,0:T(8,128)(2,1)S(1)} %collective-permute-done.13.refs_11_.refs_9_), channel_id=1, source_target_pairs={{0,32},{32,64},{64,96},{96,128},{128,160},{160,192},{192,224},{224... | collective-permute-start | bytes 786440 | tf_op jit(solution)/shard_map/ppermute | solution.py:226
  68.5 4.4 %copy-start.14 = (bf16[2,256,256]{2,1,0:T(8,128)(2,1)}, bf16[2,256,256]{2,1,0:T(8,128)(2,1)S(1)}, u32[]{:S(2)}) copy-start(bf16[2,256,256]{2,1,0:T(8,128)(2,1)S(1)} %collective-permute-done.6.refs_12_.refs_10_) | copy-start | bytes 786436
  68.5 7.6 %collective-permute-start.7 = (bf16[2,256,256]{2,1,0:T(8,128)(2,1)S(1)}, bf16[2,256,256]{2,1,0:T(8,128)(2,1)S(1)}, u32[]{:S(2)}, u32[]{:S(2)}) collective-permute-start(bf16[2,256,256]{2,1,0:T(8,128)(2,1)S(1)} %collective-permute-done.6.refs_12_.refs_10_), channel_id=1, source_target_pairs={{0,32},{32,64},{64,96},{96,128},{128,160},{160,192},{192,224},{224... | collective-permute-start | bytes 786440 | tf_op jit(solution)/shard_map/ppermute | solution.py:226
  72.9 8.7 %copy-start.1 = (bf16[2,256,256]{2,1,0:T(8,128)(2,1)}, bf16[2,256,256]{2,1,0:T(8,128)(2,1)S(1)}, u32[]{:S(2)}) copy-start(bf16[2,256,256]{2,1,0:T(8,128)(2,1)S(1)} %shard_map.29.refs_13_.refs_11_) | copy-start | bytes 786436
  72.9 9.4 %collective-permute-start.15 = (bf16[2,256,256]{2,1,0:T(8,128)(2,1)S(1)}, bf16[2,256,256]{2,1,0:T(8,128)(2,1)S(1)}, u32[]{:S(2)}, u32[]{:S(2)}) collective-permute-start(bf16[2,256,256]{2,1,0:T(8,128)(2,1)S(1)} %shard_map.29.refs_13_.refs_11_), channel_id=1, source_target_pairs={{0,32},{32,64},{64,96},{96,128},{128,160},{160,192},{192,224},{224... | collective-permute-start | bytes 786440 | tf_op jit(solution)/shard_map/ppermute | solution.py:226
  76.2 6.2 %copy-start.16 = (bf16[2,256,256]{2,1,0:T(8,128)(2,1)}, bf16[2,256,256]{2,1,0:T(8,128)(2,1)S(1)}, u32[]{:S(2)}) copy-start(bf16[2,256,256]{2,1,0:T(8,128)(2,1)S(1)} %collective-permute-done.7.refs_12_) | copy-start | bytes 786436
  76.2 12.7 %collective-permute-start.8 = (bf16[2,256,256]{2,1,0:T(8,128)(2,1)S(1)}, bf16[2,256,256]{2,1,0:T(8,128)(2,1)S(1)}, u32[]{:S(2)}, u32[]{:S(2)}) collective-permute-start(bf16[2,256,256]{2,1,0:T(8,128)(2,1)S(1)} %collective-permute-done.7.refs_12_), channel_id=1, source_target_pairs={{16,496},{48,16},{80,48},{112,80},{144,112},{176,144},{208,176},{2... | collective-permute-start | bytes 786440 | tf_op jit(solution)/shard_map/ppermute | solution.py:226
  82.4 1.9 %copy-start.2 = (bf16[2,256,256]{2,1,0:T(8,128)(2,1)}, bf16[2,256,256]{2,1,0:T(8,128)(2,1)S(1)}, u32[]{:S(2)}) copy-start(bf16[2,256,256]{2,1,0:T(8,128)(2,1)S(1)} %shard_map.31.refs_13_) | copy-start | bytes 786436
  82.4 7.1 %collective-permute-start.16 = (bf16[2,256,256]{2,1,0:T(8,128)(2,1)S(1)}, bf16[2,256,256]{2,1,0:T(8,128)(2,1)S(1)}, u32[]{:S(2)}, u32[]{:S(2)}) collective-permute-start(bf16[2,256,256]{2,1,0:T(8,128)(2,1)S(1)} %shard_map.31.refs_13_), channel_id=1, source_target_pairs={{16,496},{48,16},{80,48},{112,80},{144,112},{176,144},{208,176},{2... | collective-permute-start | bytes 786440 | tf_op jit(solution)/shard_map/ppermute | solution.py:226
  90.8 20.8 %copy-start.3 = (bf16[1,2,256,256]{3,2,1,0:T(8,128)(2,1)S(1)}, bf16[1,2,256,256]{3,2,1,0:T(8,128)(2,1)}, u32[]{:S(2)}) copy-start(bf16[1,2,256,256]{3,2,1,0:T(8,128)(2,1)} %param.3) | copy-start | bytes 786436
  90.8 3.9 %collective-permute-start.17 = (f32[2,256,256]{2,1,0:T(8,128)S(1)}, f32[2,256,256]{2,1,0:T(8,128)S(1)}, u32[]{:S(2)}, u32[]{:S(2)}) collective-permute-start(f32[2,256,256]{2,1,0:T(8,128)S(1)} %shard_map.34), channel_id=1, source_target_pairs={{0,16},{16,0},{1,17},{17,1},{2,18},{18,2},{3,19},{19,3},{4,20},{20... | collective-permute-start | bytes 1572872 | tf_op jit(solution)/shard_map/ppermute | solution.py:231

commit v12 on v10

--- a/solution.py
+++ b/solution.py
@@ -240,10 +240,11 @@
         ],
         compiler_params=params(6),
     )(own, column_ref, total, received)
-    far = [(i + planes * cores // 2) % (planes * cores) for i in range(planes * cores)]
+    sums = lax.all_gather(sums, "core", axis=0).sum(axis=0)
+    far = [(z + half) % planes for z in range(planes)]
     parts = lax.all_to_all(
-        jnp.broadcast_to(sums[None], (planes * cores, *sums.shape)),
-        ROWS,
+        jnp.broadcast_to(sums[None], (planes, *sums.shape)),
+        "z",
         0,
         0,
         axis_index_groups=[far],

time: 114 us -> 113 us (level)
    all_to_all x1, blocking collectives: 16.1 us -> 13.7 us  [on_device(): lax.all_to_all(jnp.broadcast_to(sums[None], (planes, *sums.shape)), 'z',...]
    all_gather x0 -> x1, blocking collectives: none -> 1.78 us  [on_device(): sums = lax.all_gather(sums, 'core', axis=0).sum(axis=0)]
where the time goes in v12:
time: 113 us
  starting transfers between devices  72.1 us (64%)
  blocking collectives  15.5 us (14%)
  Pallas kernels  11.3 us (10%)
  waiting for transfers between devices  9.4 us (8%)
  local copies, waits for them, and re-layouts  3.65 us (3%)
    ppermute x16, starting transfers between devices, on_device(): held.append(tuple((lax.ppermute(t, ROWS, perm) for t in held[-1])))  52.2 us
    all_to_all x1, blocking collectives, on_device(): lax.all_to_all(jnp.broadcast_to(sums[None], (planes, *sums.shape)), 'z',...  13.7 us
    all_to_all x2, starting transfers between devices, copy_for_each(): lax.all_to_all(spread, ('core', *COLS), 0, 0, axis_index_groups=lines, ti...  9.04 us
    ppermute x16, waiting for transfers between devices, on_device(): held.append(tuple((lax.ppermute(t, ROWS, perm) for t in held[-1])))  8.86 us
    ppermute x1, starting transfers between devices, on_device(): other = lax.ppermute(mine, 'core', SWAP)  8.79 us
    pallas_call x4, Pallas kernels, products(): pl.pallas_call(kernel, in_specs=[SMEM, SMEM, HBM] + [HBM] * len(tiles) +...  7.95 us
    broadcast_in_dim x2, local copies, waits for them, and re-layouts, copy_for_each(): spread = jnp.broadcast_to(value[None], (len(lines[0]), *value.shape))  3.56 us
  transfers between devices with their start and end apart: 20, of which 7 were waited for; matrix products, arithmetic and copies ran while one was open for 3% of the time, Pallas kernels for 6%

profile of v12, /device:TPU:1, one launch (start us, length us, event | category | flops | bytes accessed | tf_op | source)
XLA Modules:
  0.0 112.5 jit_solution(15567086348784842249)
XLA Ops:
  0.0 1.1 shard_map.28.refs_0_
  1.1 0.0 copy-start
  1.1 8.8 %collective-permute-start = (bf16[2,256,256]{2,1,0:T(8,128)(2,1)S(1)}, bf16[2,256,256]{2,1,0:T(8,128)(2,1)S(1)}, u32[]{:S(2)}, u32[]{:S(2)}) collective-permute-start(bf16[2,256,256]{2,1,0:T(8,128)(2,1)S(1)} %shard_map.28.refs_0_), channel_id=1, source_target_pairs={{0,16},{16,0},{1,17},{17,1},{2,18},{18,2},{3,19},{19,3},{4,20},{20... | collective-permute-start | bytes 786440 | tf_op jit(solution)/shard_map/ppermute | solution.py:187
  9.9 5.7 %collective-permute-start.1 = (bf16[2,256,256]{2,1,0:T(8,128)(2,1)S(1)}, bf16[2,256,256]{2,1,0:T(8,128)(2,1)S(1)}, u32[]{:S(2)}, u32[]{:S(2)}) collective-permute-start(bf16[2,256,256]{2,1,0:T(8,128)(2,1)S(1)} %shard_map.28.refs_0_), channel_id=1, source_target_pairs={{0,32},{32,64},{64,96},{96,128},{128,160},{160,192},{192,224},{224... | collective-permute-start | bytes 786440 | tf_op jit(solution)/shard_map/ppermute | solution.py:226
  15.7 0.0 collective-permute-done.refs_1_
  15.7 0.0 copy-start.15
  15.7 2.6 %collective-permute-start.9 = (bf16[2,256,256]{2,1,0:T(8,128)(2,1)S(1)}, bf16[2,256,256]{2,1,0:T(8,128)(2,1)S(1)}, u32[]{:S(2)}, u32[]{:S(2)}) collective-permute-start(bf16[2,256,256]{2,1,0:T(8,128)(2,1)S(1)} %collective-permute-done.refs_1_), channel_id=1, source_target_pairs={{0,32},{32,64},{64,96},{96,128},{128,160},{160,192},{192,224},{224... | collective-permute-start | bytes 786440 | tf_op jit(solution)/shard_map/ppermute | solution.py:226
  18.4 1.0 broadcast_in_dim.8
  19.5 4.2 %all-to-all-start = ((bf16[4,2,256,256]{3,2,1,0:T(8,128)(2,1)}), bf16[4,2,256,256]{3,2,1,0:T(8,128)(2,1)S(1)}, u32[]{:S(2)}, u32[]{:S(2)}) async-start(bf16[4,2,256,256]{3,2,1,0:T(8,128)(2,1)} %broadcast_in_dim.8), calls=%async_computation | async-start | bytes 2097152 | tf_op jit(solution)/shard_map/all_to_all | solution.py:209
  23.6 0.0 collective-permute-done.1.refs_2_.refs_0_
  23.6 2.6 %collective-permute-start.2 = (bf16[2,256,256]{2,1,0:T(8,128)(2,1)S(1)}, bf16[2,256,256]{2,1,0:T(8,128)(2,1)S(1)}, u32[]{:S(2)}, u32[]{:S(2)}) collective-permute-start(bf16[2,256,256]{2,1,0:T(8,128)(2,1)S(1)} %collective-permute-done.1.refs_2_.refs_0_), channel_id=1, source_target_pairs={{0,32},{32,64},{64,96},{96,128},{128,160},{160,192},{192,224},{224... | collective-permute-start | bytes 786440 | tf_op jit(solution)/shard_map/ppermute | solution.py:226
  26.3 0.0 copy-done.15
  26.3 0.0 collective-permute-done.9.refs_3_.refs_1_
  26.3 0.0 copy-start.5
  26.3 2.6 %collective-permute-start.10 = (bf16[2,256,256]{2,1,0:T(8,128)(2,1)S(1)}, bf16[2,256,256]{2,1,0:T(8,128)(2,1)S(1)}, u32[]{:S(2)}, u32[]{:S(2)}) collective-permute-start(bf16[2,256,256]{2,1,0:T(8,128)(2,1)S(1)} %collective-permute-done.9.refs_3_.refs_1_), channel_id=1, source_target_pairs={{0,32},{32,64},{64,96},{96,128},{128,160},{160,192},{192,224},{224... | collective-permute-start | bytes 786440 | tf_op jit(solution)/shard_map/ppermute | solution.py:226
  29.0 2.1 %collective-permute-done.2.refs_4_.refs_2_ = bf16[2,256,256]{2,1,0:T(8,128)(2,1)S(1)} collective-permute-done((bf16[2,256,256]{2,1,0:T(8,128)(2,1)S(1)}, bf16[2,256,256]{2,1,0:T(8,128)(2,1)S(1)}, u32[]{:S(2)}, u32[]{:S(2)}) %collective-permute-start.2) | collective-permute-done | bytes 262176 | tf_op jit(solution)/shard_map/ppermute | solution.py:226
  31.1 3.8 %collective-permute-start.3 = (bf16[2,256,256]{2,1,0:T(8,128)(2,1)S(1)}, bf16[2,256,256]{2,1,0:T(8,128)(2,1)S(1)}, u32[]{:S(2)}, u32[]{:S(2)}) collective-permute-start(bf16[2,256,256]{2,1,0:T(8,128)(2,1)S(1)} %collective-permute-done.2.refs_4_.refs_2_), channel_id=1, source_target_pairs={{0,32},{32,64},{64,96},{96,128},{128,160},{160,192},{192,224},{224... | collective-permute-start | bytes 786440 | tf_op jit(solution)/shard_map/ppermute | solution.py:226
  34.9 0.0 collective-permute-done.10.refs_5_.refs_3_
  34.9 0.0 copy-start.7
  34.9 2.5 %collective-permute-start.11 = (bf16[2,256,256]{2,1,0:T(8,128)(2,1)S(1)}, bf16[2,256,256]{2,1,0:T(8,128)(2,1)S(1)}, u32[]{:S(2)}, u32[]{:S(2)}) collective-permute-start(bf16[2,256,256]{2,1,0:T(8,128)(2,1)S(1)} %collective-permute-done.10.refs_5_.refs_3_), channel_id=1, source_target_pairs={{0,32},{32,64},{64,96},{96,128},{128,160},{160,192},{192,224},{224... | collective-permute-start | bytes 786440 | tf_op jit(solution)/shard_map/ppermute | solution.py:226
  37.4 1.0 collective-permute-done.3.refs_6_.refs_4_
  38.5 4.8 %collective-permute-start.4 = (bf16[2,256,256]{2,1,0:T(8,128)(2,1)S(1)}, bf16[2,256,256]{2,1,0:T(8,128)(2,1)S(1)}, u32[]{:S(2)}, u32[]{:S(2)}) collective-permute-start(bf16[2,256,256]{2,1,0:T(8,128)(2,1)S(1)} %collective-permute-done.3.refs_6_.refs_4_), channel_id=1, source_target_pairs={{0,32},{32,64},{64,96},{96,128},{128,160},{160,192},{192,224},{224... | collective-permute-start | bytes 786440 | tf_op jit(solution)/shard_map/ppermute | solution.py:226
  43.2 0.0 collective-permute-done.11.refs_7_.refs_5_
  43.2 0.0 copy-start.9
  43.2 2.8 %collective-permute-start.12 = (bf16[2,256,256]{2,1,0:T(8,128)(2,1)S(1)}, bf16[2,256,256]{2,1,0:T(8,128)(2,1)S(1)}, u32[]{:S(2)}, u32[]{:S(2)}) collective-permute-start(bf16[2,256,256]{2,1,0:T(8,128)(2,1)S(1)} %collective-permute-done.11.refs_7_.refs_5_), channel_id=1, source_target_pairs={{0,32},{32,64},{64,96},{96,128},{128,160},{160,192},{192,224},{224... | collective-permute-start | bytes 786440 | tf_op jit(solution)/shard_map/ppermute | solution.py:226
  46.0 0.0 all-to-all-done
  46.0 2.5 %broadcast_in_dim.9 = bf16[4,4,2,256,256]{4,3,2,1,0:T(8,128)(2,1)} broadcast(bf16[4,2,256,256]{3,2,1,0:T(8,128)(2,1)S(1)} %all-to-all-done), dimensions={1,2,3,4} | broadcast | bytes 5242880 | tf_op jit(solution)/shard_map/broadcast_in_dim | solution.py:208
  48.5 0.0 copy-done
  48.5 0.0 copy-done.4
  48.5 0.0 copy-done.5
  48.6 0.0 copy-done.6
  48.6 4.9 %all-to-all-start.1 = ((bf16[4,4,2,256,256]{4,3,2,1,0:T(8,128)(2,1)}), bf16[4,4,2,256,256]{4,3,2,1,0:T(8,128)(2,1)}, u32[]{:S(2)}, u32[]{:S(2)}) async-start(bf16[4,4,2,256,256]{4,3,2,1,0:T(8,128)(2,1)} %broadcast_in_dim.9), calls=%async_computation.1 | async-start | bytes 8388608 | tf_op jit(solution)/shard_map/all_to_all | solution.py:209
  53.5 0.0 collective-permute-done.4.refs_8_.refs_6_
  53.5 1.9 %collective-permute-start.5 = (bf16[2,256,256]{2,1,0:T(8,128)(2,1)S(1)}, bf16[2,256,256]{2,1,0:T(8,128)(2,1)S(1)}, u32[]{:S(2)}, u32[]{:S(2)}) collective-permute-start(bf16[2,256,256]{2,1,0:T(8,128)(2,1)S(1)} %collective-permute-done.4.refs_8_.refs_6_), channel_id=1, source_target_pairs={{0,32},{32,64},{64,96},{96,128},{128,160},{160,192},{192,224},{224... | collective-permute-start | bytes 786440 | tf_op jit(solution)/shard_map/ppermute | solution.py:226
  55.4 0.0 collective-permute-done.12.refs_9_.refs_7_
  55.4 2.4 %collective-permute-start.13 = (bf16[2,256,256]{2,1,0:T(8,128)(2,1)S(1)}, bf16[2,256,256]{2,1,0:T(8,128)(2,1)S(1)}, u32[]{:S(2)}, u32[]{:S(2)}) collective-permute-start(bf16[2,256,256]{2,1,0:T(8,128)(2,1)S(1)} %collective-permute-done.12.refs_9_.refs_7_), channel_id=1, source_target_pairs={{0,32},{32,64},{64,96},{96,128},{128,160},{160,192},{192,224},{224... | collective-permute-start | bytes 786440 | tf_op jit(solution)/shard_map/ppermute | solution.py:226
  57.9 3.1 %collective-permute-done.5.refs_10_.refs_8_ = bf16[2,256,256]{2,1,0:T(8,128)(2,1)S(1)} collective-permute-done((bf16[2,256,256]{2,1,0:T(8,128)(2,1)S(1)}, bf16[2,256,256]{2,1,0:T(8,128)(2,1)S(1)}, u32[]{:S(2)}, u32[]{:S(2)}) %collective-permute-start.5) | collective-permute-done | bytes 262176 | tf_op jit(solution)/shard_map/ppermute | solution.py:226
  61.0 3.1 %collective-permute-start.6 = (bf16[2,256,256]{2,1,0:T(8,128)(2,1)S(1)}, bf16[2,256,256]{2,1,0:T(8,128)(2,1)S(1)}, u32[]{:S(2)}, u32[]{:S(2)}) collective-permute-start(bf16[2,256,256]{2,1,0:T(8,128)(2,1)S(1)} %collective-permute-done.5.refs_10_.refs_8_), channel_id=1, source_target_pairs={{0,32},{32,64},{64,96},{96,128},{128,160},{160,192},{192,224},{224... | collective-permute-start | bytes 786440 | tf_op jit(solution)/shard_map/ppermute | solution.py:226
  64.1 0.0 collective-permute-done.13.refs_11_.refs_9_
  64.1 0.0 copy-start.13
  64.1 2.8 %collective-permute-start.14 = (bf16[2,256,256]{2,1,0:T(8,128)(2,1)S(1)}, bf16[2,256,256]{2,1,0:T(8,128)(2,1)S(1)}, u32[]{:S(2)}, u32[]{:S(2)}) collective-permute-start(bf16[2,256,256]{2,1,0:T(8,128)(2,1)S(1)} %collective-permute-done.13.refs_11_.refs_9_), channel_id=1, source_target_pairs={{0,32},{32,64},{64,96},{96,128},{128,160},{160,192},{192,224},{224... | collective-permute-start | bytes 786440 | tf_op jit(solution)/shard_map/ppermute | solution.py:226
  66.9 1.6 %collective-permute-done.6.refs_12_.refs_10_ = bf16[2,256,256]{2,1,0:T(8,128)(2,1)S(1)} collective-permute-done((bf16[2,256,256]{2,1,0:T(8,128)(2,1)S(1)}, bf16[2,256,256]{2,1,0:T(8,128)(2,1)S(1)}, u32[]{:S(2)}, u32[]{:S(2)}) %collective-permute-start.6) | collective-permute-done | bytes 262176 | tf_op jit(solution)/shard_map/ppermute | solution.py:226
  68.5 4.3 %collective-permute-start.7 = (bf16[2,256,256]{2,1,0:T(8,128)(2,1)S(1)}, bf16[2,256,256]{2,1,0:T(8,128)(2,1)S(1)}, u32[]{:S(2)}, u32[]{:S(2)}) collective-permute-start(bf16[2,256,256]{2,1,0:T(8,128)(2,1)S(1)} %collective-permute-done.6.refs_12_.refs_10_), channel_id=1, source_target_pairs={{0,32},{32,64},{64,96},{96,128},{128,160},{160,192},{192,224},{224... | collective-permute-start | bytes 786440 | tf_op jit(solution)/shard_map/ppermute | solution.py:226
  72.8 0.0 collective-permute-done.14.refs_0_
  72.9 2.8 %collective-permute-start.15 = (bf16[2,256,256]{2,1,0:T(8,128)(2,1)S(1)}, bf16[2,256,256]{2,1,0:T(8,128)(2,1)S(1)}, u32[]{:S(2)}, u32[]{:S(2)}) collective-permute-start(bf16[2,256,256]{2,1,0:T(8,128)(2,1)S(1)} %shard_map.29.refs_13_.refs_11_), channel_id=1, source_target_pairs={{0,32},{32,64},{64,96},{96,128},{128,160},{160,192},{192,224},{224... | collective-permute-start | bytes 786440 | tf_op jit(solution)/shard_map/ppermute | solution.py:226
  75.7 0.4 collective-permute-done.7.refs_12_
  76.1 5.4 %collective-permute-start.8 = (bf16[2,256,256]{2,1,0:T(8,128)(2,1)S(1)}, bf16[2,256,256]{2,1,0:T(8,128)(2,1)S(1)}, u32[]{:S(2)}, u32[]{:S(2)}) collective-permute-start(bf16[2,256,256]{2,1,0:T(8,128)(2,1)S(1)} %collective-permute-done.7.refs_12_), channel_id=1, source_target_pairs={{16,496},{48,16},{80,48},{112,80},{144,112},{176,144},{208,176},{2... | collective-permute-start | bytes 786440 | tf_op jit(solution)/shard_map/ppermute | solution.py:226
  81.6 0.0 all-to-all-done.1.left_ref
  81.6 0.7 shard_map.30
  82.3 0.0 collective-permute-done.15.refs_0_
  82.3 0.0 copy-start.2
  82.3 1.9 %collective-permute-start.16 = (bf16[2,256,256]{2,1,0:T(8,128)(2,1)S(1)}, bf16[2,256,256]{2,1,0:T(8,128)(2,1)S(1)}, u32[]{:S(2)}, u32[]{:S(2)}) collective-permute-start(bf16[2,256,256]{2,1,0:T(8,128)(2,1)S(1)} %shard_map.31.refs_13_), channel_id=1, source_target_pairs={{16,496},{48,16},{80,48},{112,80},{144,112},{176,144},{208,176},{2... | collective-permute-start | bytes 786440 | tf_op jit(solution)/shard_map/ppermute | solution.py:226
  84.3 4.6 %shard_map.32 = (f32[2,256,256]{2,1,0:T(8,128)S(1)}, f32[2,256,256]{2,1,0:T(8,128)S(1)}) custom-call(s32[1]{0:T(128)} %bitcast.3.plane_ref, s32[1]{0:T(128)} %bitcast.4.core_ref, bf16[4,4,2,256,256]{4,3,2,1,0:T(8,128)(2,1)} %all-to-all-done.1.left_ref, bf16[2,256,256]{2,1,0:T(8,128)(2,1)} %copy-done.4, ...), custom_call_target="tpu_custom_call", output_to_operand_aliasing={{0}: (17, {}), {1}: (18, {})} | custom-call | flops 1879048192 | bytes 14680064 | tf_op jit(solution)/shard_map/pallas_call | solution.py:112
  88.9 0.0 collective-permute-done.8.refs_0_
  88.9 0.6 collective-permute-done.16.refs_1_
  89.5 1.3 %shard_map.34 = f32[2,256,256]{2,1,0:T(8,128)S(1)} custom-call(s32[1]{0:T(128)} %bitcast.3.plane_ref, s32[1]{0:T(128)} %bitcast.4.core_ref, bf16[4,4,2,256,256]{4,3,2,1,0:T(8,128)(2,1)} %all-to-all-done.1.left_ref, bf16[2,256,256]{2,1,0:T(8,128)(2,1)S(1)} %collective-permute-done.8.refs_0_, ...), custom_call_target="tpu_custom_call", output_to_operand_aliasing={{}: (5, {})} | custom-call | flops 134217728 | bytes 1572864 | tf_op jit(solution)/shard_map/pallas_call | solution.py:112
  90.8 0.0 copy-start.3
  90.8 2.1 %collective-permute-start.17 = (f32[2,256,256]{2,1,0:T(8,128)S(1)}, f32[2,256,256]{2,1,0:T(8,128)S(1)}, u32[]{:S(2)}, u32[]{:S(2)}) collective-permute-start(f32[2,256,256]{2,1,0:T(8,128)S(1)} %shard_map.34), channel_id=1, source_target_pairs={{0,16},{16,0},{1,17},{17,1},{2,18},{18,2},{3,19},{19,3},{4,20},{20... | collective-permute-start | bytes 1572872 | tf_op jit(solution)/shard_map/ppermute | solution.py:231
  92.8 1.3 %shard_map.33.mine_ref = f32[2,256,256]{2,1,0:T(8,128)S(1)} custom-call(s32[1]{0:T(128)} %bitcast.3.plane_ref, s32[1]{0:T(128)} %bitcast.4.core_ref, bf16[4,4,2,256,256]{4,3,2,1,0:T(8,128)(2,1)} %all-to-all-done.1.left_ref, bf16[2,256,256]{2,1,0:T(8,128)(2,1)S(1)} %collective-permute-done.8.refs_0_, ...), custom_call_target="tpu_custom_call", output_to_operand_aliasing={{}: (5, {})} | custom-call | flops 134217728 | bytes 1572864 | tf_op jit(solution)/shard_map/pallas_call | solution.py:112
  94.2 0.5 collective-permute-done.17.other_ref
  94.7 0.7 shard_map.35
  95.5 1.8 %all-gather.1 = f32[2,2,256]{2,1,0:T(2,128)S(1)} all-gather(f32[1,2,256]{2,1,0:T(2,128)S(1)} %bitcast.9), channel_id=2, replica_groups=mesh['z'=16,'core'=2,'y'=4,'x'=4] {'core'}, dimensions={0}, use_global_device_ids=true | all-gather | bytes 6144 | tf_op jit(solution)/shard_map/all_gather | solution.py:243
  97.3 13.7 %all_to_all.15.parts_ref = f32[16,2,256]{2,1,0:T(2,128)S(1)} all-to-all(f32[16,2,256]{2,1,0:T(2,128)S(1)} %broadcast_in_dim.10), channel_id=1, replica_groups={{256,288,320,352,384,416,448,480,0,32,64,96,128,160,192,224},{257,289,3..., dimensions={0} | all-to-all | bytes 65536 | tf_op jit(solution)/shard_map/all_to_all | solution.py:245
  111.0 1.5 %shard_map.36 = f32[2,256,256]{2,1,0:T(8,128)} custom-call(s32[2]{0:T(128)} %bitcast.12, s32[1]{0:T(128)} %bitcast.1.column_ref, bf16[2,256,256]{2,1,0:T(8,128)(2,1)S(1)} %bitcast.8, f32[2,256,256]{2,1,0:T(8,128)S(1)} %get-tuple-element.15.inflated_ref, f32[16,2,256]{2,1,0:T(2,128)S(1)} %all_to_all.15.parts_ref), custom_call_target="tpu_custom_call" | custom-call | tf_op jit(solution)/shard_map/pallas_call | solution.py:254
  (28 shorter events, 0.1 us)
Async XLA Ops:
  1.1 47.5 %copy-start = (bf16[2,256,256]{2,1,0:T(8,128)(2,1)}, bf16[2,256,256]{2,1,0:T(8,128)(2,1)S(1)}, u32[]{:S(2)}) copy-start(bf16[2,256,256]{2,1,0:T(8,128)(2,1)S(1)} %shard_map.28.refs_0_) | copy-start | bytes 786436
  1.1 14.6 %collective-permute-start = (bf16[2,256,256]{2,1,0:T(8,128)(2,1)S(1)}, bf16[2,256,256]{2,1,0:T(8,128)(2,1)S(1)}, u32[]{:S(2)}, u32[]{:S(2)}) collective-permute-start(bf16[2,256,256]{2,1,0:T(8,128)(2,1)S(1)} %shard_map.28.refs_0_), channel_id=1, source_target_pairs={{0,16},{16,0},{1,17},{17,1},{2,18},{18,2},{3,19},{19,3},{4,20},{20... | collective-permute-start | bytes 786440 | tf_op jit(solution)/shard_map/ppermute | solution.py:187
  9.9 13.8 %collective-permute-start.1 = (bf16[2,256,256]{2,1,0:T(8,128)(2,1)S(1)}, bf16[2,256,256]{2,1,0:T(8,128)(2,1)S(1)}, u32[]{:S(2)}, u32[]{:S(2)}) collective-permute-start(bf16[2,256,256]{2,1,0:T(8,128)(2,1)S(1)} %shard_map.28.refs_0_), channel_id=1, source_target_pairs={{0,32},{32,64},{64,96},{96,128},{128,160},{160,192},{192,224},{224... | collective-permute-start | bytes 786440 | tf_op jit(solution)/shard_map/ppermute | solution.py:226
  15.7 10.6 %copy-start.15 = (bf16[2,256,256]{2,1,0:T(8,128)(2,1)}, bf16[2,256,256]{2,1,0:T(8,128)(2,1)S(1)}, u32[]{:S(2)}) copy-start(bf16[2,256,256]{2,1,0:T(8,128)(2,1)S(1)} %collective-permute-done.refs_1_) | copy-start | bytes 786436
  15.7 10.6 %collective-permute-start.9 = (bf16[2,256,256]{2,1,0:T(8,128)(2,1)S(1)}, bf16[2,256,256]{2,1,0:T(8,128)(2,1)S(1)}, u32[]{:S(2)}, u32[]{:S(2)}) collective-permute-start(bf16[2,256,256]{2,1,0:T(8,128)(2,1)S(1)} %collective-permute-done.refs_1_), channel_id=1, source_target_pairs={{0,32},{32,64},{64,96},{96,128},{128,160},{160,192},{192,224},{224... | collective-permute-start | bytes 786440 | tf_op jit(solution)/shard_map/ppermute | solution.py:226
  19.5 26.6 %all-to-all-start = ((bf16[4,2,256,256]{3,2,1,0:T(8,128)(2,1)}), bf16[4,2,256,256]{3,2,1,0:T(8,128)(2,1)S(1)}, u32[]{:S(2)}, u32[]{:S(2)}) async-start(bf16[4,2,256,256]{3,2,1,0:T(8,128)(2,1)} %broadcast_in_dim.8), calls=%async_computation | async-start | bytes 2097152 | tf_op jit(solution)/shard_map/all_to_all | solution.py:209
  23.6 24.9 %copy-start.4 = (bf16[2,256,256]{2,1,0:T(8,128)(2,1)}, bf16[2,256,256]{2,1,0:T(8,128)(2,1)S(1)}, u32[]{:S(2)}) copy-start(bf16[2,256,256]{2,1,0:T(8,128)(2,1)S(1)} %collective-permute-done.1.refs_2_.refs_0_) | copy-start | bytes 786436
  23.6 7.4 %collective-permute-start.2 = (bf16[2,256,256]{2,1,0:T(8,128)(2,1)S(1)}, bf16[2,256,256]{2,1,0:T(8,128)(2,1)S(1)}, u32[]{:S(2)}, u32[]{:S(2)}) collective-permute-start(bf16[2,256,256]{2,1,0:T(8,128)(2,1)S(1)} %collective-permute-done.1.refs_2_.refs_0_), channel_id=1, source_target_pairs={{0,32},{32,64},{64,96},{96,128},{128,160},{160,192},{192,224},{224... | collective-permute-start | bytes 786440 | tf_op jit(solution)/shard_map/ppermute | solution.py:226
  26.3 22.2 %copy-start.5 = (bf16[2,256,256]{2,1,0:T(8,128)(2,1)}, bf16[2,256,256]{2,1,0:T(8,128)(2,1)S(1)}, u32[]{:S(2)}) copy-start(bf16[2,256,256]{2,1,0:T(8,128)(2,1)S(1)} %collective-permute-done.9.refs_3_.refs_1_) | copy-start | bytes 786436
  26.3 8.6 %collective-permute-start.10 = (bf16[2,256,256]{2,1,0:T(8,128)(2,1)S(1)}, bf16[2,256,256]{2,1,0:T(8,128)(2,1)S(1)}, u32[]{:S(2)}, u32[]{:S(2)}) collective-permute-start(bf16[2,256,256]{2,1,0:T(8,128)(2,1)S(1)} %collective-permute-done.9.refs_3_.refs_1_), channel_id=1, source_target_pairs={{0,32},{32,64},{64,96},{96,128},{128,160},{160,192},{192,224},{224... | collective-permute-start | bytes 786440 | tf_op jit(solution)/shard_map/ppermute | solution.py:226
  31.1 17.5 %copy-start.6 = (bf16[2,256,256]{2,1,0:T(8,128)(2,1)}, bf16[2,256,256]{2,1,0:T(8,128)(2,1)S(1)}, u32[]{:S(2)}) copy-start(bf16[2,256,256]{2,1,0:T(8,128)(2,1)S(1)} %collective-permute-done.2.refs_4_.refs_2_) | copy-start | bytes 786436
  31.1 7.4 %collective-permute-start.3 = (bf16[2,256,256]{2,1,0:T(8,128)(2,1)S(1)}, bf16[2,256,256]{2,1,0:T(8,128)(2,1)S(1)}, u32[]{:S(2)}, u32[]{:S(2)}) collective-permute-start(bf16[2,256,256]{2,1,0:T(8,128)(2,1)S(1)} %collective-permute-done.2.refs_4_.refs_2_), channel_id=1, source_target_pairs={{0,32},{32,64},{64,96},{96,128},{128,160},{160,192},{192,224},{224... | collective-permute-start | bytes 786440 | tf_op jit(solution)/shard_map/ppermute | solution.py:226
  34.9 13.7 %copy-start.7 = (bf16[2,256,256]{2,1,0:T(8,128)(2,1)}, bf16[2,256,256]{2,1,0:T(8,128)(2,1)S(1)}, u32[]{:S(2)}) copy-start(bf16[2,256,256]{2,1,0:T(8,128)(2,1)S(1)} %collective-permute-done.10.refs_5_.refs_3_) | copy-start | bytes 786436
  34.9 8.3 %collective-permute-start.11 = (bf16[2,256,256]{2,1,0:T(8,128)(2,1)S(1)}, bf16[2,256,256]{2,1,0:T(8,128)(2,1)S(1)}, u32[]{:S(2)}, u32[]{:S(2)}) collective-permute-start(bf16[2,256,256]{2,1,0:T(8,128)(2,1)S(1)} %collective-permute-done.10.refs_5_.refs_3_), channel_id=1, source_target_pairs={{0,32},{32,64},{64,96},{96,128},{128,160},{160,192},{192,224},{224... | collective-permute-start | bytes 786440 | tf_op jit(solution)/shard_map/ppermute | solution.py:226
  38.5 10.1 %copy-start.8 = (bf16[2,256,256]{2,1,0:T(8,128)(2,1)}, bf16[2,256,256]{2,1,0:T(8,128)(2,1)S(1)}, u32[]{:S(2)}) copy-start(bf16[2,256,256]{2,1,0:T(8,128)(2,1)S(1)} %collective-permute-done.3.refs_6_.refs_4_) | copy-start | bytes 786436
  38.5 15.0 %collective-permute-start.4 = (bf16[2,256,256]{2,1,0:T(8,128)(2,1)S(1)}, bf16[2,256,256]{2,1,0:T(8,128)(2,1)S(1)}, u32[]{:S(2)}, u32[]{:S(2)}) collective-permute-start(bf16[2,256,256]{2,1,0:T(8,128)(2,1)S(1)} %collective-permute-done.3.refs_6_.refs_4_), channel_id=1, source_target_pairs={{0,32},{32,64},{64,96},{96,128},{128,160},{160,192},{192,224},{224... | collective-permute-start | bytes 786440 | tf_op jit(solution)/shard_map/ppermute | solution.py:226
  43.2 5.4 %copy-start.9 = (bf16[2,256,256]{2,1,0:T(8,128)(2,1)}, bf16[2,256,256]{2,1,0:T(8,128)(2,1)S(1)}, u32[]{:S(2)}) copy-start(bf16[2,256,256]{2,1,0:T(8,128)(2,1)S(1)} %collective-permute-done.11.refs_7_.refs_5_) | copy-start | bytes 786436
  43.2 12.2 %collective-permute-start.12 = (bf16[2,256,256]{2,1,0:T(8,128)(2,1)S(1)}, bf16[2,256,256]{2,1,0:T(8,128)(2,1)S(1)}, u32[]{:S(2)}, u32[]{:S(2)}) collective-permute-start(bf16[2,256,256]{2,1,0:T(8,128)(2,1)S(1)} %collective-permute-done.11.refs_7_.refs_5_), channel_id=1, source_target_pairs={{0,32},{32,64},{64,96},{96,128},{128,160},{160,192},{192,224},{224... | collective-permute-start | bytes 786440 | tf_op jit(solution)/shard_map/ppermute | solution.py:226
  48.6 33.0 %all-to-all-start.1 = ((bf16[4,4,2,256,256]{4,3,2,1,0:T(8,128)(2,1)}), bf16[4,4,2,256,256]{4,3,2,1,0:T(8,128)(2,1)}, u32[]{:S(2)}, u32[]{:S(2)}) async-start(bf16[4,4,2,256,256]{4,3,2,1,0:T(8,128)(2,1)} %broadcast_in_dim.9), calls=%async_computation.1 | async-start | bytes 8388608 | tf_op jit(solution)/shard_map/all_to_all | solution.py:209
  53.5 19.4 %copy-start.10 = (bf16[2,256,256]{2,1,0:T(8,128)(2,1)}, bf16[2,256,256]{2,1,0:T(8,128)(2,1)S(1)}, u32[]{:S(2)}) copy-start(bf16[2,256,256]{2,1,0:T(8,128)(2,1)S(1)} %collective-permute-done.4.refs_8_.refs_6_) | copy-start | bytes 786436
  53.5 7.5 %collective-permute-start.5 = (bf16[2,256,256]{2,1,0:T(8,128)(2,1)S(1)}, bf16[2,256,256]{2,1,0:T(8,128)(2,1)S(1)}, u32[]{:S(2)}, u32[]{:S(2)}) collective-permute-start(bf16[2,256,256]{2,1,0:T(8,128)(2,1)S(1)} %collective-permute-done.4.refs_8_.refs_6_), channel_id=1, source_target_pairs={{0,32},{32,64},{64,96},{96,128},{128,160},{160,192},{192,224},{224... | collective-permute-start | bytes 786440 | tf_op jit(solution)/shard_map/ppermute | solution.py:226
  55.4 17.5 %copy-start.11 = (bf16[2,256,256]{2,1,0:T(8,128)(2,1)}, bf16[2,256,256]{2,1,0:T(8,128)(2,1)S(1)}, u32[]{:S(2)}) copy-start(bf16[2,256,256]{2,1,0:T(8,128)(2,1)S(1)} %collective-permute-done.12.refs_9_.refs_7_) | copy-start | bytes 786436
  55.4 8.7 %collective-permute-start.13 = (bf16[2,256,256]{2,1,0:T(8,128)(2,1)S(1)}, bf16[2,256,256]{2,1,0:T(8,128)(2,1)S(1)}, u32[]{:S(2)}, u32[]{:S(2)}) collective-permute-start(bf16[2,256,256]{2,1,0:T(8,128)(2,1)S(1)} %collective-permute-done.12.refs_9_.refs_7_), channel_id=1, source_target_pairs={{0,32},{32,64},{64,96},{96,128},{128,160},{160,192},{192,224},{224... | collective-permute-start | bytes 786440 | tf_op jit(solution)/shard_map/ppermute | solution.py:226
  61.0 11.9 %copy-start.12 = (bf16[2,256,256]{2,1,0:T(8,128)(2,1)}, bf16[2,256,256]{2,1,0:T(8,128)(2,1)S(1)}, u32[]{:S(2)}) copy-start(bf16[2,256,256]{2,1,0:T(8,128)(2,1)S(1)} %collective-permute-done.5.refs_10_.refs_8_) | copy-start | bytes 786436
  61.0 7.5 %collective-permute-start.6 = (bf16[2,256,256]{2,1,0:T(8,128)(2,1)S(1)}, bf16[2,256,256]{2,1,0:T(8,128)(2,1)S(1)}, u32[]{:S(2)}, u32[]{:S(2)}) collective-permute-start(bf16[2,256,256]{2,1,0:T(8,128)(2,1)S(1)} %collective-permute-done.5.refs_10_.refs_8_), channel_id=1, source_target_pairs={{0,32},{32,64},{64,96},{96,128},{128,160},{160,192},{192,224},{224... | collective-permute-start | bytes 786440 | tf_op jit(solution)/shard_map/ppermute | solution.py:226
  64.1 8.8 %copy-start.13 = (bf16[2,256,256]{2,1,0:T(8,128)(2,1)}, bf16[2,256,256]{2,1,0:T(8,128)(2,1)S(1)}, u32[]{:S(2)}) copy-start(bf16[2,256,256]{2,1,0:T(8,128)(2,1)S(1)} %collective-permute-done.13.refs_11_.refs_9_) | copy-start | bytes 786436
  64.1 8.7 %collective-permute-start.14 = (bf16[2,256,256]{2,1,0:T(8,128)(2,1)S(1)}, bf16[2,256,256]{2,1,0:T(8,128)(2,1)S(1)}, u32[]{:S(2)}, u32[]{:S(2)}) collective-permute-start(bf16[2,256,256]{2,1,0:T(8,128)(2,1)S(1)} %collective-permute-done.13.refs_11_.refs_9_), channel_id=1, source_target_pairs={{0,32},{32,64},{64,96},{96,128},{128,160},{160,192},{192,224},{224... | collective-permute-start | bytes 786440 | tf_op jit(solution)/shard_map/ppermute | solution.py:226
  68.5 4.4 %copy-start.14 = (bf16[2,256,256]{2,1,0:T(8,128)(2,1)}, bf16[2,256,256]{2,1,0:T(8,128)(2,1)S(1)}, u32[]{:S(2)}) copy-start(bf16[2,256,256]{2,1,0:T(8,128)(2,1)S(1)} %collective-permute-done.6.refs_12_.refs_10_) | copy-start | bytes 786436
  68.5 7.6 %collective-permute-start.7 = (bf16[2,256,256]{2,1,0:T(8,128)(2,1)S(1)}, bf16[2,256,256]{2,1,0:T(8,128)(2,1)S(1)}, u32[]{:S(2)}, u32[]{:S(2)}) collective-permute-start(bf16[2,256,256]{2,1,0:T(8,128)(2,1)S(1)} %collective-permute-done.6.refs_12_.refs_10_), channel_id=1, source_target_pairs={{0,32},{32,64},{64,96},{96,128},{128,160},{160,192},{192,224},{224... | collective-permute-start | bytes 786440 | tf_op jit(solution)/shard_map/ppermute | solution.py:226
  72.9 8.7 %copy-start.1 = (bf16[2,256,256]{2,1,0:T(8,128)(2,1)}, bf16[2,256,256]{2,1,0:T(8,128)(2,1)S(1)}, u32[]{:S(2)}) copy-start(bf16[2,256,256]{2,1,0:T(8,128)(2,1)S(1)} %shard_map.29.refs_13_.refs_11_) | copy-start | bytes 786436
  72.9 9.4 %collective-permute-start.15 = (bf16[2,256,256]{2,1,0:T(8,128)(2,1)S(1)}, bf16[2,256,256]{2,1,0:T(8,128)(2,1)S(1)}, u32[]{:S(2)}, u32[]{:S(2)}) collective-permute-start(bf16[2,256,256]{2,1,0:T(8,128)(2,1)S(1)} %shard_map.29.refs_13_.refs_11_), channel_id=1, source_target_pairs={{0,32},{32,64},{64,96},{96,128},{128,160},{160,192},{192,224},{224... | collective-permute-start | bytes 786440 | tf_op jit(solution)/shard_map/ppermute | solution.py:226
  76.1 6.2 %copy-start.16 = (bf16[2,256,256]{2,1,0:T(8,128)(2,1)}, bf16[2,256,256]{2,1,0:T(8,128)(2,1)S(1)}, u32[]{:S(2)}) copy-start(bf16[2,256,256]{2,1,0:T(8,128)(2,1)S(1)} %collective-permute-done.7.refs_12_) | copy-start | bytes 786436
  76.1 12.7 %collective-permute-start.8 = (bf16[2,256,256]{2,1,0:T(8,128)(2,1)S(1)}, bf16[2,256,256]{2,1,0:T(8,128)(2,1)S(1)}, u32[]{:S(2)}, u32[]{:S(2)}) collective-permute-start(bf16[2,256,256]{2,1,0:T(8,128)(2,1)S(1)} %collective-permute-done.7.refs_12_), channel_id=1, source_target_pairs={{16,496},{48,16},{80,48},{112,80},{144,112},{176,144},{208,176},{2... | collective-permute-start | bytes 786440 | tf_op jit(solution)/shard_map/ppermute | solution.py:226
  82.3 1.9 %copy-start.2 = (bf16[2,256,256]{2,1,0:T(8,128)(2,1)}, bf16[2,256,256]{2,1,0:T(8,128)(2,1)S(1)}, u32[]{:S(2)}) copy-start(bf16[2,256,256]{2,1,0:T(8,128)(2,1)S(1)} %shard_map.31.refs_13_) | copy-start | bytes 786436
  82.3 7.1 %collective-permute-start.16 = (bf16[2,256,256]{2,1,0:T(8,128)(2,1)S(1)}, bf16[2,256,256]{2,1,0:T(8,128)(2,1)S(1)}, u32[]{:S(2)}, u32[]{:S(2)}) collective-permute-start(bf16[2,256,256]{2,1,0:T(8,128)(2,1)S(1)} %shard_map.31.refs_13_), channel_id=1, source_target_pairs={{16,496},{48,16},{80,48},{112,80},{144,112},{176,144},{208,176},{2... | collective-permute-start | bytes 786440 | tf_op jit(solution)/shard_map/ppermute | solution.py:226
  90.8 20.2 %copy-start.3 = (bf16[1,2,256,256]{3,2,1,0:T(8,128)(2,1)S(1)}, bf16[1,2,256,256]{3,2,1,0:T(8,128)(2,1)}, u32[]{:S(2)}) copy-start(bf16[1,2,256,256]{3,2,1,0:T(8,128)(2,1)} %param.3) | copy-start | bytes 786436
  90.8 3.9 %collective-permute-start.17 = (f32[2,256,256]{2,1,0:T(8,128)S(1)}, f32[2,256,256]{2,1,0:T(8,128)S(1)}, u32[]{:S(2)}, u32[]{:S(2)}) collective-permute-start(f32[2,256,256]{2,1,0:T(8,128)S(1)} %shard_map.34), channel_id=1, source_target_pairs={{0,16},{16,0},{1,17},{17,1},{2,18},{18,2},{3,19},{19,3},{4,20},{20... | collective-permute-start | bytes 1572872 | tf_op jit(solution)/shard_map/ppermute | solution.py:231

commit v13 on v12

--- a/solution.py
+++ b/solution.py
@@ -77,9 +77,12 @@
         plan.append((copies, guard))
     for group in groups:
         fetch([plan[i] for i in group], core_ref, True)
-    if not carried:
-        for total in totals:
-            total[...] = jnp.zeros_like(total)
+    if len(planes) > 1:
+        @pl.when(core == int(carried))
+        def _():
+            for total in totals:
+                total[...] = jnp.zeros_like(total)
+
     width = held.shape[-1]
     for group in groups:
         fetch([plan[i] for i in group], core_ref, False)
@@ -141,14 +144,13 @@
 
 
 def blend_kernel(scale, columns, own_ref, column_ref, tiles_ref, inflated_ref, parts_ref, out_ref):
-    totals = jnp.sum(parts_ref[...], axis=0)
+    factors = 0.5 * scale / jnp.sum(parts_ref[...], axis=0)
     for slot in range(2):
         tile = tiles_ref[slot].astype(jnp.float32)
         for place in range(2):
             @pl.when(own_ref[slot] == column_ref[0] + columns * place)
             def _():
-                normed = inflated_ref[place] * scale / totals[place : place + 1, :]
-                out_ref[slot] = 0.5 * tile + 0.5 * normed
+                out_ref[slot] = 0.5 * tile + inflated_ref[place] * factors[place : place + 1, :]
 
         @pl.when(own_ref[slot] < 0)
         def _():

time: 113 us -> 113 us (level)
  no operation moved by 1% of the time
where the time goes in v13:
time: 113 us; the launch traced here: 112 us
  starting transfers between devices  72.1 us (64%)
  blocking collectives  15.5 us (14%)
  Pallas kernels  11.3 us (10%)
  waiting for transfers between devices  9.4 us (8%)
  local copies, waits for them, and re-layouts  3.65 us (3%)
    ppermute x16, starting transfers between devices, on_device(): held.append(tuple((lax.ppermute(t, ROWS, perm) for t in held[-1])))  52.2 us
    all_to_all x1, blocking collectives, on_device(): lax.all_to_all(jnp.broadcast_to(sums[None], (planes, *sums.shape)), 'z',...  13.7 us
    all_to_all x2, starting transfers between devices, copy_for_each(): lax.all_to_all(spread, ('core', *COLS), 0, 0, axis_index_groups=lines, ti...  9.04 us
    ppermute x16, waiting for transfers between devices, on_device(): held.append(tuple((lax.ppermute(t, ROWS, perm) for t in held[-1])))  8.86 us
    ppermute x1, starting transfers between devices, on_device(): other = lax.ppermute(mine, 'core', SWAP)  8.79 us
    pallas_call x4, Pallas kernels, products(): pl.pallas_call(kernel, in_specs=[SMEM, SMEM, HBM] + [HBM] * len(tiles) +...  7.89 us
    broadcast_in_dim x2, local copies, waits for them, and re-layouts, copy_for_each(): spread = jnp.broadcast_to(value[None], (len(lines[0]), *value.shape))  3.56 us
  transfers between devices with their start and end apart: 20, of which 7 were waited for; matrix products, arithmetic and copies ran while one was open for 3% of the time, Pallas kernels for 6%

profile of v13, /device:TPU:1, one launch (start us, length us, event | category | flops | bytes accessed | tf_op | source)
XLA Modules:
  0.0 112.5 jit_solution(16762648773560104069)
XLA Ops:
  0.0 1.1 shard_map.28.refs_0_
  1.1 0.0 copy-start
  1.1 8.8 %collective-permute-start = (bf16[2,256,256]{2,1,0:T(8,128)(2,1)S(1)}, bf16[2,256,256]{2,1,0:T(8,128)(2,1)S(1)}, u32[]{:S(2)}, u32[]{:S(2)}) collective-permute-start(bf16[2,256,256]{2,1,0:T(8,128)(2,1)S(1)} %shard_map.28.refs_0_), channel_id=1, source_target_pairs={{0,16},{16,0},{1,17},{17,1},{2,18},{18,2},{3,19},{19,3},{4,20},{20... | collective-permute-start | bytes 786440 | tf_op jit(solution)/shard_map/ppermute | solution.py:189
  9.9 5.7 %collective-permute-start.1 = (bf16[2,256,256]{2,1,0:T(8,128)(2,1)S(1)}, bf16[2,256,256]{2,1,0:T(8,128)(2,1)S(1)}, u32[]{:S(2)}, u32[]{:S(2)}) collective-permute-start(bf16[2,256,256]{2,1,0:T(8,128)(2,1)S(1)} %shard_map.28.refs_0_), channel_id=1, source_target_pairs={{0,32},{32,64},{64,96},{96,128},{128,160},{160,192},{192,224},{224... | collective-permute-start | bytes 786440 | tf_op jit(solution)/shard_map/ppermute | solution.py:228
  15.7 0.0 collective-permute-done.refs_1_
  15.7 0.0 copy-start.15
  15.7 2.6 %collective-permute-start.9 = (bf16[2,256,256]{2,1,0:T(8,128)(2,1)S(1)}, bf16[2,256,256]{2,1,0:T(8,128)(2,1)S(1)}, u32[]{:S(2)}, u32[]{:S(2)}) collective-permute-start(bf16[2,256,256]{2,1,0:T(8,128)(2,1)S(1)} %collective-permute-done.refs_1_), channel_id=1, source_target_pairs={{0,32},{32,64},{64,96},{96,128},{128,160},{160,192},{192,224},{224... | collective-permute-start | bytes 786440 | tf_op jit(solution)/shard_map/ppermute | solution.py:228
  18.4 1.0 broadcast_in_dim.8
  19.5 4.2 %all-to-all-start = ((bf16[4,2,256,256]{3,2,1,0:T(8,128)(2,1)}), bf16[4,2,256,256]{3,2,1,0:T(8,128)(2,1)S(1)}, u32[]{:S(2)}, u32[]{:S(2)}) async-start(bf16[4,2,256,256]{3,2,1,0:T(8,128)(2,1)} %broadcast_in_dim.8), calls=%async_computation | async-start | bytes 2097152 | tf_op jit(solution)/shard_map/all_to_all | solution.py:211
  23.6 0.0 collective-permute-done.1.refs_2_.refs_0_
  23.6 2.6 %collective-permute-start.2 = (bf16[2,256,256]{2,1,0:T(8,128)(2,1)S(1)}, bf16[2,256,256]{2,1,0:T(8,128)(2,1)S(1)}, u32[]{:S(2)}, u32[]{:S(2)}) collective-permute-start(bf16[2,256,256]{2,1,0:T(8,128)(2,1)S(1)} %collective-permute-done.1.refs_2_.refs_0_), channel_id=1, source_target_pairs={{0,32},{32,64},{64,96},{96,128},{128,160},{160,192},{192,224},{224... | collective-permute-start | bytes 786440 | tf_op jit(solution)/shard_map/ppermute | solution.py:228
  26.3 0.0 copy-done.15
  26.3 0.0 collective-permute-done.9.refs_3_.refs_1_
  26.3 0.0 copy-start.5
  26.3 2.6 %collective-permute-start.10 = (bf16[2,256,256]{2,1,0:T(8,128)(2,1)S(1)}, bf16[2,256,256]{2,1,0:T(8,128)(2,1)S(1)}, u32[]{:S(2)}, u32[]{:S(2)}) collective-permute-start(bf16[2,256,256]{2,1,0:T(8,128)(2,1)S(1)} %collective-permute-done.9.refs_3_.refs_1_), channel_id=1, source_target_pairs={{0,32},{32,64},{64,96},{96,128},{128,160},{160,192},{192,224},{224... | collective-permute-start | bytes 786440 | tf_op jit(solution)/shard_map/ppermute | solution.py:228
  29.0 2.1 %collective-permute-done.2.refs_4_.refs_2_ = bf16[2,256,256]{2,1,0:T(8,128)(2,1)S(1)} collective-permute-done((bf16[2,256,256]{2,1,0:T(8,128)(2,1)S(1)}, bf16[2,256,256]{2,1,0:T(8,128)(2,1)S(1)}, u32[]{:S(2)}, u32[]{:S(2)}) %collective-permute-start.2) | collective-permute-done | bytes 262176 | tf_op jit(solution)/shard_map/ppermute | solution.py:228
  31.1 3.8 %collective-permute-start.3 = (bf16[2,256,256]{2,1,0:T(8,128)(2,1)S(1)}, bf16[2,256,256]{2,1,0:T(8,128)(2,1)S(1)}, u32[]{:S(2)}, u32[]{:S(2)}) collective-permute-start(bf16[2,256,256]{2,1,0:T(8,128)(2,1)S(1)} %collective-permute-done.2.refs_4_.refs_2_), channel_id=1, source_target_pairs={{0,32},{32,64},{64,96},{96,128},{128,160},{160,192},{192,224},{224... | collective-permute-start | bytes 786440 | tf_op jit(solution)/shard_map/ppermute | solution.py:228
  34.9 0.0 collective-permute-done.10.refs_5_.refs_3_
  34.9 0.0 copy-start.7
  34.9 2.5 %collective-permute-start.11 = (bf16[2,256,256]{2,1,0:T(8,128)(2,1)S(1)}, bf16[2,256,256]{2,1,0:T(8,128)(2,1)S(1)}, u32[]{:S(2)}, u32[]{:S(2)}) collective-permute-start(bf16[2,256,256]{2,1,0:T(8,128)(2,1)S(1)} %collective-permute-done.10.refs_5_.refs_3_), channel_id=1, source_target_pairs={{0,32},{32,64},{64,96},{96,128},{128,160},{160,192},{192,224},{224... | collective-permute-start | bytes 786440 | tf_op jit(solution)/shard_map/ppermute | solution.py:228
  37.4 1.0 collective-permute-done.3.refs_6_.refs_4_
  38.5 4.8 %collective-permute-start.4 = (bf16[2,256,256]{2,1,0:T(8,128)(2,1)S(1)}, bf16[2,256,256]{2,1,0:T(8,128)(2,1)S(1)}, u32[]{:S(2)}, u32[]{:S(2)}) collective-permute-start(bf16[2,256,256]{2,1,0:T(8,128)(2,1)S(1)} %collective-permute-done.3.refs_6_.refs_4_), channel_id=1, source_target_pairs={{0,32},{32,64},{64,96},{96,128},{128,160},{160,192},{192,224},{224... | collective-permute-start | bytes 786440 | tf_op jit(solution)/shard_map/ppermute | solution.py:228
  43.2 0.0 collective-permute-done.11.refs_7_.refs_5_
  43.2 0.0 copy-start.9
  43.2 2.8 %collective-permute-start.12 = (bf16[2,256,256]{2,1,0:T(8,128)(2,1)S(1)}, bf16[2,256,256]{2,1,0:T(8,128)(2,1)S(1)}, u32[]{:S(2)}, u32[]{:S(2)}) collective-permute-start(bf16[2,256,256]{2,1,0:T(8,128)(2,1)S(1)} %collective-permute-done.11.refs_7_.refs_5_), channel_id=1, source_target_pairs={{0,32},{32,64},{64,96},{96,128},{128,160},{160,192},{192,224},{224... | collective-permute-start | bytes 786440 | tf_op jit(solution)/shard_map/ppermute | solution.py:228
  46.0 0.0 all-to-all-done
  46.0 2.5 %broadcast_in_dim.9 = bf16[4,4,2,256,256]{4,3,2,1,0:T(8,128)(2,1)} broadcast(bf16[4,2,256,256]{3,2,1,0:T(8,128)(2,1)S(1)} %all-to-all-done), dimensions={1,2,3,4} | broadcast | bytes 5242880 | tf_op jit(solution)/shard_map/broadcast_in_dim | solution.py:210
  48.5 0.0 copy-done
  48.5 0.0 copy-done.4
  48.5 0.0 copy-done.5
  48.6 0.0 copy-done.6
  48.6 4.9 %all-to-all-start.1 = ((bf16[4,4,2,256,256]{4,3,2,1,0:T(8,128)(2,1)}), bf16[4,4,2,256,256]{4,3,2,1,0:T(8,128)(2,1)}, u32[]{:S(2)}, u32[]{:S(2)}) async-start(bf16[4,4,2,256,256]{4,3,2,1,0:T(8,128)(2,1)} %broadcast_in_dim.9), calls=%async_computation.1 | async-start | bytes 8388608 | tf_op jit(solution)/shard_map/all_to_all | solution.py:211
  53.5 0.0 collective-permute-done.4.refs_8_.refs_6_
  53.5 1.9 %collective-permute-start.5 = (bf16[2,256,256]{2,1,0:T(8,128)(2,1)S(1)}, bf16[2,256,256]{2,1,0:T(8,128)(2,1)S(1)}, u32[]{:S(2)}, u32[]{:S(2)}) collective-permute-start(bf16[2,256,256]{2,1,0:T(8,128)(2,1)S(1)} %collective-permute-done.4.refs_8_.refs_6_), channel_id=1, source_target_pairs={{0,32},{32,64},{64,96},{96,128},{128,160},{160,192},{192,224},{224... | collective-permute-start | bytes 786440 | tf_op jit(solution)/shard_map/ppermute | solution.py:228
  55.4 0.0 collective-permute-done.12.refs_9_.refs_7_
  55.4 2.4 %collective-permute-start.13 = (bf16[2,256,256]{2,1,0:T(8,128)(2,1)S(1)}, bf16[2,256,256]{2,1,0:T(8,128)(2,1)S(1)}, u32[]{:S(2)}, u32[]{:S(2)}) collective-permute-start(bf16[2,256,256]{2,1,0:T(8,128)(2,1)S(1)} %collective-permute-done.12.refs_9_.refs_7_), channel_id=1, source_target_pairs={{0,32},{32,64},{64,96},{96,128},{128,160},{160,192},{192,224},{224... | collective-permute-start | bytes 786440 | tf_op jit(solution)/shard_map/ppermute | solution.py:228
  57.9 3.1 %collective-permute-done.5.refs_10_.refs_8_ = bf16[2,256,256]{2,1,0:T(8,128)(2,1)S(1)} collective-permute-done((bf16[2,256,256]{2,1,0:T(8,128)(2,1)S(1)}, bf16[2,256,256]{2,1,0:T(8,128)(2,1)S(1)}, u32[]{:S(2)}, u32[]{:S(2)}) %collective-permute-start.5) | collective-permute-done | bytes 262176 | tf_op jit(solution)/shard_map/ppermute | solution.py:228
  61.0 3.1 %collective-permute-start.6 = (bf16[2,256,256]{2,1,0:T(8,128)(2,1)S(1)}, bf16[2,256,256]{2,1,0:T(8,128)(2,1)S(1)}, u32[]{:S(2)}, u32[]{:S(2)}) collective-permute-start(bf16[2,256,256]{2,1,0:T(8,128)(2,1)S(1)} %collective-permute-done.5.refs_10_.refs_8_), channel_id=1, source_target_pairs={{0,32},{32,64},{64,96},{96,128},{128,160},{160,192},{192,224},{224... | collective-permute-start | bytes 786440 | tf_op jit(solution)/shard_map/ppermute | solution.py:228
  64.1 0.0 collective-permute-done.13.refs_11_.refs_9_
  64.1 0.0 copy-start.13
  64.1 2.8 %collective-permute-start.14 = (bf16[2,256,256]{2,1,0:T(8,128)(2,1)S(1)}, bf16[2,256,256]{2,1,0:T(8,128)(2,1)S(1)}, u32[]{:S(2)}, u32[]{:S(2)}) collective-permute-start(bf16[2,256,256]{2,1,0:T(8,128)(2,1)S(1)} %collective-permute-done.13.refs_11_.refs_9_), channel_id=1, source_target_pairs={{0,32},{32,64},{64,96},{96,128},{128,160},{160,192},{192,224},{224... | collective-permute-start | bytes 786440 | tf_op jit(solution)/shard_map/ppermute | solution.py:228
  66.9 1.6 %collective-permute-done.6.refs_12_.refs_10_ = bf16[2,256,256]{2,1,0:T(8,128)(2,1)S(1)} collective-permute-done((bf16[2,256,256]{2,1,0:T(8,128)(2,1)S(1)}, bf16[2,256,256]{2,1,0:T(8,128)(2,1)S(1)}, u32[]{:S(2)}, u32[]{:S(2)}) %collective-permute-start.6) | collective-permute-done | bytes 262176 | tf_op jit(solution)/shard_map/ppermute | solution.py:228
  68.5 4.3 %collective-permute-start.7 = (bf16[2,256,256]{2,1,0:T(8,128)(2,1)S(1)}, bf16[2,256,256]{2,1,0:T(8,128)(2,1)S(1)}, u32[]{:S(2)}, u32[]{:S(2)}) collective-permute-start(bf16[2,256,256]{2,1,0:T(8,128)(2,1)S(1)} %collective-permute-done.6.refs_12_.refs_10_), channel_id=1, source_target_pairs={{0,32},{32,64},{64,96},{96,128},{128,160},{160,192},{192,224},{224... | collective-permute-start | bytes 786440 | tf_op jit(solution)/shard_map/ppermute | solution.py:228
  72.8 0.0 collective-permute-done.14.refs_0_
  72.9 2.8 %collective-permute-start.15 = (bf16[2,256,256]{2,1,0:T(8,128)(2,1)S(1)}, bf16[2,256,256]{2,1,0:T(8,128)(2,1)S(1)}, u32[]{:S(2)}, u32[]{:S(2)}) collective-permute-start(bf16[2,256,256]{2,1,0:T(8,128)(2,1)S(1)} %shard_map.29.refs_13_.refs_11_), channel_id=1, source_target_pairs={{0,32},{32,64},{64,96},{96,128},{128,160},{160,192},{192,224},{224... | collective-permute-start | bytes 786440 | tf_op jit(solution)/shard_map/ppermute | solution.py:228
  75.7 0.4 collective-permute-done.7.refs_12_
  76.1 5.4 %collective-permute-start.8 = (bf16[2,256,256]{2,1,0:T(8,128)(2,1)S(1)}, bf16[2,256,256]{2,1,0:T(8,128)(2,1)S(1)}, u32[]{:S(2)}, u32[]{:S(2)}) collective-permute-start(bf16[2,256,256]{2,1,0:T(8,128)(2,1)S(1)} %collective-permute-done.7.refs_12_), channel_id=1, source_target_pairs={{16,496},{48,16},{80,48},{112,80},{144,112},{176,144},{208,176},{2... | collective-permute-start | bytes 786440 | tf_op jit(solution)/shard_map/ppermute | solution.py:228
  81.6 0.0 all-to-all-done.1.left_ref
  81.6 0.7 shard_map.30
  82.2 0.0 collective-permute-done.15.refs_0_
  82.3 0.0 copy-start.2
  82.3 1.9 %collective-permute-start.16 = (bf16[2,256,256]{2,1,0:T(8,128)(2,1)S(1)}, bf16[2,256,256]{2,1,0:T(8,128)(2,1)S(1)}, u32[]{:S(2)}, u32[]{:S(2)}) collective-permute-start(bf16[2,256,256]{2,1,0:T(8,128)(2,1)S(1)} %shard_map.31.refs_13_), channel_id=1, source_target_pairs={{16,496},{48,16},{80,48},{112,80},{144,112},{176,144},{208,176},{2... | collective-permute-start | bytes 786440 | tf_op jit(solution)/shard_map/ppermute | solution.py:228
  84.2 4.6 %shard_map.32 = (f32[2,256,256]{2,1,0:T(8,128)S(1)}, f32[2,256,256]{2,1,0:T(8,128)S(1)}) custom-call(s32[1]{0:T(128)} %bitcast.3.plane_ref, s32[1]{0:T(128)} %bitcast.4.core_ref, bf16[4,4,2,256,256]{4,3,2,1,0:T(8,128)(2,1)} %all-to-all-done.1.left_ref, bf16[2,256,256]{2,1,0:T(8,128)(2,1)} %copy-done.4, ...), custom_call_target="tpu_custom_call", output_to_operand_aliasing={{0}: (17, {}), {1}: (18, {})} | custom-call | flops 1879048192 | bytes 14680064 | tf_op jit(solution)/shard_map/pallas_call | solution.py:115
  88.8 0.0 collective-permute-done.8.refs_0_
  88.8 0.6 collective-permute-done.16.refs_1_
  89.4 1.3 %shard_map.34 = f32[2,256,256]{2,1,0:T(8,128)S(1)} custom-call(s32[1]{0:T(128)} %bitcast.3.plane_ref, s32[1]{0:T(128)} %bitcast.4.core_ref, bf16[4,4,2,256,256]{4,3,2,1,0:T(8,128)(2,1)} %all-to-all-done.1.left_ref, bf16[2,256,256]{2,1,0:T(8,128)(2,1)S(1)} %collective-permute-done.8.refs_0_, ...), custom_call_target="tpu_custom_call", output_to_operand_aliasing={{}: (5, {})} | custom-call | flops 134217728 | bytes 1572864 | tf_op jit(solution)/shard_map/pallas_call | solution.py:115
  90.7 0.0 copy-start.3
  90.7 2.1 %collective-permute-start.17 = (f32[2,256,256]{2,1,0:T(8,128)S(1)}, f32[2,256,256]{2,1,0:T(8,128)S(1)}, u32[]{:S(2)}, u32[]{:S(2)}) collective-permute-start(f32[2,256,256]{2,1,0:T(8,128)S(1)} %shard_map.34), channel_id=1, source_target_pairs={{0,16},{16,0},{1,17},{17,1},{2,18},{18,2},{3,19},{19,3},{4,20},{20... | collective-permute-start | bytes 1572872 | tf_op jit(solution)/shard_map/ppermute | solution.py:233
  92.8 1.3 %shard_map.33.mine_ref = f32[2,256,256]{2,1,0:T(8,128)S(1)} custom-call(s32[1]{0:T(128)} %bitcast.3.plane_ref, s32[1]{0:T(128)} %bitcast.4.core_ref, bf16[4,4,2,256,256]{4,3,2,1,0:T(8,128)(2,1)} %all-to-all-done.1.left_ref, bf16[2,256,256]{2,1,0:T(8,128)(2,1)S(1)} %collective-permute-done.8.refs_0_, ...), custom_call_target="tpu_custom_call", output_to_operand_aliasing={{}: (5, {})} | custom-call | flops 134217728 | bytes 1572864 | tf_op jit(solution)/shard_map/pallas_call | solution.py:115
  94.1 0.5 collective-permute-done.17.other_ref
  94.7 0.7 shard_map.35
  95.4 1.8 %all-gather.1 = f32[2,2,256]{2,1,0:T(2,128)S(1)} all-gather(f32[1,2,256]{2,1,0:T(2,128)S(1)} %bitcast.9), channel_id=2, replica_groups=mesh['z'=16,'core'=2,'y'=4,'x'=4] {'core'}, dimensions={0}, use_global_device_ids=true | all-gather | bytes 6144 | tf_op jit(solution)/shard_map/all_gather | solution.py:245
  97.2 13.7 %all_to_all.15.parts_ref = f32[16,2,256]{2,1,0:T(2,128)S(1)} all-to-all(f32[16,2,256]{2,1,0:T(2,128)S(1)} %broadcast_in_dim.10), channel_id=1, replica_groups={{256,288,320,352,384,416,448,480,0,32,64,96,128,160,192,224},{257,289,3..., dimensions={0} | all-to-all | bytes 65536 | tf_op jit(solution)/shard_map/all_to_all | solution.py:247
  110.9 1.6 %shard_map.36 = f32[2,256,256]{2,1,0:T(8,128)} custom-call(s32[2]{0:T(128)} %bitcast.12, s32[1]{0:T(128)} %bitcast.1.column_ref, bf16[2,256,256]{2,1,0:T(8,128)(2,1)S(1)} %bitcast.8, f32[2,256,256]{2,1,0:T(8,128)S(1)} %get-tuple-element.15.inflated_ref, f32[16,2,256]{2,1,0:T(2,128)S(1)} %all_to_all.15.parts_ref), custom_call_target="tpu_custom_call" | custom-call | tf_op jit(solution)/shard_map/pallas_call | solution.py:256
  (28 shorter events, 0.1 us)
Async XLA Ops:
  1.1 47.5 %copy-start = (bf16[2,256,256]{2,1,0:T(8,128)(2,1)}, bf16[2,256,256]{2,1,0:T(8,128)(2,1)S(1)}, u32[]{:S(2)}) copy-start(bf16[2,256,256]{2,1,0:T(8,128)(2,1)S(1)} %shard_map.28.refs_0_) | copy-start | bytes 786436
  1.1 14.6 %collective-permute-start = (bf16[2,256,256]{2,1,0:T(8,128)(2,1)S(1)}, bf16[2,256,256]{2,1,0:T(8,128)(2,1)S(1)}, u32[]{:S(2)}, u32[]{:S(2)}) collective-permute-start(bf16[2,256,256]{2,1,0:T(8,128)(2,1)S(1)} %shard_map.28.refs_0_), channel_id=1, source_target_pairs={{0,16},{16,0},{1,17},{17,1},{2,18},{18,2},{3,19},{19,3},{4,20},{20... | collective-permute-start | bytes 786440 | tf_op jit(solution)/shard_map/ppermute | solution.py:189
  9.9 13.8 %collective-permute-start.1 = (bf16[2,256,256]{2,1,0:T(8,128)(2,1)S(1)}, bf16[2,256,256]{2,1,0:T(8,128)(2,1)S(1)}, u32[]{:S(2)}, u32[]{:S(2)}) collective-permute-start(bf16[2,256,256]{2,1,0:T(8,128)(2,1)S(1)} %shard_map.28.refs_0_), channel_id=1, source_target_pairs={{0,32},{32,64},{64,96},{96,128},{128,160},{160,192},{192,224},{224... | collective-permute-start | bytes 786440 | tf_op jit(solution)/shard_map/ppermute | solution.py:228
  15.7 10.6 %copy-start.15 = (bf16[2,256,256]{2,1,0:T(8,128)(2,1)}, bf16[2,256,256]{2,1,0:T(8,128)(2,1)S(1)}, u32[]{:S(2)}) copy-start(bf16[2,256,256]{2,1,0:T(8,128)(2,1)S(1)} %collective-permute-done.refs_1_) | copy-start | bytes 786436
  15.7 10.6 %collective-permute-start.9 = (bf16[2,256,256]{2,1,0:T(8,128)(2,1)S(1)}, bf16[2,256,256]{2,1,0:T(8,128)(2,1)S(1)}, u32[]{:S(2)}, u32[]{:S(2)}) collective-permute-start(bf16[2,256,256]{2,1,0:T(8,128)(2,1)S(1)} %collective-permute-done.refs_1_), channel_id=1, source_target_pairs={{0,32},{32,64},{64,96},{96,128},{128,160},{160,192},{192,224},{224... | collective-permute-start | bytes 786440 | tf_op jit(solution)/shard_map/ppermute | solution.py:228
  19.5 26.6 %all-to-all-start = ((bf16[4,2,256,256]{3,2,1,0:T(8,128)(2,1)}), bf16[4,2,256,256]{3,2,1,0:T(8,128)(2,1)S(1)}, u32[]{:S(2)}, u32[]{:S(2)}) async-start(bf16[4,2,256,256]{3,2,1,0:T(8,128)(2,1)} %broadcast_in_dim.8), calls=%async_computation | async-start | bytes 2097152 | tf_op jit(solution)/shard_map/all_to_all | solution.py:211
  23.6 24.9 %copy-start.4 = (bf16[2,256,256]{2,1,0:T(8,128)(2,1)}, bf16[2,256,256]{2,1,0:T(8,128)(2,1)S(1)}, u32[]{:S(2)}) copy-start(bf16[2,256,256]{2,1,0:T(8,128)(2,1)S(1)} %collective-permute-done.1.refs_2_.refs_0_) | copy-start | bytes 786436
  23.6 7.4 %collective-permute-start.2 = (bf16[2,256,256]{2,1,0:T(8,128)(2,1)S(1)}, bf16[2,256,256]{2,1,0:T(8,128)(2,1)S(1)}, u32[]{:S(2)}, u32[]{:S(2)}) collective-permute-start(bf16[2,256,256]{2,1,0:T(8,128)(2,1)S(1)} %collective-permute-done.1.refs_2_.refs_0_), channel_id=1, source_target_pairs={{0,32},{32,64},{64,96},{96,128},{128,160},{160,192},{192,224},{224... | collective-permute-start | bytes 786440 | tf_op jit(solution)/shard_map/ppermute | solution.py:228
  26.3 22.2 %copy-start.5 = (bf16[2,256,256]{2,1,0:T(8,128)(2,1)}, bf16[2,256,256]{2,1,0:T(8,128)(2,1)S(1)}, u32[]{:S(2)}) copy-start(bf16[2,256,256]{2,1,0:T(8,128)(2,1)S(1)} %collective-permute-done.9.refs_3_.refs_1_) | copy-start | bytes 786436
  26.3 8.6 %collective-permute-start.10 = (bf16[2,256,256]{2,1,0:T(8,128)(2,1)S(1)}, bf16[2,256,256]{2,1,0:T(8,128)(2,1)S(1)}, u32[]{:S(2)}, u32[]{:S(2)}) collective-permute-start(bf16[2,256,256]{2,1,0:T(8,128)(2,1)S(1)} %collective-permute-done.9.refs_3_.refs_1_), channel_id=1, source_target_pairs={{0,32},{32,64},{64,96},{96,128},{128,160},{160,192},{192,224},{224... | collective-permute-start | bytes 786440 | tf_op jit(solution)/shard_map/ppermute | solution.py:228
  31.1 17.5 %copy-start.6 = (bf16[2,256,256]{2,1,0:T(8,128)(2,1)}, bf16[2,256,256]{2,1,0:T(8,128)(2,1)S(1)}, u32[]{:S(2)}) copy-start(bf16[2,256,256]{2,1,0:T(8,128)(2,1)S(1)} %collective-permute-done.2.refs_4_.refs_2_) | copy-start | bytes 786436
  31.1 7.4 %collective-permute-start.3 = (bf16[2,256,256]{2,1,0:T(8,128)(2,1)S(1)}, bf16[2,256,256]{2,1,0:T(8,128)(2,1)S(1)}, u32[]{:S(2)}, u32[]{:S(2)}) collective-permute-start(bf16[2,256,256]{2,1,0:T(8,128)(2,1)S(1)} %collective-permute-done.2.refs_4_.refs_2_), channel_id=1, source_target_pairs={{0,32},{32,64},{64,96},{96,128},{128,160},{160,192},{192,224},{224... | collective-permute-start | bytes 786440 | tf_op jit(solution)/shard_map/ppermute | solution.py:228
  34.9 13.7 %copy-start.7 = (bf16[2,256,256]{2,1,0:T(8,128)(2,1)}, bf16[2,256,256]{2,1,0:T(8,128)(2,1)S(1)}, u32[]{:S(2)}) copy-start(bf16[2,256,256]{2,1,0:T(8,128)(2,1)S(1)} %collective-permute-done.10.refs_5_.refs_3_) | copy-start | bytes 786436
  34.9 8.3 %collective-permute-start.11 = (bf16[2,256,256]{2,1,0:T(8,128)(2,1)S(1)}, bf16[2,256,256]{2,1,0:T(8,128)(2,1)S(1)}, u32[]{:S(2)}, u32[]{:S(2)}) collective-permute-start(bf16[2,256,256]{2,1,0:T(8,128)(2,1)S(1)} %collective-permute-done.10.refs_5_.refs_3_), channel_id=1, source_target_pairs={{0,32},{32,64},{64,96},{96,128},{128,160},{160,192},{192,224},{224... | collective-permute-start | bytes 786440 | tf_op jit(solution)/shard_map/ppermute | solution.py:228
  38.5 10.1 %copy-start.8 = (bf16[2,256,256]{2,1,0:T(8,128)(2,1)}, bf16[2,256,256]{2,1,0:T(8,128)(2,1)S(1)}, u32[]{:S(2)}) copy-start(bf16[2,256,256]{2,1,0:T(8,128)(2,1)S(1)} %collective-permute-done.3.refs_6_.refs_4_) | copy-start | bytes 786436
  38.5 15.0 %collective-permute-start.4 = (bf16[2,256,256]{2,1,0:T(8,128)(2,1)S(1)}, bf16[2,256,256]{2,1,0:T(8,128)(2,1)S(1)}, u32[]{:S(2)}, u32[]{:S(2)}) collective-permute-start(bf16[2,256,256]{2,1,0:T(8,128)(2,1)S(1)} %collective-permute-done.3.refs_6_.refs_4_), channel_id=1, source_target_pairs={{0,32},{32,64},{64,96},{96,128},{128,160},{160,192},{192,224},{224... | collective-permute-start | bytes 786440 | tf_op jit(solution)/shard_map/ppermute | solution.py:228
  43.2 5.4 %copy-start.9 = (bf16[2,256,256]{2,1,0:T(8,128)(2,1)}, bf16[2,256,256]{2,1,0:T(8,128)(2,1)S(1)}, u32[]{:S(2)}) copy-start(bf16[2,256,256]{2,1,0:T(8,128)(2,1)S(1)} %collective-permute-done.11.refs_7_.refs_5_) | copy-start | bytes 786436
  43.2 12.2 %collective-permute-start.12 = (bf16[2,256,256]{2,1,0:T(8,128)(2,1)S(1)}, bf16[2,256,256]{2,1,0:T(8,128)(2,1)S(1)}, u32[]{:S(2)}, u32[]{:S(2)}) collective-permute-start(bf16[2,256,256]{2,1,0:T(8,128)(2,1)S(1)} %collective-permute-done.11.refs_7_.refs_5_), channel_id=1, source_target_pairs={{0,32},{32,64},{64,96},{96,128},{128,160},{160,192},{192,224},{224... | collective-permute-start | bytes 786440 | tf_op jit(solution)/shard_map/ppermute | solution.py:228
  48.6 33.0 %all-to-all-start.1 = ((bf16[4,4,2,256,256]{4,3,2,1,0:T(8,128)(2,1)}), bf16[4,4,2,256,256]{4,3,2,1,0:T(8,128)(2,1)}, u32[]{:S(2)}, u32[]{:S(2)}) async-start(bf16[4,4,2,256,256]{4,3,2,1,0:T(8,128)(2,1)} %broadcast_in_dim.9), calls=%async_computation.1 | async-start | bytes 8388608 | tf_op jit(solution)/shard_map/all_to_all | solution.py:211
  53.5 19.4 %copy-start.10 = (bf16[2,256,256]{2,1,0:T(8,128)(2,1)}, bf16[2,256,256]{2,1,0:T(8,128)(2,1)S(1)}, u32[]{:S(2)}) copy-start(bf16[2,256,256]{2,1,0:T(8,128)(2,1)S(1)} %collective-permute-done.4.refs_8_.refs_6_) | copy-start | bytes 786436
  53.5 7.5 %collective-permute-start.5 = (bf16[2,256,256]{2,1,0:T(8,128)(2,1)S(1)}, bf16[2,256,256]{2,1,0:T(8,128)(2,1)S(1)}, u32[]{:S(2)}, u32[]{:S(2)}) collective-permute-start(bf16[2,256,256]{2,1,0:T(8,128)(2,1)S(1)} %collective-permute-done.4.refs_8_.refs_6_), channel_id=1, source_target_pairs={{0,32},{32,64},{64,96},{96,128},{128,160},{160,192},{192,224},{224... | collective-permute-start | bytes 786440 | tf_op jit(solution)/shard_map/ppermute | solution.py:228
  55.4 17.5 %copy-start.11 = (bf16[2,256,256]{2,1,0:T(8,128)(2,1)}, bf16[2,256,256]{2,1,0:T(8,128)(2,1)S(1)}, u32[]{:S(2)}) copy-start(bf16[2,256,256]{2,1,0:T(8,128)(2,1)S(1)} %collective-permute-done.12.refs_9_.refs_7_) | copy-start | bytes 786436
  55.4 8.7 %collective-permute-start.13 = (bf16[2,256,256]{2,1,0:T(8,128)(2,1)S(1)}, bf16[2,256,256]{2,1,0:T(8,128)(2,1)S(1)}, u32[]{:S(2)}, u32[]{:S(2)}) collective-permute-start(bf16[2,256,256]{2,1,0:T(8,128)(2,1)S(1)} %collective-permute-done.12.refs_9_.refs_7_), channel_id=1, source_target_pairs={{0,32},{32,64},{64,96},{96,128},{128,160},{160,192},{192,224},{224... | collective-permute-start | bytes 786440 | tf_op jit(solution)/shard_map/ppermute | solution.py:228
  61.0 11.9 %copy-start.12 = (bf16[2,256,256]{2,1,0:T(8,128)(2,1)}, bf16[2,256,256]{2,1,0:T(8,128)(2,1)S(1)}, u32[]{:S(2)}) copy-start(bf16[2,256,256]{2,1,0:T(8,128)(2,1)S(1)} %collective-permute-done.5.refs_10_.refs_8_) | copy-start | bytes 786436
  61.0 7.5 %collective-permute-start.6 = (bf16[2,256,256]{2,1,0:T(8,128)(2,1)S(1)}, bf16[2,256,256]{2,1,0:T(8,128)(2,1)S(1)}, u32[]{:S(2)}, u32[]{:S(2)}) collective-permute-start(bf16[2,256,256]{2,1,0:T(8,128)(2,1)S(1)} %collective-permute-done.5.refs_10_.refs_8_), channel_id=1, source_target_pairs={{0,32},{32,64},{64,96},{96,128},{128,160},{160,192},{192,224},{224... | collective-permute-start | bytes 786440 | tf_op jit(solution)/shard_map/ppermute | solution.py:228
  64.1 8.8 %copy-start.13 = (bf16[2,256,256]{2,1,0:T(8,128)(2,1)}, bf16[2,256,256]{2,1,0:T(8,128)(2,1)S(1)}, u32[]{:S(2)}) copy-start(bf16[2,256,256]{2,1,0:T(8,128)(2,1)S(1)} %collective-permute-done.13.refs_11_.refs_9_) | copy-start | bytes 786436
  64.1 8.7 %collective-permute-start.14 = (bf16[2,256,256]{2,1,0:T(8,128)(2,1)S(1)}, bf16[2,256,256]{2,1,0:T(8,128)(2,1)S(1)}, u32[]{:S(2)}, u32[]{:S(2)}) collective-permute-start(bf16[2,256,256]{2,1,0:T(8,128)(2,1)S(1)} %collective-permute-done.13.refs_11_.refs_9_), channel_id=1, source_target_pairs={{0,32},{32,64},{64,96},{96,128},{128,160},{160,192},{192,224},{224... | collective-permute-start | bytes 786440 | tf_op jit(solution)/shard_map/ppermute | solution.py:228
  68.5 4.4 %copy-start.14 = (bf16[2,256,256]{2,1,0:T(8,128)(2,1)}, bf16[2,256,256]{2,1,0:T(8,128)(2,1)S(1)}, u32[]{:S(2)}) copy-start(bf16[2,256,256]{2,1,0:T(8,128)(2,1)S(1)} %collective-permute-done.6.refs_12_.refs_10_) | copy-start | bytes 786436
  68.5 7.6 %collective-permute-start.7 = (bf16[2,256,256]{2,1,0:T(8,128)(2,1)S(1)}, bf16[2,256,256]{2,1,0:T(8,128)(2,1)S(1)}, u32[]{:S(2)}, u32[]{:S(2)}) collective-permute-start(bf16[2,256,256]{2,1,0:T(8,128)(2,1)S(1)} %collective-permute-done.6.refs_12_.refs_10_), channel_id=1, source_target_pairs={{0,32},{32,64},{64,96},{96,128},{128,160},{160,192},{192,224},{224... | collective-permute-start | bytes 786440 | tf_op jit(solution)/shard_map/ppermute | solution.py:228
  72.9 8.7 %copy-start.1 = (bf16[2,256,256]{2,1,0:T(8,128)(2,1)}, bf16[2,256,256]{2,1,0:T(8,128)(2,1)S(1)}, u32[]{:S(2)}) copy-start(bf16[2,256,256]{2,1,0:T(8,128)(2,1)S(1)} %shard_map.29.refs_13_.refs_11_) | copy-start | bytes 786436
  72.9 9.3 %collective-permute-start.15 = (bf16[2,256,256]{2,1,0:T(8,128)(2,1)S(1)}, bf16[2,256,256]{2,1,0:T(8,128)(2,1)S(1)}, u32[]{:S(2)}, u32[]{:S(2)}) collective-permute-start(bf16[2,256,256]{2,1,0:T(8,128)(2,1)S(1)} %shard_map.29.refs_13_.refs_11_), channel_id=1, source_target_pairs={{0,32},{32,64},{64,96},{96,128},{128,160},{160,192},{192,224},{224... | collective-permute-start | bytes 786440 | tf_op jit(solution)/shard_map/ppermute | solution.py:228
  76.1 6.1 %copy-start.16 = (bf16[2,256,256]{2,1,0:T(8,128)(2,1)}, bf16[2,256,256]{2,1,0:T(8,128)(2,1)S(1)}, u32[]{:S(2)}) copy-start(bf16[2,256,256]{2,1,0:T(8,128)(2,1)S(1)} %collective-permute-done.7.refs_12_) | copy-start | bytes 786436
  76.1 12.7 %collective-permute-start.8 = (bf16[2,256,256]{2,1,0:T(8,128)(2,1)S(1)}, bf16[2,256,256]{2,1,0:T(8,128)(2,1)S(1)}, u32[]{:S(2)}, u32[]{:S(2)}) collective-permute-start(bf16[2,256,256]{2,1,0:T(8,128)(2,1)S(1)} %collective-permute-done.7.refs_12_), channel_id=1, source_target_pairs={{16,496},{48,16},{80,48},{112,80},{144,112},{176,144},{208,176},{2... | collective-permute-start | bytes 786440 | tf_op jit(solution)/shard_map/ppermute | solution.py:228
  82.3 1.9 %copy-start.2 = (bf16[2,256,256]{2,1,0:T(8,128)(2,1)}, bf16[2,256,256]{2,1,0:T(8,128)(2,1)S(1)}, u32[]{:S(2)}) copy-start(bf16[2,256,256]{2,1,0:T(8,128)(2,1)S(1)} %shard_map.31.refs_13_) | copy-start | bytes 786436
  82.3 7.1 %collective-permute-start.16 = (bf16[2,256,256]{2,1,0:T(8,128)(2,1)S(1)}, bf16[2,256,256]{2,1,0:T(8,128)(2,1)S(1)}, u32[]{:S(2)}, u32[]{:S(2)}) collective-permute-start(bf16[2,256,256]{2,1,0:T(8,128)(2,1)S(1)} %shard_map.31.refs_13_), channel_id=1, source_target_pairs={{16,496},{48,16},{80,48},{112,80},{144,112},{176,144},{208,176},{2... | collective-permute-start | bytes 786440 | tf_op jit(solution)/shard_map/ppermute | solution.py:228
  90.7 20.2 %copy-start.3 = (bf16[1,2,256,256]{3,2,1,0:T(8,128)(2,1)S(1)}, bf16[1,2,256,256]{3,2,1,0:T(8,128)(2,1)}, u32[]{:S(2)}) copy-start(bf16[1,2,256,256]{3,2,1,0:T(8,128)(2,1)} %param.3) | copy-start | bytes 786436
  90.7 3.9 %collective-permute-start.17 = (f32[2,256,256]{2,1,0:T(8,128)S(1)}, f32[2,256,256]{2,1,0:T(8,128)S(1)}, u32[]{:S(2)}, u32[]{:S(2)}) collective-permute-start(f32[2,256,256]{2,1,0:T(8,128)S(1)} %shard_map.34), channel_id=1, source_target_pairs={{0,16},{16,0},{1,17},{17,1},{2,18},{18,2},{3,19},{19,3},{4,20},{20... | collective-permute-start | bytes 1572872 | tf_op jit(solution)/shard_map/ppermute | solution.py:233

commit v14 on v13

--- a/solution.py
+++ b/solution.py
@@ -69,11 +69,12 @@
                 copies.append(
                     pltpu.make_async_copy(source, held.at[2 * i + j, n], sems.at[2 * i + j, n])
                 )
-            copies.append(
-                pltpu.make_async_copy(
-                    rights[2 * i + j], kept.at[2 * i + j], sems.at[2 * i + j, len(rows)]
+            if len(planes) > 1:
+                copies.append(
+                    pltpu.make_async_copy(
+                        rights[2 * i + j], kept.at[2 * i + j], sems.at[2 * i + j, len(rows)]
+                    )
                 )
-            )
         plan.append((copies, guard))
     for group in groups:
         fetch([plan[i] for i in group], core_ref, True)
@@ -93,7 +94,8 @@
                 [held[i].reshape(len(rows) * width, width) for i in tiles], axis=1
             )
             for column in range(2):
-                right = jnp.concatenate([kept[i, column] for i in tiles], axis=0)
+                right = [kept[i, column] if len(planes) > 1 else rights[i][column] for i in tiles]
+                right = jnp.concatenate(right, axis=0)
                 product = jnp.dot(left, right, preferred_element_type=jnp.float32)
                 for n, total in enumerate(totals):
                     total[column] += product[n * width : (n + 1) * width]
@@ -114,7 +116,9 @@
     kernel = functools.partial(product_kernel, planes, rows, groups)
     out = pl.pallas_call(
         kernel,
-        in_specs=[SMEM, SMEM, HBM] + [HBM] * len(tiles) + [VMEM] * len(given),
+        in_specs=[SMEM, SMEM, HBM]
+        + [HBM if len(planes) > 1 else VMEM] * len(tiles)
+        + [VMEM] * len(given),
         out_specs=[VMEM] * len(rows),
         out_shape=[jax.ShapeDtypeStruct((2, width, width), jnp.float32)] * len(rows),
         scratch_shapes=[

time: 113 us -> 113 us (level)
  no operation moved by 1% of the time
where the time goes in v14:
time: 113 us
  starting transfers between devices  72.1 us (64%)
  blocking collectives  15.5 us (14%)
  Pallas kernels  11.3 us (10%)
  waiting for transfers between devices  9.41 us (8%)
  local copies, waits for them, and re-layouts  3.65 us (3%)
    ppermute x16, starting transfers between devices, on_device(): held.append(tuple((lax.ppermute(t, ROWS, perm) for t in held[-1])))  52.2 us
    all_to_all x1, blocking collectives, on_device(): lax.all_to_all(jnp.broadcast_to(sums[None], (planes, *sums.shape)), 'z',...  13.7 us
    all_to_all x2, starting transfers between devices, copy_for_each(): lax.all_to_all(spread, ('core', *COLS), 0, 0, axis_index_groups=lines, ti...  9.04 us
    ppermute x16, waiting for transfers between devices, on_device(): held.append(tuple((lax.ppermute(t, ROWS, perm) for t in held[-1])))  8.86 us
    ppermute x1, starting transfers between devices, on_device(): other = lax.ppermute(mine, 'core', SWAP)  8.79 us
    pallas_call x4, Pallas kernels, products(): pl.pallas_call(kernel, in_specs=[SMEM, SMEM, HBM] + [HBM if len(planes) >...  7.87 us
    broadcast_in_dim x2, local copies, waits for them, and re-layouts, copy_for_each(): spread = jnp.broadcast_to(value[None], (len(lines[0]), *value.shape))  3.56 us
  transfers between devices with their start and end apart: 20, of which 7 were waited for; matrix products, arithmetic and copies ran while one was open for 3% of the time, Pallas kernels for 6%

profile of v14, /device:TPU:1, one launch (start us, length us, event | category | flops | bytes accessed | tf_op | source)
XLA Modules:
  0.0 112.5 jit_solution(4191611545986009750)
XLA Ops:
  0.0 1.1 shard_map.28.refs_0_
  1.1 0.0 copy-start
  1.1 8.8 %collective-permute-start = (bf16[2,256,256]{2,1,0:T(8,128)(2,1)S(1)}, bf16[2,256,256]{2,1,0:T(8,128)(2,1)S(1)}, u32[]{:S(2)}, u32[]{:S(2)}) collective-permute-start(bf16[2,256,256]{2,1,0:T(8,128)(2,1)S(1)} %shard_map.28.refs_0_), channel_id=1, source_target_pairs={{0,16},{16,0},{1,17},{17,1},{2,18},{18,2},{3,19},{19,3},{4,20},{20... | collective-permute-start | bytes 786440 | tf_op jit(solution)/shard_map/ppermute | solution.py:193
  9.9 5.7 %collective-permute-start.1 = (bf16[2,256,256]{2,1,0:T(8,128)(2,1)S(1)}, bf16[2,256,256]{2,1,0:T(8,128)(2,1)S(1)}, u32[]{:S(2)}, u32[]{:S(2)}) collective-permute-start(bf16[2,256,256]{2,1,0:T(8,128)(2,1)S(1)} %shard_map.28.refs_0_), channel_id=1, source_target_pairs={{0,32},{32,64},{64,96},{96,128},{128,160},{160,192},{192,224},{224... | collective-permute-start | bytes 786440 | tf_op jit(solution)/shard_map/ppermute | solution.py:232
  15.7 0.0 collective-permute-done.refs_1_
  15.7 0.0 copy-start.15
  15.7 2.6 %collective-permute-start.9 = (bf16[2,256,256]{2,1,0:T(8,128)(2,1)S(1)}, bf16[2,256,256]{2,1,0:T(8,128)(2,1)S(1)}, u32[]{:S(2)}, u32[]{:S(2)}) collective-permute-start(bf16[2,256,256]{2,1,0:T(8,128)(2,1)S(1)} %collective-permute-done.refs_1_), channel_id=1, source_target_pairs={{0,32},{32,64},{64,96},{96,128},{128,160},{160,192},{192,224},{224... | collective-permute-start | bytes 786440 | tf_op jit(solution)/shard_map/ppermute | solution.py:232
  18.4 1.0 broadcast_in_dim.8
  19.5 4.2 %all-to-all-start = ((bf16[4,2,256,256]{3,2,1,0:T(8,128)(2,1)}), bf16[4,2,256,256]{3,2,1,0:T(8,128)(2,1)S(1)}, u32[]{:S(2)}, u32[]{:S(2)}) async-start(bf16[4,2,256,256]{3,2,1,0:T(8,128)(2,1)} %broadcast_in_dim.8), calls=%async_computation | async-start | bytes 2097152 | tf_op jit(solution)/shard_map/all_to_all | solution.py:215
  23.6 0.0 collective-permute-done.1.refs_2_.refs_0_
  23.6 2.6 %collective-permute-start.2 = (bf16[2,256,256]{2,1,0:T(8,128)(2,1)S(1)}, bf16[2,256,256]{2,1,0:T(8,128)(2,1)S(1)}, u32[]{:S(2)}, u32[]{:S(2)}) collective-permute-start(bf16[2,256,256]{2,1,0:T(8,128)(2,1)S(1)} %collective-permute-done.1.refs_2_.refs_0_), channel_id=1, source_target_pairs={{0,32},{32,64},{64,96},{96,128},{128,160},{160,192},{192,224},{224... | collective-permute-start | bytes 786440 | tf_op jit(solution)/shard_map/ppermute | solution.py:232
  26.3 0.0 copy-done.15
  26.3 0.0 collective-permute-done.9.refs_3_.refs_1_
  26.3 0.0 copy-start.5
  26.3 2.6 %collective-permute-start.10 = (bf16[2,256,256]{2,1,0:T(8,128)(2,1)S(1)}, bf16[2,256,256]{2,1,0:T(8,128)(2,1)S(1)}, u32[]{:S(2)}, u32[]{:S(2)}) collective-permute-start(bf16[2,256,256]{2,1,0:T(8,128)(2,1)S(1)} %collective-permute-done.9.refs_3_.refs_1_), channel_id=1, source_target_pairs={{0,32},{32,64},{64,96},{96,128},{128,160},{160,192},{192,224},{224... | collective-permute-start | bytes 786440 | tf_op jit(solution)/shard_map/ppermute | solution.py:232
  29.0 2.1 %collective-permute-done.2.refs_4_.refs_2_ = bf16[2,256,256]{2,1,0:T(8,128)(2,1)S(1)} collective-permute-done((bf16[2,256,256]{2,1,0:T(8,128)(2,1)S(1)}, bf16[2,256,256]{2,1,0:T(8,128)(2,1)S(1)}, u32[]{:S(2)}, u32[]{:S(2)}) %collective-permute-start.2) | collective-permute-done | bytes 262176 | tf_op jit(solution)/shard_map/ppermute | solution.py:232
  31.1 3.8 %collective-permute-start.3 = (bf16[2,256,256]{2,1,0:T(8,128)(2,1)S(1)}, bf16[2,256,256]{2,1,0:T(8,128)(2,1)S(1)}, u32[]{:S(2)}, u32[]{:S(2)}) collective-permute-start(bf16[2,256,256]{2,1,0:T(8,128)(2,1)S(1)} %collective-permute-done.2.refs_4_.refs_2_), channel_id=1, source_target_pairs={{0,32},{32,64},{64,96},{96,128},{128,160},{160,192},{192,224},{224... | collective-permute-start | bytes 786440 | tf_op jit(solution)/shard_map/ppermute | solution.py:232
  34.9 0.0 collective-permute-done.10.refs_5_.refs_3_
  34.9 0.0 copy-start.7
  34.9 2.5 %collective-permute-start.11 = (bf16[2,256,256]{2,1,0:T(8,128)(2,1)S(1)}, bf16[2,256,256]{2,1,0:T(8,128)(2,1)S(1)}, u32[]{:S(2)}, u32[]{:S(2)}) collective-permute-start(bf16[2,256,256]{2,1,0:T(8,128)(2,1)S(1)} %collective-permute-done.10.refs_5_.refs_3_), channel_id=1, source_target_pairs={{0,32},{32,64},{64,96},{96,128},{128,160},{160,192},{192,224},{224... | collective-permute-start | bytes 786440 | tf_op jit(solution)/shard_map/ppermute | solution.py:232
  37.4 1.0 collective-permute-done.3.refs_6_.refs_4_
  38.5 4.8 %collective-permute-start.4 = (bf16[2,256,256]{2,1,0:T(8,128)(2,1)S(1)}, bf16[2,256,256]{2,1,0:T(8,128)(2,1)S(1)}, u32[]{:S(2)}, u32[]{:S(2)}) collective-permute-start(bf16[2,256,256]{2,1,0:T(8,128)(2,1)S(1)} %collective-permute-done.3.refs_6_.refs_4_), channel_id=1, source_target_pairs={{0,32},{32,64},{64,96},{96,128},{128,160},{160,192},{192,224},{224... | collective-permute-start | bytes 786440 | tf_op jit(solution)/shard_map/ppermute | solution.py:232
  43.2 0.0 collective-permute-done.11.refs_7_.refs_5_
  43.2 0.0 copy-start.9
  43.2 2.8 %collective-permute-start.12 = (bf16[2,256,256]{2,1,0:T(8,128)(2,1)S(1)}, bf16[2,256,256]{2,1,0:T(8,128)(2,1)S(1)}, u32[]{:S(2)}, u32[]{:S(2)}) collective-permute-start(bf16[2,256,256]{2,1,0:T(8,128)(2,1)S(1)} %collective-permute-done.11.refs_7_.refs_5_), channel_id=1, source_target_pairs={{0,32},{32,64},{64,96},{96,128},{128,160},{160,192},{192,224},{224... | collective-permute-start | bytes 786440 | tf_op jit(solution)/shard_map/ppermute | solution.py:232
  46.0 0.0 all-to-all-done
  46.0 2.5 %broadcast_in_dim.9 = bf16[4,4,2,256,256]{4,3,2,1,0:T(8,128)(2,1)} broadcast(bf16[4,2,256,256]{3,2,1,0:T(8,128)(2,1)S(1)} %all-to-all-done), dimensions={1,2,3,4} | broadcast | bytes 5242880 | tf_op jit(solution)/shard_map/broadcast_in_dim | solution.py:214
  48.5 0.0 copy-done
  48.5 0.0 copy-done.4
  48.5 0.0 copy-done.5
  48.6 4.9 %all-to-all-start.1 = ((bf16[4,4,2,256,256]{4,3,2,1,0:T(8,128)(2,1)}), bf16[4,4,2,256,256]{4,3,2,1,0:T(8,128)(2,1)}, u32[]{:S(2)}, u32[]{:S(2)}) async-start(bf16[4,4,2,256,256]{4,3,2,1,0:T(8,128)(2,1)} %broadcast_in_dim.9), calls=%async_computation.1 | async-start | bytes 8388608 | tf_op jit(solution)/shard_map/all_to_all | solution.py:215
  53.5 0.0 collective-permute-done.4.refs_8_.refs_6_
  53.5 0.0 copy-start.10
  53.5 1.9 %collective-permute-start.5 = (bf16[2,256,256]{2,1,0:T(8,128)(2,1)S(1)}, bf16[2,256,256]{2,1,0:T(8,128)(2,1)S(1)}, u32[]{:S(2)}, u32[]{:S(2)}) collective-permute-start(bf16[2,256,256]{2,1,0:T(8,128)(2,1)S(1)} %collective-permute-done.4.refs_8_.refs_6_), channel_id=1, source_target_pairs={{0,32},{32,64},{64,96},{96,128},{128,160},{160,192},{192,224},{224... | collective-permute-start | bytes 786440 | tf_op jit(solution)/shard_map/ppermute | solution.py:232
  55.4 0.0 collective-permute-done.12.refs_9_.refs_7_
  55.4 2.4 %collective-permute-start.13 = (bf16[2,256,256]{2,1,0:T(8,128)(2,1)S(1)}, bf16[2,256,256]{2,1,0:T(8,128)(2,1)S(1)}, u32[]{:S(2)}, u32[]{:S(2)}) collective-permute-start(bf16[2,256,256]{2,1,0:T(8,128)(2,1)S(1)} %collective-permute-done.12.refs_9_.refs_7_), channel_id=1, source_target_pairs={{0,32},{32,64},{64,96},{96,128},{128,160},{160,192},{192,224},{224... | collective-permute-start | bytes 786440 | tf_op jit(solution)/shard_map/ppermute | solution.py:232
  57.9 3.1 %collective-permute-done.5.refs_10_.refs_8_ = bf16[2,256,256]{2,1,0:T(8,128)(2,1)S(1)} collective-permute-done((bf16[2,256,256]{2,1,0:T(8,128)(2,1)S(1)}, bf16[2,256,256]{2,1,0:T(8,128)(2,1)S(1)}, u32[]{:S(2)}, u32[]{:S(2)}) %collective-permute-start.5) | collective-permute-done | bytes 262176 | tf_op jit(solution)/shard_map/ppermute | solution.py:232
  61.0 3.1 %collective-permute-start.6 = (bf16[2,256,256]{2,1,0:T(8,128)(2,1)S(1)}, bf16[2,256,256]{2,1,0:T(8,128)(2,1)S(1)}, u32[]{:S(2)}, u32[]{:S(2)}) collective-permute-start(bf16[2,256,256]{2,1,0:T(8,128)(2,1)S(1)} %collective-permute-done.5.refs_10_.refs_8_), channel_id=1, source_target_pairs={{0,32},{32,64},{64,96},{96,128},{128,160},{160,192},{192,224},{224... | collective-permute-start | bytes 786440 | tf_op jit(solution)/shard_map/ppermute | solution.py:232
  64.1 0.0 collective-permute-done.13.refs_11_.refs_9_
  64.1 0.0 copy-start.13
  64.1 2.8 %collective-permute-start.14 = (bf16[2,256,256]{2,1,0:T(8,128)(2,1)S(1)}, bf16[2,256,256]{2,1,0:T(8,128)(2,1)S(1)}, u32[]{:S(2)}, u32[]{:S(2)}) collective-permute-start(bf16[2,256,256]{2,1,0:T(8,128)(2,1)S(1)} %collective-permute-done.13.refs_11_.refs_9_), channel_id=1, source_target_pairs={{0,32},{32,64},{64,96},{96,128},{128,160},{160,192},{192,224},{224... | collective-permute-start | bytes 786440 | tf_op jit(solution)/shard_map/ppermute | solution.py:232
  66.9 1.6 %collective-permute-done.6.refs_12_.refs_10_ = bf16[2,256,256]{2,1,0:T(8,128)(2,1)S(1)} collective-permute-done((bf16[2,256,256]{2,1,0:T(8,128)(2,1)S(1)}, bf16[2,256,256]{2,1,0:T(8,128)(2,1)S(1)}, u32[]{:S(2)}, u32[]{:S(2)}) %collective-permute-start.6) | collective-permute-done | bytes 262176 | tf_op jit(solution)/shard_map/ppermute | solution.py:232
  68.5 4.3 %collective-permute-start.7 = (bf16[2,256,256]{2,1,0:T(8,128)(2,1)S(1)}, bf16[2,256,256]{2,1,0:T(8,128)(2,1)S(1)}, u32[]{:S(2)}, u32[]{:S(2)}) collective-permute-start(bf16[2,256,256]{2,1,0:T(8,128)(2,1)S(1)} %collective-permute-done.6.refs_12_.refs_10_), channel_id=1, source_target_pairs={{0,32},{32,64},{64,96},{96,128},{128,160},{160,192},{192,224},{224... | collective-permute-start | bytes 786440 | tf_op jit(solution)/shard_map/ppermute | solution.py:232
  72.8 0.0 collective-permute-done.14.refs_0_
  72.9 2.8 %collective-permute-start.15 = (bf16[2,256,256]{2,1,0:T(8,128)(2,1)S(1)}, bf16[2,256,256]{2,1,0:T(8,128)(2,1)S(1)}, u32[]{:S(2)}, u32[]{:S(2)}) collective-permute-start(bf16[2,256,256]{2,1,0:T(8,128)(2,1)S(1)} %shard_map.29.refs_13_.refs_11_), channel_id=1, source_target_pairs={{0,32},{32,64},{64,96},{96,128},{128,160},{160,192},{192,224},{224... | collective-permute-start | bytes 786440 | tf_op jit(solution)/shard_map/ppermute | solution.py:232
  75.7 0.4 collective-permute-done.7.refs_12_
  76.1 5.4 %collective-permute-start.8 = (bf16[2,256,256]{2,1,0:T(8,128)(2,1)S(1)}, bf16[2,256,256]{2,1,0:T(8,128)(2,1)S(1)}, u32[]{:S(2)}, u32[]{:S(2)}) collective-permute-start(bf16[2,256,256]{2,1,0:T(8,128)(2,1)S(1)} %collective-permute-done.7.refs_12_), channel_id=1, source_target_pairs={{16,496},{48,16},{80,48},{112,80},{144,112},{176,144},{208,176},{2... | collective-permute-start | bytes 786440 | tf_op jit(solution)/shard_map/ppermute | solution.py:232
  81.6 0.0 all-to-all-done.1.left_ref
  81.6 0.7 shard_map.30
  82.2 0.0 collective-permute-done.15.refs_0_
  82.3 0.0 copy-start.2
  82.3 1.9 %collective-permute-start.16 = (bf16[2,256,256]{2,1,0:T(8,128)(2,1)S(1)}, bf16[2,256,256]{2,1,0:T(8,128)(2,1)S(1)}, u32[]{:S(2)}, u32[]{:S(2)}) collective-permute-start(bf16[2,256,256]{2,1,0:T(8,128)(2,1)S(1)} %shard_map.31.refs_13_), channel_id=1, source_target_pairs={{16,496},{48,16},{80,48},{112,80},{144,112},{176,144},{208,176},{2... | collective-permute-start | bytes 786440 | tf_op jit(solution)/shard_map/ppermute | solution.py:232
  84.2 4.6 %shard_map.32 = (f32[2,256,256]{2,1,0:T(8,128)S(1)}, f32[2,256,256]{2,1,0:T(8,128)S(1)}) custom-call(s32[1]{0:T(128)} %bitcast.3.plane_ref, s32[1]{0:T(128)} %bitcast.4.core_ref, bf16[4,4,2,256,256]{4,3,2,1,0:T(8,128)(2,1)} %all-to-all-done.1.left_ref, bf16[2,256,256]{2,1,0:T(8,128)(2,1)} %copy-done.4, ...), custom_call_target="tpu_custom_call", output_to_operand_aliasing={{0}: (17, {}), {1}: (18, {})} | custom-call | flops 1879048192 | bytes 14680064 | tf_op jit(solution)/shard_map/pallas_call | solution.py:117
  88.8 0.0 collective-permute-done.8.refs_0_
  88.8 0.6 collective-permute-done.16.refs_1_
  89.4 1.3 %shard_map.34 = f32[2,256,256]{2,1,0:T(8,128)S(1)} custom-call(s32[1]{0:T(128)} %bitcast.3.plane_ref, s32[1]{0:T(128)} %bitcast.4.core_ref, bf16[4,4,2,256,256]{4,3,2,1,0:T(8,128)(2,1)} %all-to-all-done.1.left_ref, bf16[2,256,256]{2,1,0:T(8,128)(2,1)S(1)} %collective-permute-done.8.refs_0_, ...), custom_call_target="tpu_custom_call", output_to_operand_aliasing={{}: (5, {})} | custom-call | flops 134217728 | bytes 1572864 | tf_op jit(solution)/shard_map/pallas_call | solution.py:117
  90.7 0.0 copy-start.3
  90.7 2.1 %collective-permute-start.17 = (f32[2,256,256]{2,1,0:T(8,128)S(1)}, f32[2,256,256]{2,1,0:T(8,128)S(1)}, u32[]{:S(2)}, u32[]{:S(2)}) collective-permute-start(f32[2,256,256]{2,1,0:T(8,128)S(1)} %shard_map.34), channel_id=1, source_target_pairs={{0,16},{16,0},{1,17},{17,1},{2,18},{18,2},{3,19},{19,3},{4,20},{20... | collective-permute-start | bytes 1572872 | tf_op jit(solution)/shard_map/ppermute | solution.py:237
  92.8 1.3 %shard_map.33.mine_ref = f32[2,256,256]{2,1,0:T(8,128)S(1)} custom-call(s32[1]{0:T(128)} %bitcast.3.plane_ref, s32[1]{0:T(128)} %bitcast.4.core_ref, bf16[4,4,2,256,256]{4,3,2,1,0:T(8,128)(2,1)} %all-to-all-done.1.left_ref, bf16[2,256,256]{2,1,0:T(8,128)(2,1)S(1)} %collective-permute-done.8.refs_0_, ...), custom_call_target="tpu_custom_call", output_to_operand_aliasing={{}: (5, {})} | custom-call | flops 134217728 | bytes 1572864 | tf_op jit(solution)/shard_map/pallas_call | solution.py:117
  94.1 0.5 collective-permute-done.17.other_ref
  94.7 0.7 shard_map.35
  95.4 1.8 %all-gather.1 = f32[2,2,256]{2,1,0:T(2,128)S(1)} all-gather(f32[1,2,256]{2,1,0:T(2,128)S(1)} %bitcast.9), channel_id=2, replica_groups=mesh['z'=16,'core'=2,'y'=4,'x'=4] {'core'}, dimensions={0}, use_global_device_ids=true | all-gather | bytes 6144 | tf_op jit(solution)/shard_map/all_gather | solution.py:249
  97.2 13.7 %all_to_all.15.parts_ref = f32[16,2,256]{2,1,0:T(2,128)S(1)} all-to-all(f32[16,2,256]{2,1,0:T(2,128)S(1)} %broadcast_in_dim.10), channel_id=1, replica_groups={{256,288,320,352,384,416,448,480,0,32,64,96,128,160,192,224},{257,289,3..., dimensions={0} | all-to-all | bytes 65536 | tf_op jit(solution)/shard_map/all_to_all | solution.py:251
  110.9 1.6 %shard_map.36 = f32[2,256,256]{2,1,0:T(8,128)} custom-call(s32[2]{0:T(128)} %bitcast.12, s32[1]{0:T(128)} %bitcast.1.column_ref, bf16[2,256,256]{2,1,0:T(8,128)(2,1)S(1)} %bitcast.8, f32[2,256,256]{2,1,0:T(8,128)S(1)} %get-tuple-element.15.inflated_ref, f32[16,2,256]{2,1,0:T(2,128)S(1)} %all_to_all.15.parts_ref), custom_call_target="tpu_custom_call" | custom-call | tf_op jit(solution)/shard_map/pallas_call | solution.py:260
  (28 shorter events, 0.1 us)
Async XLA Ops:
  1.1 47.5 %copy-start = (bf16[2,256,256]{2,1,0:T(8,128)(2,1)}, bf16[2,256,256]{2,1,0:T(8,128)(2,1)S(1)}, u32[]{:S(2)}) copy-start(bf16[2,256,256]{2,1,0:T(8,128)(2,1)S(1)} %shard_map.28.refs_0_) | copy-start | bytes 786436
  1.1 14.6 %collective-permute-start = (bf16[2,256,256]{2,1,0:T(8,128)(2,1)S(1)}, bf16[2,256,256]{2,1,0:T(8,128)(2,1)S(1)}, u32[]{:S(2)}, u32[]{:S(2)}) collective-permute-start(bf16[2,256,256]{2,1,0:T(8,128)(2,1)S(1)} %shard_map.28.refs_0_), channel_id=1, source_target_pairs={{0,16},{16,0},{1,17},{17,1},{2,18},{18,2},{3,19},{19,3},{4,20},{20... | collective-permute-start | bytes 786440 | tf_op jit(solution)/shard_map/ppermute | solution.py:193
  9.9 13.8 %collective-permute-start.1 = (bf16[2,256,256]{2,1,0:T(8,128)(2,1)S(1)}, bf16[2,256,256]{2,1,0:T(8,128)(2,1)S(1)}, u32[]{:S(2)}, u32[]{:S(2)}) collective-permute-start(bf16[2,256,256]{2,1,0:T(8,128)(2,1)S(1)} %shard_map.28.refs_0_), channel_id=1, source_target_pairs={{0,32},{32,64},{64,96},{96,128},{128,160},{160,192},{192,224},{224... | collective-permute-start | bytes 786440 | tf_op jit(solution)/shard_map/ppermute | solution.py:232
  15.7 10.6 %copy-start.15 = (bf16[2,256,256]{2,1,0:T(8,128)(2,1)}, bf16[2,256,256]{2,1,0:T(8,128)(2,1)S(1)}, u32[]{:S(2)}) copy-start(bf16[2,256,256]{2,1,0:T(8,128)(2,1)S(1)} %collective-permute-done.refs_1_) | copy-start | bytes 786436
  15.7 10.6 %collective-permute-start.9 = (bf16[2,256,256]{2,1,0:T(8,128)(2,1)S(1)}, bf16[2,256,256]{2,1,0:T(8,128)(2,1)S(1)}, u32[]{:S(2)}, u32[]{:S(2)}) collective-permute-start(bf16[2,256,256]{2,1,0:T(8,128)(2,1)S(1)} %collective-permute-done.refs_1_), channel_id=1, source_target_pairs={{0,32},{32,64},{64,96},{96,128},{128,160},{160,192},{192,224},{224... | collective-permute-start | bytes 786440 | tf_op jit(solution)/shard_map/ppermute | solution.py:232
  19.5 26.6 %all-to-all-start = ((bf16[4,2,256,256]{3,2,1,0:T(8,128)(2,1)}), bf16[4,2,256,256]{3,2,1,0:T(8,128)(2,1)S(1)}, u32[]{:S(2)}, u32[]{:S(2)}) async-start(bf16[4,2,256,256]{3,2,1,0:T(8,128)(2,1)} %broadcast_in_dim.8), calls=%async_computation | async-start | bytes 2097152 | tf_op jit(solution)/shard_map/all_to_all | solution.py:215
  23.6 24.9 %copy-start.4 = (bf16[2,256,256]{2,1,0:T(8,128)(2,1)}, bf16[2,256,256]{2,1,0:T(8,128)(2,1)S(1)}, u32[]{:S(2)}) copy-start(bf16[2,256,256]{2,1,0:T(8,128)(2,1)S(1)} %collective-permute-done.1.refs_2_.refs_0_) | copy-start | bytes 786436
  23.6 7.4 %collective-permute-start.2 = (bf16[2,256,256]{2,1,0:T(8,128)(2,1)S(1)}, bf16[2,256,256]{2,1,0:T(8,128)(2,1)S(1)}, u32[]{:S(2)}, u32[]{:S(2)}) collective-permute-start(bf16[2,256,256]{2,1,0:T(8,128)(2,1)S(1)} %collective-permute-done.1.refs_2_.refs_0_), channel_id=1, source_target_pairs={{0,32},{32,64},{64,96},{96,128},{128,160},{160,192},{192,224},{224... | collective-permute-start | bytes 786440 | tf_op jit(solution)/shard_map/ppermute | solution.py:232
  26.3 22.2 %copy-start.5 = (bf16[2,256,256]{2,1,0:T(8,128)(2,1)}, bf16[2,256,256]{2,1,0:T(8,128)(2,1)S(1)}, u32[]{:S(2)}) copy-start(bf16[2,256,256]{2,1,0:T(8,128)(2,1)S(1)} %collective-permute-done.9.refs_3_.refs_1_) | copy-start | bytes 786436
  26.3 8.6 %collective-permute-start.10 = (bf16[2,256,256]{2,1,0:T(8,128)(2,1)S(1)}, bf16[2,256,256]{2,1,0:T(8,128)(2,1)S(1)}, u32[]{:S(2)}, u32[]{:S(2)}) collective-permute-start(bf16[2,256,256]{2,1,0:T(8,128)(2,1)S(1)} %collective-permute-done.9.refs_3_.refs_1_), channel_id=1, source_target_pairs={{0,32},{32,64},{64,96},{96,128},{128,160},{160,192},{192,224},{224... | collective-permute-start | bytes 786440 | tf_op jit(solution)/shard_map/ppermute | solution.py:232
  31.1 17.5 %copy-start.6 = (bf16[2,256,256]{2,1,0:T(8,128)(2,1)}, bf16[2,256,256]{2,1,0:T(8,128)(2,1)S(1)}, u32[]{:S(2)}) copy-start(bf16[2,256,256]{2,1,0:T(8,128)(2,1)S(1)} %collective-permute-done.2.refs_4_.refs_2_) | copy-start | bytes 786436
  31.1 7.4 %collective-permute-start.3 = (bf16[2,256,256]{2,1,0:T(8,128)(2,1)S(1)}, bf16[2,256,256]{2,1,0:T(8,128)(2,1)S(1)}, u32[]{:S(2)}, u32[]{:S(2)}) collective-permute-start(bf16[2,256,256]{2,1,0:T(8,128)(2,1)S(1)} %collective-permute-done.2.refs_4_.refs_2_), channel_id=1, source_target_pairs={{0,32},{32,64},{64,96},{96,128},{128,160},{160,192},{192,224},{224... | collective-permute-start | bytes 786440 | tf_op jit(solution)/shard_map/ppermute | solution.py:232
  34.9 13.7 %copy-start.7 = (bf16[2,256,256]{2,1,0:T(8,128)(2,1)}, bf16[2,256,256]{2,1,0:T(8,128)(2,1)S(1)}, u32[]{:S(2)}) copy-start(bf16[2,256,256]{2,1,0:T(8,128)(2,1)S(1)} %collective-permute-done.10.refs_5_.refs_3_) | copy-start | bytes 786436
  34.9 8.3 %collective-permute-start.11 = (bf16[2,256,256]{2,1,0:T(8,128)(2,1)S(1)}, bf16[2,256,256]{2,1,0:T(8,128)(2,1)S(1)}, u32[]{:S(2)}, u32[]{:S(2)}) collective-permute-start(bf16[2,256,256]{2,1,0:T(8,128)(2,1)S(1)} %collective-permute-done.10.refs_5_.refs_3_), channel_id=1, source_target_pairs={{0,32},{32,64},{64,96},{96,128},{128,160},{160,192},{192,224},{224... | collective-permute-start | bytes 786440 | tf_op jit(solution)/shard_map/ppermute | solution.py:232
  38.5 10.1 %copy-start.8 = (bf16[2,256,256]{2,1,0:T(8,128)(2,1)}, bf16[2,256,256]{2,1,0:T(8,128)(2,1)S(1)}, u32[]{:S(2)}) copy-start(bf16[2,256,256]{2,1,0:T(8,128)(2,1)S(1)} %collective-permute-done.3.refs_6_.refs_4_) | copy-start | bytes 786436
  38.5 15.0 %collective-permute-start.4 = (bf16[2,256,256]{2,1,0:T(8,128)(2,1)S(1)}, bf16[2,256,256]{2,1,0:T(8,128)(2,1)S(1)}, u32[]{:S(2)}, u32[]{:S(2)}) collective-permute-start(bf16[2,256,256]{2,1,0:T(8,128)(2,1)S(1)} %collective-permute-done.3.refs_6_.refs_4_), channel_id=1, source_target_pairs={{0,32},{32,64},{64,96},{96,128},{128,160},{160,192},{192,224},{224... | collective-permute-start | bytes 786440 | tf_op jit(solution)/shard_map/ppermute | solution.py:232
  43.2 5.4 %copy-start.9 = (bf16[2,256,256]{2,1,0:T(8,128)(2,1)}, bf16[2,256,256]{2,1,0:T(8,128)(2,1)S(1)}, u32[]{:S(2)}) copy-start(bf16[2,256,256]{2,1,0:T(8,128)(2,1)S(1)} %collective-permute-done.11.refs_7_.refs_5_) | copy-start | bytes 786436
  43.2 12.2 %collective-permute-start.12 = (bf16[2,256,256]{2,1,0:T(8,128)(2,1)S(1)}, bf16[2,256,256]{2,1,0:T(8,128)(2,1)S(1)}, u32[]{:S(2)}, u32[]{:S(2)}) collective-permute-start(bf16[2,256,256]{2,1,0:T(8,128)(2,1)S(1)} %collective-permute-done.11.refs_7_.refs_5_), channel_id=1, source_target_pairs={{0,32},{32,64},{64,96},{96,128},{128,160},{160,192},{192,224},{224... | collective-permute-start | bytes 786440 | tf_op jit(solution)/shard_map/ppermute | solution.py:232
  48.6 33.0 %all-to-all-start.1 = ((bf16[4,4,2,256,256]{4,3,2,1,0:T(8,128)(2,1)}), bf16[4,4,2,256,256]{4,3,2,1,0:T(8,128)(2,1)}, u32[]{:S(2)}, u32[]{:S(2)}) async-start(bf16[4,4,2,256,256]{4,3,2,1,0:T(8,128)(2,1)} %broadcast_in_dim.9), calls=%async_computation.1 | async-start | bytes 8388608 | tf_op jit(solution)/shard_map/all_to_all | solution.py:215
  53.5 19.4 %copy-start.10 = (bf16[2,256,256]{2,1,0:T(8,128)(2,1)}, bf16[2,256,256]{2,1,0:T(8,128)(2,1)S(1)}, u32[]{:S(2)}) copy-start(bf16[2,256,256]{2,1,0:T(8,128)(2,1)S(1)} %collective-permute-done.4.refs_8_.refs_6_) | copy-start | bytes 786436
  53.5 7.5 %collective-permute-start.5 = (bf16[2,256,256]{2,1,0:T(8,128)(2,1)S(1)}, bf16[2,256,256]{2,1,0:T(8,128)(2,1)S(1)}, u32[]{:S(2)}, u32[]{:S(2)}) collective-permute-start(bf16[2,256,256]{2,1,0:T(8,128)(2,1)S(1)} %collective-permute-done.4.refs_8_.refs_6_), channel_id=1, source_target_pairs={{0,32},{32,64},{64,96},{96,128},{128,160},{160,192},{192,224},{224... | collective-permute-start | bytes 786440 | tf_op jit(solution)/shard_map/ppermute | solution.py:232
  55.4 17.5 %copy-start.11 = (bf16[2,256,256]{2,1,0:T(8,128)(2,1)}, bf16[2,256,256]{2,1,0:T(8,128)(2,1)S(1)}, u32[]{:S(2)}) copy-start(bf16[2,256,256]{2,1,0:T(8,128)(2,1)S(1)} %collective-permute-done.12.refs_9_.refs_7_) | copy-start | bytes 786436
  55.4 8.7 %collective-permute-start.13 = (bf16[2,256,256]{2,1,0:T(8,128)(2,1)S(1)}, bf16[2,256,256]{2,1,0:T(8,128)(2,1)S(1)}, u32[]{:S(2)}, u32[]{:S(2)}) collective-permute-start(bf16[2,256,256]{2,1,0:T(8,128)(2,1)S(1)} %collective-permute-done.12.refs_9_.refs_7_), channel_id=1, source_target_pairs={{0,32},{32,64},{64,96},{96,128},{128,160},{160,192},{192,224},{224... | collective-permute-start | bytes 786440 | tf_op jit(solution)/shard_map/ppermute | solution.py:232
  61.0 11.9 %copy-start.12 = (bf16[2,256,256]{2,1,0:T(8,128)(2,1)}, bf16[2,256,256]{2,1,0:T(8,128)(2,1)S(1)}, u32[]{:S(2)}) copy-start(bf16[2,256,256]{2,1,0:T(8,128)(2,1)S(1)} %collective-permute-done.5.refs_10_.refs_8_) | copy-start | bytes 786436
  61.0 7.5 %collective-permute-start.6 = (bf16[2,256,256]{2,1,0:T(8,128)(2,1)S(1)}, bf16[2,256,256]{2,1,0:T(8,128)(2,1)S(1)}, u32[]{:S(2)}, u32[]{:S(2)}) collective-permute-start(bf16[2,256,256]{2,1,0:T(8,128)(2,1)S(1)} %collective-permute-done.5.refs_10_.refs_8_), channel_id=1, source_target_pairs={{0,32},{32,64},{64,96},{96,128},{128,160},{160,192},{192,224},{224... | collective-permute-start | bytes 786440 | tf_op jit(solution)/shard_map/ppermute | solution.py:232
  64.1 8.8 %copy-start.13 = (bf16[2,256,256]{2,1,0:T(8,128)(2,1)}, bf16[2,256,256]{2,1,0:T(8,128)(2,1)S(1)}, u32[]{:S(2)}) copy-start(bf16[2,256,256]{2,1,0:T(8,128)(2,1)S(1)} %collective-permute-done.13.refs_11_.refs_9_) | copy-start | bytes 786436
  64.1 8.7 %collective-permute-start.14 = (bf16[2,256,256]{2,1,0:T(8,128)(2,1)S(1)}, bf16[2,256,256]{2,1,0:T(8,128)(2,1)S(1)}, u32[]{:S(2)}, u32[]{:S(2)}) collective-permute-start(bf16[2,256,256]{2,1,0:T(8,128)(2,1)S(1)} %collective-permute-done.13.refs_11_.refs_9_), channel_id=1, source_target_pairs={{0,32},{32,64},{64,96},{96,128},{128,160},{160,192},{192,224},{224... | collective-permute-start | bytes 786440 | tf_op jit(solution)/shard_map/ppermute | solution.py:232
  68.5 4.4 %copy-start.14 = (bf16[2,256,256]{2,1,0:T(8,128)(2,1)}, bf16[2,256,256]{2,1,0:T(8,128)(2,1)S(1)}, u32[]{:S(2)}) copy-start(bf16[2,256,256]{2,1,0:T(8,128)(2,1)S(1)} %collective-permute-done.6.refs_12_.refs_10_) | copy-start | bytes 786436
  68.5 7.6 %collective-permute-start.7 = (bf16[2,256,256]{2,1,0:T(8,128)(2,1)S(1)}, bf16[2,256,256]{2,1,0:T(8,128)(2,1)S(1)}, u32[]{:S(2)}, u32[]{:S(2)}) collective-permute-start(bf16[2,256,256]{2,1,0:T(8,128)(2,1)S(1)} %collective-permute-done.6.refs_12_.refs_10_), channel_id=1, source_target_pairs={{0,32},{32,64},{64,96},{96,128},{128,160},{160,192},{192,224},{224... | collective-permute-start | bytes 786440 | tf_op jit(solution)/shard_map/ppermute | solution.py:232
  72.9 8.7 %copy-start.1 = (bf16[2,256,256]{2,1,0:T(8,128)(2,1)}, bf16[2,256,256]{2,1,0:T(8,128)(2,1)S(1)}, u32[]{:S(2)}) copy-start(bf16[2,256,256]{2,1,0:T(8,128)(2,1)S(1)} %shard_map.29.refs_13_.refs_11_) | copy-start | bytes 786436
  72.9 9.3 %collective-permute-start.15 = (bf16[2,256,256]{2,1,0:T(8,128)(2,1)S(1)}, bf16[2,256,256]{2,1,0:T(8,128)(2,1)S(1)}, u32[]{:S(2)}, u32[]{:S(2)}) collective-permute-start(bf16[2,256,256]{2,1,0:T(8,128)(2,1)S(1)} %shard_map.29.refs_13_.refs_11_), channel_id=1, source_target_pairs={{0,32},{32,64},{64,96},{96,128},{128,160},{160,192},{192,224},{224... | collective-permute-start | bytes 786440 | tf_op jit(solution)/shard_map/ppermute | solution.py:232
  76.1 6.1 %copy-start.16 = (bf16[2,256,256]{2,1,0:T(8,128)(2,1)}, bf16[2,256,256]{2,1,0:T(8,128)(2,1)S(1)}, u32[]{:S(2)}) copy-start(bf16[2,256,256]{2,1,0:T(8,128)(2,1)S(1)} %collective-permute-done.7.refs_12_) | copy-start | bytes 786436
  76.1 12.7 %collective-permute-start.8 = (bf16[2,256,256]{2,1,0:T(8,128)(2,1)S(1)}, bf16[2,256,256]{2,1,0:T(8,128)(2,1)S(1)}, u32[]{:S(2)}, u32[]{:S(2)}) collective-permute-start(bf16[2,256,256]{2,1,0:T(8,128)(2,1)S(1)} %collective-permute-done.7.refs_12_), channel_id=1, source_target_pairs={{16,496},{48,16},{80,48},{112,80},{144,112},{176,144},{208,176},{2... | collective-permute-start | bytes 786440 | tf_op jit(solution)/shard_map/ppermute | solution.py:232
  82.3 1.9 %copy-start.2 = (bf16[2,256,256]{2,1,0:T(8,128)(2,1)}, bf16[2,256,256]{2,1,0:T(8,128)(2,1)S(1)}, u32[]{:S(2)}) copy-start(bf16[2,256,256]{2,1,0:T(8,128)(2,1)S(1)} %shard_map.31.refs_13_) | copy-start | bytes 786436
  82.3 7.1 %collective-permute-start.16 = (bf16[2,256,256]{2,1,0:T(8,128)(2,1)S(1)}, bf16[2,256,256]{2,1,0:T(8,128)(2,1)S(1)}, u32[]{:S(2)}, u32[]{:S(2)}) collective-permute-start(bf16[2,256,256]{2,1,0:T(8,128)(2,1)S(1)} %shard_map.31.refs_13_), channel_id=1, source_target_pairs={{16,496},{48,16},{80,48},{112,80},{144,112},{176,144},{208,176},{2... | collective-permute-start | bytes 786440 | tf_op jit(solution)/shard_map/ppermute | solution.py:232
  90.7 20.2 %copy-start.3 = (bf16[1,2,256,256]{3,2,1,0:T(8,128)(2,1)S(1)}, bf16[1,2,256,256]{3,2,1,0:T(8,128)(2,1)}, u32[]{:S(2)}) copy-start(bf16[1,2,256,256]{3,2,1,0:T(8,128)(2,1)} %param.3) | copy-start | bytes 786436
  90.7 3.9 %collective-permute-start.17 = (f32[2,256,256]{2,1,0:T(8,128)S(1)}, f32[2,256,256]{2,1,0:T(8,128)S(1)}, u32[]{:S(2)}, u32[]{:S(2)}) collective-permute-start(f32[2,256,256]{2,1,0:T(8,128)S(1)} %shard_map.34), channel_id=1, source_target_pairs={{0,16},{16,0},{1,17},{17,1},{2,18},{18,2},{3,19},{19,3},{4,20},{20... | collective-permute-start | bytes 1572872 | tf_op jit(solution)/shard_map/ppermute | solution.py:237

commit v15 on v14

--- a/solution.py
+++ b/solution.py
@@ -225,7 +225,7 @@
             known = (plane_ref, core_ref, left, held)
             early = [(i, 0) for i in range(half - 1)]
             totals = products(None, (0, 1), *known, early, [[0, 1], [2, 3], [4, 5], [6]])
-            held[-1] = (held[-1][0], settle(held[-1][1], totals.values(), 0))
+            held[-1] = (settle(held[-1][0], totals.values(), 0), held[-1][1])
         elif step == half - 1:
             held[-1] = (held[-1][0], settle(held[-1][1], (), FLOPS))
         perm = ring + back if step < half else back

time: 113 us -> 121 us (1.071)
  waiting for transfers between devices: 9.41 us -> 18 us
  starting transfers between devices: 72.1 us -> 70 us
  blocking collectives: 15.5 us -> 16.8 us
    ppermute x16, waiting for transfers between devices: 8.86 us -> 13.2 us  [on_device(): held.append(tuple((lax.ppermute(t, ROWS, perm) for t in held[-1])))]
    all_to_all x2, waiting for transfers between devices: 0.01 us -> 4.31 us  [copy_for_each(): lax.all_to_all(spread, ('core', *COLS), 0, 0, axis_index_groups=lines, ti...]
    ppermute x16, starting transfers between devices: 52.2 us -> 50.1 us  [on_device(): held.append(tuple((lax.ppermute(t, ROWS, perm) for t in held[-1])))]
    all_to_all x1, blocking collectives: 13.7 us -> 15.1 us  [on_device(): lax.all_to_all(jnp.broadcast_to(sums[None], (planes, *sums.shape)), 'z',...]
  transfers between devices with their start and end apart: 20 -> 20, of which waited for: 7 -> 8; matrix products, arithmetic and copies ran while one was open for 3% -> 3% of each run, Pallas kernels for 6% -> 5%
where the time goes in v15:
time: 121 us; the launch traced here: 120 us
  starting transfers between devices  70 us (58%)
  waiting for transfers between devices  18 us (15%)
  blocking collectives  16.8 us (14%)
  Pallas kernels  11 us (9%)
  local copies, waits for them, and re-layouts  3.62 us (3%)
    ppermute x16, starting transfers between devices, on_device(): held.append(tuple((lax.ppermute(t, ROWS, perm) for t in held[-1])))  50.1 us
    all_to_all x1, blocking collectives, on_device(): lax.all_to_all(jnp.broadcast_to(sums[None], (planes, *sums.shape)), 'z',...  15.1 us
    ppermute x16, waiting for transfers between devices, on_device(): held.append(tuple((lax.ppermute(t, ROWS, perm) for t in held[-1])))  13.2 us
    all_to_all x2, starting transfers between devices, copy_for_each(): lax.all_to_all(spread, ('core', *COLS), 0, 0, axis_index_groups=lines, ti...  9.03 us
    ppermute x1, starting transfers between devices, on_device(): other = lax.ppermute(mine, 'core', SWAP)  8.79 us
    pallas_call x4, Pallas kernels, products(): pl.pallas_call(kernel, in_specs=[SMEM, SMEM, HBM] + [HBM if len(planes) >...  7.6 us
    all_to_all x2, waiting for transfers between devices, copy_for_each(): lax.all_to_all(spread, ('core', *COLS), 0, 0, axis_index_groups=lines, ti...  4.31 us
    broadcast_in_dim x2, local copies, waits for them, and re-layouts, copy_for_each(): spread = jnp.broadcast_to(value[None], (len(lines[0]), *value.shape))  3.53 us
  transfers between devices with their start and end apart: 20, of which 8 were waited for; matrix products, arithmetic and copies ran while one was open for 3% of the time, Pallas kernels for 5%

profile of v15, /device:TPU:1, one launch (start us, length us, event | category | flops | bytes accessed | tf_op | source)
XLA Modules:
  0.0 120.0 jit_solution(10379651702630322728)
XLA Ops:
  0.0 1.1 shard_map.28.refs_0_
  1.1 0.0 copy-start
  1.1 8.8 %collective-permute-start = (bf16[2,256,256]{2,1,0:T(8,128)(2,1)S(1)}, bf16[2,256,256]{2,1,0:T(8,128)(2,1)S(1)}, u32[]{:S(2)}, u32[]{:S(2)}) collective-permute-start(bf16[2,256,256]{2,1,0:T(8,128)(2,1)S(1)} %shard_map.28.refs_0_), channel_id=1, source_target_pairs={{0,16},{16,0},{1,17},{17,1},{2,18},{18,2},{3,19},{19,3},{4,20},{20... | collective-permute-start | bytes 786440 | tf_op jit(solution)/shard_map/ppermute | solution.py:193
  9.9 5.7 %collective-permute-start.1 = (bf16[2,256,256]{2,1,0:T(8,128)(2,1)S(1)}, bf16[2,256,256]{2,1,0:T(8,128)(2,1)S(1)}, u32[]{:S(2)}, u32[]{:S(2)}) collective-permute-start(bf16[2,256,256]{2,1,0:T(8,128)(2,1)S(1)} %shard_map.28.refs_0_), channel_id=1, source_target_pairs={{0,32},{32,64},{64,96},{96,128},{128,160},{160,192},{192,224},{224... | collective-permute-start | bytes 786440 | tf_op jit(solution)/shard_map/ppermute | solution.py:232
  15.7 0.0 collective-permute-done.refs_1_
  15.7 0.0 copy-start.14
  15.7 2.6 %collective-permute-start.8 = (bf16[2,256,256]{2,1,0:T(8,128)(2,1)S(1)}, bf16[2,256,256]{2,1,0:T(8,128)(2,1)S(1)}, u32[]{:S(2)}, u32[]{:S(2)}) collective-permute-start(bf16[2,256,256]{2,1,0:T(8,128)(2,1)S(1)} %collective-permute-done.refs_1_), channel_id=1, source_target_pairs={{0,32},{32,64},{64,96},{96,128},{128,160},{160,192},{192,224},{224... | collective-permute-start | bytes 786440 | tf_op jit(solution)/shard_map/ppermute | solution.py:232
  18.4 4.4 %collective-permute-done.8.refs_3_.refs_1_ = bf16[2,256,256]{2,1,0:T(8,128)(2,1)S(1)} collective-permute-done((bf16[2,256,256]{2,1,0:T(8,128)(2,1)S(1)}, bf16[2,256,256]{2,1,0:T(8,128)(2,1)S(1)}, u32[]{:S(2)}, u32[]{:S(2)}) %collective-permute-start.8) | collective-permute-done | bytes 262176 | tf_op jit(solution)/shard_map/ppermute | solution.py:232
  22.8 4.0 %collective-permute-start.9 = (bf16[2,256,256]{2,1,0:T(8,128)(2,1)S(1)}, bf16[2,256,256]{2,1,0:T(8,128)(2,1)S(1)}, u32[]{:S(2)}, u32[]{:S(2)}) collective-permute-start(bf16[2,256,256]{2,1,0:T(8,128)(2,1)S(1)} %collective-permute-done.8.refs_3_.refs_1_), channel_id=1, source_target_pairs={{0,32},{32,64},{64,96},{96,128},{128,160},{160,192},{192,224},{224... | collective-permute-start | bytes 786440 | tf_op jit(solution)/shard_map/ppermute | solution.py:232
  26.8 1.0 broadcast_in_dim.8
  27.8 0.0 copy-done.14
  27.8 4.2 %all-to-all-start = ((bf16[4,2,256,256]{3,2,1,0:T(8,128)(2,1)}), bf16[4,2,256,256]{3,2,1,0:T(8,128)(2,1)S(1)}, u32[]{:S(2)}, u32[]{:S(2)}) async-start(bf16[4,2,256,256]{3,2,1,0:T(8,128)(2,1)} %broadcast_in_dim.8), calls=%async_computation | async-start | bytes 2097152 | tf_op jit(solution)/shard_map/all_to_all | solution.py:215
  32.0 0.0 collective-permute-done.1.refs_2_.refs_0_
  32.0 1.9 %collective-permute-start.2 = (bf16[2,256,256]{2,1,0:T(8,128)(2,1)S(1)}, bf16[2,256,256]{2,1,0:T(8,128)(2,1)S(1)}, u32[]{:S(2)}, u32[]{:S(2)}) collective-permute-start(bf16[2,256,256]{2,1,0:T(8,128)(2,1)S(1)} %collective-permute-done.1.refs_2_.refs_0_), channel_id=1, source_target_pairs={{0,32},{32,64},{64,96},{96,128},{128,160},{160,192},{192,224},{224... | collective-permute-start | bytes 786440 | tf_op jit(solution)/shard_map/ppermute | solution.py:232
  33.9 0.0 collective-permute-done.9.refs_5_.refs_3_
  34.0 0.0 copy-start.6
  34.0 2.4 %collective-permute-start.10 = (bf16[2,256,256]{2,1,0:T(8,128)(2,1)S(1)}, bf16[2,256,256]{2,1,0:T(8,128)(2,1)S(1)}, u32[]{:S(2)}, u32[]{:S(2)}) collective-permute-start(bf16[2,256,256]{2,1,0:T(8,128)(2,1)S(1)} %collective-permute-done.9.refs_5_.refs_3_), channel_id=1, source_target_pairs={{0,32},{32,64},{64,96},{96,128},{128,160},{160,192},{192,224},{224... | collective-permute-start | bytes 786440 | tf_op jit(solution)/shard_map/ppermute | solution.py:232
  36.4 3.0 %collective-permute-done.2.refs_4_.refs_2_ = bf16[2,256,256]{2,1,0:T(8,128)(2,1)S(1)} collective-permute-done((bf16[2,256,256]{2,1,0:T(8,128)(2,1)S(1)}, bf16[2,256,256]{2,1,0:T(8,128)(2,1)S(1)}, u32[]{:S(2)}, u32[]{:S(2)}) %collective-permute-start.2) | collective-permute-done | bytes 262176 | tf_op jit(solution)/shard_map/ppermute | solution.py:232
  39.4 3.1 %collective-permute-start.3 = (bf16[2,256,256]{2,1,0:T(8,128)(2,1)S(1)}, bf16[2,256,256]{2,1,0:T(8,128)(2,1)S(1)}, u32[]{:S(2)}, u32[]{:S(2)}) collective-permute-start(bf16[2,256,256]{2,1,0:T(8,128)(2,1)S(1)} %collective-permute-done.2.refs_4_.refs_2_), channel_id=1, source_target_pairs={{0,32},{32,64},{64,96},{96,128},{128,160},{160,192},{192,224},{224... | collective-permute-start | bytes 786440 | tf_op jit(solution)/shard_map/ppermute | solution.py:232
  42.6 0.0 collective-permute-done.10.refs_7_.refs_5_
  42.6 0.0 copy-start.8
  42.6 2.8 %collective-permute-start.11 = (bf16[2,256,256]{2,1,0:T(8,128)(2,1)S(1)}, bf16[2,256,256]{2,1,0:T(8,128)(2,1)S(1)}, u32[]{:S(2)}, u32[]{:S(2)}) collective-permute-start(bf16[2,256,256]{2,1,0:T(8,128)(2,1)S(1)} %collective-permute-done.10.refs_7_.refs_5_), channel_id=1, source_target_pairs={{0,32},{32,64},{64,96},{96,128},{128,160},{160,192},{192,224},{224... | collective-permute-start | bytes 786440 | tf_op jit(solution)/shard_map/ppermute | solution.py:232
  45.4 1.5 %collective-permute-done.3.refs_6_.refs_4_ = bf16[2,256,256]{2,1,0:T(8,128)(2,1)S(1)} collective-permute-done((bf16[2,256,256]{2,1,0:T(8,128)(2,1)S(1)}, bf16[2,256,256]{2,1,0:T(8,128)(2,1)S(1)}, u32[]{:S(2)}, u32[]{:S(2)}) %collective-permute-start.3) | collective-permute-done | bytes 262176 | tf_op jit(solution)/shard_map/ppermute | solution.py:232
  46.8 4.0 %collective-permute-start.4 = (bf16[2,256,256]{2,1,0:T(8,128)(2,1)S(1)}, bf16[2,256,256]{2,1,0:T(8,128)(2,1)S(1)}, u32[]{:S(2)}, u32[]{:S(2)}) collective-permute-start(bf16[2,256,256]{2,1,0:T(8,128)(2,1)S(1)} %collective-permute-done.3.refs_6_.refs_4_), channel_id=1, source_target_pairs={{0,32},{32,64},{64,96},{96,128},{128,160},{160,192},{192,224},{224... | collective-permute-start | bytes 786440 | tf_op jit(solution)/shard_map/ppermute | solution.py:232
  50.9 0.0 collective-permute-done.11.refs_9_.refs_7_
  50.9 0.0 copy-start.10
  50.9 2.8 %collective-permute-start.12 = (bf16[2,256,256]{2,1,0:T(8,128)(2,1)S(1)}, bf16[2,256,256]{2,1,0:T(8,128)(2,1)}, u32[]{:S(2)}, u32[]{:S(2)}) collective-permute-start(bf16[2,256,256]{2,1,0:T(8,128)(2,1)S(1)} %collective-permute-done.11.refs_9_.refs_7_), channel_id=1, source_target_pairs={{0,32},{32,64},{64,96},{96,128},{128,160},{160,192},{192,224},{224... | collective-permute-start | bytes 786440 | tf_op jit(solution)/shard_map/ppermute | solution.py:232
  53.7 0.0 all-to-all-done
  53.7 2.5 %broadcast_in_dim.9 = bf16[4,4,2,256,256]{4,3,2,1,0:T(8,128)(2,1)} broadcast(bf16[4,2,256,256]{3,2,1,0:T(8,128)(2,1)S(1)} %all-to-all-done), dimensions={1,2,3,4} | broadcast | bytes 5242880 | tf_op jit(solution)/shard_map/broadcast_in_dim | solution.py:214
  56.2 0.0 copy-done
  56.2 0.0 copy-done.5
  56.2 0.0 copy-done.4
  56.2 4.8 %all-to-all-start.1 = ((bf16[4,4,2,256,256]{4,3,2,1,0:T(8,128)(2,1)}), bf16[4,4,2,256,256]{4,3,2,1,0:T(8,128)(2,1)}, u32[]{:S(2)}, u32[]{:S(2)}) async-start(bf16[4,4,2,256,256]{4,3,2,1,0:T(8,128)(2,1)} %broadcast_in_dim.9), calls=%async_computation.1 | async-start | bytes 8388608 | tf_op jit(solution)/shard_map/all_to_all | solution.py:215
  61.1 0.0 collective-permute-done.4.refs_8_.refs_6_
  61.1 1.9 %collective-permute-start.5 = (bf16[2,256,256]{2,1,0:T(8,128)(2,1)S(1)}, bf16[2,256,256]{2,1,0:T(8,128)(2,1)S(1)}, u32[]{:S(2)}, u32[]{:S(2)}) collective-permute-start(bf16[2,256,256]{2,1,0:T(8,128)(2,1)S(1)} %collective-permute-done.4.refs_8_.refs_6_), channel_id=1, source_target_pairs={{0,32},{32,64},{64,96},{96,128},{128,160},{160,192},{192,224},{224... | collective-permute-start | bytes 786440 | tf_op jit(solution)/shard_map/ppermute | solution.py:232
  63.0 0.0 collective-permute-done.12.refs_11_.refs_9_
  63.1 3.0 %collective-permute-start.13 = (bf16[2,256,256]{2,1,0:T(8,128)(2,1)}, bf16[2,256,256]{2,1,0:T(8,128)(2,1)S(1)}, u32[]{:S(2)}, u32[]{:S(2)}) collective-permute-start(bf16[2,256,256]{2,1,0:T(8,128)(2,1)} %collective-permute-done.12.refs_11_.refs_9_), channel_id=1, source_target_pairs={{0,32},{32,64},{64,96},{96,128},{128,160},{160,192},{192,224},{224... | collective-permute-start | bytes 786440 | tf_op jit(solution)/shard_map/ppermute | solution.py:232
  66.1 2.6 %collective-permute-done.5.refs_10_.refs_8_ = bf16[2,256,256]{2,1,0:T(8,128)(2,1)S(1)} collective-permute-done((bf16[2,256,256]{2,1,0:T(8,128)(2,1)S(1)}, bf16[2,256,256]{2,1,0:T(8,128)(2,1)S(1)}, u32[]{:S(2)}, u32[]{:S(2)}) %collective-permute-start.5) | collective-permute-done | bytes 262176 | tf_op jit(solution)/shard_map/ppermute | solution.py:232
  68.6 3.1 %collective-permute-start.6 = (bf16[2,256,256]{2,1,0:T(8,128)(2,1)S(1)}, bf16[2,256,256]{2,1,0:T(8,128)(2,1)S(1)}, u32[]{:S(2)}, u32[]{:S(2)}) collective-permute-start(bf16[2,256,256]{2,1,0:T(8,128)(2,1)S(1)} %collective-permute-done.5.refs_10_.refs_8_), channel_id=1, source_target_pairs={{0,32},{32,64},{64,96},{96,128},{128,160},{160,192},{192,224},{224... | collective-permute-start | bytes 786440 | tf_op jit(solution)/shard_map/ppermute | solution.py:232
  71.8 0.0 collective-permute-done.13.refs_0_
  71.8 3.2 %collective-permute-start.15 = (bf16[2,256,256]{2,1,0:T(8,128)(2,1)S(1)}, bf16[2,256,256]{2,1,0:T(8,128)(2,1)S(1)}, u32[]{:S(2)}, u32[]{:S(2)}) collective-permute-start(bf16[2,256,256]{2,1,0:T(8,128)(2,1)S(1)} %shard_map.29.refs_13_.refs_11_), channel_id=1, source_target_pairs={{0,32},{32,64},{64,96},{96,128},{128,160},{160,192},{192,224},{224... | collective-permute-start | bytes 786440 | tf_op jit(solution)/shard_map/ppermute | solution.py:232
  75.0 1.1 collective-permute-done.6.refs_12_.refs_10_
  76.1 4.3 %collective-permute-start.7 = (bf16[2,256,256]{2,1,0:T(8,128)(2,1)S(1)}, bf16[2,256,256]{2,1,0:T(8,128)(2,1)S(1)}, u32[]{:S(2)}, u32[]{:S(2)}) collective-permute-start(bf16[2,256,256]{2,1,0:T(8,128)(2,1)S(1)} %collective-permute-done.6.refs_12_.refs_10_), channel_id=1, source_target_pairs={{0,32},{32,64},{64,96},{96,128},{128,160},{160,192},{192,224},{224... | collective-permute-start | bytes 786440 | tf_op jit(solution)/shard_map/ppermute | solution.py:232
  80.5 0.0 collective-permute-done.15.refs_13_
  80.5 3.2 %collective-permute-start.16 = (bf16[2,256,256]{2,1,0:T(8,128)(2,1)S(1)}, bf16[2,256,256]{2,1,0:T(8,128)(2,1)S(1)}, u32[]{:S(2)}, u32[]{:S(2)}) collective-permute-start(bf16[2,256,256]{2,1,0:T(8,128)(2,1)S(1)} %collective-permute-done.15.refs_13_), channel_id=1, source_target_pairs={{16,496},{48,16},{80,48},{112,80},{144,112},{176,144},{208,176},{2... | collective-permute-start | bytes 786440 | tf_op jit(solution)/shard_map/ppermute | solution.py:232
  83.7 4.3 %all-to-all-done.1.left_ref = bf16[4,4,2,256,256]{4,3,2,1,0:T(8,128)(2,1)} async-done(((bf16[4,4,2,256,256]{4,3,2,1,0:T(8,128)(2,1)}), bf16[4,4,2,256,256]{4,3,2,1,0:T(8,128)(2,1)}, u32[]{:S(2)}, u32[]{:S(2)}) %all-to-all-start.1) | async-done | bytes 4194336 | tf_op jit(solution)/shard_map/all_to_all | solution.py:215
  88.0 0.0 copy-done.1
  88.1 0.4 shard_map.30
  88.4 0.0 collective-permute-done.7.refs_0_
  88.5 0.0 copy-start.2
  88.5 1.9 %collective-permute-start.14 = (bf16[2,256,256]{2,1,0:T(8,128)(2,1)S(1)}, bf16[2,256,256]{2,1,0:T(8,128)(2,1)S(1)}, u32[]{:S(2)}, u32[]{:S(2)}) collective-permute-start(bf16[2,256,256]{2,1,0:T(8,128)(2,1)S(1)} %shard_map.31.refs_12_), channel_id=1, source_target_pairs={{16,496},{48,16},{80,48},{112,80},{144,112},{176,144},{208,176},{2... | collective-permute-start | bytes 786440 | tf_op jit(solution)/shard_map/ppermute | solution.py:232
  90.4 0.0 copy-done.2
  90.4 4.6 %shard_map.32 = (f32[2,256,256]{2,1,0:T(8,128)S(1)}, f32[2,256,256]{2,1,0:T(8,128)S(1)}) custom-call(s32[1]{0:T(128)} %bitcast.3.plane_ref, s32[1]{0:T(128)} %bitcast.4.core_ref, bf16[4,4,2,256,256]{4,3,2,1,0:T(8,128)(2,1)} %all-to-all-done.1.left_ref, bf16[2,256,256]{2,1,0:T(8,128)(2,1)} %copy-done.4, ...), custom_call_target="tpu_custom_call", output_to_operand_aliasing={{0}: (17, {}), {1}: (18, {})} | custom-call | flops 1879048192 | bytes 14680064 | tf_op jit(solution)/shard_map/pallas_call | solution.py:117
  95.0 0.0 collective-permute-done.16.refs_1_
  95.0 0.6 collective-permute-done.14.refs_0_
  95.6 1.3 %shard_map.34 = f32[2,256,256]{2,1,0:T(8,128)S(1)} custom-call(s32[1]{0:T(128)} %bitcast.3.plane_ref, s32[1]{0:T(128)} %bitcast.4.core_ref, bf16[4,4,2,256,256]{4,3,2,1,0:T(8,128)(2,1)} %all-to-all-done.1.left_ref, bf16[2,256,256]{2,1,0:T(8,128)(2,1)S(1)} %collective-permute-done.14.refs_0_, ...), custom_call_target="tpu_custom_call", output_to_operand_aliasing={{}: (5, {})} | custom-call | flops 134217728 | bytes 1572864 | tf_op jit(solution)/shard_map/pallas_call | solution.py:117
  96.9 0.0 copy-start.3
  96.9 2.1 %collective-permute-start.17 = (f32[2,256,256]{2,1,0:T(8,128)S(1)}, f32[2,256,256]{2,1,0:T(8,128)S(1)}, u32[]{:S(2)}, u32[]{:S(2)}) collective-permute-start(f32[2,256,256]{2,1,0:T(8,128)S(1)} %shard_map.34), channel_id=1, source_target_pairs={{0,16},{16,0},{1,17},{17,1},{2,18},{18,2},{3,19},{19,3},{4,20},{20... | collective-permute-start | bytes 1572872 | tf_op jit(solution)/shard_map/ppermute | solution.py:237
  99.0 1.3 %shard_map.33.mine_ref = f32[2,256,256]{2,1,0:T(8,128)S(1)} custom-call(s32[1]{0:T(128)} %bitcast.3.plane_ref, s32[1]{0:T(128)} %bitcast.4.core_ref, bf16[4,4,2,256,256]{4,3,2,1,0:T(8,128)(2,1)} %all-to-all-done.1.left_ref, bf16[2,256,256]{2,1,0:T(8,128)(2,1)S(1)} %collective-permute-done.14.refs_0_, ...), custom_call_target="tpu_custom_call", output_to_operand_aliasing={{}: (5, {})} | custom-call | flops 134217728 | bytes 1572864 | tf_op jit(solution)/shard_map/pallas_call | solution.py:117
  100.3 0.5 collective-permute-done.17.other_ref
  100.9 0.7 shard_map.35
  101.6 1.8 %all-gather.1 = f32[2,2,256]{2,1,0:T(2,128)S(1)} all-gather(f32[1,2,256]{2,1,0:T(2,128)S(1)} %bitcast.9), channel_id=2, replica_groups=mesh['z'=16,'core'=2,'y'=4,'x'=4] {'core'}, dimensions={0}, use_global_device_ids=true | all-gather | bytes 6144 | tf_op jit(solution)/shard_map/all_gather | solution.py:249
  103.4 15.1 %all_to_all.15.parts_ref = f32[16,2,256]{2,1,0:T(2,128)S(1)} all-to-all(f32[16,2,256]{2,1,0:T(2,128)S(1)} %broadcast_in_dim.10), channel_id=1, replica_groups={{256,288,320,352,384,416,448,480,0,32,64,96,128,160,192,224},{257,289,3..., dimensions={0} | all-to-all | bytes 65536 | tf_op jit(solution)/shard_map/all_to_all | solution.py:251
  118.5 1.6 %shard_map.36 = f32[2,256,256]{2,1,0:T(8,128)} custom-call(s32[2]{0:T(128)} %bitcast.12, s32[1]{0:T(128)} %bitcast.1.column_ref, bf16[2,256,256]{2,1,0:T(8,128)(2,1)S(1)} %bitcast.8, f32[2,256,256]{2,1,0:T(8,128)S(1)} %get-tuple-element.15.inflated_ref, f32[16,2,256]{2,1,0:T(2,128)S(1)} %all_to_all.15.parts_ref), custom_call_target="tpu_custom_call" | custom-call | tf_op jit(solution)/shard_map/pallas_call | solution.py:260
  (26 shorter events, 0.1 us)
Async XLA Ops:
  1.1 55.1 %copy-start = (bf16[2,256,256]{2,1,0:T(8,128)(2,1)}, bf16[2,256,256]{2,1,0:T(8,128)(2,1)S(1)}, u32[]{:S(2)}) copy-start(bf16[2,256,256]{2,1,0:T(8,128)(2,1)S(1)} %shard_map.28.refs_0_) | copy-start | bytes 786436
  1.1 14.6 %collective-permute-start = (bf16[2,256,256]{2,1,0:T(8,128)(2,1)S(1)}, bf16[2,256,256]{2,1,0:T(8,128)(2,1)S(1)}, u32[]{:S(2)}, u32[]{:S(2)}) collective-permute-start(bf16[2,256,256]{2,1,0:T(8,128)(2,1)S(1)} %shard_map.28.refs_0_), channel_id=1, source_target_pairs={{0,16},{16,0},{1,17},{17,1},{2,18},{18,2},{3,19},{19,3},{4,20},{20... | collective-permute-start | bytes 786440 | tf_op jit(solution)/shard_map/ppermute | solution.py:193
  9.9 22.1 %collective-permute-start.1 = (bf16[2,256,256]{2,1,0:T(8,128)(2,1)S(1)}, bf16[2,256,256]{2,1,0:T(8,128)(2,1)S(1)}, u32[]{:S(2)}, u32[]{:S(2)}) collective-permute-start(bf16[2,256,256]{2,1,0:T(8,128)(2,1)S(1)} %shard_map.28.refs_0_), channel_id=1, source_target_pairs={{0,32},{32,64},{64,96},{96,128},{128,160},{160,192},{192,224},{224... | collective-permute-start | bytes 786440 | tf_op jit(solution)/shard_map/ppermute | solution.py:232
  15.7 12.2 %copy-start.14 = (bf16[2,256,256]{2,1,0:T(8,128)(2,1)}, bf16[2,256,256]{2,1,0:T(8,128)(2,1)S(1)}, u32[]{:S(2)}) copy-start(bf16[2,256,256]{2,1,0:T(8,128)(2,1)S(1)} %collective-permute-done.refs_1_) | copy-start | bytes 786436
  15.7 7.1 %collective-permute-start.8 = (bf16[2,256,256]{2,1,0:T(8,128)(2,1)S(1)}, bf16[2,256,256]{2,1,0:T(8,128)(2,1)S(1)}, u32[]{:S(2)}, u32[]{:S(2)}) collective-permute-start(bf16[2,256,256]{2,1,0:T(8,128)(2,1)S(1)} %collective-permute-done.refs_1_), channel_id=1, source_target_pairs={{0,32},{32,64},{64,96},{96,128},{128,160},{160,192},{192,224},{224... | collective-permute-start | bytes 786440 | tf_op jit(solution)/shard_map/ppermute | solution.py:232
  22.8 33.4 %copy-start.5 = (bf16[2,256,256]{2,1,0:T(8,128)(2,1)}, bf16[2,256,256]{2,1,0:T(8,128)(2,1)S(1)}, u32[]{:S(2)}) copy-start(bf16[2,256,256]{2,1,0:T(8,128)(2,1)S(1)} %collective-permute-done.8.refs_3_.refs_1_) | copy-start | bytes 786436
  22.8 11.1 %collective-permute-start.9 = (bf16[2,256,256]{2,1,0:T(8,128)(2,1)S(1)}, bf16[2,256,256]{2,1,0:T(8,128)(2,1)S(1)}, u32[]{:S(2)}, u32[]{:S(2)}) collective-permute-start(bf16[2,256,256]{2,1,0:T(8,128)(2,1)S(1)} %collective-permute-done.8.refs_3_.refs_1_), channel_id=1, source_target_pairs={{0,32},{32,64},{64,96},{96,128},{128,160},{160,192},{192,224},{224... | collective-permute-start | bytes 786440 | tf_op jit(solution)/shard_map/ppermute | solution.py:232
  27.8 25.9 %all-to-all-start = ((bf16[4,2,256,256]{3,2,1,0:T(8,128)(2,1)}), bf16[4,2,256,256]{3,2,1,0:T(8,128)(2,1)S(1)}, u32[]{:S(2)}, u32[]{:S(2)}) async-start(bf16[4,2,256,256]{3,2,1,0:T(8,128)(2,1)} %broadcast_in_dim.8), calls=%async_computation | async-start | bytes 2097152 | tf_op jit(solution)/shard_map/all_to_all | solution.py:215
  32.0 24.2 %copy-start.4 = (bf16[2,256,256]{2,1,0:T(8,128)(2,1)}, bf16[2,256,256]{2,1,0:T(8,128)(2,1)S(1)}, u32[]{:S(2)}) copy-start(bf16[2,256,256]{2,1,0:T(8,128)(2,1)S(1)} %collective-permute-done.1.refs_2_.refs_0_) | copy-start | bytes 786436
  32.0 7.4 %collective-permute-start.2 = (bf16[2,256,256]{2,1,0:T(8,128)(2,1)S(1)}, bf16[2,256,256]{2,1,0:T(8,128)(2,1)S(1)}, u32[]{:S(2)}, u32[]{:S(2)}) collective-permute-start(bf16[2,256,256]{2,1,0:T(8,128)(2,1)S(1)} %collective-permute-done.1.refs_2_.refs_0_), channel_id=1, source_target_pairs={{0,32},{32,64},{64,96},{96,128},{128,160},{160,192},{192,224},{224... | collective-permute-start | bytes 786440 | tf_op jit(solution)/shard_map/ppermute | solution.py:232
  34.0 22.2 %copy-start.6 = (bf16[2,256,256]{2,1,0:T(8,128)(2,1)}, bf16[2,256,256]{2,1,0:T(8,128)(2,1)S(1)}, u32[]{:S(2)}) copy-start(bf16[2,256,256]{2,1,0:T(8,128)(2,1)S(1)} %collective-permute-done.9.refs_5_.refs_3_) | copy-start | bytes 786436
  34.0 8.6 %collective-permute-start.10 = (bf16[2,256,256]{2,1,0:T(8,128)(2,1)S(1)}, bf16[2,256,256]{2,1,0:T(8,128)(2,1)S(1)}, u32[]{:S(2)}, u32[]{:S(2)}) collective-permute-start(bf16[2,256,256]{2,1,0:T(8,128)(2,1)S(1)} %collective-permute-done.9.refs_5_.refs_3_), channel_id=1, source_target_pairs={{0,32},{32,64},{64,96},{96,128},{128,160},{160,192},{192,224},{224... | collective-permute-start | bytes 786440 | tf_op jit(solution)/shard_map/ppermute | solution.py:232
  39.4 16.8 %copy-start.7 = (bf16[2,256,256]{2,1,0:T(8,128)(2,1)}, bf16[2,256,256]{2,1,0:T(8,128)(2,1)S(1)}, u32[]{:S(2)}) copy-start(bf16[2,256,256]{2,1,0:T(8,128)(2,1)S(1)} %collective-permute-done.2.refs_4_.refs_2_) | copy-start | bytes 786436
  39.4 7.4 %collective-permute-start.3 = (bf16[2,256,256]{2,1,0:T(8,128)(2,1)S(1)}, bf16[2,256,256]{2,1,0:T(8,128)(2,1)S(1)}, u32[]{:S(2)}, u32[]{:S(2)}) collective-permute-start(bf16[2,256,256]{2,1,0:T(8,128)(2,1)S(1)} %collective-permute-done.2.refs_4_.refs_2_), channel_id=1, source_target_pairs={{0,32},{32,64},{64,96},{96,128},{128,160},{160,192},{192,224},{224... | collective-permute-start | bytes 786440 | tf_op jit(solution)/shard_map/ppermute | solution.py:232
  42.6 13.6 %copy-start.8 = (bf16[2,256,256]{2,1,0:T(8,128)(2,1)}, bf16[2,256,256]{2,1,0:T(8,128)(2,1)S(1)}, u32[]{:S(2)}) copy-start(bf16[2,256,256]{2,1,0:T(8,128)(2,1)S(1)} %collective-permute-done.10.refs_7_.refs_5_) | copy-start | bytes 786436
  42.6 8.3 %collective-permute-start.11 = (bf16[2,256,256]{2,1,0:T(8,128)(2,1)S(1)}, bf16[2,256,256]{2,1,0:T(8,128)(2,1)S(1)}, u32[]{:S(2)}, u32[]{:S(2)}) collective-permute-start(bf16[2,256,256]{2,1,0:T(8,128)(2,1)S(1)} %collective-permute-done.10.refs_7_.refs_5_), channel_id=1, source_target_pairs={{0,32},{32,64},{64,96},{96,128},{128,160},{160,192},{192,224},{224... | collective-permute-start | bytes 786440 | tf_op jit(solution)/shard_map/ppermute | solution.py:232
  46.8 9.4 %copy-start.9 = (bf16[2,256,256]{2,1,0:T(8,128)(2,1)}, bf16[2,256,256]{2,1,0:T(8,128)(2,1)S(1)}, u32[]{:S(2)}) copy-start(bf16[2,256,256]{2,1,0:T(8,128)(2,1)S(1)} %collective-permute-done.3.refs_6_.refs_4_) | copy-start | bytes 786436
  46.8 14.3 %collective-permute-start.4 = (bf16[2,256,256]{2,1,0:T(8,128)(2,1)S(1)}, bf16[2,256,256]{2,1,0:T(8,128)(2,1)S(1)}, u32[]{:S(2)}, u32[]{:S(2)}) collective-permute-start(bf16[2,256,256]{2,1,0:T(8,128)(2,1)S(1)} %collective-permute-done.3.refs_6_.refs_4_), channel_id=1, source_target_pairs={{0,32},{32,64},{64,96},{96,128},{128,160},{160,192},{192,224},{224... | collective-permute-start | bytes 786440 | tf_op jit(solution)/shard_map/ppermute | solution.py:232
  50.9 5.4 %copy-start.10 = (bf16[2,256,256]{2,1,0:T(8,128)(2,1)}, bf16[2,256,256]{2,1,0:T(8,128)(2,1)S(1)}, u32[]{:S(2)}) copy-start(bf16[2,256,256]{2,1,0:T(8,128)(2,1)S(1)} %collective-permute-done.11.refs_9_.refs_7_) | copy-start | bytes 786436
  50.9 12.2 %collective-permute-start.12 = (bf16[2,256,256]{2,1,0:T(8,128)(2,1)S(1)}, bf16[2,256,256]{2,1,0:T(8,128)(2,1)}, u32[]{:S(2)}, u32[]{:S(2)}) collective-permute-start(bf16[2,256,256]{2,1,0:T(8,128)(2,1)S(1)} %collective-permute-done.11.refs_9_.refs_7_), channel_id=1, source_target_pairs={{0,32},{32,64},{64,96},{96,128},{128,160},{160,192},{192,224},{224... | collective-permute-start | bytes 786440 | tf_op jit(solution)/shard_map/ppermute | solution.py:232
  56.2 31.8 %all-to-all-start.1 = ((bf16[4,4,2,256,256]{4,3,2,1,0:T(8,128)(2,1)}), bf16[4,4,2,256,256]{4,3,2,1,0:T(8,128)(2,1)}, u32[]{:S(2)}, u32[]{:S(2)}) async-start(bf16[4,4,2,256,256]{4,3,2,1,0:T(8,128)(2,1)} %broadcast_in_dim.9), calls=%async_computation.1 | async-start | bytes 8388608 | tf_op jit(solution)/shard_map/all_to_all | solution.py:215
  61.1 10.7 %copy-start.11 = (bf16[2,256,256]{2,1,0:T(8,128)(2,1)}, bf16[2,256,256]{2,1,0:T(8,128)(2,1)S(1)}, u32[]{:S(2)}) copy-start(bf16[2,256,256]{2,1,0:T(8,128)(2,1)S(1)} %collective-permute-done.4.refs_8_.refs_6_) | copy-start | bytes 786436
  61.1 7.5 %collective-permute-start.5 = (bf16[2,256,256]{2,1,0:T(8,128)(2,1)S(1)}, bf16[2,256,256]{2,1,0:T(8,128)(2,1)S(1)}, u32[]{:S(2)}, u32[]{:S(2)}) collective-permute-start(bf16[2,256,256]{2,1,0:T(8,128)(2,1)S(1)} %collective-permute-done.4.refs_8_.refs_6_), channel_id=1, source_target_pairs={{0,32},{32,64},{64,96},{96,128},{128,160},{160,192},{192,224},{224... | collective-permute-start | bytes 786440 | tf_op jit(solution)/shard_map/ppermute | solution.py:232
  63.1 8.7 %collective-permute-start.13 = (bf16[2,256,256]{2,1,0:T(8,128)(2,1)}, bf16[2,256,256]{2,1,0:T(8,128)(2,1)S(1)}, u32[]{:S(2)}, u32[]{:S(2)}) collective-permute-start(bf16[2,256,256]{2,1,0:T(8,128)(2,1)} %collective-permute-done.12.refs_11_.refs_9_), channel_id=1, source_target_pairs={{0,32},{32,64},{64,96},{96,128},{128,160},{160,192},{192,224},{224... | collective-permute-start | bytes 786440 | tf_op jit(solution)/shard_map/ppermute | solution.py:232
  68.6 3.2 %copy-start.12 = (bf16[2,256,256]{2,1,0:T(8,128)(2,1)}, bf16[2,256,256]{2,1,0:T(8,128)(2,1)S(1)}, u32[]{:S(2)}) copy-start(bf16[2,256,256]{2,1,0:T(8,128)(2,1)S(1)} %collective-permute-done.5.refs_10_.refs_8_) | copy-start | bytes 786436
  68.6 7.5 %collective-permute-start.6 = (bf16[2,256,256]{2,1,0:T(8,128)(2,1)S(1)}, bf16[2,256,256]{2,1,0:T(8,128)(2,1)S(1)}, u32[]{:S(2)}, u32[]{:S(2)}) collective-permute-start(bf16[2,256,256]{2,1,0:T(8,128)(2,1)S(1)} %collective-permute-done.5.refs_10_.refs_8_), channel_id=1, source_target_pairs={{0,32},{32,64},{64,96},{96,128},{128,160},{160,192},{192,224},{224... | collective-permute-start | bytes 786440 | tf_op jit(solution)/shard_map/ppermute | solution.py:232
  71.8 16.2 %copy-start.1 = (bf16[2,256,256]{2,1,0:T(8,128)(2,1)}, bf16[2,256,256]{2,1,0:T(8,128)(2,1)S(1)}, u32[]{:S(2)}) copy-start(bf16[2,256,256]{2,1,0:T(8,128)(2,1)S(1)} %shard_map.29.refs_13_.refs_11_) | copy-start | bytes 786436
  71.8 8.7 %collective-permute-start.15 = (bf16[2,256,256]{2,1,0:T(8,128)(2,1)S(1)}, bf16[2,256,256]{2,1,0:T(8,128)(2,1)S(1)}, u32[]{:S(2)}, u32[]{:S(2)}) collective-permute-start(bf16[2,256,256]{2,1,0:T(8,128)(2,1)S(1)} %shard_map.29.refs_13_.refs_11_), channel_id=1, source_target_pairs={{0,32},{32,64},{64,96},{96,128},{128,160},{160,192},{192,224},{224... | collective-permute-start | bytes 786440 | tf_op jit(solution)/shard_map/ppermute | solution.py:232
  76.1 11.9 %copy-start.13 = (bf16[2,256,256]{2,1,0:T(8,128)(2,1)}, bf16[2,256,256]{2,1,0:T(8,128)(2,1)S(1)}, u32[]{:S(2)}) copy-start(bf16[2,256,256]{2,1,0:T(8,128)(2,1)S(1)} %collective-permute-done.6.refs_12_.refs_10_) | copy-start | bytes 786436
  76.1 12.3 %collective-permute-start.7 = (bf16[2,256,256]{2,1,0:T(8,128)(2,1)S(1)}, bf16[2,256,256]{2,1,0:T(8,128)(2,1)S(1)}, u32[]{:S(2)}, u32[]{:S(2)}) collective-permute-start(bf16[2,256,256]{2,1,0:T(8,128)(2,1)S(1)} %collective-permute-done.6.refs_12_.refs_10_), channel_id=1, source_target_pairs={{0,32},{32,64},{64,96},{96,128},{128,160},{160,192},{192,224},{224... | collective-permute-start | bytes 786440 | tf_op jit(solution)/shard_map/ppermute | solution.py:232
  80.5 8.0 %copy-start.15 = (bf16[2,256,256]{2,1,0:T(8,128)(2,1)}, bf16[2,256,256]{2,1,0:T(8,128)(2,1)S(1)}, u32[]{:S(2)}) copy-start(bf16[2,256,256]{2,1,0:T(8,128)(2,1)S(1)} %collective-permute-done.15.refs_13_) | copy-start | bytes 786436
  80.5 14.5 %collective-permute-start.16 = (bf16[2,256,256]{2,1,0:T(8,128)(2,1)S(1)}, bf16[2,256,256]{2,1,0:T(8,128)(2,1)S(1)}, u32[]{:S(2)}, u32[]{:S(2)}) collective-permute-start(bf16[2,256,256]{2,1,0:T(8,128)(2,1)S(1)} %collective-permute-done.15.refs_13_), channel_id=1, source_target_pairs={{16,496},{48,16},{80,48},{112,80},{144,112},{176,144},{208,176},{2... | collective-permute-start | bytes 786440 | tf_op jit(solution)/shard_map/ppermute | solution.py:232
  88.5 1.9 %copy-start.2 = (bf16[2,256,256]{2,1,0:T(8,128)(2,1)}, bf16[2,256,256]{2,1,0:T(8,128)(2,1)S(1)}, u32[]{:S(2)}) copy-start(bf16[2,256,256]{2,1,0:T(8,128)(2,1)S(1)} %shard_map.31.refs_12_) | copy-start | bytes 786436
  88.5 7.1 %collective-permute-start.14 = (bf16[2,256,256]{2,1,0:T(8,128)(2,1)S(1)}, bf16[2,256,256]{2,1,0:T(8,128)(2,1)S(1)}, u32[]{:S(2)}, u32[]{:S(2)}) collective-permute-start(bf16[2,256,256]{2,1,0:T(8,128)(2,1)S(1)} %shard_map.31.refs_12_), channel_id=1, source_target_pairs={{16,496},{48,16},{80,48},{112,80},{144,112},{176,144},{208,176},{2... | collective-permute-start | bytes 786440 | tf_op jit(solution)/shard_map/ppermute | solution.py:232
  96.9 21.6 %copy-start.3 = (bf16[1,2,256,256]{3,2,1,0:T(8,128)(2,1)S(1)}, bf16[1,2,256,256]{3,2,1,0:T(8,128)(2,1)}, u32[]{:S(2)}) copy-start(bf16[1,2,256,256]{3,2,1,0:T(8,128)(2,1)} %param.3) | copy-start | bytes 786436
  96.9 3.9 %collective-permute-start.17 = (f32[2,256,256]{2,1,0:T(8,128)S(1)}, f32[2,256,256]{2,1,0:T(8,128)S(1)}, u32[]{:S(2)}, u32[]{:S(2)}) collective-permute-start(f32[2,256,256]{2,1,0:T(8,128)S(1)} %shard_map.34), channel_id=1, source_target_pairs={{0,16},{16,0},{1,17},{17,1},{2,18},{18,2},{3,19},{19,3},{4,20},{20... | collective-permute-start | bytes 1572872 | tf_op jit(solution)/shard_map/ppermute | solution.py:237

commit v16 on v14

--- a/solution.py
+++ b/solution.py
@@ -15,7 +15,7 @@
 HBM = pl.BlockSpec(memory_space=pltpu.HBM)
 MIB = 1024 * 1024
 SWAP = [(0, 1), (1, 0)]
-FLOPS = 26 * 10**9
+FLOPS = 25 * 10**9
 
 
 def params(mib):

time: 113 us -> 113 us (level)
  no operation moved by 1% of the time
where the time goes in v16:
time: 113 us; the launch traced here: 112 us
  starting transfers between devices  72.1 us (64%)
  blocking collectives  15.5 us (14%)
  Pallas kernels  11.2 us (10%)
  waiting for transfers between devices  9.41 us (8%)
  local copies, waits for them, and re-layouts  3.65 us (3%)
    ppermute x16, starting transfers between devices, on_device(): held.append(tuple((lax.ppermute(t, ROWS, perm) for t in held[-1])))  52.2 us
    all_to_all x1, blocking collectives, on_device(): lax.all_to_all(jnp.broadcast_to(sums[None], (planes, *sums.shape)), 'z',...  13.7 us
    all_to_all x2, starting transfers between devices, copy_for_each(): lax.all_to_all(spread, ('core', *COLS), 0, 0, axis_index_groups=lines, ti...  9.04 us
    ppermute x16, waiting for transfers between devices, on_device(): held.append(tuple((lax.ppermute(t, ROWS, perm) for t in held[-1])))  8.86 us
    ppermute x1, starting transfers between devices, on_device(): other = lax.ppermute(mine, 'core', SWAP)  8.79 us
    pallas_call x4, Pallas kernels, products(): pl.pallas_call(kernel, in_specs=[SMEM, SMEM, HBM] + [HBM if len(planes) >...  7.87 us
    broadcast_in_dim x2, local copies, waits for them, and re-layouts, copy_for_each(): spread = jnp.broadcast_to(value[None], (len(lines[0]), *value.shape))  3.56 us
  transfers between devices with their start and end apart: 20, of which 7 were waited for; matrix products, arithmetic and copies ran while one was open for 3% of the time, Pallas kernels for 6%

profile of v16, /device:TPU:1, one launch (start us, length us, event | category | flops | bytes accessed | tf_op | source)
XLA Modules:
  0.0 112.5 jit_solution(6559859263186004566)
XLA Ops:
  0.0 1.1 shard_map.28.refs_0_
  1.1 0.0 copy-start
  1.1 8.8 %collective-permute-start = (bf16[2,256,256]{2,1,0:T(8,128)(2,1)S(1)}, bf16[2,256,256]{2,1,0:T(8,128)(2,1)S(1)}, u32[]{:S(2)}, u32[]{:S(2)}) collective-permute-start(bf16[2,256,256]{2,1,0:T(8,128)(2,1)S(1)} %shard_map.28.refs_0_), channel_id=1, source_target_pairs={{0,16},{16,0},{1,17},{17,1},{2,18},{18,2},{3,19},{19,3},{4,20},{20... | collective-permute-start | bytes 786440 | tf_op jit(solution)/shard_map/ppermute | solution.py:193
  9.9 5.7 %collective-permute-start.1 = (bf16[2,256,256]{2,1,0:T(8,128)(2,1)S(1)}, bf16[2,256,256]{2,1,0:T(8,128)(2,1)S(1)}, u32[]{:S(2)}, u32[]{:S(2)}) collective-permute-start(bf16[2,256,256]{2,1,0:T(8,128)(2,1)S(1)} %shard_map.28.refs_0_), channel_id=1, source_target_pairs={{0,32},{32,64},{64,96},{96,128},{128,160},{160,192},{192,224},{224... | collective-permute-start | bytes 786440 | tf_op jit(solution)/shard_map/ppermute | solution.py:232
  15.7 0.0 collective-permute-done.refs_1_
  15.7 0.0 copy-start.15
  15.7 2.6 %collective-permute-start.9 = (bf16[2,256,256]{2,1,0:T(8,128)(2,1)S(1)}, bf16[2,256,256]{2,1,0:T(8,128)(2,1)S(1)}, u32[]{:S(2)}, u32[]{:S(2)}) collective-permute-start(bf16[2,256,256]{2,1,0:T(8,128)(2,1)S(1)} %collective-permute-done.refs_1_), channel_id=1, source_target_pairs={{0,32},{32,64},{64,96},{96,128},{128,160},{160,192},{192,224},{224... | collective-permute-start | bytes 786440 | tf_op jit(solution)/shard_map/ppermute | solution.py:232
  18.4 1.0 broadcast_in_dim.8
  19.5 4.2 %all-to-all-start = ((bf16[4,2,256,256]{3,2,1,0:T(8,128)(2,1)}), bf16[4,2,256,256]{3,2,1,0:T(8,128)(2,1)S(1)}, u32[]{:S(2)}, u32[]{:S(2)}) async-start(bf16[4,2,256,256]{3,2,1,0:T(8,128)(2,1)} %broadcast_in_dim.8), calls=%async_computation | async-start | bytes 2097152 | tf_op jit(solution)/shard_map/all_to_all | solution.py:215
  23.6 0.0 collective-permute-done.1.refs_2_.refs_0_
  23.6 2.6 %collective-permute-start.2 = (bf16[2,256,256]{2,1,0:T(8,128)(2,1)S(1)}, bf16[2,256,256]{2,1,0:T(8,128)(2,1)S(1)}, u32[]{:S(2)}, u32[]{:S(2)}) collective-permute-start(bf16[2,256,256]{2,1,0:T(8,128)(2,1)S(1)} %collective-permute-done.1.refs_2_.refs_0_), channel_id=1, source_target_pairs={{0,32},{32,64},{64,96},{96,128},{128,160},{160,192},{192,224},{224... | collective-permute-start | bytes 786440 | tf_op jit(solution)/shard_map/ppermute | solution.py:232
  26.3 0.0 copy-done.15
  26.3 0.0 collective-permute-done.9.refs_3_.refs_1_
  26.3 0.0 copy-start.5
  26.3 2.6 %collective-permute-start.10 = (bf16[2,256,256]{2,1,0:T(8,128)(2,1)S(1)}, bf16[2,256,256]{2,1,0:T(8,128)(2,1)S(1)}, u32[]{:S(2)}, u32[]{:S(2)}) collective-permute-start(bf16[2,256,256]{2,1,0:T(8,128)(2,1)S(1)} %collective-permute-done.9.refs_3_.refs_1_), channel_id=1, source_target_pairs={{0,32},{32,64},{64,96},{96,128},{128,160},{160,192},{192,224},{224... | collective-permute-start | bytes 786440 | tf_op jit(solution)/shard_map/ppermute | solution.py:232
  29.0 2.1 %collective-permute-done.2.refs_4_.refs_2_ = bf16[2,256,256]{2,1,0:T(8,128)(2,1)S(1)} collective-permute-done((bf16[2,256,256]{2,1,0:T(8,128)(2,1)S(1)}, bf16[2,256,256]{2,1,0:T(8,128)(2,1)S(1)}, u32[]{:S(2)}, u32[]{:S(2)}) %collective-permute-start.2) | collective-permute-done | bytes 262176 | tf_op jit(solution)/shard_map/ppermute | solution.py:232
  31.1 3.8 %collective-permute-start.3 = (bf16[2,256,256]{2,1,0:T(8,128)(2,1)S(1)}, bf16[2,256,256]{2,1,0:T(8,128)(2,1)S(1)}, u32[]{:S(2)}, u32[]{:S(2)}) collective-permute-start(bf16[2,256,256]{2,1,0:T(8,128)(2,1)S(1)} %collective-permute-done.2.refs_4_.refs_2_), channel_id=1, source_target_pairs={{0,32},{32,64},{64,96},{96,128},{128,160},{160,192},{192,224},{224... | collective-permute-start | bytes 786440 | tf_op jit(solution)/shard_map/ppermute | solution.py:232
  34.9 0.0 collective-permute-done.10.refs_5_.refs_3_
  34.9 0.0 copy-start.7
  34.9 2.5 %collective-permute-start.11 = (bf16[2,256,256]{2,1,0:T(8,128)(2,1)S(1)}, bf16[2,256,256]{2,1,0:T(8,128)(2,1)S(1)}, u32[]{:S(2)}, u32[]{:S(2)}) collective-permute-start(bf16[2,256,256]{2,1,0:T(8,128)(2,1)S(1)} %collective-permute-done.10.refs_5_.refs_3_), channel_id=1, source_target_pairs={{0,32},{32,64},{64,96},{96,128},{128,160},{160,192},{192,224},{224... | collective-permute-start | bytes 786440 | tf_op jit(solution)/shard_map/ppermute | solution.py:232
  37.4 1.0 collective-permute-done.3.refs_6_.refs_4_
  38.5 4.8 %collective-permute-start.4 = (bf16[2,256,256]{2,1,0:T(8,128)(2,1)S(1)}, bf16[2,256,256]{2,1,0:T(8,128)(2,1)S(1)}, u32[]{:S(2)}, u32[]{:S(2)}) collective-permute-start(bf16[2,256,256]{2,1,0:T(8,128)(2,1)S(1)} %collective-permute-done.3.refs_6_.refs_4_), channel_id=1, source_target_pairs={{0,32},{32,64},{64,96},{96,128},{128,160},{160,192},{192,224},{224... | collective-permute-start | bytes 786440 | tf_op jit(solution)/shard_map/ppermute | solution.py:232
  43.2 0.0 collective-permute-done.11.refs_7_.refs_5_
  43.2 0.0 copy-start.9
  43.2 2.8 %collective-permute-start.12 = (bf16[2,256,256]{2,1,0:T(8,128)(2,1)S(1)}, bf16[2,256,256]{2,1,0:T(8,128)(2,1)S(1)}, u32[]{:S(2)}, u32[]{:S(2)}) collective-permute-start(bf16[2,256,256]{2,1,0:T(8,128)(2,1)S(1)} %collective-permute-done.11.refs_7_.refs_5_), channel_id=1, source_target_pairs={{0,32},{32,64},{64,96},{96,128},{128,160},{160,192},{192,224},{224... | collective-permute-start | bytes 786440 | tf_op jit(solution)/shard_map/ppermute | solution.py:232
  46.0 0.0 all-to-all-done
  46.0 2.5 %broadcast_in_dim.9 = bf16[4,4,2,256,256]{4,3,2,1,0:T(8,128)(2,1)} broadcast(bf16[4,2,256,256]{3,2,1,0:T(8,128)(2,1)S(1)} %all-to-all-done), dimensions={1,2,3,4} | broadcast | bytes 5242880 | tf_op jit(solution)/shard_map/broadcast_in_dim | solution.py:214
  48.5 0.0 copy-done
  48.5 0.0 copy-done.4
  48.5 0.0 copy-done.5
  48.6 0.0 copy-done.6
  48.6 4.9 %all-to-all-start.1 = ((bf16[4,4,2,256,256]{4,3,2,1,0:T(8,128)(2,1)}), bf16[4,4,2,256,256]{4,3,2,1,0:T(8,128)(2,1)}, u32[]{:S(2)}, u32[]{:S(2)}) async-start(bf16[4,4,2,256,256]{4,3,2,1,0:T(8,128)(2,1)} %broadcast_in_dim.9), calls=%async_computation.1 | async-start | bytes 8388608 | tf_op jit(solution)/shard_map/all_to_all | solution.py:215
  53.5 0.0 collective-permute-done.4.refs_8_.refs_6_
  53.5 1.9 %collective-permute-start.5 = (bf16[2,256,256]{2,1,0:T(8,128)(2,1)S(1)}, bf16[2,256,256]{2,1,0:T(8,128)(2,1)S(1)}, u32[]{:S(2)}, u32[]{:S(2)}) collective-permute-start(bf16[2,256,256]{2,1,0:T(8,128)(2,1)S(1)} %collective-permute-done.4.refs_8_.refs_6_), channel_id=1, source_target_pairs={{0,32},{32,64},{64,96},{96,128},{128,160},{160,192},{192,224},{224... | collective-permute-start | bytes 786440 | tf_op jit(solution)/shard_map/ppermute | solution.py:232
  55.4 0.0 collective-permute-done.12.refs_9_.refs_7_
  55.4 2.4 %collective-permute-start.13 = (bf16[2,256,256]{2,1,0:T(8,128)(2,1)S(1)}, bf16[2,256,256]{2,1,0:T(8,128)(2,1)S(1)}, u32[]{:S(2)}, u32[]{:S(2)}) collective-permute-start(bf16[2,256,256]{2,1,0:T(8,128)(2,1)S(1)} %collective-permute-done.12.refs_9_.refs_7_), channel_id=1, source_target_pairs={{0,32},{32,64},{64,96},{96,128},{128,160},{160,192},{192,224},{224... | collective-permute-start | bytes 786440 | tf_op jit(solution)/shard_map/ppermute | solution.py:232
  57.9 3.1 %collective-permute-done.5.refs_10_.refs_8_ = bf16[2,256,256]{2,1,0:T(8,128)(2,1)S(1)} collective-permute-done((bf16[2,256,256]{2,1,0:T(8,128)(2,1)S(1)}, bf16[2,256,256]{2,1,0:T(8,128)(2,1)S(1)}, u32[]{:S(2)}, u32[]{:S(2)}) %collective-permute-start.5) | collective-permute-done | bytes 262176 | tf_op jit(solution)/shard_map/ppermute | solution.py:232
  61.0 3.1 %collective-permute-start.6 = (bf16[2,256,256]{2,1,0:T(8,128)(2,1)S(1)}, bf16[2,256,256]{2,1,0:T(8,128)(2,1)S(1)}, u32[]{:S(2)}, u32[]{:S(2)}) collective-permute-start(bf16[2,256,256]{2,1,0:T(8,128)(2,1)S(1)} %collective-permute-done.5.refs_10_.refs_8_), channel_id=1, source_target_pairs={{0,32},{32,64},{64,96},{96,128},{128,160},{160,192},{192,224},{224... | collective-permute-start | bytes 786440 | tf_op jit(solution)/shard_map/ppermute | solution.py:232
  64.1 0.0 collective-permute-done.13.refs_11_.refs_9_
  64.1 0.0 copy-start.13
  64.1 2.8 %collective-permute-start.14 = (bf16[2,256,256]{2,1,0:T(8,128)(2,1)S(1)}, bf16[2,256,256]{2,1,0:T(8,128)(2,1)S(1)}, u32[]{:S(2)}, u32[]{:S(2)}) collective-permute-start(bf16[2,256,256]{2,1,0:T(8,128)(2,1)S(1)} %collective-permute-done.13.refs_11_.refs_9_), channel_id=1, source_target_pairs={{0,32},{32,64},{64,96},{96,128},{128,160},{160,192},{192,224},{224... | collective-permute-start | bytes 786440 | tf_op jit(solution)/shard_map/ppermute | solution.py:232
  66.9 1.6 %collective-permute-done.6.refs_12_.refs_10_ = bf16[2,256,256]{2,1,0:T(8,128)(2,1)S(1)} collective-permute-done((bf16[2,256,256]{2,1,0:T(8,128)(2,1)S(1)}, bf16[2,256,256]{2,1,0:T(8,128)(2,1)S(1)}, u32[]{:S(2)}, u32[]{:S(2)}) %collective-permute-start.6) | collective-permute-done | bytes 262176 | tf_op jit(solution)/shard_map/ppermute | solution.py:232
  68.5 4.3 %collective-permute-start.7 = (bf16[2,256,256]{2,1,0:T(8,128)(2,1)S(1)}, bf16[2,256,256]{2,1,0:T(8,128)(2,1)S(1)}, u32[]{:S(2)}, u32[]{:S(2)}) collective-permute-start(bf16[2,256,256]{2,1,0:T(8,128)(2,1)S(1)} %collective-permute-done.6.refs_12_.refs_10_), channel_id=1, source_target_pairs={{0,32},{32,64},{64,96},{96,128},{128,160},{160,192},{192,224},{224... | collective-permute-start | bytes 786440 | tf_op jit(solution)/shard_map/ppermute | solution.py:232
  72.8 0.0 collective-permute-done.14.refs_0_
  72.9 2.8 %collective-permute-start.15 = (bf16[2,256,256]{2,1,0:T(8,128)(2,1)S(1)}, bf16[2,256,256]{2,1,0:T(8,128)(2,1)S(1)}, u32[]{:S(2)}, u32[]{:S(2)}) collective-permute-start(bf16[2,256,256]{2,1,0:T(8,128)(2,1)S(1)} %shard_map.29.refs_13_.refs_11_), channel_id=1, source_target_pairs={{0,32},{32,64},{64,96},{96,128},{128,160},{160,192},{192,224},{224... | collective-permute-start | bytes 786440 | tf_op jit(solution)/shard_map/ppermute | solution.py:232
  75.7 0.4 collective-permute-done.7.refs_12_
  76.1 5.4 %collective-permute-start.8 = (bf16[2,256,256]{2,1,0:T(8,128)(2,1)S(1)}, bf16[2,256,256]{2,1,0:T(8,128)(2,1)S(1)}, u32[]{:S(2)}, u32[]{:S(2)}) collective-permute-start(bf16[2,256,256]{2,1,0:T(8,128)(2,1)S(1)} %collective-permute-done.7.refs_12_), channel_id=1, source_target_pairs={{16,496},{48,16},{80,48},{112,80},{144,112},{176,144},{208,176},{2... | collective-permute-start | bytes 786440 | tf_op jit(solution)/shard_map/ppermute | solution.py:232
  81.6 0.0 all-to-all-done.1.left_ref
  81.6 0.7 shard_map.30
  82.2 0.0 collective-permute-done.15.refs_0_
  82.3 0.0 copy-start.2
  82.3 1.9 %collective-permute-start.16 = (bf16[2,256,256]{2,1,0:T(8,128)(2,1)S(1)}, bf16[2,256,256]{2,1,0:T(8,128)(2,1)S(1)}, u32[]{:S(2)}, u32[]{:S(2)}) collective-permute-start(bf16[2,256,256]{2,1,0:T(8,128)(2,1)S(1)} %shard_map.31.refs_13_), channel_id=1, source_target_pairs={{16,496},{48,16},{80,48},{112,80},{144,112},{176,144},{208,176},{2... | collective-permute-start | bytes 786440 | tf_op jit(solution)/shard_map/ppermute | solution.py:232
  84.2 4.6 %shard_map.32 = (f32[2,256,256]{2,1,0:T(8,128)S(1)}, f32[2,256,256]{2,1,0:T(8,128)S(1)}) custom-call(s32[1]{0:T(128)} %bitcast.3.plane_ref, s32[1]{0:T(128)} %bitcast.4.core_ref, bf16[4,4,2,256,256]{4,3,2,1,0:T(8,128)(2,1)} %all-to-all-done.1.left_ref, bf16[2,256,256]{2,1,0:T(8,128)(2,1)} %copy-done.4, ...), custom_call_target="tpu_custom_call", output_to_operand_aliasing={{0}: (17, {}), {1}: (18, {})} | custom-call | flops 1879048192 | bytes 14680064 | tf_op jit(solution)/shard_map/pallas_call | solution.py:117
  88.8 0.0 collective-permute-done.8.refs_0_
  88.8 0.6 collective-permute-done.16.refs_1_
  89.4 1.3 %shard_map.34 = f32[2,256,256]{2,1,0:T(8,128)S(1)} custom-call(s32[1]{0:T(128)} %bitcast.3.plane_ref, s32[1]{0:T(128)} %bitcast.4.core_ref, bf16[4,4,2,256,256]{4,3,2,1,0:T(8,128)(2,1)} %all-to-all-done.1.left_ref, bf16[2,256,256]{2,1,0:T(8,128)(2,1)S(1)} %collective-permute-done.8.refs_0_, ...), custom_call_target="tpu_custom_call", output_to_operand_aliasing={{}: (5, {})} | custom-call | flops 134217728 | bytes 1572864 | tf_op jit(solution)/shard_map/pallas_call | solution.py:117
  90.7 0.0 copy-start.3
  90.7 2.1 %collective-permute-start.17 = (f32[2,256,256]{2,1,0:T(8,128)S(1)}, f32[2,256,256]{2,1,0:T(8,128)S(1)}, u32[]{:S(2)}, u32[]{:S(2)}) collective-permute-start(f32[2,256,256]{2,1,0:T(8,128)S(1)} %shard_map.34), channel_id=1, source_target_pairs={{0,16},{16,0},{1,17},{17,1},{2,18},{18,2},{3,19},{19,3},{4,20},{20... | collective-permute-start | bytes 1572872 | tf_op jit(solution)/shard_map/ppermute | solution.py:237
  92.8 1.3 %shard_map.33.mine_ref = f32[2,256,256]{2,1,0:T(8,128)S(1)} custom-call(s32[1]{0:T(128)} %bitcast.3.plane_ref, s32[1]{0:T(128)} %bitcast.4.core_ref, bf16[4,4,2,256,256]{4,3,2,1,0:T(8,128)(2,1)} %all-to-all-done.1.left_ref, bf16[2,256,256]{2,1,0:T(8,128)(2,1)S(1)} %collective-permute-done.8.refs_0_, ...), custom_call_target="tpu_custom_call", output_to_operand_aliasing={{}: (5, {})} | custom-call | flops 134217728 | bytes 1572864 | tf_op jit(solution)/shard_map/pallas_call | solution.py:117
  94.1 0.5 collective-permute-done.17.other_ref
  94.7 0.7 shard_map.35
  95.4 1.8 %all-gather.1 = f32[2,2,256]{2,1,0:T(2,128)S(1)} all-gather(f32[1,2,256]{2,1,0:T(2,128)S(1)} %bitcast.9), channel_id=2, replica_groups=mesh['z'=16,'core'=2,'y'=4,'x'=4] {'core'}, dimensions={0}, use_global_device_ids=true | all-gather | bytes 6144 | tf_op jit(solution)/shard_map/all_gather | solution.py:249
  97.2 13.7 %all_to_all.15.parts_ref = f32[16,2,256]{2,1,0:T(2,128)S(1)} all-to-all(f32[16,2,256]{2,1,0:T(2,128)S(1)} %broadcast_in_dim.10), channel_id=1, replica_groups={{256,288,320,352,384,416,448,480,0,32,64,96,128,160,192,224},{257,289,3..., dimensions={0} | all-to-all | bytes 65536 | tf_op jit(solution)/shard_map/all_to_all | solution.py:251
  110.9 1.6 %shard_map.36 = f32[2,256,256]{2,1,0:T(8,128)} custom-call(s32[2]{0:T(128)} %bitcast.12, s32[1]{0:T(128)} %bitcast.1.column_ref, bf16[2,256,256]{2,1,0:T(8,128)(2,1)S(1)} %bitcast.8, f32[2,256,256]{2,1,0:T(8,128)S(1)} %get-tuple-element.15.inflated_ref, f32[16,2,256]{2,1,0:T(2,128)S(1)} %all_to_all.15.parts_ref), custom_call_target="tpu_custom_call" | custom-call | tf_op jit(solution)/shard_map/pallas_call | solution.py:260
  (28 shorter events, 0.1 us)
Async XLA Ops:
  1.1 47.5 %copy-start = (bf16[2,256,256]{2,1,0:T(8,128)(2,1)}, bf16[2,256,256]{2,1,0:T(8,128)(2,1)S(1)}, u32[]{:S(2)}) copy-start(bf16[2,256,256]{2,1,0:T(8,128)(2,1)S(1)} %shard_map.28.refs_0_) | copy-start | bytes 786436
  1.1 14.6 %collective-permute-start = (bf16[2,256,256]{2,1,0:T(8,128)(2,1)S(1)}, bf16[2,256,256]{2,1,0:T(8,128)(2,1)S(1)}, u32[]{:S(2)}, u32[]{:S(2)}) collective-permute-start(bf16[2,256,256]{2,1,0:T(8,128)(2,1)S(1)} %shard_map.28.refs_0_), channel_id=1, source_target_pairs={{0,16},{16,0},{1,17},{17,1},{2,18},{18,2},{3,19},{19,3},{4,20},{20... | collective-permute-start | bytes 786440 | tf_op jit(solution)/shard_map/ppermute | solution.py:193
  9.9 13.8 %collective-permute-start.1 = (bf16[2,256,256]{2,1,0:T(8,128)(2,1)S(1)}, bf16[2,256,256]{2,1,0:T(8,128)(2,1)S(1)}, u32[]{:S(2)}, u32[]{:S(2)}) collective-permute-start(bf16[2,256,256]{2,1,0:T(8,128)(2,1)S(1)} %shard_map.28.refs_0_), channel_id=1, source_target_pairs={{0,32},{32,64},{64,96},{96,128},{128,160},{160,192},{192,224},{224... | collective-permute-start | bytes 786440 | tf_op jit(solution)/shard_map/ppermute | solution.py:232
  15.7 10.6 %copy-start.15 = (bf16[2,256,256]{2,1,0:T(8,128)(2,1)}, bf16[2,256,256]{2,1,0:T(8,128)(2,1)S(1)}, u32[]{:S(2)}) copy-start(bf16[2,256,256]{2,1,0:T(8,128)(2,1)S(1)} %collective-permute-done.refs_1_) | copy-start | bytes 786436
  15.7 10.6 %collective-permute-start.9 = (bf16[2,256,256]{2,1,0:T(8,128)(2,1)S(1)}, bf16[2,256,256]{2,1,0:T(8,128)(2,1)S(1)}, u32[]{:S(2)}, u32[]{:S(2)}) collective-permute-start(bf16[2,256,256]{2,1,0:T(8,128)(2,1)S(1)} %collective-permute-done.refs_1_), channel_id=1, source_target_pairs={{0,32},{32,64},{64,96},{96,128},{128,160},{160,192},{192,224},{224... | collective-permute-start | bytes 786440 | tf_op jit(solution)/shard_map/ppermute | solution.py:232
  19.5 26.6 %all-to-all-start = ((bf16[4,2,256,256]{3,2,1,0:T(8,128)(2,1)}), bf16[4,2,256,256]{3,2,1,0:T(8,128)(2,1)S(1)}, u32[]{:S(2)}, u32[]{:S(2)}) async-start(bf16[4,2,256,256]{3,2,1,0:T(8,128)(2,1)} %broadcast_in_dim.8), calls=%async_computation | async-start | bytes 2097152 | tf_op jit(solution)/shard_map/all_to_all | solution.py:215
  23.6 24.9 %copy-start.4 = (bf16[2,256,256]{2,1,0:T(8,128)(2,1)}, bf16[2,256,256]{2,1,0:T(8,128)(2,1)S(1)}, u32[]{:S(2)}) copy-start(bf16[2,256,256]{2,1,0:T(8,128)(2,1)S(1)} %collective-permute-done.1.refs_2_.refs_0_) | copy-start | bytes 786436
  23.6 7.4 %collective-permute-start.2 = (bf16[2,256,256]{2,1,0:T(8,128)(2,1)S(1)}, bf16[2,256,256]{2,1,0:T(8,128)(2,1)S(1)}, u32[]{:S(2)}, u32[]{:S(2)}) collective-permute-start(bf16[2,256,256]{2,1,0:T(8,128)(2,1)S(1)} %collective-permute-done.1.refs_2_.refs_0_), channel_id=1, source_target_pairs={{0,32},{32,64},{64,96},{96,128},{128,160},{160,192},{192,224},{224... | collective-permute-start | bytes 786440 | tf_op jit(solution)/shard_map/ppermute | solution.py:232
  26.3 22.2 %copy-start.5 = (bf16[2,256,256]{2,1,0:T(8,128)(2,1)}, bf16[2,256,256]{2,1,0:T(8,128)(2,1)S(1)}, u32[]{:S(2)}) copy-start(bf16[2,256,256]{2,1,0:T(8,128)(2,1)S(1)} %collective-permute-done.9.refs_3_.refs_1_) | copy-start | bytes 786436
  26.3 8.6 %collective-permute-start.10 = (bf16[2,256,256]{2,1,0:T(8,128)(2,1)S(1)}, bf16[2,256,256]{2,1,0:T(8,128)(2,1)S(1)}, u32[]{:S(2)}, u32[]{:S(2)}) collective-permute-start(bf16[2,256,256]{2,1,0:T(8,128)(2,1)S(1)} %collective-permute-done.9.refs_3_.refs_1_), channel_id=1, source_target_pairs={{0,32},{32,64},{64,96},{96,128},{128,160},{160,192},{192,224},{224... | collective-permute-start | bytes 786440 | tf_op jit(solution)/shard_map/ppermute | solution.py:232
  31.1 17.5 %copy-start.6 = (bf16[2,256,256]{2,1,0:T(8,128)(2,1)}, bf16[2,256,256]{2,1,0:T(8,128)(2,1)S(1)}, u32[]{:S(2)}) copy-start(bf16[2,256,256]{2,1,0:T(8,128)(2,1)S(1)} %collective-permute-done.2.refs_4_.refs_2_) | copy-start | bytes 786436
  31.1 7.4 %collective-permute-start.3 = (bf16[2,256,256]{2,1,0:T(8,128)(2,1)S(1)}, bf16[2,256,256]{2,1,0:T(8,128)(2,1)S(1)}, u32[]{:S(2)}, u32[]{:S(2)}) collective-permute-start(bf16[2,256,256]{2,1,0:T(8,128)(2,1)S(1)} %collective-permute-done.2.refs_4_.refs_2_), channel_id=1, source_target_pairs={{0,32},{32,64},{64,96},{96,128},{128,160},{160,192},{192,224},{224... | collective-permute-start | bytes 786440 | tf_op jit(solution)/shard_map/ppermute | solution.py:232
  34.9 13.7 %copy-start.7 = (bf16[2,256,256]{2,1,0:T(8,128)(2,1)}, bf16[2,256,256]{2,1,0:T(8,128)(2,1)S(1)}, u32[]{:S(2)}) copy-start(bf16[2,256,256]{2,1,0:T(8,128)(2,1)S(1)} %collective-permute-done.10.refs_5_.refs_3_) | copy-start | bytes 786436
  34.9 8.3 %collective-permute-start.11 = (bf16[2,256,256]{2,1,0:T(8,128)(2,1)S(1)}, bf16[2,256,256]{2,1,0:T(8,128)(2,1)S(1)}, u32[]{:S(2)}, u32[]{:S(2)}) collective-permute-start(bf16[2,256,256]{2,1,0:T(8,128)(2,1)S(1)} %collective-permute-done.10.refs_5_.refs_3_), channel_id=1, source_target_pairs={{0,32},{32,64},{64,96},{96,128},{128,160},{160,192},{192,224},{224... | collective-permute-start | bytes 786440 | tf_op jit(solution)/shard_map/ppermute | solution.py:232
  38.5 10.1 %copy-start.8 = (bf16[2,256,256]{2,1,0:T(8,128)(2,1)}, bf16[2,256,256]{2,1,0:T(8,128)(2,1)S(1)}, u32[]{:S(2)}) copy-start(bf16[2,256,256]{2,1,0:T(8,128)(2,1)S(1)} %collective-permute-done.3.refs_6_.refs_4_) | copy-start | bytes 786436
  38.5 15.0 %collective-permute-start.4 = (bf16[2,256,256]{2,1,0:T(8,128)(2,1)S(1)}, bf16[2,256,256]{2,1,0:T(8,128)(2,1)S(1)}, u32[]{:S(2)}, u32[]{:S(2)}) collective-permute-start(bf16[2,256,256]{2,1,0:T(8,128)(2,1)S(1)} %collective-permute-done.3.refs_6_.refs_4_), channel_id=1, source_target_pairs={{0,32},{32,64},{64,96},{96,128},{128,160},{160,192},{192,224},{224... | collective-permute-start | bytes 786440 | tf_op jit(solution)/shard_map/ppermute | solution.py:232
  43.2 5.4 %copy-start.9 = (bf16[2,256,256]{2,1,0:T(8,128)(2,1)}, bf16[2,256,256]{2,1,0:T(8,128)(2,1)S(1)}, u32[]{:S(2)}) copy-start(bf16[2,256,256]{2,1,0:T(8,128)(2,1)S(1)} %collective-permute-done.11.refs_7_.refs_5_) | copy-start | bytes 786436
  43.2 12.2 %collective-permute-start.12 = (bf16[2,256,256]{2,1,0:T(8,128)(2,1)S(1)}, bf16[2,256,256]{2,1,0:T(8,128)(2,1)S(1)}, u32[]{:S(2)}, u32[]{:S(2)}) collective-permute-start(bf16[2,256,256]{2,1,0:T(8,128)(2,1)S(1)} %collective-permute-done.11.refs_7_.refs_5_), channel_id=1, source_target_pairs={{0,32},{32,64},{64,96},{96,128},{128,160},{160,192},{192,224},{224... | collective-permute-start | bytes 786440 | tf_op jit(solution)/shard_map/ppermute | solution.py:232
  48.6 33.0 %all-to-all-start.1 = ((bf16[4,4,2,256,256]{4,3,2,1,0:T(8,128)(2,1)}), bf16[4,4,2,256,256]{4,3,2,1,0:T(8,128)(2,1)}, u32[]{:S(2)}, u32[]{:S(2)}) async-start(bf16[4,4,2,256,256]{4,3,2,1,0:T(8,128)(2,1)} %broadcast_in_dim.9), calls=%async_computation.1 | async-start | bytes 8388608 | tf_op jit(solution)/shard_map/all_to_all | solution.py:215
  53.5 19.4 %copy-start.10 = (bf16[2,256,256]{2,1,0:T(8,128)(2,1)}, bf16[2,256,256]{2,1,0:T(8,128)(2,1)S(1)}, u32[]{:S(2)}) copy-start(bf16[2,256,256]{2,1,0:T(8,128)(2,1)S(1)} %collective-permute-done.4.refs_8_.refs_6_) | copy-start | bytes 786436
  53.5 7.5 %collective-permute-start.5 = (bf16[2,256,256]{2,1,0:T(8,128)(2,1)S(1)}, bf16[2,256,256]{2,1,0:T(8,128)(2,1)S(1)}, u32[]{:S(2)}, u32[]{:S(2)}) collective-permute-start(bf16[2,256,256]{2,1,0:T(8,128)(2,1)S(1)} %collective-permute-done.4.refs_8_.refs_6_), channel_id=1, source_target_pairs={{0,32},{32,64},{64,96},{96,128},{128,160},{160,192},{192,224},{224... | collective-permute-start | bytes 786440 | tf_op jit(solution)/shard_map/ppermute | solution.py:232
  55.4 17.5 %copy-start.11 = (bf16[2,256,256]{2,1,0:T(8,128)(2,1)}, bf16[2,256,256]{2,1,0:T(8,128)(2,1)S(1)}, u32[]{:S(2)}) copy-start(bf16[2,256,256]{2,1,0:T(8,128)(2,1)S(1)} %collective-permute-done.12.refs_9_.refs_7_) | copy-start | bytes 786436
  55.4 8.7 %collective-permute-start.13 = (bf16[2,256,256]{2,1,0:T(8,128)(2,1)S(1)}, bf16[2,256,256]{2,1,0:T(8,128)(2,1)S(1)}, u32[]{:S(2)}, u32[]{:S(2)}) collective-permute-start(bf16[2,256,256]{2,1,0:T(8,128)(2,1)S(1)} %collective-permute-done.12.refs_9_.refs_7_), channel_id=1, source_target_pairs={{0,32},{32,64},{64,96},{96,128},{128,160},{160,192},{192,224},{224... | collective-permute-start | bytes 786440 | tf_op jit(solution)/shard_map/ppermute | solution.py:232
  61.0 11.9 %copy-start.12 = (bf16[2,256,256]{2,1,0:T(8,128)(2,1)}, bf16[2,256,256]{2,1,0:T(8,128)(2,1)S(1)}, u32[]{:S(2)}) copy-start(bf16[2,256,256]{2,1,0:T(8,128)(2,1)S(1)} %collective-permute-done.5.refs_10_.refs_8_) | copy-start | bytes 786436
  61.0 7.5 %collective-permute-start.6 = (bf16[2,256,256]{2,1,0:T(8,128)(2,1)S(1)}, bf16[2,256,256]{2,1,0:T(8,128)(2,1)S(1)}, u32[]{:S(2)}, u32[]{:S(2)}) collective-permute-start(bf16[2,256,256]{2,1,0:T(8,128)(2,1)S(1)} %collective-permute-done.5.refs_10_.refs_8_), channel_id=1, source_target_pairs={{0,32},{32,64},{64,96},{96,128},{128,160},{160,192},{192,224},{224... | collective-permute-start | bytes 786440 | tf_op jit(solution)/shard_map/ppermute | solution.py:232
  64.1 8.8 %copy-start.13 = (bf16[2,256,256]{2,1,0:T(8,128)(2,1)}, bf16[2,256,256]{2,1,0:T(8,128)(2,1)S(1)}, u32[]{:S(2)}) copy-start(bf16[2,256,256]{2,1,0:T(8,128)(2,1)S(1)} %collective-permute-done.13.refs_11_.refs_9_) | copy-start | bytes 786436
  64.1 8.7 %collective-permute-start.14 = (bf16[2,256,256]{2,1,0:T(8,128)(2,1)S(1)}, bf16[2,256,256]{2,1,0:T(8,128)(2,1)S(1)}, u32[]{:S(2)}, u32[]{:S(2)}) collective-permute-start(bf16[2,256,256]{2,1,0:T(8,128)(2,1)S(1)} %collective-permute-done.13.refs_11_.refs_9_), channel_id=1, source_target_pairs={{0,32},{32,64},{64,96},{96,128},{128,160},{160,192},{192,224},{224... | collective-permute-start | bytes 786440 | tf_op jit(solution)/shard_map/ppermute | solution.py:232
  68.5 4.4 %copy-start.14 = (bf16[2,256,256]{2,1,0:T(8,128)(2,1)}, bf16[2,256,256]{2,1,0:T(8,128)(2,1)S(1)}, u32[]{:S(2)}) copy-start(bf16[2,256,256]{2,1,0:T(8,128)(2,1)S(1)} %collective-permute-done.6.refs_12_.refs_10_) | copy-start | bytes 786436
  68.5 7.6 %collective-permute-start.7 = (bf16[2,256,256]{2,1,0:T(8,128)(2,1)S(1)}, bf16[2,256,256]{2,1,0:T(8,128)(2,1)S(1)}, u32[]{:S(2)}, u32[]{:S(2)}) collective-permute-start(bf16[2,256,256]{2,1,0:T(8,128)(2,1)S(1)} %collective-permute-done.6.refs_12_.refs_10_), channel_id=1, source_target_pairs={{0,32},{32,64},{64,96},{96,128},{128,160},{160,192},{192,224},{224... | collective-permute-start | bytes 786440 | tf_op jit(solution)/shard_map/ppermute | solution.py:232
  72.9 8.7 %copy-start.1 = (bf16[2,256,256]{2,1,0:T(8,128)(2,1)}, bf16[2,256,256]{2,1,0:T(8,128)(2,1)S(1)}, u32[]{:S(2)}) copy-start(bf16[2,256,256]{2,1,0:T(8,128)(2,1)S(1)} %shard_map.29.refs_13_.refs_11_) | copy-start | bytes 786436
  72.9 9.3 %collective-permute-start.15 = (bf16[2,256,256]{2,1,0:T(8,128)(2,1)S(1)}, bf16[2,256,256]{2,1,0:T(8,128)(2,1)S(1)}, u32[]{:S(2)}, u32[]{:S(2)}) collective-permute-start(bf16[2,256,256]{2,1,0:T(8,128)(2,1)S(1)} %shard_map.29.refs_13_.refs_11_), channel_id=1, source_target_pairs={{0,32},{32,64},{64,96},{96,128},{128,160},{160,192},{192,224},{224... | collective-permute-start | bytes 786440 | tf_op jit(solution)/shard_map/ppermute | solution.py:232
  76.1 6.1 %copy-start.16 = (bf16[2,256,256]{2,1,0:T(8,128)(2,1)}, bf16[2,256,256]{2,1,0:T(8,128)(2,1)S(1)}, u32[]{:S(2)}) copy-start(bf16[2,256,256]{2,1,0:T(8,128)(2,1)S(1)} %collective-permute-done.7.refs_12_) | copy-start | bytes 786436
  76.1 12.7 %collective-permute-start.8 = (bf16[2,256,256]{2,1,0:T(8,128)(2,1)S(1)}, bf16[2,256,256]{2,1,0:T(8,128)(2,1)S(1)}, u32[]{:S(2)}, u32[]{:S(2)}) collective-permute-start(bf16[2,256,256]{2,1,0:T(8,128)(2,1)S(1)} %collective-permute-done.7.refs_12_), channel_id=1, source_target_pairs={{16,496},{48,16},{80,48},{112,80},{144,112},{176,144},{208,176},{2... | collective-permute-start | bytes 786440 | tf_op jit(solution)/shard_map/ppermute | solution.py:232
  82.3 1.9 %copy-start.2 = (bf16[2,256,256]{2,1,0:T(8,128)(2,1)}, bf16[2,256,256]{2,1,0:T(8,128)(2,1)S(1)}, u32[]{:S(2)}) copy-start(bf16[2,256,256]{2,1,0:T(8,128)(2,1)S(1)} %shard_map.31.refs_13_) | copy-start | bytes 786436
  82.3 7.1 %collective-permute-start.16 = (bf16[2,256,256]{2,1,0:T(8,128)(2,1)S(1)}, bf16[2,256,256]{2,1,0:T(8,128)(2,1)S(1)}, u32[]{:S(2)}, u32[]{:S(2)}) collective-permute-start(bf16[2,256,256]{2,1,0:T(8,128)(2,1)S(1)} %shard_map.31.refs_13_), channel_id=1, source_target_pairs={{16,496},{48,16},{80,48},{112,80},{144,112},{176,144},{208,176},{2... | collective-permute-start | bytes 786440 | tf_op jit(solution)/shard_map/ppermute | solution.py:232
  90.7 20.2 %copy-start.3 = (bf16[1,2,256,256]{3,2,1,0:T(8,128)(2,1)S(1)}, bf16[1,2,256,256]{3,2,1,0:T(8,128)(2,1)}, u32[]{:S(2)}) copy-start(bf16[1,2,256,256]{3,2,1,0:T(8,128)(2,1)} %param.3) | copy-start | bytes 786436
  90.7 3.9 %collective-permute-start.17 = (f32[2,256,256]{2,1,0:T(8,128)S(1)}, f32[2,256,256]{2,1,0:T(8,128)S(1)}, u32[]{:S(2)}, u32[]{:S(2)}) collective-permute-start(f32[2,256,256]{2,1,0:T(8,128)S(1)} %shard_map.34), channel_id=1, source_target_pairs={{0,16},{16,0},{1,17},{17,1},{2,18},{18,2},{3,19},{19,3},{4,20},{20... | collective-permute-start | bytes 1572872 | tf_op jit(solution)/shard_map/ppermute | solution.py:237
